TPU v7x, 32 devices: a whole 2x2x4 slice. The times are simulated.
32 devices in a mesh: seq: 4 (over y, core), fsdp: 8 (over z, x).
Axes of the slice: x: 2, y: 2, z: 4, core: 2. Of those that a mesh axis runs over, the one named last changes fastest.
Arguments:
- inputs: float32 [8, 1024, 2048], P('fsdp', 'seq'), may hold values from -9 to 9
- cotangent: float32 [8, 1024, 2048], P('fsdp', 'seq'), may hold values from -9 to 9
- lengths: int32 [8], P('fsdp'), may hold values from 0 to 1024, as said below
- positions: int32 [8, 1024], P('fsdp', 'seq'), may hold values from 0 to 1023, as said below
- query_key_value_weight: float32 [2048, 4096], P(('seq', 'fsdp')), may hold values from -0.0625 to 0.0625
- out_weight: float32 [2048, 2048], P(('seq', 'fsdp')), may hold values from -0.5 to 0.5
- gateup_weight: float32 [2048, 16384], P(('seq', 'fsdp')), may hold values from -0.09375 to 0.09375
- down_weight: float32 [2048, 8192], P(('seq', 'fsdp')), may hold values from -0.0625 to 0.0625
- norm_gains: float32 [2048, 2], P(('seq', 'fsdp')), may hold values from 0.8 to 6
- query_key_value_moment: float32 [2048, 4096], P(('seq', 'fsdp')), may hold values from -7.6293945e-05 to 7.6293945e-05
- output_weight_moment: float32 [2048, 2048], P(('seq', 'fsdp')), may hold values from -2.2888184e-05 to 2.2888184e-05
- gate_up_moment: float32 [2048, 16384], P(('seq', 'fsdp')), may hold values from -7.6293945e-05 to 7.6293945e-05
- down_weight_moment: float32 [2048, 8192], P(('seq', 'fsdp')), may hold values from -0.00010681152 to 0.00010681152
- norm_gains_moment: float32 [2048, 2], P(('seq', 'fsdp')), may hold values from -3.8146973e-05 to 3.8146973e-05
- query_key_value_variance: float32 [2048, 4096], P(('seq', 'fsdp')), may hold values from 3.0994415e-10 to 5.00679e-09
- out_second: float32 [2048, 2048], P(('seq', 'fsdp')), may hold values from 2.8014183e-11 to 4.5001508e-10
- gateup_second: float32 [2048, 16384], P(('seq', 'fsdp')), may hold values from 3.427267e-10 to 5.5134297e-09
- down_second: float32 [2048, 8192], P(('seq', 'fsdp')), may hold values from 7.4505807e-10 to 1.1920929e-08
- gains_second: float32 [2048, 2], P(('seq', 'fsdp')), may hold values from 7.748604e-11 to 1.2516975e-09
Outputs:
- layer_output: float32 [8, 1024, 2048], P('fsdp', 'seq')
- input_grad: float32 [8, 1024, 2048], P('fsdp', 'seq')
- grad_norm: float32 [], replicated
- qkv_next: float32 [2048, 4096], P(('seq', 'fsdp'))
- out_next: float32 [2048, 2048], P(('seq', 'fsdp'))
- gateup_next: float32 [2048, 16384], P(('seq', 'fsdp'))
- down_next: float32 [2048, 8192], P(('seq', 'fsdp'))
- gains_next: float32 [2048, 2], P(('seq', 'fsdp'))
- qkv_first_next: float32 [2048, 4096], P(('seq', 'fsdp'))
- out_first_next: float32 [2048, 2048], P(('seq', 'fsdp'))
- gateup_first_next: float32 [2048, 16384], P(('seq', 'fsdp'))
- down_first_next: float32 [2048, 8192], P(('seq', 'fsdp'))
- gains_first_next: float32 [2048, 2], P(('seq', 'fsdp'))
- qkv_second_next: float32 [2048, 4096], P(('seq', 'fsdp'))
- out_second_next: float32 [2048, 2048], P(('seq', 'fsdp'))
- gateup_second_next: float32 [2048, 16384], P(('seq', 'fsdp'))
- down_second_next: float32 [2048, 8192], P(('seq', 'fsdp'))
- gains_second_next: float32 [2048, 2], P(('seq', 'fsdp'))
Inputs may be any that keep to these rules, and one draw needn't show every extreme that they name: `lengths`: exactly 2 sequences have length 0, all others 1024. Within a sequence, positions count up by one from 0 at its first token and restart at 0 at some tokens.
All inputs are finite; a program needn't handle non-finite values.
Results may differ from a plain program's by a relative error of at most 0.025.
Values may be sent and summed in bfloat16 or wider, within the bound.
A program may use at most 768 MiB of HBM per device.

v0:
```python
import math

import jax
import jax.numpy as jnp
from jax import lax
from jax.sharding import PartitionSpec as P

QUERY_HEAD_COUNT = 8
KEY_VALUE_HEADS = 4
HEAD_SIZE = 256
FEED_UNITS = 8192
STEP = 10


NORM_EPSILON = 1e-06
ROPE_BASE = 1000042.0
MASKED_SCORE = -1000000000.0
CLIP_NORM = 1.0
BETA_ONE = 0.9
BETA_TWO = 0.95
ADAM_EPSILON = 1e-08
DECAY_MATRIX = 0.1
RATE_MATRIX = 0.02
RATE_OUTPUT = 0.1
RATE_GAIN = 1.0


def rotary_tables(positions, width):
    half = width // 2
    freqs = jnp.exp(-(jnp.arange(half, dtype=jnp.float32) * 2.0 / width) * math.log(ROPE_BASE))
    angles = positions.astype(jnp.float32)[..., None] * freqs
    angles = jnp.concatenate([angles, angles], -1)
    return (jnp.cos(angles)[..., None, :], jnp.sin(angles)[..., None, :])


def rotate_half(value_rows):
    half = value_rows.shape[-1] // 2
    return jnp.concatenate([-value_rows[..., half:], value_rows[..., :half]], -1)


def apply_rotary(value_rows, cosine_table, sine_table):
    return value_rows * cosine_table + rotate_half(value_rows) * sine_table


def rope_back(grads, cosine_table, sine_table):
    return grads * cosine_table - rotate_half(grads * sine_table)


def rms_normalize(value_rows):
    inverse_scale = lax.rsqrt(jnp.mean(value_rows * value_rows, -1, keepdims=True) + NORM_EPSILON)
    return (value_rows * inverse_scale, inverse_scale)


def norm_backward(normed_gradient, unit_input, inverse_scale, norm_gain_vector):
    unit_input_gradient = normed_gradient * norm_gain_vector
    backward_pass = inverse_scale * (
        unit_input_gradient
        - unit_input * jnp.mean(unit_input_gradient * unit_input, -1, keepdims=True)
    )
    gradient_term = jnp.sum((normed_gradient * unit_input).reshape(-1, unit_input.shape[-1]), 0)
    return (backward_pass, gradient_term)


def adam_step(weight, grad, first, second, factor, rate, decay):
    clipped = grad * factor
    first_new = BETA_ONE * first + (1.0 - BETA_ONE) * clipped
    second_new = BETA_TWO * second + (1.0 - BETA_TWO) * clipped * clipped
    corr_one = 1.0 - BETA_ONE**STEP
    corr_two = 1.0 - BETA_TWO**STEP
    update = first_new / corr_one / (jnp.sqrt(second_new / corr_two) + ADAM_EPSILON)
    return (weight - rate * (update + decay * weight), first_new, second_new)


def transpose_product(left, right):
    return lax.dot_general(
        left, right, (((0,), (0,)), ((), ())), preferred_element_type=jnp.float32
    )


def gather_rows(pieces):
    inner = (
        lax.all_gather(pieces[0], "fsdp", axis=0, tiled=True),
        lax.all_gather(pieces[1], "fsdp", axis=0, tiled=True),
        lax.all_gather(pieces[2], "fsdp", axis=0, tiled=True),
        lax.all_gather(pieces[3], "fsdp", axis=0, tiled=True),
        lax.all_gather(pieces[4], "fsdp", axis=0, tiled=True),
    )
    return (
        lax.all_gather(inner[0], "seq", axis=0, tiled=True),
        lax.all_gather(inner[1], "seq", axis=0, tiled=True),
        lax.all_gather(inner[2], "seq", axis=0, tiled=True),
        lax.all_gather(inner[3], "seq", axis=0, tiled=True),
        lax.all_gather(inner[4], "seq", axis=0, tiled=True),
    )


def reduce_rows(terms):
    inner = (
        lax.psum_scatter(
            terms[0].astype(jnp.bfloat16), "seq", scatter_dimension=0, tiled=True
        ).astype(jnp.float32),
        lax.psum_scatter(
            terms[1].astype(jnp.bfloat16), "seq", scatter_dimension=0, tiled=True
        ).astype(jnp.float32),
        lax.psum_scatter(
            terms[2].astype(jnp.bfloat16), "seq", scatter_dimension=0, tiled=True
        ).astype(jnp.float32),
    )
    return (
        lax.psum_scatter(
            inner[0].astype(jnp.bfloat16), "fsdp", scatter_dimension=0, tiled=True
        ).astype(jnp.float32),
        lax.psum_scatter(
            inner[1].astype(jnp.bfloat16), "fsdp", scatter_dimension=0, tiled=True
        ).astype(jnp.float32),
        lax.psum_scatter(
            inner[2].astype(jnp.bfloat16), "fsdp", scatter_dimension=0, tiled=True
        ).astype(jnp.float32),
    )


def reduce_product(term_rows, total_rows):
    inner = lax.psum_scatter(
        term_rows(jnp.int32(0), total_rows // lax.axis_size("seq") * lax.axis_size("seq")).astype(
            jnp.bfloat16
        ),
        "seq",
        scatter_dimension=0,
        tiled=True,
    )
    return lax.psum_scatter(inner, "fsdp", scatter_dimension=0, tiled=True).astype(jnp.float32)


def shards(
    inputs,
    cotangent,
    lengths,
    positions,
    query_key_value_weight,
    out_weight,
    gateup_weight,
    down_weight,
    norm_gains,
    query_key_value_moment,
    output_weight_moment,
    gate_up_moment,
    down_weight_moment,
    norm_gains_moment,
    query_key_value_variance,
    out_second,
    gateup_second,
    down_second,
    gains_second,
):
    sequence_batch, device_local, width = inputs.shape
    partition_count = lax.axis_size("seq")
    full = device_local * partition_count
    tokens_here = sequence_batch * device_local
    query_width = QUERY_HEAD_COUNT * HEAD_SIZE
    key_width = KEY_VALUE_HEADS * HEAD_SIZE
    heads_here = QUERY_HEAD_COUNT // partition_count
    local_key_value = KEY_VALUE_HEADS // partition_count
    shard_portion = QUERY_HEAD_COUNT // KEY_VALUE_HEADS
    factor = 1.0 / math.sqrt(HEAD_SIZE)
    pieces = (
        query_key_value_weight.astype(jnp.bfloat16),
        out_weight.astype(jnp.bfloat16),
        gateup_weight.astype(jnp.bfloat16),
        down_weight.astype(jnp.bfloat16),
        norm_gains.astype(jnp.bfloat16),
    )
    qkv_low, out_low, gateup_low, down_low, gains_low = gather_rows(pieces)
    first_norm_gain = gains_low[:, 0].astype(jnp.float32)
    second_norm_gain = gains_low[:, 1].astype(jnp.float32)
    first_unit_input, first_inverse_scale = rms_normalize(inputs)
    first_normed = (first_unit_input * first_norm_gain).astype(jnp.bfloat16)
    merged_heads = jnp.einsum(
        "std,dc->stc", first_normed, qkv_low, preferred_element_type=jnp.float32
    )
    cosine_table, sine_table = rotary_tables(positions, HEAD_SIZE)
    queries = apply_rotary(
        merged_heads[..., :query_width].reshape(
            sequence_batch, device_local, QUERY_HEAD_COUNT, HEAD_SIZE
        ),
        cosine_table,
        sine_table,
    ).astype(jnp.bfloat16)
    key_rows = apply_rotary(
        merged_heads[..., query_width : query_width + key_width].reshape(
            sequence_batch, device_local, KEY_VALUE_HEADS, HEAD_SIZE
        ),
        cosine_table,
        sine_table,
    ).astype(jnp.bfloat16)
    value_rows = (
        merged_heads[..., query_width + key_width :]
        .reshape(sequence_batch, device_local, KEY_VALUE_HEADS, HEAD_SIZE)
        .astype(jnp.bfloat16)
    )
    query_heads, key_heads, value_heads = (
        lax.all_to_all(queries, "seq", split_axis=2, concat_axis=1, tiled=True),
        lax.all_to_all(key_rows, "seq", split_axis=2, concat_axis=1, tiled=True),
        lax.all_to_all(value_rows, "seq", split_axis=2, concat_axis=1, tiled=True),
    )
    query_heads = query_heads.reshape(
        sequence_batch, full, local_key_value, shard_portion, HEAD_SIZE
    )
    block = 512
    blocks = full // block
    key_spot = jnp.arange(full)
    key_live = key_spot[None, :] < lengths[:, None]

    def block_masks(index):
        query_spot = index * block + jnp.arange(block)
        causal = key_spot[None, :] <= query_spot[:, None]
        visible = causal[None, None, None] & key_live[:, None, None, None, :]
        query_live = query_spot[None, :] < lengths[:, None]
        return (visible, query_live[:, :, None, None, None])

    def block_scores(index, visible):
        rows = query_heads[:, index * block : (index + 1) * block]
        scores = (
            jnp.einsum("sqkgd,sjkd->skgqj", rows, key_heads, preferred_element_type=jnp.float32)
            * factor
        )
        return (rows, jnp.where(visible, scores, MASKED_SCORE))

    outputs, peaks, totals = ([], [], [])
    for index in range(blocks):
        visible, query_live = block_masks(index)
        rows, scores = block_scores(index, visible)
        peak = jnp.max(scores, -1, keepdims=True)
        expo = jnp.exp(scores - peak)
        total = jnp.sum(expo, -1, keepdims=True)
        probs = (expo / total).astype(jnp.bfloat16)
        result = jnp.einsum(
            "skgqj,sjkd->sqkgd", probs, value_heads, preferred_element_type=jnp.float32
        )
        outputs.append((result * query_live).astype(jnp.bfloat16))
        peaks.append(peak)
        totals.append(total)
    heads_out = jnp.concatenate(outputs, 1).reshape(sequence_batch, full, heads_here, HEAD_SIZE)
    heads_tok = lax.all_to_all(heads_out, "seq", split_axis=1, concat_axis=2, tiled=True).reshape(
        sequence_batch, device_local, query_width
    )
    attended = jnp.einsum("stj,dj->std", heads_tok, out_low, preferred_element_type=jnp.float32)
    residual_hidden = inputs + attended
    second_unit_input, second_inverse_scale = rms_normalize(residual_hidden)
    second_normed = (second_unit_input * second_norm_gain).astype(jnp.bfloat16)
    gateup = jnp.einsum(
        "std,dc->stc", second_normed, gateup_low, preferred_element_type=jnp.float32
    )
    gate = gateup[..., :FEED_UNITS]
    upper = gateup[..., FEED_UNITS:]
    sig = jax.nn.sigmoid(gate)
    act = (gate * sig * upper).astype(jnp.bfloat16)
    layer_output = residual_hidden + jnp.einsum(
        "stf,df->std", act, down_low, preferred_element_type=jnp.float32
    )
    dout_low = cotangent.astype(jnp.bfloat16)
    dact = jnp.einsum("std,df->stf", dout_low, down_low, preferred_element_type=jnp.float32)
    dgate = dact * upper * sig * (1.0 + gate * (1.0 - sig))
    dupper = dact * gate * sig
    dgateup = jnp.concatenate([dgate, dupper], -1).astype(jnp.bfloat16)
    second_normed_gradient = jnp.einsum(
        "stc,dc->std", dgateup, gateup_low, preferred_element_type=jnp.float32
    )
    backward_second_norm, second_gain_gradient = norm_backward(
        second_normed_gradient, second_unit_input, second_inverse_scale, second_norm_gain
    )
    dhidden = cotangent + backward_second_norm
    flat_normed_two = second_normed.reshape(tokens_here, width)
    flat_dout = dout_low.reshape(tokens_here, width)
    flat_dgateup = dgateup.reshape(tokens_here, 2 * FEED_UNITS)
    flat_act = act.reshape(tokens_here, FEED_UNITS)

    def mlp_terms(start, count):
        return jnp.concatenate(
            [
                transpose_product(flat_normed_two, flat_dgateup),
                transpose_product(flat_dout, flat_act),
            ],
            1,
        )

    mlp_grads = reduce_product(mlp_terms, width)
    grad_gateup = mlp_grads[:, : 2 * FEED_UNITS]
    grad_down = mlp_grads[:, 2 * FEED_UNITS :]
    dattended = dhidden.astype(jnp.bfloat16)
    flat_dattended = dattended.reshape(tokens_here, width)
    grad_out_term = transpose_product(flat_dattended, heads_tok.reshape(tokens_here, query_width))
    dheads = jnp.einsum("std,dj->stj", dattended, out_low, preferred_element_type=jnp.float32)
    dheads = dheads.astype(jnp.bfloat16).reshape(
        sequence_batch, device_local, QUERY_HEAD_COUNT, HEAD_SIZE
    )
    dheads_h = lax.all_to_all(dheads, "seq", split_axis=2, concat_axis=1, tiled=True).reshape(
        sequence_batch, full, local_key_value, shard_portion, HEAD_SIZE
    )
    dquery_blocks = []
    dkey_sum = jnp.zeros((sequence_batch, full, local_key_value, HEAD_SIZE), jnp.float32)
    dvalue_sum = jnp.zeros((sequence_batch, full, local_key_value, HEAD_SIZE), jnp.float32)
    for index in range(blocks):
        visible, query_live = block_masks(index)
        rows, scores = block_scores(index, visible)
        probs = jnp.exp(scores - peaks[index]) / totals[index]
        douts = dheads_h[:, index * block : (index + 1) * block] * query_live.astype(jnp.bfloat16)
        dvalue_sum = dvalue_sum + jnp.einsum(
            "skgqj,sqkgd->sjkd",
            probs.astype(jnp.bfloat16),
            douts,
            preferred_element_type=jnp.float32,
        )
        dprobs = jnp.einsum(
            "sqkgd,sjkd->skgqj", douts, value_heads, preferred_element_type=jnp.float32
        )
        inner = jnp.sum(probs * dprobs, -1, keepdims=True)
        dscores = jnp.where(
            visible, (probs * (dprobs - inner)).astype(jnp.bfloat16), jnp.zeros((), jnp.bfloat16)
        )
        dquery_part = (
            jnp.einsum("skgqj,sjkd->sqkgd", dscores, key_heads, preferred_element_type=jnp.float32)
            * factor
        )
        dquery_blocks.append(dquery_part.astype(jnp.bfloat16))
        dkey_sum = (
            dkey_sum
            + jnp.einsum("skgqj,sqkgd->sjkd", dscores, rows, preferred_element_type=jnp.float32)
            * factor
        )
    dquery_h = jnp.concatenate(dquery_blocks, 1).reshape(
        sequence_batch, full, heads_here, HEAD_SIZE
    )
    dquery_t, dkey_t, dvalue_t = (
        lax.all_to_all(dquery_h, "seq", split_axis=1, concat_axis=2, tiled=True),
        lax.all_to_all(
            dkey_sum.astype(jnp.bfloat16), "seq", split_axis=1, concat_axis=2, tiled=True
        ),
        lax.all_to_all(
            dvalue_sum.astype(jnp.bfloat16), "seq", split_axis=1, concat_axis=2, tiled=True
        ),
    )
    dquery_t = rope_back(dquery_t.astype(jnp.float32), cosine_table, sine_table).reshape(
        sequence_batch, device_local, query_width
    )
    dkey_t = rope_back(dkey_t.astype(jnp.float32), cosine_table, sine_table).reshape(
        sequence_batch, device_local, key_width
    )
    dfused = jnp.concatenate(
        [
            dquery_t,
            dkey_t,
            dvalue_t.reshape(sequence_batch, device_local, key_width).astype(jnp.float32),
        ],
        -1,
    ).astype(jnp.bfloat16)
    first_normed_gradient = jnp.einsum(
        "stc,dc->std", dfused, qkv_low, preferred_element_type=jnp.float32
    )
    backward_first_norm, first_gain_gradient = norm_backward(
        first_normed_gradient, first_unit_input, first_inverse_scale, first_norm_gain
    )
    input_grad = dhidden + backward_first_norm
    grad_qkv_term = transpose_product(
        first_normed.reshape(tokens_here, width),
        dfused.reshape(tokens_here, query_width + 2 * key_width),
    )
    gains_term = jnp.stack([first_gain_gradient, second_gain_gradient], 1)
    grad_qkv, grad_out, grad_gains = reduce_rows((grad_qkv_term, grad_out_term, gains_term))
    local_squares = (
        jnp.sum(grad_qkv * grad_qkv)
        + jnp.sum(grad_out * grad_out)
        + jnp.sum(grad_gateup * grad_gateup)
        + jnp.sum(grad_down * grad_down)
        + jnp.sum(grad_gains * grad_gains)
    )
    grad_norm = jnp.sqrt(lax.psum(local_squares, ("seq", "fsdp")))
    clip_factor = CLIP_NORM / jnp.maximum(grad_norm, CLIP_NORM)
    qkv_next, qkv_first_next, qkv_second_next = adam_step(
        query_key_value_weight,
        grad_qkv,
        query_key_value_moment,
        query_key_value_variance,
        clip_factor,
        RATE_MATRIX,
        DECAY_MATRIX,
    )
    out_next, out_first_next, out_second_next = adam_step(
        out_weight,
        grad_out,
        output_weight_moment,
        out_second,
        clip_factor,
        RATE_OUTPUT,
        DECAY_MATRIX,
    )
    gateup_next, gateup_first_next, gateup_second_next = adam_step(
        gateup_weight,
        grad_gateup,
        gate_up_moment,
        gateup_second,
        clip_factor,
        RATE_MATRIX,
        DECAY_MATRIX,
    )
    down_next, down_first_next, down_second_next = adam_step(
        down_weight,
        grad_down,
        down_weight_moment,
        down_second,
        clip_factor,
        RATE_MATRIX,
        DECAY_MATRIX,
    )
    gains_next, gains_first_next, gains_second_next = adam_step(
        norm_gains, grad_gains, norm_gains_moment, gains_second, clip_factor, RATE_GAIN, 0.0
    )
    return (
        layer_output,
        input_grad,
        grad_norm,
        qkv_next,
        out_next,
        gateup_next,
        down_next,
        gains_next,
        qkv_first_next,
        out_first_next,
        gateup_first_next,
        down_first_next,
        gains_first_next,
        qkv_second_next,
        out_second_next,
        gateup_second_next,
        down_second_next,
        gains_second_next,
    )


def solution(mesh):
    return jax.shard_map(
        shards,
        mesh=mesh,
        in_specs=(
            P("fsdp", "seq", None),
            P("fsdp", "seq", None),
            P("fsdp"),
            P("fsdp", "seq"),
            P(("seq", "fsdp"), None),
            P(("seq", "fsdp"), None),
            P(("seq", "fsdp"), None),
            P(("seq", "fsdp"), None),
            P(("seq", "fsdp"), None),
            P(("seq", "fsdp"), None),
            P(("seq", "fsdp"), None),
            P(("seq", "fsdp"), None),
            P(("seq", "fsdp"), None),
            P(("seq", "fsdp"), None),
            P(("seq", "fsdp"), None),
            P(("seq", "fsdp"), None),
            P(("seq", "fsdp"), None),
            P(("seq", "fsdp"), None),
            P(("seq", "fsdp"), None),
        ),
        out_specs=(
            P("fsdp", "seq", None),
            P("fsdp", "seq", None),
            P(),
            P(("seq", "fsdp"), None),
            P(("seq", "fsdp"), None),
            P(("seq", "fsdp"), None),
            P(("seq", "fsdp"), None),
            P(("seq", "fsdp"), None),
            P(("seq", "fsdp"), None),
            P(("seq", "fsdp"), None),
            P(("seq", "fsdp"), None),
            P(("seq", "fsdp"), None),
            P(("seq", "fsdp"), None),
            P(("seq", "fsdp"), None),
            P(("seq", "fsdp"), None),
            P(("seq", "fsdp"), None),
            P(("seq", "fsdp"), None),
            P(("seq", "fsdp"), None),
        ),
        check_vma=False,
    )
```

profile of v0, /device:TPU:0, one launch (start us, length us, event | category | flops | bytes accessed | tf_op | source)
XLA Modules:
  0.0 3103.2 jit_solution(14987145242741657039)
XLA Ops:
  16.3 70.5 %all-gather.10.cloned.1.call-done = bf16[512,4096]{1,0:T(8,128)(2,1)} async-done(((bf16[64,4096]{1,0:T(8,128)(2,1)}), bf16[512,4096]{1,0:T(8,128)(2,1)}) %all-gather.10.cloned.1.call-update) | async-done | bytes 4194320 | tf_op jit(solution)/shard_map/all_gather | solution.py:82
  86.9 50.2 %all-gather.14.cloned.1.call-done = bf16[512,2048]{1,0:T(8,128)(2,1)} async-done(((bf16[64,2048]{1,0:T(8,128)(2,1)}), bf16[512,2048]{1,0:T(8,128)(2,1)}) %all-gather.14.cloned.1.call-update) | async-done | bytes 2097168 | tf_op jit(solution)/shard_map/all_gather | solution.py:83
  137.2 228.8 %all-gather.18.cloned.1.call-done = bf16[512,16384]{1,0:T(8,128)(2,1)} async-done(((bf16[64,16384]{1,0:T(8,128)(2,1)}), bf16[512,16384]{1,0:T(8,128)(2,1)}) %all-gather.18.cloned.1.call-update) | async-done | bytes 16777232 | tf_op jit(solution)/shard_map/all_gather | solution.py:84
  366.0 125.6 %all-gather.22.cloned.1.call-done = bf16[512,8192]{1,0:T(8,128)(2,1)} async-done(((bf16[64,8192]{1,0:T(8,128)(2,1)}), bf16[512,8192]{1,0:T(8,128)(2,1)}) %all-gather.22.cloned.1.call-update) | async-done | bytes 8388624 | tf_op jit(solution)/shard_map/all_gather | solution.py:85
  492.4 17.5 all-gather
  516.5 80.8 %all-gather.12.cloned.1.call-done = bf16[2048,4096]{1,0:T(8,128)(2,1)} async-done(((bf16[512,4096]{1,0:T(8,128)(2,1)}), bf16[2048,4096]{1,0:T(8,128)(2,1)}) %all-gather.12.cloned.1.call-update) | async-done | bytes 16777232 | tf_op jit(solution)/shard_map/all_gather | solution.py:89
  617.1 22.4 all-to-all-done.2
  689.2 18.3 all_to_all.102
  721.3 352.5 %all-gather.20.cloned.1.call-done = bf16[2048,16384]{1,0:T(8,128)(2,1)} async-done(((bf16[512,16384]{1,0:T(8,128)(2,1)}), bf16[2048,16384]{1,0:T(8,128)(2,1)}) %all-gather.20.cloned.1.call-update) | async-done | bytes 67108880 | tf_op jit(solution)/shard_map/all_gather | solution.py:91
  1073.8 41.2 %convolution_bitcast_fusion = f32[1,256,16384]{2,1,0:T(8,128)} fusion(bf16[2048,16384]{1,0:T(8,128)(2,1)} %all-gather.20.cloned.1.call-done, f32[1,256,2048]{2,1,0:T(8,128)} %get-tuple-element.59, f32[2048]{0:T(1024)S(1)} %bitcast.441, f32[256]{0:T(256)S(1)} %add_rsqrt_fusion), kind=kOutput, calls=%fused_computation.3 | convolution fusion | flops 17181442048 | bytes 85992448 | tf_op jit(solution)/shard_map/std,dc->stc/dot_general | solution.py:250
  1115.0 161.9 %all-gather.24.cloned.1.call-done = bf16[2048,8192]{1,0:T(8,128)(2,1)} async-done(((bf16[512,8192]{1,0:T(8,128)(2,1)}), bf16[2048,8192]{1,0:T(8,128)(2,1)}) %all-gather.24.cloned.1.call-update) | async-done | bytes 33554448 | tf_op jit(solution)/shard_map/all_gather | solution.py:92
  1276.9 28.5 fusion.12
  1305.4 30.1 fusion.33
  1346.0 17.8 all_to_all.103
  1510.5 18.7 convert_bitcast_fusion
  1529.3 30.4 convolution_convert_fusion
  1559.7 70.6 %pad_maximum_fusion = bf16[2048,24576]{1,0:T(8,128)(2,1)} fusion(bf16[2048,8192]{1,0:T(8,128)(2,1)} %convert_bitcast_fusion, bf16[2048,16384]{1,0:T(8,128)(2,1)} %convolution_convert_fusion), kind=kLoop, calls=%fused_computation | loop fusion | flops 201326592 | bytes 201326592 | tf_op jit(solution)/shard_map/concatenate | solution.py:278
  1631.7 85.1 %reduce-scatter.13.cloned.1.call-done = bf16[512,4096]{1,0:T(8,128)(2,1)} async-done(((bf16[2048,4096]{1,0:T(8,128)(2,1)}), bf16[512,4096]{1,0:T(8,128)(2,1)}) %reduce-scatter.13.cloned.1.call-update) | async-done | bytes 4194320 | tf_op jit(solution)/shard_map/reduce_scatter | solution.py:99
  1716.9 671.3 %reduce-scatter.21.cloned.1.call-done = bf16[512,24576]{1,0:T(8,128)(2,1)} async-done(((bf16[2048,24576]{1,0:T(8,128)(2,1)}), bf16[512,24576]{1,0:T(8,128)(2,1)}) %reduce-scatter.21.cloned.1.call-update) | async-done | bytes 25165840 | tf_op jit(solution)/shard_map/reduce_scatter | solution.py:123
  2407.2 45.3 %reduce-scatter.27.cloned.1.call-done = bf16[64,2]{1,0:T(8,128)(2,1)} async-done(((bf16[512,2]{1,0:T(8,128)(2,1)}), bf16[64,2]{1,0:T(8,128)(2,1)}) %reduce-scatter.27.cloned.1.call-update) | async-done | bytes 272
  2453.9 68.7 %reduce-scatter.19.cloned.1.call-done = bf16[64,2048]{1,0:T(8,128)(2,1)} async-done(((bf16[512,2048]{1,0:T(8,128)(2,1)}), bf16[64,2048]{1,0:T(8,128)(2,1)}) %reduce-scatter.19.cloned.1.call-update) | async-done | bytes 262160 | tf_op jit(solution)/shard_map/reduce_scatter | solution.py:113
  2524.3 88.7 %reduce-scatter.15.cloned.1.call-done = bf16[64,4096]{1,0:T(8,128)(2,1)} async-done(((bf16[512,4096]{1,0:T(8,128)(2,1)}), bf16[64,4096]{1,0:T(8,128)(2,1)}) %reduce-scatter.15.cloned.1.call-update) | async-done | bytes 524304 | tf_op jit(solution)/shard_map/reduce_scatter | solution.py:110
  2616.2 404.5 %reduce-scatter.23.cloned.1.call-done = bf16[64,24576]{1,0:T(8,128)(2,1)} async-done(((bf16[512,24576]{1,0:T(8,128)(2,1)}), bf16[64,24576]{1,0:T(8,128)(2,1)}) %reduce-scatter.23.cloned.1.call-update) | async-done | bytes 3145744 | tf_op jit(solution)/shard_map/reduce_scatter | solution.py:131
  3034.2 39.3 %psum.7 = f32[]{:T(128)} all-reduce(f32[]{:T(128)S(6)} %add.208), channel_id=1, replica_groups=mesh['seq'=4,'fsdp'=8] {'seq','fsdp'}, use_global_device_ids=true, to_apply=%region_25.26 | all-reduce | flops 1 | bytes 8 | tf_op jit(solution)/shard_map/psum | solution.py:376
  (263 shorter events, 313.5 us)
Async XLA Ops:
  7.2 79.7 %all-gather.10.cloned.1.call-start = ((), (), s32[]{:S(2)}) async-start(), calls=%async_computation.16 | async-start | bytes 4718592 | tf_op jit(solution)/shard_map/all_gather | solution.py:82
  9.3 127.8 %all-gather.14.cloned.1.call-start = ((), (), s32[]{:S(2)}) async-start(), calls=%async_computation.18 | async-start | bytes 2359296 | tf_op jit(solution)/shard_map/all_gather | solution.py:83
  11.2 354.8 %all-gather.18.cloned.1.call-start = ((), (), s32[]{:S(2)}) async-start(), calls=%async_computation.20 | async-start | bytes 18874368 | tf_op jit(solution)/shard_map/all_gather | solution.py:84
  15.1 476.5 %all-gather.22.cloned.1.call-start = ((), (), s32[]{:S(2)}) async-start(), calls=%async_computation.22 | async-start | bytes 9437184 | tf_op jit(solution)/shard_map/all_gather | solution.py:85
  16.3 581.0 %all-gather.12.cloned.1.call-start = ((), (), s32[]{:S(2)}) async-start(), calls=%async_computation.17 | async-start | bytes 20971520 | tf_op jit(solution)/shard_map/all_gather | solution.py:89
  86.9 624.2 %all-gather.16.cloned.1.call-start = ((), (), s32[]{:S(2)}) async-start(), calls=%async_computation.19 | async-start | bytes 10485760 | tf_op jit(solution)/shard_map/all_gather | solution.py:90
  137.2 936.6 %all-gather.20.cloned.1.call-start = ((), (), s32[]{:S(2)}) async-start(), calls=%async_computation.21 | async-start | bytes 83886080 | tf_op jit(solution)/shard_map/all_gather | solution.py:91
  366.0 910.9 %all-gather.24.cloned.1.call-start = ((), (), s32[]{:S(2)}) async-start(), calls=%async_computation.23 | async-start | bytes 41943040 | tf_op jit(solution)/shard_map/all_gather | solution.py:92
  609.1 30.4 all-to-all-start.2
  639.4 19.0 all-to-all-start.1
  658.4 19.2 all-to-all-start
  1073.8 203.1 %copy-start.12 = (f32[1,256,2048]{2,1,0:T(8,128)S(1)}, f32[1,256,2048]{2,1,0:T(8,128)}, u32[]{:S(2)}) copy-start(f32[1,256,2048]{2,1,0:T(8,128)} %param.20) | copy-start | bytes 6291460
  1338.9 151.7 %copy-start.1 = (f32[1,256,2048]{2,1,0:T(8,128)}, f32[1,256,2048]{2,1,0:T(8,128)S(1)}, u32[]{:S(2)}) copy-start(f32[1,256,2048]{2,1,0:T(8,128)S(1)} %fusion.41) | copy-start | bytes 6291460
  1396.2 27.4 all-to-all-start.7
  1423.6 13.1 all-to-all-start.6
  1436.7 23.1 all-to-all-start.5
  1440.9 189.5 %reduce-scatter.25.cloned.1.call-start = ((), (), s32[]{:S(2)}) async-start(), calls=%async_computation.30 | async-start | bytes 655360
  1490.6 140.6 %reduce-scatter.17.cloned.1.call-start = ((), (), s32[]{:S(2)}) async-start(), calls=%async_computation.26 | async-start | bytes 10485760 | tf_op jit(solution)/shard_map/reduce_scatter | solution.py:102
  1497.6 219.3 %reduce-scatter.13.cloned.1.call-start = ((), (), s32[]{:S(2)}) async-start(), calls=%async_computation.24 | async-start | bytes 20971520 | tf_op jit(solution)/shard_map/reduce_scatter | solution.py:99
  1509.0 879.3 %reduce-scatter.21.cloned.1.call-start = ((), (), s32[]{:S(2)}) async-start(), calls=%async_computation.28 | async-start | bytes 125829120 | tf_op jit(solution)/shard_map/reduce_scatter | solution.py:123
  1630.4 822.2 %reduce-scatter.27.cloned.1.call-start = ((), (), s32[]{:S(2)}) async-start(), calls=%async_computation.31 | async-start | bytes 147456
  1631.1 891.5 %reduce-scatter.19.cloned.1.call-start = ((), (), s32[]{:S(2)}) async-start(), calls=%async_computation.27 | async-start | bytes 2359296 | tf_op jit(solution)/shard_map/reduce_scatter | solution.py:113
  1631.7 981.3 %reduce-scatter.15.cloned.1.call-start = ((), (), s32[]{:S(2)}) async-start(), calls=%async_computation.25 | async-start | bytes 4718592 | tf_op jit(solution)/shard_map/reduce_scatter | solution.py:110
  1716.9 1303.8 %reduce-scatter.23.cloned.1.call-start = ((), (), s32[]{:S(2)}) async-start(), calls=%async_computation.29 | async-start | bytes 28311552 | tf_op jit(solution)/shard_map/reduce_scatter | solution.py:131
  (50 other events, 815.6 us)
Sparse Core Ops, SparseCore 0:
  10.7 76.0 all-gather.9
  89.5 47.5 all-gather.13
  139.8 226.0 all-gather.17
  368.5 123.1 all-gather.21
  493.1 104.1 all-gather.11
  598.7 80.7 all-gather.15
  681.0 392.7 all-gather.19
  1075.4 201.5 all-gather.23
  1490.7 23.0 reduce-scatter.24
  1516.4 71.7 reduce-scatter.16
  1590.7 126.1 reduce-scatter.12
  1719.5 668.7 reduce-scatter.20
  2391.6 60.9 reduce-scatter.26
  2455.9 66.6 reduce-scatter.18
  2526.1 86.8 reduce-scatter.14
  2617.2 403.4 reduce-scatter.22
where the time goes:
time: 3110 us; the launch traced here: 3100 us
  waiting for transfers between devices  2480 us (80%)
  matrix products  257 us (8%)
  other arithmetic  153 us (5%)
  blocking collectives  98 us (3%)
  local copies, waits for them, and re-layouts  72 us (2%)
    reduce_scatter x1, waiting for transfers between devices, reduce_product(): lax.psum_scatter(term_rows(jnp.int32(0), total_rows // lax.axis_size('seq...  671 us
    reduce_scatter x1, waiting for transfers between devices, reduce_product(): lax.psum_scatter(inner, 'fsdp', scatter_dimension=0, tiled=True)  405 us
    all_gather x1, waiting for transfers between devices, gather_rows(): lax.all_gather(inner[2], 'seq', axis=0, tiled=True)  353 us
    all_gather x1, waiting for transfers between devices, gather_rows(): lax.all_gather(pieces[2], 'fsdp', axis=0, tiled=True)  229 us
    all_gather x1, waiting for transfers between devices, gather_rows(): lax.all_gather(inner[3], 'seq', axis=0, tiled=True)  162 us
    all_gather x1, waiting for transfers between devices, gather_rows(): lax.all_gather(pieces[3], 'fsdp', axis=0, tiled=True)  126 us
    reduce_scatter x1, waiting for transfers between devices, reduce_rows(): lax.psum_scatter(inner[0].astype(jnp.bfloat16), 'fsdp', scatter_dimension...  88.7 us
    reduce_scatter x1, waiting for transfers between devices, reduce_rows(): lax.psum_scatter(terms[0].astype(jnp.bfloat16), 'seq', scatter_dimension=...  85.1 us
  transfers between devices with their start and end apart: 22, of which 17 were waited for; matrix products, arithmetic and copies ran while one was open for 10% of the time, Pallas kernels for 0%

commit v1 on v0

v1 whole, which is shorter than its diff:
```python
import math

import jax
import jax.numpy as jnp
from jax import lax
from jax.sharding import Mesh, PartitionSpec as P

QUERY_HEAD_COUNT = 8
KEY_VALUE_HEADS = 4
HEAD_SIZE = 256
FEED_UNITS = 8192
STEP = 10

NORM_EPSILON = 1e-06
ROPE_BASE = 1000042.0
MASKED_SCORE = -1000000000.0
CLIP_NORM = 1.0
BETA_ONE = 0.9
BETA_TWO = 0.95
ADAM_EPSILON = 1e-08
DECAY_MATRIX = 0.1
RATE_MATRIX = 0.02
RATE_OUTPUT = 0.1
RATE_GAIN = 1.0

TP = ("seq", "near")
EVERY = ("seq", "far", "near")


def rotary_tables(positions, width):
    half = width // 2
    freqs = jnp.exp(-(jnp.arange(half, dtype=jnp.float32) * 2.0 / width) * math.log(ROPE_BASE))
    angles = positions.astype(jnp.float32)[..., None] * freqs
    angles = jnp.concatenate([angles, angles], -1)
    return (jnp.cos(angles)[..., None, :], jnp.sin(angles)[..., None, :])


def rotate_half(value_rows):
    half = value_rows.shape[-1] // 2
    return jnp.concatenate([-value_rows[..., half:], value_rows[..., :half]], -1)


def apply_rotary(value_rows, cosine_table, sine_table):
    return value_rows * cosine_table + rotate_half(value_rows) * sine_table


def rope_back(grads, cosine_table, sine_table):
    return grads * cosine_table - rotate_half(grads * sine_table)


def rms_normalize(value_rows):
    inverse_scale = lax.rsqrt(jnp.mean(value_rows * value_rows, -1, keepdims=True) + NORM_EPSILON)
    return (value_rows * inverse_scale, inverse_scale)


def norm_backward(normed_gradient, unit_input, inverse_scale, norm_gain_vector):
    unit_input_gradient = normed_gradient * norm_gain_vector
    backward_pass = inverse_scale * (
        unit_input_gradient
        - unit_input * jnp.mean(unit_input_gradient * unit_input, -1, keepdims=True)
    )
    gradient_term = jnp.sum((normed_gradient * unit_input).reshape(-1, unit_input.shape[-1]), 0)
    return (backward_pass, gradient_term)


def adam_step(weight, grad, first, second, factor, rate, decay):
    clipped = grad * factor
    first_new = BETA_ONE * first + (1.0 - BETA_ONE) * clipped
    second_new = BETA_TWO * second + (1.0 - BETA_TWO) * clipped * clipped
    corr_one = 1.0 - BETA_ONE**STEP
    corr_two = 1.0 - BETA_TWO**STEP
    update = first_new / corr_one / (jnp.sqrt(second_new / corr_two) + ADAM_EPSILON)
    return (weight - rate * (update + decay * weight), first_new, second_new)


def product(left, right, left_dim, right_dim):
    return lax.dot_general(
        left, right, (((left_dim,), (right_dim,)), ((), ())), preferred_element_type=jnp.float32
    )


def columns_out(pieces, group, over):
    parts, rows, columns = pieces.shape
    mine = lax.all_to_all(pieces, group, 0, 0, tiled=True)
    full = lax.all_gather(mine.reshape(-1, columns), over, axis=0, tiled=True)
    far = lax.axis_size(over)
    seq = lax.axis_size("seq")
    near = parts // seq
    full = full.reshape(far, seq, near, rows, columns).transpose(1, 0, 2, 3, 4)
    return full.reshape(-1, columns)


def columns_back(grad, group, over, rows):
    seq = lax.axis_size("seq")
    far = lax.axis_size(over)
    columns = grad.shape[1]
    near = grad.shape[0] // (seq * far * rows)
    terms = grad.astype(jnp.bfloat16).reshape(seq, far, near, rows, columns)
    terms = terms.transpose(1, 0, 2, 3, 4).reshape(-1, columns)
    mine = lax.psum_scatter(terms, over, scatter_dimension=0, tiled=True)
    return lax.all_to_all(mine.reshape(seq * near, rows, columns), group, 0, 0, tiled=True)


def shards(
    inputs,
    cotangent,
    lengths,
    positions,
    query_key_value_weight,
    out_weight,
    gateup_weight,
    down_weight,
    norm_gains,
    query_key_value_moment,
    output_weight_moment,
    gate_up_moment,
    down_weight_moment,
    norm_gains_moment,
    query_key_value_variance,
    out_second,
    gateup_second,
    down_second,
    gains_second,
):
    _, here, width = inputs.shape
    seq = lax.axis_size("seq")
    group = seq * lax.axis_size("near")
    rows = out_weight.shape[0]
    full = here * seq
    heads_here = QUERY_HEAD_COUNT // seq
    local_kv = KEY_VALUE_HEADS // seq
    per_kv = QUERY_HEAD_COUNT // KEY_VALUE_HEADS
    query_width = QUERY_HEAD_COUNT * HEAD_SIZE
    key_width = KEY_VALUE_HEADS * HEAD_SIZE
    mine_q, mine_k = query_width // seq, key_width // seq
    units = FEED_UNITS // group
    factor = 1.0 / math.sqrt(HEAD_SIZE)
    low = jnp.bfloat16

    inputs = inputs[0]
    cotangent = cotangent[0]
    length = lengths[0]

    qkv_low = query_key_value_weight.astype(low)
    qkv_pieces = jnp.concatenate(
        [
            qkv_low[:, :query_width].reshape(rows, seq, mine_q),
            qkv_low[:, query_width : query_width + key_width].reshape(rows, seq, mine_k),
            qkv_low[:, query_width + key_width :].reshape(rows, seq, mine_k),
        ],
        2,
    ).transpose(1, 0, 2)
    qkv = columns_out(qkv_pieces, "seq", ("far", "near"))
    out = columns_out(
        out_weight.astype(low).reshape(rows, seq, mine_q).transpose(1, 0, 2),
        "seq",
        ("far", "near"),
    )
    gains = lax.all_gather(norm_gains.astype(low), EVERY, axis=0, tiled=True).astype(jnp.float32)
    gain_one, gain_two = gains[:, 0], gains[:, 1]
    all_positions = lax.all_gather(positions[0], "seq", axis=0, tiled=True)

    unit_one, scale_one = rms_normalize(inputs)
    normed_one = lax.all_gather((unit_one * gain_one).astype(low), "seq", axis=0, tiled=True)
    cos, sin = rotary_tables(all_positions, HEAD_SIZE)
    merged = product(normed_one, qkv, 1, 0)
    queries = apply_rotary(merged[:, :mine_q].reshape(full, heads_here, HEAD_SIZE), cos, sin)
    queries = queries.astype(low).reshape(full, local_kv, per_kv, HEAD_SIZE)
    keys = apply_rotary(
        merged[:, mine_q : mine_q + mine_k].reshape(full, local_kv, HEAD_SIZE), cos, sin
    ).astype(low)
    values = merged[:, mine_q + mine_k :].reshape(full, local_kv, HEAD_SIZE).astype(low)

    gateup_pieces = gateup_weight.astype(low).reshape(rows, 2, group, units).transpose(2, 0, 1, 3)
    gateup_w = columns_out(gateup_pieces.reshape(group, rows, 2 * units), TP, "far")
    down_w = columns_out(
        down_weight.astype(low).reshape(rows, group, units).transpose(1, 0, 2), TP, "far"
    )
    dout = lax.all_gather(cotangent.astype(low), TP, axis=0, tiled=True)

    spot = jnp.arange(full)
    visible = (spot[None, :] <= spot[:, None]) & (spot < length)[None, :]
    live = (spot < length)[:, None, None, None]
    scores = jnp.einsum("qkgd,jkd->kgqj", queries, keys, preferred_element_type=jnp.float32)
    scores = jnp.where(visible, scores * factor, MASKED_SCORE)
    peak = jnp.max(scores, -1, keepdims=True)
    expo = jnp.exp(scores - peak)
    probs = expo / jnp.sum(expo, -1, keepdims=True)
    probs_low = probs.astype(low)
    heads = jnp.einsum("kgqj,jkd->qkgd", probs_low, values, preferred_element_type=jnp.float32)
    heads = (heads * live).astype(low).reshape(full, mine_q)
    attended = lax.psum_scatter(
        product(heads, out, 1, 1).astype(low), "seq", scatter_dimension=0, tiled=True
    )
    hidden = inputs + attended.astype(jnp.float32)
    unit_two, scale_two = rms_normalize(hidden)
    normed_two = lax.all_gather((unit_two * gain_two).astype(low), TP, axis=0, tiled=True)

    gate = product(normed_two, gateup_w[:, :units], 1, 0)
    upper = product(normed_two, gateup_w[:, units:], 1, 0)
    sig = jax.nn.sigmoid(gate)
    act = (gate * sig * upper).astype(low)
    dact = product(dout, down_w, 1, 0)
    dgate = dact * upper * sig * (1.0 + gate * (1.0 - sig))
    dupper = dact * gate * sig
    dgateup = jnp.concatenate([dgate.astype(low), dupper.astype(low)], 1)
    dnormed_two = lax.psum_scatter(
        product(dgateup, gateup_w, 1, 1).astype(low), TP, scatter_dimension=0, tiled=True
    ).astype(jnp.float32)
    grad_gateup = columns_back(product(normed_two, dgateup, 0, 0), TP, "far", rows)
    grad_down = columns_back(product(dout, act, 0, 0), TP, "far", rows)
    back_two, gain_term_two = norm_backward(dnormed_two, unit_two, scale_two, gain_two)
    dhidden = cotangent + back_two

    dattended = lax.all_gather(dhidden.astype(low), "seq", axis=0, tiled=True)
    dheads = product(dattended, out, 1, 0).astype(low).reshape(full, local_kv, per_kv, HEAD_SIZE)
    dheads = dheads * live.astype(low)
    grad_out = columns_back(product(dattended, heads, 0, 0), "seq", ("far", "near"), rows)
    dvalues = jnp.einsum("kgqj,qkgd->jkd", probs_low, dheads, preferred_element_type=jnp.float32)
    dprobs = jnp.einsum("qkgd,jkd->kgqj", dheads, values, preferred_element_type=jnp.float32)
    inner = jnp.sum(probs * dprobs, -1, keepdims=True)
    dscores = jnp.where(visible, (probs * (dprobs - inner)).astype(low), jnp.zeros((), low))
    dqueries = jnp.einsum("kgqj,jkd->qkgd", dscores, keys, preferred_element_type=jnp.float32)
    dkeys = jnp.einsum("kgqj,qkgd->jkd", dscores, queries, preferred_element_type=jnp.float32)
    dqueries = (dqueries * factor).astype(low).reshape(full, heads_here, HEAD_SIZE)
    dkeys = (dkeys * factor).astype(low)
    dfused = jnp.concatenate(
        [
            rope_back(dqueries.astype(jnp.float32), cos, sin).astype(low).reshape(full, mine_q),
            rope_back(dkeys.astype(jnp.float32), cos, sin).astype(low).reshape(full, mine_k),
            dvalues.astype(low).reshape(full, mine_k),
        ],
        1,
    )
    dnormed_one = lax.psum_scatter(
        product(dfused, qkv, 1, 1).astype(low), "seq", scatter_dimension=0, tiled=True
    ).astype(jnp.float32)
    grad_qkv = columns_back(product(normed_one, dfused, 0, 0), "seq", ("far", "near"), rows)
    back_one, gain_term_one = norm_backward(dnormed_one, unit_one, scale_one, gain_one)
    input_grad = dhidden + back_one
    layer_output = hidden + lax.psum_scatter(
        product(act, down_w, 1, 1).astype(low), TP, scatter_dimension=0, tiled=True
    ).astype(jnp.float32)

    gain_terms = jnp.stack([gain_term_one, gain_term_two], 1)
    grad_gains = lax.psum_scatter(gain_terms, EVERY, scatter_dimension=0, tiled=True)

    grad_qkv = grad_qkv.astype(jnp.float32)
    grad_qkv = jnp.concatenate(
        [
            grad_qkv[:, :, :mine_q].transpose(1, 0, 2).reshape(rows, query_width),
            grad_qkv[:, :, mine_q : mine_q + mine_k].transpose(1, 0, 2).reshape(rows, key_width),
            grad_qkv[:, :, mine_q + mine_k :].transpose(1, 0, 2).reshape(rows, key_width),
        ],
        1,
    )
    grad_out = grad_out.astype(jnp.float32).transpose(1, 0, 2).reshape(rows, query_width)
    grad_gateup = grad_gateup.astype(jnp.float32).reshape(group, rows, 2, units)
    grad_gateup = grad_gateup.transpose(1, 2, 0, 3).reshape(rows, 2 * FEED_UNITS)
    grad_down = grad_down.astype(jnp.float32).transpose(1, 0, 2).reshape(rows, FEED_UNITS)

    local_squares = (
        jnp.sum(grad_qkv * grad_qkv)
        + jnp.sum(grad_out * grad_out)
        + jnp.sum(grad_gateup * grad_gateup)
        + jnp.sum(grad_down * grad_down)
        + jnp.sum(grad_gains * grad_gains)
    )
    grad_norm = jnp.sqrt(lax.psum(local_squares, EVERY))
    clip = CLIP_NORM / jnp.maximum(grad_norm, CLIP_NORM)
    steps = (
        (query_key_value_weight, grad_qkv, query_key_value_moment, query_key_value_variance, RATE_MATRIX, DECAY_MATRIX),
        (out_weight, grad_out, output_weight_moment, out_second, RATE_OUTPUT, DECAY_MATRIX),
        (gateup_weight, grad_gateup, gate_up_moment, gateup_second, RATE_MATRIX, DECAY_MATRIX),
        (down_weight, grad_down, down_weight_moment, down_second, RATE_MATRIX, DECAY_MATRIX),
        (norm_gains, grad_gains, norm_gains_moment, gains_second, RATE_GAIN, 0.0),
    )
    stepped = [adam_step(w, g, m, v, clip, rate, decay) for w, g, m, v, rate, decay in steps]
    nexts, firsts, seconds = zip(*stepped)
    return (layer_output[None], input_grad[None], grad_norm, *nexts, *firsts, *seconds)


def solution(mesh):
    seq, fsdp = mesh.shape["seq"], mesh.shape["fsdp"]
    cut = Mesh(mesh.devices.reshape(seq, fsdp // 2, 2), EVERY)
    tokens = P(("far", "near"), "seq", None)
    matrix = P(EVERY, None)
    return jax.shard_map(
        shards,
        mesh=cut,
        in_specs=(tokens, tokens, P(("far", "near")), P(("far", "near"), "seq")) + (matrix,) * 15,
        out_specs=(tokens, tokens, P()) + (matrix,) * 15,
        check_vma=False,
    )
```

time: 3110 us -> 1530 us (0.49)
  waiting for transfers between devices: 2480 us -> 937 us
  blocking collectives: 98 us -> 205 us
  other arithmetic: 153 us -> 70.6 us
  matrix products: 257 us -> 184 us
    reduce_scatter x6 -> x8, waiting for transfers between devices: 1320 us -> 415 us  [the longest x4 281 us: columns_back(): mine = lax.psum_scatter(terms, over, scatter_dimension=0, tiled=True)]
    all_gather x8, waiting for transfers between devices: 1070 us -> 355 us  [the longest x4 202 us: columns_out(): full = lax.all_gather(mine.reshape(-1, columns), over, axis=0, tiled=True)]
    unnamed x18, waiting for transfers between devices: 46.8 us -> 133 us
    dot_general x24 -> x19, matrix products: 257 us -> 184 us  [the longest x13 164 us: product(): lax.dot_general(left, right, (((left_dim,), (right_dim,)), ((), ())), pre...]
    concatenate x1, other arithmetic: 70.6 us -> 1.1 us  [rotary_tables(): angles = jnp.concatenate([angles, angles], -1)]
    all_to_all x2 -> x5, blocking collectives: 36.1 us -> 92.1 us  [the longest x4 73.6 us: columns_out(): mine = lax.all_to_all(pieces, group, 0, 0, tiled=True)]
    all_gather x2, blocking collectives: 22.6 us -> 72.7 us  [the longest x1 67.7 us: shards(): lax.all_gather(norm_gains.astype(low), EVERY, axis=0, tiled=True)]
  transfers between devices with their start and end apart: 22 -> 20, of which waited for: 17 -> 16; matrix products, arithmetic and copies ran while one was open for 10% -> 11% of each run, Pallas kernels for 0% -> 0%
where the time goes in v1:
time: 1530 us; the launch traced here: 1520 us
  waiting for transfers between devices  937 us (61%)
  blocking collectives  205 us (13%)
  matrix products  184 us (12%)
  local copies, waits for them, and re-layouts  89.9 us (6%)
  other arithmetic  70.6 us (5%)
  between operations  22.8 us (1%)
    reduce_scatter x4, waiting for transfers between devices, columns_back(): mine = lax.psum_scatter(terms, over, scatter_dimension=0, tiled=True)  281 us
    all_gather x4, waiting for transfers between devices, columns_out(): full = lax.all_gather(mine.reshape(-1, columns), over, axis=0, tiled=True)  202 us
    dot_general x13, matrix products, product(): lax.dot_general(left, right, (((left_dim,), (right_dim,)), ((), ())), pre...  164 us
    unnamed x18, waiting for transfers between devices  133 us
    all_to_all x4, blocking collectives, columns_out(): mine = lax.all_to_all(pieces, group, 0, 0, tiled=True)  73.6 us
    reduce_scatter x1, waiting for transfers between devices, shards(): lax.psum_scatter(product(dgateup, gateup_w, 1, 1).astype(low), TP, scatte...  71 us
    all_gather x1, blocking collectives, shards(): lax.all_gather(norm_gains.astype(low), EVERY, axis=0, tiled=True)  67.7 us
    reduce_scatter x1, waiting for transfers between devices, shards(): lax.psum_scatter(product(act, down_w, 1, 1).astype(low), TP, scatter_dime...  62.7 us
  transfers between devices with their start and end apart: 20, of which 16 were waited for; matrix products, arithmetic and copies ran while one was open for 11% of the time, Pallas kernels for 0%

profile of v1, /device:TPU:0, one launch (start us, length us, event | category | flops | bytes accessed | tf_op | source)
XLA Modules:
  0.0 1522.4 jit_solution(3765496452494421987)
XLA Ops:
  33.9 67.7 %all-gather.1 = bf16[32,64,2]{1,2,0:T(2,128)(2,1)S(1)} all-gather(bf16[1,64,2]{1,2,0:T(2,128)(2,1)S(1)} %convert_bitcast_fusion.1), channel_id=1, replica_groups=mesh['seq'=4,'far'=4,'near'=2] {'seq','far','near'}, dimensions={0}, use_global_device_ids=true | all-gather | bytes 8448 | tf_op jit(solution)/shard_map/all_gather | solution.py:159
  114.6 29.4 %all-gather.13.cloned.1.call-done = bf16[2048,1024]{1,0:T(8,128)(2,1)} async-done(((bf16[256,1024]{1,0:T(8,128)(2,1)}), bf16[2048,1024]{1,0:T(8,128)(2,1)}) %all-gather.13.cloned.1.call-update) | async-done | bytes 4194320 | tf_op jit(solution)/shard_map/all_gather | solution.py:85
  148.9 30.0 %all-gather.11.cloned.1.call-done = bf16[1024,2048]{1,0:T(8,128)(2,1)} async-done(((bf16[256,2048]{1,0:T(8,128)(2,1)}), bf16[1024,2048]{1,0:T(8,128)(2,1)}) %all-gather.11.cloned.1.call-update) | async-done | bytes 4194320 | tf_op jit(solution)/shard_map/all_gather | solution.py:164
  211.6 18.0 %all_to_all.42 = bf16[8,64,1024]{2,1,0:T(8,128)(2,1)} all-to-all(bf16[8,64,1024]{2,1,0:T(8,128)(2,1)S(1)} %copy.129), channel_id=1, replica_groups=mesh['seq'=4,'far'=4,'near'=2] {'seq','near'}, dimensions={0} | all-to-all | bytes 2097152 | tf_op jit(solution)/shard_map/all_to_all | solution.py:84
  241.4 33.3 %all_to_all.43 = bf16[8,64,2048]{2,1,0:T(8,128)(2,1)} all-to-all(bf16[8,64,2048]{2,1,0:T(8,128)(2,1)} %reshape.460), channel_id=1, replica_groups=mesh['seq'=4,'far'=4,'near'=2] {'seq','near'}, dimensions={0} | all-to-all | bytes 4194304 | tf_op jit(solution)/shard_map/all_to_all | solution.py:84
  282.3 27.6 %all-gather.21.cloned.1.call-done = bf16[2048,1024]{1,0:T(8,128)(2,1)} async-done(((bf16[512,1024]{1,0:T(8,128)(2,1)}), bf16[2048,1024]{1,0:T(8,128)(2,1)}) %all-gather.21.cloned.1.call-update) | async-done | bytes 4194320 | tf_op jit(solution)/shard_map/all_gather | solution.py:85
  314.9 144.6 %all-gather.19.cloned.1.call-done = bf16[2048,2048]{1,0:T(8,128)(2,1)} async-done(((bf16[512,2048]{1,0:T(8,128)(2,1)}), bf16[2048,2048]{1,0:T(8,128)(2,1)}) %all-gather.19.cloned.1.call-update) | async-done | bytes 8388624 | tf_op jit(solution)/shard_map/all_gather | solution.py:85
  468.0 46.5 %all-gather.23.cloned.1.call-done = bf16[2048,2048]{1,0:T(8,128)(2,1)} async-done(((bf16[256,2048]{1,0:T(8,128)(2,1)}), bf16[2048,2048]{1,0:T(8,128)(2,1)}) %all-gather.23.cloned.1.call-update) | async-done | bytes 8388624 | tf_op jit(solution)/shard_map/all_gather | solution.py:179
  514.5 14.7 fusion.103
  529.2 42.2 %all-gather.17.cloned.1.call-done = bf16[2048,2048]{1,0:T(8,128)(2,1)} async-done(((bf16[256,2048]{1,0:T(8,128)(2,1)}), bf16[2048,2048]{1,0:T(8,128)(2,1)}) %all-gather.17.cloned.1.call-update) | async-done | bytes 8388624 | tf_op jit(solution)/shard_map/all_gather | solution.py:197
  586.0 22.9 %multiply_convert_fusion.1 = (bf16[2048,1024]{0,1:T(8,128)(2,1)}, bf16[2048,1024]{0,1:T(8,128)(2,1)}, bf16[2048,1024]{0,1:T(8,128)(2,1)}) fusion(f32[2048,1024]{0,1:T(8,128)} %fusion.103, f32[2048,1024]{0,1:T(8,128)} %fusion.10, bf16[2048,2048]{1,0:T(8,128)(2,1)} %all-gather.17.cloned.1.call-done, bf16[2048,2048]{1,0:T(8,128)(2,1)} %bitcast.315), kind=kOutput, calls=%fused_computation.8 | convolution fusion | flops 8623489024 | bytes 41943040 | tf_op jit(solution)/shard_map/dot_general | solution.py:77
  609.0 23.7 %convolution_convert_fusion.1 = bf16[2048,2048]{1,0:T(8,128)(2,1)} fusion(bf16[2048,2048]{1,0:T(8,128)(2,1)} %bitcast.316, bf16[2048,1024]{0,1:T(8,128)(2,1)} %get-tuple-element.39, bf16[2048,1024]{0,1:T(8,128)(2,1)} %get-tuple-element.37), kind=kOutput, calls=%fused_computation.13 | convolution fusion | flops 17200840704 | bytes 25165824 | tf_op jit(solution)/shard_map/dot_general | solution.py:77
  632.9 71.0 %reduce-scatter.16.cloned.1.call-done = bf16[256,2048]{1,0:T(8,128)(2,1)} async-done(((bf16[2048,2048]{1,0:T(8,128)(2,1)}), bf16[256,2048]{1,0:T(8,128)(2,1)}) %reduce-scatter.16.cloned.1.call-update) | async-done | bytes 1048592 | tf_op jit(solution)/shard_map/reduce_scatter | solution.py:207
  708.5 34.6 %all-gather.25.cloned.1.call-done = bf16[1024,2048]{1,0:T(8,128)(2,1)} async-done(((bf16[256,2048]{1,0:T(8,128)(2,1)}), bf16[1024,2048]{1,0:T(8,128)(2,1)}) %all-gather.25.cloned.1.call-update) | async-done | bytes 4194320 | tf_op jit(solution)/shard_map/all_gather | solution.py:215
  806.7 23.9 %convolution_convert_fusion = bf16[2048,2048]{1,0:T(8,128)(2,1)} fusion(bf16[2048,2048]{1,0:T(8,128)(2,1)} %all-gather.17.cloned.1.call-done, bf16[2048,1024]{0,1:T(8,128)(2,1)} %get-tuple-element.39, bf16[2048,1024]{0,1:T(8,128)(2,1)} %get-tuple-element.37), kind=kOutput, calls=%fused_computation.12 | convolution fusion | flops 17200840704 | bytes 25165824 | tf_op jit(solution)/shard_map/dot_general | solution.py:77
  873.4 31.7 %reduce-scatter.26.cloned.1.call-done = bf16[512,1024]{1,0:T(8,128)(2,1)} async-done(((bf16[2048,1024]{1,0:T(8,128)(2,1)}), bf16[512,1024]{1,0:T(8,128)(2,1)}) %reduce-scatter.26.cloned.1.call-update) | async-done | bytes 1048592 | tf_op jit(solution)/shard_map/reduce_scatter | solution.py:100
  905.1 18.5 %all_to_all.44 = bf16[8,64,1024]{2,1,0:T(8,128)(2,1)S(1)} all-to-all(bf16[8,64,1024]{2,1,0:T(8,128)(2,1)} %bitcast.340), channel_id=1, replica_groups=mesh['seq'=4,'far'=4,'near'=2] {'seq','near'}, dimensions={0} | all-to-all | bytes 2097152 | tf_op jit(solution)/shard_map/all_to_all | solution.py:101
  923.7 128.8 %reduce-scatter.24.cloned.1.call-done = bf16[512,2048]{1,0:T(8,128)(2,1)} async-done(((bf16[2048,2048]{1,0:T(8,128)(2,1)}), bf16[512,2048]{1,0:T(8,128)(2,1)}) %reduce-scatter.24.cloned.1.call-update) | async-done | bytes 2097168 | tf_op jit(solution)/shard_map/reduce_scatter | solution.py:100
  1058.0 30.6 %all-to-all-done.6 = bf16[8,64,2048]{2,1,0:T(8,128)(2,1)} async-done(((bf16[8,64,2048]{2,1,0:T(8,128)(2,1)}), bf16[8,64,2048]{2,1,0:T(8,128)(2,1)}, u32[]{:S(2)}, u32[]{:S(2)}) %all-to-all-start.6) | async-done | bytes 2097184 | tf_op jit(solution)/shard_map/all_to_all | solution.py:101
  1088.6 39.3 %reduce-scatter.22.cloned.1.call-done = bf16[256,512]{1,0:T(8,128)(2,1)} async-done(((bf16[2048,512]{1,0:T(8,128)(2,1)}), bf16[256,512]{1,0:T(8,128)(2,1)}) %reduce-scatter.22.cloned.1.call-update) | async-done | bytes 262160 | tf_op jit(solution)/shard_map/reduce_scatter | solution.py:100
  1137.4 81.6 %reduce-scatter.20.cloned.1.call-done = bf16[256,1024]{1,0:T(8,128)(2,1)} async-done(((bf16[2048,1024]{1,0:T(8,128)(2,1)}), bf16[256,1024]{1,0:T(8,128)(2,1)}) %reduce-scatter.20.cloned.1.call-update) | async-done | bytes 524304 | tf_op jit(solution)/shard_map/reduce_scatter | solution.py:100
  1223.8 133.1 %reduce-scatter.28.cloned.1.call-done = f32[64,2]{1,0:T(8,128)} async-done(((f32[2048,2]{1,0:T(8,128)}), f32[64,2]{1,0:T(8,128)}) %reduce-scatter.28.cloned.1.call-update) | async-done | bytes 528
  1365.0 62.7 %reduce-scatter.14.cloned.1.call-done = bf16[256,2048]{1,0:T(8,128)(2,1)} async-done(((bf16[2048,2048]{1,0:T(8,128)(2,1)}), bf16[256,2048]{1,0:T(8,128)(2,1)}) %reduce-scatter.14.cloned.1.call-update) | async-done | bytes 1048592 | tf_op jit(solution)/shard_map/reduce_scatter | solution.py:241
  1433.6 39.7 %psum.7 = f32[]{:T(128)} all-reduce(f32[]{:T(128)S(6)} %add.168), channel_id=1, replica_groups=mesh['seq'=4,'far'=4,'near'=2] {'seq','far','near'}, use_global_device_ids=true, to_apply=%region_23.24 | all-reduce | flops 1 | bytes 8 | tf_op jit(solution)/shard_map/psum | solution.py:269
  (273 shorter events, 303.4 us)
Async XLA Ops:
  8.0 103.1 %all-gather.15.cloned.1.call-start = ((), (), s32[]{:S(2)}) async-start(), calls=%async_computation.19 | async-start | bytes 2359296 | tf_op jit(solution)/shard_map/all_gather | solution.py:85
  9.4 92.3 %copy-start = (f32[1,256,2048]{2,1,0:T(8,128)S(1)}, f32[1,256,2048]{2,1,0:T(8,128)}, u32[]{:S(2)}) copy-start(f32[1,256,2048]{2,1,0:T(8,128)} %param.19) | copy-start | bytes 6291460
  19.7 124.3 %all-gather.13.cloned.1.call-start = ((), (), s32[]{:S(2)}) async-start(), calls=%async_computation.18 | async-start | bytes 4718592 | tf_op jit(solution)/shard_map/all_gather | solution.py:85
  33.8 145.1 %all-gather.11.cloned.1.call-start = ((), (), s32[]{:S(2)}) async-start(), calls=%async_computation.17 | async-start | bytes 5242880 | tf_op jit(solution)/shard_map/all_gather | solution.py:164
  102.0 604.2 %copy-start.40 = (f32[2048,1]{0,1:T(1,128)}, f32[2048,1]{0,1:T(1,128)S(1)}, u32[]{:S(2)}) copy-start(f32[2048,1]{0,1:T(1,128)S(1)} %get-tuple-element.58) | copy-start | bytes 24580
  103.8 173.8 %reduce-scatter.12.cloned.1.call-start = ((), (), s32[]{:S(2)}) async-start(), calls=%async_computation.20 | async-start | bytes 5242880 | tf_op jit(solution)/shard_map/reduce_scatter | solution.py:192
  208.4 101.6 %all-gather.21.cloned.1.call-start = ((), (), s32[]{:S(2)}) async-start(), calls=%async_computation.23 | async-start | bytes 5242880 | tf_op jit(solution)/shard_map/all_gather | solution.py:85
  229.7 229.8 %all-gather.19.cloned.1.call-start = ((), (), s32[]{:S(2)}) async-start(), calls=%async_computation.22 | async-start | bytes 10485760 | tf_op jit(solution)/shard_map/all_gather | solution.py:85
  274.7 239.7 %all-gather.23.cloned.1.call-start = ((), (), s32[]{:S(2)}) async-start(), calls=%async_computation.25 | async-start | bytes 9437184 | tf_op jit(solution)/shard_map/all_gather | solution.py:179
  277.5 293.9 %all-gather.17.cloned.1.call-start = ((), (), s32[]{:S(2)}) async-start(), calls=%async_computation.21 | async-start | bytes 9437184 | tf_op jit(solution)/shard_map/all_gather | solution.py:197
  279.2 427.0 %copy-start.44 = (f32[256]{0:T(256)}, f32[256]{0:T(256)S(1)}, u32[]{:S(2)}) copy-start(f32[256]{0:T(256)S(1)} %add_rsqrt_fusion) | copy-start | bytes 3076
  281.8 422.1 %reduce-scatter.16.cloned.1.call-start = ((), (), s32[]{:S(2)}) async-start(), calls=%async_computation.26 | async-start | bytes 9437184 | tf_op jit(solution)/shard_map/reduce_scatter | solution.py:207
  632.7 110.4 %all-gather.25.cloned.1.call-start = ((), (), s32[]{:S(2)}) async-start(), calls=%async_computation.27 | async-start | bytes 5242880 | tf_op jit(solution)/shard_map/all_gather | solution.py:215
  708.4 146.9 %reduce-scatter.18.cloned.1.call-start = ((), (), s32[]{:S(2)}) async-start(), calls=%async_computation.28 | async-start | bytes 5242880 | tf_op jit(solution)/shard_map/reduce_scatter | solution.py:235
  781.2 123.9 %reduce-scatter.26.cloned.1.call-start = ((), (), s32[]{:S(2)}) async-start(), calls=%async_computation.32 | async-start | bytes 5242880 | tf_op jit(solution)/shard_map/reduce_scatter | solution.py:100
  806.6 245.9 %reduce-scatter.24.cloned.1.call-start = ((), (), s32[]{:S(2)}) async-start(), calls=%async_computation.31 | async-start | bytes 10485760 | tf_op jit(solution)/shard_map/reduce_scatter | solution.py:100
  838.9 289.0 %reduce-scatter.22.cloned.1.call-start = ((), (), s32[]{:S(2)}) async-start(), calls=%async_computation.30 | async-start | bytes 2359296 | tf_op jit(solution)/shard_map/reduce_scatter | solution.py:100
  845.4 373.5 %reduce-scatter.20.cloned.1.call-start = ((), (), s32[]{:S(2)}) async-start(), calls=%async_computation.29 | async-start | bytes 4718592 | tf_op jit(solution)/shard_map/reduce_scatter | solution.py:100
  855.2 501.7 %reduce-scatter.28.cloned.1.call-start = ((), (), s32[]{:S(2)}) async-start(), calls=%async_computation.33 | async-start | bytes 1081344
  859.3 568.4 %reduce-scatter.14.cloned.1.call-start = ((), (), s32[]{:S(2)}) async-start(), calls=%async_computation.24 | async-start | bytes 9437184 | tf_op jit(solution)/shard_map/reduce_scatter | solution.py:241
  923.7 295.3 %copy-start.18 = (bf16[8,64,1024]{2,1,0:T(8,128)(2,1)}, bf16[8,64,1024]{2,1,0:T(8,128)(2,1)S(1)}, u32[]{:S(2)}) copy-start(bf16[8,64,1024]{2,1,0:T(8,128)(2,1)S(1)} %all_to_all.44) | copy-start | bytes 3145732
  1052.5 36.1 %all-to-all-start.6 = ((bf16[8,64,2048]{2,1,0:T(8,128)(2,1)}), bf16[8,64,2048]{2,1,0:T(8,128)(2,1)}, u32[]{:S(2)}, u32[]{:S(2)}) async-start(bf16[8,64,2048]{2,1,0:T(8,128)(2,1)} %bitcast.335), calls=%async_computation.13 | async-start | bytes 4194304 | tf_op jit(solution)/shard_map/all_to_all | solution.py:101
  1127.9 9.4 all-to-all-start.5
  1218.9 139.4 %all-to-all-start.4 = ((bf16[4,64,1024]{2,1,0:T(8,128)(2,1)}), bf16[4,64,1024]{2,1,0:T(8,128)(2,1)}, u32[]{:S(2)}, u32[]{:S(2)}) async-start(bf16[4,64,1024]{2,1,0:T(8,128)(2,1)} %bitcast.346), calls=%async_computation.9 | async-start | bytes 1048576 | tf_op jit(solution)/shard_map/all_to_all | solution.py:101
  (55 other events, 739.7 us)
Sparse Core Ops, SparseCore 0:
  19.9 50.0 all-gather.14
  72.1 71.9 all-gather.12
  146.2 32.7 all-gather.10
  208.5 53.7 reduce-scatter.11
  708.5 34.4 all-gather.24
  781.4 44.5 reduce-scatter.17
  828.3 76.7 reduce-scatter.25
  907.5 144.9 reduce-scatter.23
  1056.6 71.2 reduce-scatter.21
  1132.0 86.8 reduce-scatter.19
  1221.8 135.0 reduce-scatter.27
  1360.2 67.4 reduce-scatter.13
Sparse Core Ops, SparseCore 1:
  229.8 80.1 all-gather.20
  311.5 148.0 all-gather.18
  462.0 52.4 all-gather.22
  517.1 54.2 all-gather.16
  632.7 71.1 reduce-scatter.15

commit v2 on v1

v2 whole, which is shorter than its diff:
```python
import functools
import math

import jax
import jax.numpy as jnp
from jax import lax
from jax.experimental import pallas as pl
from jax.experimental.pallas import tpu as pltpu
from jax.sharding import Mesh, PartitionSpec as P

QUERY_HEAD_COUNT = 8
KEY_VALUE_HEADS = 4
HEAD_SIZE = 256
FEED_UNITS = 8192
STEP = 10

NORM_EPSILON = 1e-06
ROPE_BASE = 1000042.0
MASKED_SCORE = -1000000000.0
CLIP_NORM = 1.0
BETA_ONE = 0.9
BETA_TWO = 0.95
ADAM_EPSILON = 1e-08
DECAY_MATRIX = 0.1
RATE_MATRIX = 0.02
RATE_OUTPUT = 0.1
RATE_GAIN = 1.0

EVERY = ("seq", "far", "near")


MESH_IDS = pl.DeviceIdType.MESH
ANYWHERE = pl.BlockSpec(memory_space=pl.ANY)
IN_VMEM = pl.BlockSpec(memory_space=pltpu.VMEM)
VMEM_LIMIT = 60 * 1024 * 1024


def places():
    s, n = lax.axis_index("seq"), lax.axis_index("near")
    return s, n, s + 1 - 2 * (s % 2), (s + 2) % 4, 1 - n


def meet(*others):
    barrier = pltpu.get_barrier_semaphore()
    for other in others:
        pl.semaphore_signal(barrier, inc=1, device_id=other, device_id_type=MESH_IDS)
    pl.semaphore_wait(barrier, len(others))


def sender(send_sems, recv_sems):
    copies = {}

    def send(key, source, target, device):
        at = len(copies)
        copies[key] = pltpu.make_async_remote_copy(
            src_ref=source,
            dst_ref=target,
            send_sem=send_sems.at[at],
            recv_sem=recv_sems.at[at],
            device_id=device,
            device_id_type=MESH_IDS,
        )
        copies[key].start()

    return copies, send


def gather_plane_kernel(rows, x_ref, o_ref, local_sem, send_sems, recv_sems):
    s, n, core, across, beside = places()
    half = rows // 2
    to_core, to_y, to_x = {"seq": core}, {"seq": across}, {"near": beside}

    def block(seq, near, part):
        return o_ref.at[pl.ds((seq * 2 + near) * rows + part * half, half)]

    def own(part):
        return x_ref.at[pl.ds(part * half, half)]

    meet(to_core, to_y, to_x)
    local = pltpu.make_async_copy(x_ref, o_ref.at[pl.ds((s * 2 + n) * rows, rows)], local_sem)
    local.start()
    copies, send = sender(send_sems, recv_sems)
    send("y0", own(0), block(s, n, 0), to_y)
    send("x1", own(1), block(s, n, 1), to_x)
    send("y1", own(1), block(s, n, 1), to_y)
    send("x0", own(0), block(s, n, 0), to_x)
    send("c0", own(0), block(s, n, 0), to_core)
    send("c1", own(1), block(s, n, 1), to_core)
    copies["y0"].wait_recv()
    send("yx", block(across, n, 0), block(across, n, 0), to_x)
    send("yc0", block(across, n, 0), block(across, n, 0), to_core)
    copies["x1"].wait_recv()
    send("xy", block(s, beside, 1), block(s, beside, 1), to_y)
    send("xc1", block(s, beside, 1), block(s, beside, 1), to_core)
    copies["y1"].wait_recv()
    send("yc1", block(across, n, 1), block(across, n, 1), to_core)
    copies["x0"].wait_recv()
    send("xc0", block(s, beside, 0), block(s, beside, 0), to_core)
    copies["yx"].wait_recv()
    send("dc0", block(across, beside, 0), block(across, beside, 0), to_core)
    copies["xy"].wait_recv()
    send("dc1", block(across, beside, 1), block(across, beside, 1), to_core)
    for key in ("c0", "c1", "yc0", "yc1", "xc0", "xc1", "dc0", "dc1"):
        copies[key].wait_recv()
    for copy in copies.values():
        copy.wait_send()
    local.wait()


def gather_plane(x, collective_id):
    rows, columns = x.shape
    return pl.pallas_call(
        functools.partial(gather_plane_kernel, rows),
        out_shape=jax.ShapeDtypeStruct((8 * rows, columns), x.dtype),
        in_specs=[ANYWHERE],
        out_specs=ANYWHERE,
        scratch_shapes=[
            pltpu.SemaphoreType.DMA,
            pltpu.SemaphoreType.DMA((14,)),
            pltpu.SemaphoreType.DMA((14,)),
        ],
        compiler_params=pltpu.CompilerParams(collective_id=collective_id, has_side_effects=True),
    )(x)


def gather_seq_kernel(rows, x_ref, o_ref, local_sem, send_sems, recv_sems):
    s, _, core, across, _ = places()
    half = rows // 2
    to_core, to_y = {"seq": core}, {"seq": across}

    def block(seq, part):
        return o_ref.at[pl.ds(seq * rows + part * half, half)]

    def own(part):
        return x_ref.at[pl.ds(part * half, half)]

    meet(to_core, to_y)
    local = pltpu.make_async_copy(x_ref, o_ref.at[pl.ds(s * rows, rows)], local_sem)
    local.start()
    copies, send = sender(send_sems, recv_sems)
    for part in range(2):
        send(("y", part), own(part), block(s, part), to_y)
    for part in range(2):
        send(("c", part), own(part), block(s, part), to_core)
    for part in range(2):
        copies["y", part].wait_recv()
        send(("yc", part), block(across, part), block(across, part), to_core)
    for part in range(2):
        copies["c", part].wait_recv()
        copies["yc", part].wait_recv()
    for copy in copies.values():
        copy.wait_send()
    local.wait()


def gather_seq(x, collective_id):
    rows, columns = x.shape
    return pl.pallas_call(
        functools.partial(gather_seq_kernel, rows),
        out_shape=jax.ShapeDtypeStruct((4 * rows, columns), x.dtype),
        in_specs=[ANYWHERE],
        out_specs=ANYWHERE,
        scratch_shapes=[
            pltpu.SemaphoreType.DMA,
            pltpu.SemaphoreType.DMA((6,)),
            pltpu.SemaphoreType.DMA((6,)),
        ],
        compiler_params=pltpu.CompilerParams(collective_id=collective_id, has_side_effects=True),
    )(x)


def add_rows(target, first, second, third=None, step=64):
    rows = target.shape[0]

    def body(i, carry):
        at = pl.ds(pl.multiple_of(i * step, step), step)
        total = first[at, :].astype(jnp.float32) + second[at, :].astype(jnp.float32)
        if third is not None:
            total = total + third[at, :].astype(jnp.float32)
        target[at, :] = total.astype(target.dtype)
        return carry

    lax.fori_loop(0, rows // step, body, 0)


def scatter_plane_kernel(rows, p_ref, o_ref, mine, far, hop_x, hop_y, last_x, last_y, local_sems, send_sems, recv_sems):
    s, n, core, across, beside = places()
    half = rows // 2
    to_core, to_y, to_x = {"seq": core}, {"seq": across}, {"near": beside}

    def block(seq, near):
        return p_ref.at[pl.ds((seq * 2 + near) * rows, rows)]

    def part(ref, at, p):
        return ref.at[at, pl.ds(p * half, half)]

    meet(to_core, to_y, to_x)
    copies, send = sender(send_sems, recv_sems)
    other = (core + 2) % 4
    given = [block(other, beside), block(other, n), block(core, beside), block(core, n)]
    kept = [block(across, beside), block(across, n), block(s, beside), block(s, n)]
    locals_ = []
    for k in range(4):
        send(k, given[k], far.at[k], to_core)
        locals_.append(pltpu.make_async_copy(kept[k], mine.at[k], local_sems.at[k]))
        locals_[k].start()
    for k in range(3):
        locals_[k].wait()
        copies[k].wait_recv()
        add_rows(mine.at[k], mine.at[k], far.at[k])
        if k == 0:
            send("hx", part(mine, 0, 0), hop_x, to_x)
            send("hy", part(mine, 0, 1), hop_y, to_y)
        elif k == 1:
            send("y1", part(mine, 1, 1), part(last_y, 0, 1), to_y)
        else:
            send("x0", part(mine, 2, 0), part(last_x, 0, 0), to_x)
    copies["hx"].wait_recv()
    add_rows(part(mine, 1, 0), part(mine, 1, 0), hop_x)
    send("y0", part(mine, 1, 0), part(last_y, 0, 0), to_y)
    copies["hy"].wait_recv()
    add_rows(part(mine, 2, 1), part(mine, 2, 1), hop_y)
    send("x1", part(mine, 2, 1), part(last_x, 0, 1), to_x)
    locals_[3].wait()
    copies[3].wait_recv()
    add_rows(o_ref, mine.at[3], far.at[3])
    for p, first, second in ((1, "y1", "x1"), (0, "x0", "y0")):
        copies[first].wait_recv()
        copies[second].wait_recv()
        here = o_ref.at[pl.ds(p * half, half)]
        add_rows(here, here, part(last_x, 0, p), part(last_y, 0, p))
    for copy in copies.values():
        copy.wait_send()


def scatter_plane(p, collective_id):
    rows, columns = p.shape[0] // 8, p.shape[1]
    low = jnp.bfloat16
    return pl.pallas_call(
        functools.partial(scatter_plane_kernel, rows),
        out_shape=jax.ShapeDtypeStruct((rows, columns), jnp.float32),
        in_specs=[ANYWHERE],
        out_specs=IN_VMEM,
        scratch_shapes=[
            pltpu.VMEM((4, rows, columns), low),
            pltpu.VMEM((4, rows, columns), low),
            pltpu.VMEM((rows // 2, columns), low),
            pltpu.VMEM((rows // 2, columns), low),
            pltpu.VMEM((1, rows, columns), low),
            pltpu.VMEM((1, rows, columns), low),
            pltpu.SemaphoreType.DMA((4,)),
            pltpu.SemaphoreType.DMA((10,)),
            pltpu.SemaphoreType.DMA((10,)),
        ],
        compiler_params=pltpu.CompilerParams(
            collective_id=collective_id, has_side_effects=True, vmem_limit_bytes=VMEM_LIMIT
        ),
    )(p)


def scatter_seq_kernel(rows, p_ref, o_ref, mine, far, last, local_sems, send_sems, recv_sems):
    s, _, core, across, _ = places()
    half = rows // 2
    to_core, to_y = {"seq": core}, {"seq": across}

    def block(seq):
        return p_ref.at[pl.ds(seq * rows, rows)]

    meet(to_core, to_y)
    copies, send = sender(send_sems, recv_sems)
    given = [block((core + 2) % 4), block(core)]
    kept = [block(across), block(s)]
    locals_ = []
    for k in range(2):
        send(k, given[k], far.at[k], to_core)
        locals_.append(pltpu.make_async_copy(kept[k], mine.at[k], local_sems.at[k]))
        locals_[k].start()
    locals_[0].wait()
    copies[0].wait_recv()
    for p in range(2):
        at = pl.ds(p * half, half)
        add_rows(mine.at[0, at], mine.at[0, at], far.at[0, at])
        send(("y", p), mine.at[0, at], last.at[at], to_y)
    locals_[1].wait()
    copies[1].wait_recv()
    add_rows(o_ref, mine.at[1], far.at[1])
    for p in range(2):
        at = pl.ds(p * half, half)
        copies["y", p].wait_recv()
        add_rows(o_ref.at[at], o_ref.at[at], last.at[at])
    for copy in copies.values():
        copy.wait_send()


def scatter_seq(p, collective_id):
    rows, columns = p.shape[0] // 4, p.shape[1]
    low = jnp.bfloat16
    return pl.pallas_call(
        functools.partial(scatter_seq_kernel, rows),
        out_shape=jax.ShapeDtypeStruct((rows, columns), jnp.float32),
        in_specs=[ANYWHERE],
        out_specs=IN_VMEM,
        scratch_shapes=[
            pltpu.VMEM((2, rows, columns), low),
            pltpu.VMEM((2, rows, columns), low),
            pltpu.VMEM((rows, columns), low),
            pltpu.SemaphoreType.DMA((2,)),
            pltpu.SemaphoreType.DMA((4,)),
            pltpu.SemaphoreType.DMA((4,)),
        ],
        compiler_params=pltpu.CompilerParams(
            collective_id=collective_id, has_side_effects=True, vmem_limit_bytes=VMEM_LIMIT
        ),
    )(p)


def exchange_plane_kernel(rows, x_ref, o_ref, local_sem, send_sems, recv_sems):
    s, n, core, across, beside = places()
    diagonal = (core + 2) % 4
    mine = s * 2 + n
    others = [
        (seq, near)
        for near in (beside, n)
        for seq in (diagonal, across, core, s)
    ][:-1]

    def at(p):
        return pl.ds(p * rows, rows)

    meet(*[{"seq": seq, "near": near} for seq, near in others])
    copies, send = sender(send_sems, recv_sems)
    for seq, near in others:
        send((len(copies),), x_ref.at[at(seq * 2 + near)], o_ref.at[at(mine)], {"seq": seq, "near": near})
    local = pltpu.make_async_copy(x_ref.at[at(mine)], o_ref.at[at(mine)], local_sem)
    local.start()
    for copy in copies.values():
        copy.wait_recv()
    for copy in copies.values():
        copy.wait_send()
    local.wait()


def exchange_plane(x, collective_id):
    return pl.pallas_call(
        functools.partial(exchange_plane_kernel, x.shape[0] // 8),
        out_shape=jax.ShapeDtypeStruct(x.shape, x.dtype),
        in_specs=[ANYWHERE],
        out_specs=ANYWHERE,
        scratch_shapes=[
            pltpu.SemaphoreType.DMA,
            pltpu.SemaphoreType.DMA((7,)),
            pltpu.SemaphoreType.DMA((7,)),
        ],
        compiler_params=pltpu.CompilerParams(collective_id=collective_id, has_side_effects=True),
    )(x)


def gather_heads_kernel(far_size, w_ref, x_ref, i_ref, o_ref, ox_ref, oi_ref, local_sems, send_sems, recv_sems):
    s, n, core, across, beside = places()
    diagonal = (core + 2) % 4
    f = lax.axis_index("far")
    half = x_ref.shape[0] // 2
    to_core, to_y, to_x = {"seq": core}, {"seq": across}, {"near": beside}
    right, left = {"far": (f + 1) % far_size}, {"far": (f + far_size - 1) % far_size}

    meet(to_core, to_y, {"seq": diagonal}, to_x, right, left)
    copies, send = sender(send_sems, recv_sems)
    keep = pltpu.make_async_copy(w_ref.at[s], o_ref.at[s, f, n], local_sems.at[0])
    keep.start()
    keep_x = pltpu.make_async_copy(x_ref, ox_ref.at[s], local_sems.at[1])
    keep_x.start()
    keep_i = pltpu.make_async_copy(i_ref, oi_ref.at[s], local_sems.at[2])
    keep_i.start()
    for k, seq in enumerate((diagonal, across, core)):
        send(("w", k), w_ref.at[seq], o_ref.at[s, f, n], {"seq": seq})
        send(("i", k), i_ref, oi_ref.at[s], {"seq": seq})
    for p in range(2):
        at = pl.ds(p * half, half)
        send(("y", p), x_ref.at[at], ox_ref.at[s, at], to_y)
        send(("c", p), x_ref.at[at], ox_ref.at[s, at], to_core)
    keep.wait()
    for k in range(3):
        copies["w", k].wait_recv()

    def group(far, near):
        return o_ref.at[:, far, near]

    def along(key, far, device, sem):
        return pltpu.make_async_remote_copy(
            src_ref=group(far, n),
            dst_ref=group(far, n),
            send_sem=send_sems.at[sem],
            recv_sem=recv_sems.at[sem],
            device_id=device,
            device_id_type=MESH_IDS,
        )

    base = 12

    def beside_copy(far, sem):
        return along("x", far, to_x, sem)

    def to_right(k):
        return along("r", (f + far_size - k) % far_size, right, base + k)

    def to_left(k):
        return along("l", (f + k) % far_size, left, base + far_size + k)

    def x_from_left(k):
        return beside_copy((f + far_size - k) % far_size, base + 2 * far_size + k)

    def x_from_right(k):
        return beside_copy((f + k) % far_size, base + 3 * far_size + k)

    for k in range(far_size):
        if k > 0:

            @pl.when(f >= k)
            def _():
                to_right(k - 1).wait_recv()

        @pl.when((f >= k) & (f < far_size - 1))
        def _():
            to_right(k).start()

        if k > 0:

            @pl.when(f + k < far_size)
            def _():
                to_left(k - 1).wait_recv()

        @pl.when((f + k < far_size) & (f > 0))
        def _():
            to_left(k).start()

        if k == 0:
            x_from_left(0).start()
        else:

            @pl.when(f >= k)
            def _():
                x_from_left(k).start()

            @pl.when(f + k < far_size)
            def _():
                x_from_right(k).start()

        if k == 0:
            for p in range(2):
                at = pl.ds(p * half, half)
                copies["y", p].wait_recv()
                send(("yc", p), ox_ref.at[across, at], ox_ref.at[across, at], to_core)
    for p in range(2):
        copies["c", p].wait_recv()
        copies["yc", p].wait_recv()
    for k in range(3):
        copies["i", k].wait_recv()
    for k in range(far_size):

        @pl.when((f >= k) & (f < far_size - 1))
        def _():
            to_right(k).wait_send()

        @pl.when((f + k < far_size) & (f > 0))
        def _():
            to_left(k).wait_send()

        @pl.when(f >= k)
        def _():
            x_from_left(k).wait_recv()
            x_from_left(k).wait_send()

        if k > 0:

            @pl.when(f + k < far_size)
            def _():
                x_from_right(k).wait_recv()
                x_from_right(k).wait_send()

    for copy in copies.values():
        copy.wait_send()
    keep_x.wait()
    keep_i.wait()


def gather_heads(w, x, i, collective_id):
    far_size = lax.axis_size("far")
    _, rows, columns = w.shape
    tokens, width = x.shape
    sems = 12 + 4 * far_size
    full, all_x, all_i = pl.pallas_call(
        functools.partial(gather_heads_kernel, far_size),
        out_shape=[
            jax.ShapeDtypeStruct((4, far_size, 2, rows, columns), w.dtype),
            jax.ShapeDtypeStruct((4, tokens, width), x.dtype),
            jax.ShapeDtypeStruct((4, *i.shape), i.dtype),
        ],
        in_specs=[ANYWHERE] * 3,
        out_specs=[ANYWHERE] * 3,
        scratch_shapes=[
            pltpu.SemaphoreType.DMA((3,)),
            pltpu.SemaphoreType.DMA((sems,)),
            pltpu.SemaphoreType.DMA((sems,)),
        ],
        compiler_params=pltpu.CompilerParams(collective_id=collective_id, has_side_effects=True),
    )(w, x, i)
    return full.reshape(-1, columns), all_x.reshape(-1, width), all_i


def rotary_tables(positions, width):
    half = width // 2
    freqs = jnp.exp(-(jnp.arange(half, dtype=jnp.float32) * 2.0 / width) * math.log(ROPE_BASE))
    angles = positions.astype(jnp.float32)[..., None] * freqs
    angles = jnp.concatenate([angles, angles], -1)
    return (jnp.cos(angles)[..., None, :], jnp.sin(angles)[..., None, :])


def rotate_half(value_rows):
    half = value_rows.shape[-1] // 2
    return jnp.concatenate([-value_rows[..., half:], value_rows[..., :half]], -1)


def apply_rotary(value_rows, cosine_table, sine_table):
    return value_rows * cosine_table + rotate_half(value_rows) * sine_table


def rope_back(grads, cosine_table, sine_table):
    return grads * cosine_table - rotate_half(grads * sine_table)


def rms_normalize(value_rows):
    inverse_scale = lax.rsqrt(jnp.mean(value_rows * value_rows, -1, keepdims=True) + NORM_EPSILON)
    return (value_rows * inverse_scale, inverse_scale)


def norm_backward(unit_gradient, unit_input, inverse_scale):
    return inverse_scale * (
        unit_gradient - unit_input * jnp.mean(unit_gradient * unit_input, -1, keepdims=True)
    )


def adam_step(weight, grad, first, second, factor, rate, decay):
    clipped = grad * factor
    first_new = BETA_ONE * first + (1.0 - BETA_ONE) * clipped
    second_new = BETA_TWO * second + (1.0 - BETA_TWO) * clipped * clipped
    corr_one = 1.0 - BETA_ONE**STEP
    corr_two = 1.0 - BETA_TWO**STEP
    update = first_new / corr_one / (jnp.sqrt(second_new / corr_two) + ADAM_EPSILON)
    return (weight - rate * (update + decay * weight), first_new, second_new)


def product(left, right, left_dim, right_dim):
    return lax.dot_general(
        left, right, (((left_dim,), (right_dim,)), ((), ())), preferred_element_type=jnp.float32
    )


CHUNKS = 2


def shards(
    inputs,
    cotangent,
    lengths,
    positions,
    query_key_value_weight,
    out_weight,
    gateup_weight,
    down_weight,
    norm_gains,
    query_key_value_moment,
    output_weight_moment,
    gate_up_moment,
    down_weight_moment,
    norm_gains_moment,
    query_key_value_variance,
    out_second,
    gateup_second,
    down_second,
    gains_second,
):
    _, here, width = inputs.shape
    seq = lax.axis_size("seq")
    far = lax.axis_size("far")
    group = seq * 2
    rows = out_weight.shape[0]
    full = here * seq
    heads_here = QUERY_HEAD_COUNT // seq
    local_kv = KEY_VALUE_HEADS // seq
    per_kv = QUERY_HEAD_COUNT // KEY_VALUE_HEADS
    query_width = QUERY_HEAD_COUNT * HEAD_SIZE
    key_width = KEY_VALUE_HEADS * HEAD_SIZE
    mine_q, mine_k = query_width // seq, key_width // seq
    mine_qkv = mine_q + 2 * mine_k
    units = FEED_UNITS // group
    part = units // CHUNKS
    factor = 1.0 / math.sqrt(HEAD_SIZE)
    low = jnp.bfloat16

    inputs = inputs[0]
    cotangent = cotangent[0]
    length = lengths[0]
    gains = norm_gains.astype(low).astype(jnp.float32)
    gain_one, gain_two = gains[:, :1], gains[:, 1:]

    def rounded(weight, gain=None):
        weight = weight.astype(low)
        return weight if gain is None else (weight.astype(jnp.float32) * gain).astype(low)

    def far_first(x):
        x = x.reshape(-1, seq, far, 2 * rows).transpose(0, 2, 1, 3)
        return x.reshape(-1, width)

    def far_last(x):
        return x.reshape(-1, far, seq, 2 * rows).transpose(0, 2, 1, 3).reshape(-1, width)

    gateup_low = rounded(gateup_weight, gain_two).reshape(rows, 2, group, CHUNKS, part)
    down_low = rounded(down_weight).reshape(rows, 1, group, CHUNKS, part)
    feed_pieces = jnp.concatenate([gateup_low, down_low], 1).transpose(3, 2, 0, 1, 4)
    feed_pieces = feed_pieces.reshape(CHUNKS, group * rows, 3 * part)
    feed = []
    for c in range(CHUNKS):
        piece = exchange_plane(feed_pieces[c], 1)
        feed.append(lax.all_gather(piece, "far", axis=0, tiled=True))

    qkv_low = rounded(query_key_value_weight, gain_one)
    head_pieces = jnp.concatenate(
        [
            qkv_low[:, :query_width].reshape(rows, seq, mine_q),
            qkv_low[:, query_width : query_width + key_width].reshape(rows, seq, mine_k),
            qkv_low[:, query_width + key_width :].reshape(rows, seq, mine_k),
            rounded(out_weight).reshape(rows, seq, mine_q),
        ],
        2,
    ).transpose(1, 0, 2)
    unit_one, scale_one = rms_normalize(inputs)
    spots = jnp.pad(positions.reshape(-1, 128), ((0, 8 - here // 128), (0, 0)))
    head_w, normed_one, all_spots = gather_heads(head_pieces, unit_one.astype(low), spots, 2)
    qkv, out = head_w[:, :mine_qkv], head_w[:, mine_qkv:]
    all_positions = all_spots[:, : here // 128].reshape(full)

    cos, sin = rotary_tables(all_positions, HEAD_SIZE)
    merged = product(normed_one, qkv, 1, 0)
    queries = apply_rotary(merged[:, :mine_q].reshape(full, heads_here, HEAD_SIZE), cos, sin)
    queries = queries.astype(low).reshape(full, local_kv, per_kv, HEAD_SIZE)
    keys = apply_rotary(
        merged[:, mine_q : mine_q + mine_k].reshape(full, local_kv, HEAD_SIZE), cos, sin
    ).astype(low)
    values = merged[:, mine_q + mine_k :].reshape(full, local_kv, HEAD_SIZE).astype(low)

    spot = jnp.arange(full)
    visible = (spot[None, :] <= spot[:, None]) & (spot < length)[None, :]
    live = (spot < length)[:, None, None, None]
    scores = jnp.einsum("qkgd,jkd->kgqj", queries, keys, preferred_element_type=jnp.float32)
    scores = jnp.where(visible, scores * factor, MASKED_SCORE)
    peak = jnp.max(scores, -1, keepdims=True)
    expo = jnp.exp(scores - peak)
    probs = expo / jnp.sum(expo, -1, keepdims=True)
    probs_low = probs.astype(low)
    heads = jnp.einsum("kgqj,jkd->qkgd", probs_low, values, preferred_element_type=jnp.float32)
    heads = (heads * live).astype(low).reshape(full, mine_q)
    hidden = inputs + scatter_seq(product(heads, out, 1, 1).astype(low), 3)
    unit_two, scale_two = rms_normalize(hidden)
    normed_two = gather_plane(far_first(unit_two.astype(low)), 4)
    dout = gather_plane(far_first(cotangent.astype(low)), 4)

    dnormed_two, output_terms, feed_grads = 0.0, 0.0, []
    for w in feed:
        gateup_w, down_w = w[:, : 2 * part], w[:, 2 * part :]
        gate = product(normed_two, gateup_w[:, :part], 1, 0)
        upper = product(normed_two, gateup_w[:, part:], 1, 0)
        sig = jax.nn.sigmoid(gate)
        act = (gate * sig * upper).astype(low)
        dact = product(dout, down_w, 1, 0)
        dgate = dact * upper * sig * (1.0 + gate * (1.0 - sig))
        dupper = dact * gate * sig
        dgateup = jnp.concatenate([dgate.astype(low), dupper.astype(low)], 1)
        terms = jnp.concatenate(
            [
                product(normed_two, dgateup, 0, 0).astype(low),
                product(dout, act, 0, 0).astype(low),
            ],
            1,
        )
        feed_grads.append(lax.psum_scatter(terms, "far", scatter_dimension=0, tiled=True))
        dnormed_two = dnormed_two + product(dgateup, gateup_w, 1, 1)
        output_terms = output_terms + product(act, down_w, 1, 1)
    dnormed_two = far_last(scatter_plane(dnormed_two.astype(low), 5))
    back_two = norm_backward(dnormed_two, unit_two, scale_two)
    dhidden = cotangent + back_two

    dattended = gather_seq(dhidden.astype(low), 6)
    dheads = product(dattended, out, 1, 0).astype(low).reshape(full, local_kv, per_kv, HEAD_SIZE)
    dheads = dheads * live.astype(low)
    dvalues = jnp.einsum("kgqj,qkgd->jkd", probs_low, dheads, preferred_element_type=jnp.float32)
    dprobs = jnp.einsum("qkgd,jkd->kgqj", dheads, values, preferred_element_type=jnp.float32)
    inner = jnp.sum(probs * dprobs, -1, keepdims=True)
    dscores = jnp.where(visible, (probs * (dprobs - inner)).astype(low), jnp.zeros((), low))
    dqueries = jnp.einsum("kgqj,jkd->qkgd", dscores, keys, preferred_element_type=jnp.float32)
    dkeys = jnp.einsum("kgqj,qkgd->jkd", dscores, queries, preferred_element_type=jnp.float32)
    dqueries = (dqueries * factor).astype(low).reshape(full, heads_here, HEAD_SIZE)
    dkeys = (dkeys * factor).astype(low)
    dfused = jnp.concatenate(
        [
            rope_back(dqueries.astype(jnp.float32), cos, sin).astype(low).reshape(full, mine_q),
            rope_back(dkeys.astype(jnp.float32), cos, sin).astype(low).reshape(full, mine_k),
            dvalues.astype(low).reshape(full, mine_k),
        ],
        1,
    )
    head_terms = jnp.concatenate(
        [
            product(normed_one, dfused, 0, 0).astype(low),
            product(dattended, heads, 0, 0).astype(low),
        ],
        1,
    )
    head_terms = head_terms.reshape(seq, far * 2, rows, -1).transpose(1, 0, 2, 3)
    head_terms = lax.psum_scatter(
        head_terms.reshape(width, -1), ("far", "near"), scatter_dimension=0, tiled=True
    )
    dnormed_one = scatter_seq(product(dfused, qkv, 1, 1).astype(low), 3)
    back_one = norm_backward(dnormed_one, unit_one, scale_one)
    input_grad = dhidden + back_one
    layer_output = hidden + far_last(scatter_plane(output_terms.astype(low), 5))

    head_grads = lax.all_to_all(head_terms.reshape(seq, rows, -1), "seq", 0, 0, tiled=True)
    head_grads = head_grads.astype(jnp.float32)

    def head_rows(start, size):
        return head_grads[:, :, start : start + size].transpose(1, 0, 2).reshape(rows, -1)

    grad_qkv = jnp.concatenate(
        [head_rows(0, mine_q), head_rows(mine_q, mine_k), head_rows(mine_q + mine_k, mine_k)], 1
    )
    grad_out = head_rows(mine_qkv, mine_q)
    feed_grads = jnp.stack(
        [exchange_plane(grads, 1).reshape(group, rows, 3, part) for grads in feed_grads], 3
    ).astype(jnp.float32)
    feed_grads = feed_grads.transpose(1, 2, 0, 3, 4)
    grad_gateup = feed_grads[:, :2].reshape(rows, 2 * FEED_UNITS)
    grad_down = feed_grads[:, 2].reshape(rows, FEED_UNITS)

    gain_term_one = jnp.sum(rounded(query_key_value_weight) * grad_qkv, 1, keepdims=True)
    gain_term_two = jnp.sum(rounded(gateup_weight) * grad_gateup, 1, keepdims=True)
    grad_gains = jnp.concatenate([gain_term_one, gain_term_two], 1)
    grad_qkv = grad_qkv * gain_one
    grad_gateup = grad_gateup * gain_two

    local_squares = (
        jnp.sum(grad_qkv * grad_qkv)
        + jnp.sum(grad_out * grad_out)
        + jnp.sum(grad_gateup * grad_gateup)
        + jnp.sum(grad_down * grad_down)
        + jnp.sum(grad_gains * grad_gains)
    )
    grad_norm = jnp.sqrt(lax.psum(local_squares, EVERY))
    clip = CLIP_NORM / jnp.maximum(grad_norm, CLIP_NORM)
    steps = (
        (query_key_value_weight, grad_qkv, query_key_value_moment, query_key_value_variance, RATE_MATRIX, DECAY_MATRIX),
        (out_weight, grad_out, output_weight_moment, out_second, RATE_OUTPUT, DECAY_MATRIX),
        (gateup_weight, grad_gateup, gate_up_moment, gateup_second, RATE_MATRIX, DECAY_MATRIX),
        (down_weight, grad_down, down_weight_moment, down_second, RATE_MATRIX, DECAY_MATRIX),
        (norm_gains, grad_gains, norm_gains_moment, gains_second, RATE_GAIN, 0.0),
    )
    stepped = [adam_step(w, g, m, v, clip, rate, decay) for w, g, m, v, rate, decay in steps]
    nexts, firsts, seconds = zip(*stepped)
    return (layer_output[None], input_grad[None], grad_norm, *nexts, *firsts, *seconds)


def solution(mesh):
    seq, fsdp = mesh.shape["seq"], mesh.shape["fsdp"]
    cut = Mesh(mesh.devices.reshape(seq, fsdp // 2, 2), EVERY)
    tokens = P(("far", "near"), "seq", None)
    matrix = P(EVERY, None)
    return jax.shard_map(
        shards,
        mesh=cut,
        in_specs=(tokens, tokens, P(("far", "near")), P(("far", "near"), "seq")) + (matrix,) * 15,
        out_specs=(tokens, tokens, P()) + (matrix,) * 15,
        check_vma=False,
    )
```

time: 1530 us -> 1010 us (0.66)
  waiting for transfers between devices: 937 us -> 6.97 us
  Pallas kernels: 0 us -> 517 us
  blocking collectives: 205 us -> 38.4 us
  other arithmetic: 70.6 us -> 94.9 us
  matrix products: 184 us -> 208 us
  local copies, waits for them, and re-layouts: 89.9 us -> 113 us
    pallas_call x0 -> x12, Pallas kernels: none -> 517 us  [the longest x1 167 us: gather_heads(): pl.pallas_call(functools.partial(gather_heads_kernel, far_size), out_shap...]
    reduce_scatter x8 -> x3, waiting for transfers between devices: 415 us -> 1.84 us  [the longest x1 1.82 us: shards(): lax.psum_scatter(head_terms.reshape(width, -1), ('far', 'near'), scatter_...]
    all_gather x8 -> x2, waiting for transfers between devices: 355 us -> 0.04 us  [shards(): feed.append(lax.all_gather(piece, 'far', axis=0, tiled=True))]
    unnamed x18 -> x5, waiting for transfers between devices: 133 us -> 0.08 us
    all_to_all x5 -> x0, blocking collectives: 92.1 us -> none  [the longest x4 73.6 us: columns_out(): mine = lax.all_to_all(pieces, group, 0, 0, tiled=True)]
    all_gather x2 -> x0, blocking collectives: 72.7 us -> none  [the longest x1 67.7 us: shards(): lax.all_gather(norm_gains.astype(low), EVERY, axis=0, tiled=True)]
    all_to_all x3 -> x1, waiting for transfers between devices: 33.3 us -> 5.01 us  [shards(): lax.all_to_all(head_terms.reshape(seq, rows, -1), 'seq', 0, 0, tiled=True)]
    dot_general x13 -> x20, matrix products: 164 us -> 188 us  [product(): lax.dot_general(left, right, (((left_dim,), (right_dim,)), ((), ())), pre...]
  transfers between devices with their start and end apart: 20 -> 6, of which waited for: 16 -> 2; matrix products, arithmetic and copies ran while one was open for 11% -> 34% of each run, Pallas kernels for 0% -> 49%
where the time goes in v2:
time: 1010 us; the launch traced here: 1000 us
  Pallas kernels  517 us (51%)
  matrix products  208 us (21%)
  local copies, waits for them, and re-layouts  113 us (11%)
  other arithmetic  94.9 us (9%)
  blocking collectives  38.4 us (4%)
  between operations  21.4 us (2%)
    dot_general x20, matrix products, product(): lax.dot_general(left, right, (((left_dim,), (right_dim,)), ((), ())), pre...  188 us
    pallas_call x1, Pallas kernels, gather_heads(): pl.pallas_call(functools.partial(gather_heads_kernel, far_size), out_shap...  167 us
    pallas_call x4, Pallas kernels, exchange_plane(): pl.pallas_call(functools.partial(exchange_plane_kernel, x.shape[0] // 8),...  92.8 us
    pallas_call x2, Pallas kernels, scatter_plane(): pl.pallas_call(functools.partial(scatter_plane_kernel, rows), out_shape=j...  83.4 us
    pallas_call x2, Pallas kernels, gather_plane(): pl.pallas_call(functools.partial(gather_plane_kernel, rows), out_shape=ja...  80.1 us
    pallas_call x2, Pallas kernels, scatter_seq(): pl.pallas_call(functools.partial(scatter_seq_kernel, rows), out_shape=jax...  59.7 us
    psum x1, blocking collectives, shards(): grad_norm = jnp.sqrt(lax.psum(local_squares, EVERY))  38.4 us
    pallas_call x1, Pallas kernels, gather_seq(): pl.pallas_call(functools.partial(gather_seq_kernel, rows), out_shape=jax....  33.7 us
  transfers between devices with their start and end apart: 6, of which 2 were waited for; matrix products, arithmetic and copies ran while one was open for 34% of the time, Pallas kernels for 49%

profile of v2, /device:TPU:0, one launch (start us, length us, event | category | flops | bytes accessed | tf_op | source)
XLA Modules:
  0.0 1005.0 jit_solution(3950998788836176185)
XLA Ops:
  30.4 22.8 %shard_map.326 = bf16[512,1536]{1,0:T(8,128)(2,1)} custom-call(bf16[512,1536]{1,0:T(8,128)(2,1)} %bitcast.301), custom_call_target="tpu_custom_call" | custom-call | tf_op jit(solution)/shard_map/pallas_call | solution.py:344
  55.0 21.2 %shard_map.325 = bf16[512,1536]{1,0:T(8,128)(2,1)} custom-call(bf16[512,1536]{1,0:T(8,128)(2,1)} %bitcast.302), custom_call_target="tpu_custom_call" | custom-call | tf_op jit(solution)/shard_map/pallas_call | solution.py:344
  80.3 167.0 %shard_map.322 = (bf16[4,4,2,64,1536]{4,3,2,1,0:T(8,128)(2,1)}, bf16[4,256,2048]{2,1,0:T(8,128)(2,1)}, s32[4,8,128]{2,1,0:T(8,128)}) custom-call(bf16[4,64,1536]{2,1,0:T(8,128)(2,1)} %maximum_bitcast_fusion.1.w_ref, bf16[256,2048]{1,0:T(8,128)(2,1)} %fusion.50.x_ref, s32[8,128]{1,0:T(8,128)} %pad.4.i_ref), custom_call_target="tpu_custom_call" | custom-call | tf_op jit(solution)/shard_map/pallas_call | solution.py:491
  268.5 40.0 %shard_map.328 = bf16[2048,2048]{1,0:T(8,128)(2,1)} custom-call(bf16[256,2048]{1,0:T(8,128)(2,1)} %reshape.438.x_ref), custom_call_target="tpu_custom_call" | custom-call | tf_op jit(solution)/shard_map/pallas_call | solution.py:112
  335.4 29.9 %shard_map.323 = f32[256,2048]{1,0:T(8,128)} custom-call(bf16[1024,2048]{1,0:T(8,128)(2,1)} %convolution_convert_fusion.p_ref), custom_call_target="tpu_custom_call" | custom-call | tf_op jit(solution)/shard_map/pallas_call | solution.py:298
  371.7 40.1 %shard_map.324 = bf16[2048,2048]{1,0:T(8,128)(2,1)} custom-call(bf16[256,2048]{1,0:T(8,128)(2,1)} %reshape.433.x_ref), custom_call_target="tpu_custom_call" | custom-call | tf_op jit(solution)/shard_map/pallas_call | solution.py:112
  411.8 10.7 %fusion.51 = f32[512,2048]{1,0:T(8,128)} fusion(bf16[2048,2048]{1,0:T(8,128)(2,1)} %shard_map.328, bf16[2048,1536]{1,0:T(8,128)(2,1)} %all-gather.5.cloned.1.call-done), kind=kOutput, calls=%fused_computation.113 | convolution fusion | flops 4294967296 | bytes 14680064 | tf_op jit(solution)/shard_map/dot_general | solution.py:553
  430.7 12.1 %fusion.16 = (bf16[2048,512]{0,1:T(8,128)(2,1)S(1)}, bf16[2048,512]{0,1:T(8,128)(2,1)}, bf16[2048,512]{0,1:T(8,128)(2,1)S(1)}) fusion(f32[512,2048]{1,0:T(8,128)} %fusion.51, f32[2048,512]{0,1:T(8,128)} %fusion.42, bf16[2048,2048]{1,0:T(8,128)(2,1)} %shard_map.324, bf16[2048,1536]{1,0:T(8,128)(2,1)} %all-gather.5.cloned.1.call-done), kind=kOutput, calls=%fused_computation.34 | convolution fusion | flops 4311744512 | bytes 25165824 | tf_op jit(solution)/shard_map/dot_general | solution.py:553
  447.7 11.4 %convolution_convert_fusion.3 = bf16[2048,1024]{1,0:T(8,128)(2,1)S(1)} fusion(bf16[2048,2048]{1,0:T(8,128)(2,1)} %shard_map.324, bf16[2048,512]{0,1:T(8,128)(2,1)S(1)} %copy-done.65, bf16[2048,512]{0,1:T(8,128)(2,1)S(1)} %get-tuple-element.45), kind=kOutput, calls=%fused_computation.61 | convolution fusion | flops 8600420352 | bytes 16777216 | tf_op jit(solution)/shard_map/dot_general | solution.py:553
  477.5 11.8 %fusion.21 = (bf16[2048,512]{0,1:T(8,128)(2,1)}, bf16[2048,512]{0,1:T(8,128)(2,1)}, bf16[2048,512]{0,1:T(8,128)(2,1)}) fusion(f32[512,2048]{1,0:T(8,128)S(1)} %fusion.54, f32[2048,512]{0,1:T(8,128)S(1)} %fusion.46, bf16[2048,2048]{1,0:T(8,128)(2,1)} %shard_map.324, bf16[2048,1536]{1,0:T(8,128)(2,1)S(1)} %copy-done.57), kind=kOutput, calls=%fused_computation.41 | convolution fusion | flops 4311744512 | bytes 25165824 | tf_op jit(solution)/shard_map/dot_general | solution.py:553
  489.3 14.6 %fusion.12 = f32[2048,2048]{1,0:T(8,128)} fusion(bf16[2048,1536]{1,0:T(8,128)(2,1)S(1)} %copy-done.57, bf16[2048,512]{0,1:T(8,128)(2,1)} %get-tuple-element.49, bf16[2048,512]{0,1:T(8,128)(2,1)} %get-tuple-element.48), kind=kOutput, calls=%fused_computation.25 | convolution fusion | flops 8598323200 | bytes 25165824 | tf_op jit(solution)/shard_map/dot_general | solution.py:553
  504.0 16.0 %add_convert_fusion.p_ref = bf16[2048,2048]{1,0:T(8,128)(2,1)} fusion(f32[2048,2048]{1,0:T(8,128)} %fusion.12, bf16[2048,1536]{1,0:T(8,128)(2,1)} %all-gather.5.cloned.1.call-done, bf16[2048,512]{0,1:T(8,128)(2,1)} %get-tuple-element.46, bf16[2048,512]{0,1:T(8,128)(2,1)S(1)} %copy-done.64), kind=kOutput, calls=%fused_computation | convolution fusion | flops 8606711808 | bytes 33554432 | tf_op jit(solution)/shard_map/dot_general | solution.py:553
  520.0 41.6 %shard_map.329 = f32[256,2048]{1,0:T(8,128)} custom-call(bf16[2048,2048]{1,0:T(8,128)(2,1)} %add_convert_fusion.p_ref), custom_call_target="tpu_custom_call" | custom-call | tf_op jit(solution)/shard_map/pallas_call | solution.py:239
  569.4 10.6 %fusion.33 = bf16[2048,512]{1,0:T(8,128)(2,1)S(1)} fusion(bf16[2048,512]{0,1:T(8,128)(2,1)S(1)} %copy-done.61, bf16[2048,2048]{1,0:T(8,128)(2,1)} %shard_map.328), kind=kOutput, calls=%fused_computation.73 | convolution fusion | flops 4296015872 | bytes 12582912 | tf_op jit(solution)/shard_map/dot_general | solution.py:553
  580.1 11.4 %convolution_convert_fusion.4 = bf16[2048,1024]{1,0:T(8,128)(2,1)S(1)} fusion(bf16[2048,2048]{1,0:T(8,128)(2,1)} %shard_map.324, bf16[2048,512]{0,1:T(8,128)(2,1)S(1)} %copy-done.67, bf16[2048,512]{0,1:T(8,128)(2,1)S(1)} %copy-done.66), kind=kOutput, calls=%fused_computation.62 | convolution fusion | flops 8600420352 | bytes 16777216 | tf_op jit(solution)/shard_map/dot_general | solution.py:553
  594.7 10.0 fusion.56
  604.8 15.0 %add_convert_fusion.1.p_ref = bf16[2048,2048]{1,0:T(8,128)(2,1)} fusion(f32[2048,2048]{1,0:T(8,128)} %fusion.56, bf16[2048,512]{0,1:T(8,128)(2,1)} %copy-done.62, bf16[2048,1536]{1,0:T(8,128)(2,1)} %all-gather.5.cloned.1.call-done), kind=kOutput, calls=%fused_computation.1 | convolution fusion | flops 4303355904 | bytes 29360128 | tf_op jit(solution)/shard_map/dot_general | solution.py:553
  619.8 41.8 %shard_map.327 = f32[256,2048]{1,0:T(8,128)} custom-call(bf16[2048,2048]{1,0:T(8,128)(2,1)} %add_convert_fusion.1.p_ref), custom_call_target="tpu_custom_call" | custom-call | tf_op jit(solution)/shard_map/pallas_call | solution.py:239
  679.7 33.7 %shard_map.330 = bf16[1024,2048]{1,0:T(8,128)(2,1)} custom-call(bf16[256,2048]{1,0:T(8,128)(2,1)} %get-tuple-element.41.x_ref), custom_call_target="tpu_custom_call" | custom-call | tf_op jit(solution)/shard_map/pallas_call | solution.py:158
  779.7 29.8 %shard_map.331 = f32[256,2048]{1,0:T(8,128)} custom-call(bf16[1024,2048]{1,0:T(8,128)(2,1)} %convolution_convert_fusion.2.p_ref), custom_call_target="tpu_custom_call" | custom-call | tf_op jit(solution)/shard_map/pallas_call | solution.py:298
  811.6 26.8 %shard_map.333 = bf16[512,1536]{1,0:T(8,128)(2,1)} custom-call(bf16[512,1536]{1,0:T(8,128)(2,1)} %reduce-scatter.8.cloned.1.call-done.x_ref), custom_call_target="tpu_custom_call" | custom-call | tf_op jit(solution)/shard_map/pallas_call | solution.py:344
  848.7 22.0 %shard_map.332 = bf16[512,1536]{1,0:T(8,128)(2,1)} custom-call(bf16[512,1536]{1,0:T(8,128)(2,1)} %reduce-scatter.6.cloned.1.call-done.x_ref), custom_call_target="tpu_custom_call" | custom-call | tf_op jit(solution)/shard_map/pallas_call | solution.py:344
  926.7 38.4 %psum.7 = f32[]{:T(128)} all-reduce(f32[]{:T(128)S(6)} %add.174), channel_id=1, replica_groups=mesh['seq'=4,'far'=4,'near'=2] {'seq','far','near'}, use_global_device_ids=true, to_apply=%region_17.18 | all-reduce | flops 1 | bytes 8 | tf_op jit(solution)/shard_map/psum | solution.py:757
  981.1 9.7 multiply_subtract_fusion
  (279 shorter events, 294.9 us)
Async XLA Ops:
  7.2 404.6 %all-gather.5.cloned.1.call-start = ((), (), s32[]{:S(2)}) async-start(), calls=%async_computation.5 | async-start | bytes 7864320 | tf_op jit(solution)/shard_map/all_gather | solution.py:624
  7.9 68.6 %copy-start.50 = (f32[64]{0:T(128)}, f32[64]{0:T(128)S(1)}, u32[]{:S(2)}) copy-start(f32[64]{0:T(128)S(1)} %get-tuple-element.76) | copy-start | bytes 772
  53.2 409.2 %all-gather.3.cloned.1.call-start = ((), (), s32[]{:S(2)}) async-start(), calls=%async_computation.4 | async-start | bytes 7864320 | tf_op jit(solution)/shard_map/all_gather | solution.py:624
  53.3 23.2 %copy-start.19 = (f32[64,4096]{1,0:T(8,128)S(1)}, f32[64,4096]{1,0:T(8,128)}, u32[]{:S(2)}) copy-start(f32[64,4096]{1,0:T(8,128)} %param.23) | copy-start | bytes 3145732
  55.0 21.8 %copy-start = (f32[1,256,2048]{2,1,0:T(8,128)S(1)}, f32[1,256,2048]{2,1,0:T(8,128)}, u32[]{:S(2)}) copy-start(f32[1,256,2048]{2,1,0:T(8,128)} %param.19) | copy-start | bytes 6291460
  76.2 735.3 %reduce-scatter.8.cloned.1.call-start = ((), (), s32[]{:S(2)}) async-start(), calls=%async_computation.8 | async-start | bytes 7864320 | tf_op jit(solution)/shard_map/reduce_scatter | solution.py:685
  259.3 64.2 %copy-start.15 = (pred[1024,1024]{0,1:T(8,128)(4,1)}, pred[1024,1024]{0,1:T(8,128)(4,1)S(1)}, u32[]{:S(2)}) copy-start(pred[1024,1024]{0,1:T(8,128)(4,1)S(1)} %fusion.28) | copy-start | bytes 3145732
  411.8 10.8 %copy-start.23 = (bf16[2048,2048]{1,0:T(8,128)(2,1)S(1)}, bf16[2048,2048]{1,0:T(8,128)(2,1)}, u32[]{:S(2)}) copy-start(bf16[2048,2048]{1,0:T(8,128)(2,1)} %shard_map.324) | copy-start | bytes 25165828
  422.6 20.2 %slice-start.2 = ((s8[8388608]{0:T(1024)(128)(4,1)}), s8[4194304]{0:T(1024)(128)(4,1)S(1)}, s32[]{:S(2)}) async-start(s8[8388608]{0:T(1024)(128)(4,1)} %bitcast.295), calls=%async_computation.11 | async-start | bytes 8388608
  430.7 12.1 %slice-start.3 = ((s8[8388608]{0:T(1024)(128)(4,1)}), s8[4194304]{0:T(1024)(128)(4,1)S(1)}, s32[]{:S(2)}) async-start(s8[8388608]{0:T(1024)(128)(4,1)} %bitcast.295), calls=%async_computation.12 | async-start | bytes 8388608
  462.4 386.3 %reduce-scatter.6.cloned.1.call-start = ((), (), s32[]{:S(2)}) async-start(), calls=%async_computation.7 | async-start | bytes 7864320 | tf_op jit(solution)/shard_map/reduce_scatter | solution.py:685
  489.3 14.6 %copy-start.64 = (bf16[2048,512]{0,1:T(8,128)(2,1)S(1)}, bf16[2048,512]{0,1:T(8,128)(2,1)}, u32[]{:S(2)}) copy-start(bf16[2048,512]{0,1:T(8,128)(2,1)} %copy-done.63) | copy-start | bytes 6291460
  569.4 10.7 %copy-start.66 = (bf16[2048,512]{0,1:T(8,128)(2,1)S(1)}, bf16[2048,512]{0,1:T(8,128)(2,1)}, u32[]{:S(2)}) copy-start(bf16[2048,512]{0,1:T(8,128)(2,1)} %get-tuple-element.48) | copy-start | bytes 6291460
  569.4 10.7 %copy-start.67 = (bf16[2048,512]{0,1:T(8,128)(2,1)S(1)}, bf16[2048,512]{0,1:T(8,128)(2,1)}, u32[]{:S(2)}) copy-start(bf16[2048,512]{0,1:T(8,128)(2,1)} %get-tuple-element.49) | copy-start | bytes 6291460
  594.7 302.9 %reduce-scatter.4.cloned.1.call-start = ((), (), s32[]{:S(2)}) async-start(), calls=%async_computation.6 | async-start | bytes 7077888 | tf_op jit(solution)/shard_map/reduce_scatter | solution.py:719
  679.7 33.7 %copy-start.53 = (bf16[1024]{0:T(1024)(128)(2,1)S(1)}, bf16[1024]{0:T(1024)(128)(2,1)}, u32[]{:S(2)}) copy-start(bf16[1024]{0:T(1024)(128)(2,1)} %get-tuple-element.88) | copy-start | bytes 6148
  779.7 29.8 %copy-start.1 = (f32[1,256,2048]{2,1,0:T(8,128)S(1)}, f32[1,256,2048]{2,1,0:T(8,128)}, u32[]{:S(2)}) copy-start(f32[1,256,2048]{2,1,0:T(8,128)} %param.19) | copy-start | bytes 6291460
  779.7 29.8 %copy-start.45 = (f32[256]{0:T(256)S(1)}, f32[256]{0:T(256)}, u32[]{:S(2)}) copy-start(f32[256]{0:T(256)} %copy-done.44) | copy-start | bytes 3076
  897.6 15.9 %all-to-all-start = ((bf16[4,64,1536]{2,1,0:T(8,128)(2,1)}), bf16[4,64,1536]{2,1,0:T(8,128)(2,1)}, u32[]{:S(2)}, u32[]{:S(2)}) async-start(bf16[4,64,1536]{2,1,0:T(8,128)(2,1)} %bitcast.312), calls=%async_computation.1 | async-start | bytes 1572864 | tf_op jit(solution)/shard_map/all_to_all | solution.py:727
  981.0 9.8 copy-start.35
  981.0 9.8 copy-start.38
  981.1 9.8 copy-start.39
  981.1 11.2 %copy-start.31 = (f32[64,8192]{1,0:T(8,128)S(1)}, f32[64,8192]{1,0:T(8,128)}, u32[]{:S(2)}) copy-start(f32[64,8192]{1,0:T(8,128)} %param.31) | copy-start | bytes 6291460
  981.1 11.2 %copy-start.32 = (f32[64,8192]{1,0:T(8,128)S(1)}, f32[64,8192]{1,0:T(8,128)}, u32[]{:S(2)}) copy-start(f32[64,8192]{1,0:T(8,128)} %param.36) | copy-start | bytes 6291460
  (54 other events, 211.9 us)
Sparse Core Ops, SparseCore 0:
  53.4 149.0 all-gather.4
  204.0 116.0 all-gather.2
  462.5 108.0 reduce-scatter.7
  594.8 107.9 reduce-scatter.5
  771.5 126.1 reduce-scatter.3

commit v3 on v2

--- a/solution.py
+++ b/solution.py
@@ -27,6 +27,7 @@
 RATE_GAIN = 1.0
 
 EVERY = ("seq", "far", "near")
+TP = ("seq", "near")
 
 
 MESH_IDS = pl.DeviceIdType.MESH
@@ -314,48 +315,112 @@
     )(p)
 
 
-def exchange_plane_kernel(rows, x_ref, o_ref, local_sem, send_sems, recv_sems):
+def exchange_plane_kernel(count, *refs):
+    x_refs, o_refs = refs[:count], refs[count : 2 * count]
+    local_sems, send_sems, recv_sems = refs[2 * count :]
     s, n, core, across, beside = places()
     diagonal = (core + 2) % 4
     mine = s * 2 + n
-    others = [
-        (seq, near)
-        for near in (beside, n)
-        for seq in (diagonal, across, core, s)
-    ][:-1]
-
-    def at(p):
-        return pl.ds(p * rows, rows)
+    others = [(seq, near) for near in (beside, n) for seq in (diagonal, across, core, s)][:-1]
 
     meet(*[{"seq": seq, "near": near} for seq, near in others])
     copies, send = sender(send_sems, recv_sems)
-    for seq, near in others:
-        send((len(copies),), x_ref.at[at(seq * 2 + near)], o_ref.at[at(mine)], {"seq": seq, "near": near})
-    local = pltpu.make_async_copy(x_ref.at[at(mine)], o_ref.at[at(mine)], local_sem)
-    local.start()
+    locals_ = []
+    for k, (x_ref, o_ref) in enumerate(zip(x_refs, o_refs)):
+        rows = x_ref.shape[0] // 8
+
+        def at(p):
+            return pl.ds(p * rows, rows)
+
+        for seq, near in others:
+            target = {"seq": seq, "near": near}
+            send(len(copies), x_ref.at[at(seq * 2 + near)], o_ref.at[at(mine)], target)
+        locals_.append(pltpu.make_async_copy(x_ref.at[at(mine)], o_ref.at[at(mine)], local_sems.at[k]))
+        locals_[k].start()
     for copy in copies.values():
         copy.wait_recv()
     for copy in copies.values():
         copy.wait_send()
-    local.wait()
-
-
-def exchange_plane(x, collective_id):
+    for copy in locals_:
+        copy.wait()
+
+
+def exchange_plane(arrays, collective_id):
+    count = len(arrays)
     return pl.pallas_call(
-        functools.partial(exchange_plane_kernel, x.shape[0] // 8),
-        out_shape=jax.ShapeDtypeStruct(x.shape, x.dtype),
+        functools.partial(exchange_plane_kernel, count),
+        out_shape=[jax.ShapeDtypeStruct(x.shape, x.dtype) for x in arrays],
+        in_specs=[ANYWHERE] * count,
+        out_specs=[ANYWHERE] * count,
+        scratch_shapes=[
+            pltpu.SemaphoreType.DMA((count,)),
+            pltpu.SemaphoreType.DMA((7 * count,)),
+            pltpu.SemaphoreType.DMA((7 * count,)),
+        ],
+        compiler_params=pltpu.CompilerParams(collective_id=collective_id, has_side_effects=True),
+    )(*arrays)
+
+
+def scatter_near_kernel(p_ref, o_ref, mine, theirs, local_sems, out_sems, send_sems, recv_sems):
+    _, n, _, _, beside = places()
+    to_x = {"near": beside}
+    far_size = p_ref.shape[1]
+    meet(to_x)
+    copies, send = sender(send_sems, recv_sems)
+    locals_, outs = [], []
+    for f in range(far_size):
+        send(f, p_ref.at[:, f, beside], theirs.at[f], to_x)
+        locals_.append(pltpu.make_async_copy(p_ref.at[:, f, n], mine.at[f], local_sems.at[f]))
+        locals_[f].start()
+    for f in range(far_size):
+        locals_[f].wait()
+        copies[f].wait_recv()
+        for q in range(4):
+            add_rows(mine.at[f, q], mine.at[f, q], theirs.at[f, q], step=16)
+        outs.append(pltpu.make_async_copy(mine.at[f], o_ref.at[f], out_sems.at[f]))
+        outs[f].start()
+    for f in range(far_size):
+        outs[f].wait()
+        copies[f].wait_send()
+
+
+def scatter_near(p, collective_id):
+    seq, far_size, _, rows, columns = p.shape
+    return pl.pallas_call(
+        scatter_near_kernel,
+        out_shape=jax.ShapeDtypeStruct((far_size, seq, rows, columns), p.dtype),
         in_specs=[ANYWHERE],
         out_specs=ANYWHERE,
         scratch_shapes=[
-            pltpu.SemaphoreType.DMA,
-            pltpu.SemaphoreType.DMA((7,)),
-            pltpu.SemaphoreType.DMA((7,)),
+            pltpu.VMEM((far_size, seq, rows, columns), p.dtype),
+            pltpu.VMEM((far_size, seq, rows, columns), p.dtype),
+            pltpu.SemaphoreType.DMA((far_size,)),
+            pltpu.SemaphoreType.DMA((far_size,)),
+            pltpu.SemaphoreType.DMA((far_size,)),
+            pltpu.SemaphoreType.DMA((far_size,)),
         ],
-        compiler_params=pltpu.CompilerParams(collective_id=collective_id, has_side_effects=True),
-    )(x)
-
-
-def gather_heads_kernel(far_size, w_ref, x_ref, i_ref, o_ref, ox_ref, oi_ref, local_sems, send_sems, recv_sems):
+        compiler_params=pltpu.CompilerParams(
+            collective_id=collective_id, has_side_effects=True, vmem_limit_bytes=VMEM_LIMIT
+        ),
+    )(p)
+
+
+def gather_heads_kernel(
+    far_size,
+    w_ref,
+    x_ref,
+    i_ref,
+    d_ref,
+    e_ref,
+    o_ref,
+    ox_ref,
+    oi_ref,
+    od_ref,
+    oe_ref,
+    local_sems,
+    send_sems,
+    recv_sems,
+):
     s, n, core, across, beside = places()
     diagonal = (core + 2) % 4
     f = lax.axis_index("far")
@@ -363,7 +428,8 @@
     to_core, to_y, to_x = {"seq": core}, {"seq": across}, {"near": beside}
     right, left = {"far": (f + 1) % far_size}, {"far": (f + far_size - 1) % far_size}
 
-    meet(to_core, to_y, {"seq": diagonal}, to_x, right, left)
+    others = [(seq, near) for near in (beside, n) for seq in (diagonal, across, core, s)][:-1]
+    meet(*[{"seq": seq, "near": near} for seq, near in others], right, left)
     copies, send = sender(send_sems, recv_sems)
     keep = pltpu.make_async_copy(w_ref.at[s], o_ref.at[s, f, n], local_sems.at[0])
     keep.start()
@@ -378,6 +444,26 @@
         at = pl.ds(p * half, half)
         send(("y", p), x_ref.at[at], ox_ref.at[s, at], to_y)
         send(("c", p), x_ref.at[at], ox_ref.at[s, at], to_core)
+
+    def block(seq, near, p):
+        return od_ref.at[seq * 2 + near, pl.ds(p * half, half)]
+
+    def own(p):
+        return d_ref.at[pl.ds(p * half, half)]
+
+    keep_d = pltpu.make_async_copy(d_ref, od_ref.at[s * 2 + n], local_sems.at[3])
+    keep_d.start()
+    send("y0", own(0), block(s, n, 0), to_y)
+    send("x1", own(1), block(s, n, 1), to_x)
+    send("y1", own(1), block(s, n, 1), to_y)
+    send("x0", own(0), block(s, n, 0), to_x)
+    send("c0", own(0), block(s, n, 0), to_core)
+    send("c1", own(1), block(s, n, 1), to_core)
+    keep_e = pltpu.make_async_copy(e_ref.at[s * 2 + n], oe_ref.at[s * 2 + n], local_sems.at[4])
+    keep_e.start()
+    for k, (seq, near) in enumerate(others):
+        target = {"seq": seq, "near": near}
+        send(("e", k), e_ref.at[seq * 2 + near], oe_ref.at[s * 2 + n], target)
     keep.wait()
     for k in range(3):
         copies["w", k].wait_recv()
@@ -395,7 +481,7 @@
             device_id_type=MESH_IDS,
         )
 
-    base = 12
+    base = 33
 
     def beside_copy(far, sem):
         return along("x", far, to_x, sem)
@@ -450,11 +536,31 @@
                 at = pl.ds(p * half, half)
                 copies["y", p].wait_recv()
                 send(("yc", p), ox_ref.at[across, at], ox_ref.at[across, at], to_core)
+        if k == 1:
+            copies["y0"].wait_recv()
+            send("yx", block(across, n, 0), block(across, n, 0), to_x)
+            send("yc0", block(across, n, 0), block(across, n, 0), to_core)
+            copies["x1"].wait_recv()
+            send("xy", block(s, beside, 1), block(s, beside, 1), to_y)
+            send("xc1", block(s, beside, 1), block(s, beside, 1), to_core)
+            copies["y1"].wait_recv()
+            send("yc1", block(across, n, 1), block(across, n, 1), to_core)
+            copies["x0"].wait_recv()
+            send("xc0", block(s, beside, 0), block(s, beside, 0), to_core)
+        if k == min(2, far_size - 1):
+            copies["yx"].wait_recv()
+            send("dc0", block(across, beside, 0), block(across, beside, 0), to_core)
+            copies["xy"].wait_recv()
+            send("dc1", block(across, beside, 1), block(across, beside, 1), to_core)
+    for key in ("c0", "c1", "yc0", "yc1", "xc0", "xc1", "dc0", "dc1"):
+        copies[key].wait_recv()
     for p in range(2):
         copies["c", p].wait_recv()
         copies["yc", p].wait_recv()
     for k in range(3):
         copies["i", k].wait_recv()
+    for k in range(7):
+        copies["e", k].wait_recv()
     for k in range(far_size):
 
         @pl.when((f >= k) & (f < far_size - 1))
@@ -481,30 +587,103 @@
         copy.wait_send()
     keep_x.wait()
     keep_i.wait()
-
-
-def gather_heads(w, x, i, collective_id):
+    keep_d.wait()
+    keep_e.wait()
+
+
+def gather_heads(w, x, i, d, e, collective_id):
     far_size = lax.axis_size("far")
     _, rows, columns = w.shape
     tokens, width = x.shape
-    sems = 12 + 4 * far_size
-    full, all_x, all_i = pl.pallas_call(
+    sems = 33 + 4 * far_size
+    full, all_x, all_i, all_d, mine_e = pl.pallas_call(
         functools.partial(gather_heads_kernel, far_size),
         out_shape=[
             jax.ShapeDtypeStruct((4, far_size, 2, rows, columns), w.dtype),
             jax.ShapeDtypeStruct((4, tokens, width), x.dtype),
             jax.ShapeDtypeStruct((4, *i.shape), i.dtype),
+            jax.ShapeDtypeStruct((8, *d.shape), d.dtype),
+            jax.ShapeDtypeStruct(e.shape, e.dtype),
         ],
-        in_specs=[ANYWHERE] * 3,
-        out_specs=[ANYWHERE] * 3,
+        in_specs=[ANYWHERE] * 5,
+        out_specs=[ANYWHERE] * 5,
         scratch_shapes=[
-            pltpu.SemaphoreType.DMA((3,)),
+            pltpu.SemaphoreType.DMA((5,)),
             pltpu.SemaphoreType.DMA((sems,)),
             pltpu.SemaphoreType.DMA((sems,)),
         ],
         compiler_params=pltpu.CompilerParams(collective_id=collective_id, has_side_effects=True),
-    )(w, x, i)
-    return full.reshape(-1, columns), all_x.reshape(-1, width), all_i
+    )(w, x, i, d, e)
+    all_x, all_d = all_x.reshape(-1, width), all_d.reshape(-1, d.shape[1])
+    return full.reshape(-1, columns), all_x, all_i, all_d, mine_e
+
+
+def feed_kernel(x_ref, d_ref, w_ref, *refs):
+    before, (act_ref, dgu_ref, y_ref, dx_ref) = refs[:-4], refs[-4:]
+    part = w_ref.shape[1] // 3
+    low = jnp.bfloat16
+    x = x_ref[...]
+    gate = product(x, w_ref[:, :part], 1, 0)
+    upper = product(x, w_ref[:, part : 2 * part], 1, 0)
+    dact = product(d_ref[...], w_ref[:, 2 * part :], 1, 0)
+    sig = 1.0 / (1.0 + jnp.exp(-gate))
+    silu = gate * sig
+    act = (silu * upper).astype(low)
+    act_ref[...] = act
+    dgu_ref[:, :part] = (dact * upper * (sig + silu * (1.0 - sig))).astype(low)
+    dgu_ref[:, part:] = (dact * silu).astype(low)
+    y = product(act, w_ref[:, 2 * part :], 1, 1)
+    dx = product(dgu_ref[...], w_ref[:, : 2 * part], 1, 1)
+    if before:
+        y = y + before[0][...].astype(jnp.float32)
+        dx = dx + before[1][...].astype(jnp.float32)
+    y_ref[...] = y.astype(low)
+    dx_ref[...] = dx.astype(low)
+
+
+def feed(x, d, w, before, tile=512):
+    tokens, width = x.shape
+    part = w.shape[1] // 3
+    low = jnp.bfloat16
+
+    def tokens_of(columns):
+        return pl.BlockSpec((tile, columns), lambda t: (t, 0))
+
+    whole = pl.BlockSpec(w.shape, lambda t: (0, 0), pipeline_mode=pl.Buffered(1))
+    sizes = (part, 2 * part, width, width)
+    return pl.pallas_call(
+        feed_kernel,
+        grid=(tokens // tile,),
+        out_shape=[jax.ShapeDtypeStruct((tokens, columns), low) for columns in sizes],
+        in_specs=[tokens_of(width), tokens_of(width), whole] + [tokens_of(width)] * len(before),
+        out_specs=[tokens_of(columns) for columns in sizes],
+        compiler_params=pltpu.CompilerParams(vmem_limit_bytes=VMEM_LIMIT),
+        cost_estimate=pl.CostEstimate(flops=12 * tokens * width * part, bytes_accessed=60_000_000, transcendentals=0),
+    )(x, d, w, *before)
+
+
+def feed_grads_kernel(x_ref, d_ref, dgu_ref, act_ref, o_ref):
+    split = dgu_ref.shape[1]
+    o_ref[:, :split] = product(x_ref[...], dgu_ref[...], 0, 0).astype(o_ref.dtype)
+    o_ref[:, split:] = product(d_ref[...], act_ref[...], 0, 0).astype(o_ref.dtype)
+
+def feed_grads(x, d, dgu, act, tile=256):
+    tokens, width = x.shape
+    columns = dgu.shape[1] + act.shape[1]
+    some = pl.BlockSpec((tokens, tile), lambda t: (0, t))
+
+    def whole(array):
+        return pl.BlockSpec(array.shape, lambda t: (0, 0), pipeline_mode=pl.Buffered(1))
+
+    return pl.pallas_call(
+        feed_grads_kernel,
+        grid=(width // tile,),
+        out_shape=jax.ShapeDtypeStruct((width, columns), x.dtype),
+        in_specs=[some, some, whole(dgu), whole(act)],
+        out_specs=pl.BlockSpec((tile, columns), lambda t: (t, 0)),
+        compiler_params=pltpu.CompilerParams(vmem_limit_bytes=VMEM_LIMIT),
+        cost_estimate=pl.CostEstimate(flops=2 * tokens * width * columns, bytes_accessed=40_000_000, transcendentals=0),
+    )(x, d, dgu, act)
 
 
 def rotary_tables(positions, width):
@@ -539,23 +718,158 @@
     )
 
 
-def adam_step(weight, grad, first, second, factor, rate, decay):
-    clipped = grad * factor
-    first_new = BETA_ONE * first + (1.0 - BETA_ONE) * clipped
-    second_new = BETA_TWO * second + (1.0 - BETA_TWO) * clipped * clipped
+def adam_step(weight, grad, first, second, rate, decay):
+    first_new = BETA_ONE * first + (1.0 - BETA_ONE) * grad
+    second_new = BETA_TWO * second + (1.0 - BETA_TWO) * grad * grad
     corr_one = 1.0 - BETA_ONE**STEP
     corr_two = 1.0 - BETA_TWO**STEP
-    update = first_new / corr_one / (jnp.sqrt(second_new / corr_two) + ADAM_EPSILON)
+    update = (first_new * (1.0 / corr_one)) / (jnp.sqrt(second_new * (1.0 / corr_two)) + ADAM_EPSILON)
     return (weight - rate * (update + decay * weight), first_new, second_new)
+
+
+def feed_pieces(part):
+    gateup, down = [], []
+    for half in range(2):
+        for device in range(8):
+            start = (half * 8 + device) * part
+            gateup.append((half, device, 0, start))
+            gateup.append((half, device, part, FEED_UNITS + start))
+            down.append((half, device, 2 * part, start))
+    return gateup, down
+
+
+def head_pieces_of(columns):
+    key = columns // 6
+    query = 2 * key
+    qkv, out = [], []
+    for device in range(4):
+        qkv.append((device, 0, device * query, query))
+        qkv.append((device, query, 4 * query + device * key, key))
+        qkv.append((device, query + key, 4 * (query + key) + device * key, key))
+        out.append((device, query + 2 * key, device * query, query))
+    return qkv, out
+
+
+def norm_kernel(zero_ref, one_ref, head_ref, qkv_ref, gateup_ref, gains_ref, square_ref, gain_grads_ref):
+    halves = (zero_ref, one_ref)
+    part = zero_ref.shape[2] // 3
+    gateup, down = feed_pieces(part)
+    qkv, out = head_pieces_of(head_ref.shape[2])
+    gains = gains_ref[...].astype(jnp.bfloat16).astype(jnp.float32)
+
+    def low(x):
+        return x.astype(jnp.bfloat16).astype(jnp.float32)
+
+    def over(x):
+        return jnp.sum(x, 1, keepdims=True)
+
+    two_squares = two_terms = down_squares = 0.0
+    for half, device, at, column in gateup:
+        grad = halves[half][device, :, at : at + part].astype(jnp.float32)
+        two_squares = two_squares + grad * grad
+        two_terms = two_terms + grad * low(gateup_ref[:, column : column + part])
+    for half, device, at, column in down:
+        grad = halves[half][device, :, at : at + part].astype(jnp.float32)
+        down_squares = down_squares + grad * grad
+    one_squares = one_terms = out_squares = 0.0
+    for device, at, column, size in qkv:
+        grad = head_ref[device, :, at : at + size].astype(jnp.float32)
+        one_squares = one_squares + over(grad * grad)
+        one_terms = one_terms + over(grad * low(qkv_ref[:, column : column + size]))
+    for device, at, column, size in out:
+        grad = head_ref[device, :, at : at + size].astype(jnp.float32)
+        out_squares = out_squares + over(grad * grad)
+    two_terms = over(two_terms)
+    gain_grads_ref[:, 0:1] = one_terms
+    gain_grads_ref[:, 1:2] = two_terms
+    one, two = gains[:, 0:1], gains[:, 1:2]
+    rows = (
+        one * one * one_squares
+        + two * two * over(two_squares)
+        + over(down_squares)
+        + out_squares
+        + one_terms * one_terms
+        + two_terms * two_terms
+    )
+    total = jnp.sum(rows)
+
+    @pl.when(pl.program_id(0) == 0)
+    def _():
+        square_ref[0, 0] = total
+
+    @pl.when(pl.program_id(0) > 0)
+    def _():
+        square_ref[0, 0] = square_ref[0, 0] + total
+
+
+ROWS = 16
+
+
+def rows_of(array):
+    if array.ndim == 3:
+        return pl.BlockSpec((array.shape[0], ROWS, array.shape[2]), lambda r: (0, r, 0))
+    return pl.BlockSpec((ROWS, array.shape[1]), lambda r: (r, 0))
+
+
+def gradient_norm(zero, one, head, qkv, gateup, gains):
+    arrays = (zero, one, head, qkv, gateup, gains)
+    return pl.pallas_call(
+        norm_kernel,
+        grid=(gains.shape[0] // ROWS,),
+        out_shape=[jax.ShapeDtypeStruct((1, 1), jnp.float32), jax.ShapeDtypeStruct(gains.shape, jnp.float32)],
+        in_specs=[rows_of(x) for x in arrays],
+        out_specs=[pl.BlockSpec(memory_space=pltpu.SMEM), rows_of(gains)],
+        compiler_params=pltpu.CompilerParams(vmem_limit_bytes=VMEM_LIMIT),
+    )(*arrays)
+
+
+def adam_kernel(clip_ref, zero_ref, one_ref, head_ref, gain_grads_ref, *refs):
+    weights, firsts, seconds = refs[0:5], refs[5:10], refs[10:15]
+    weights_out, firsts_out, seconds_out = refs[15:20], refs[20:25], refs[25:30]
+    halves = (zero_ref, one_ref)
+    part = zero_ref.shape[2] // 3
+    gateup, down = feed_pieces(part)
+    qkv, out = head_pieces_of(head_ref.shape[2])
+    clip = clip_ref[0, 0]
+    gains = weights[4][...].astype(jnp.bfloat16).astype(jnp.float32) * clip
+    one, two = gains[:, 0:1], gains[:, 1:2]
+
+    def step(which, columns, grad, rate, decay):
+        new = adam_step(
+            weights[which][:, columns], grad, firsts[which][:, columns], seconds[which][:, columns], rate, decay
+        )
+        weights_out[which][:, columns] = new[0]
+        firsts_out[which][:, columns] = new[1]
+        seconds_out[which][:, columns] = new[2]
+
+    for pieces, which, scale, rate in ((qkv, 0, one, RATE_MATRIX), (out, 1, clip, RATE_OUTPUT)):
+        for device, at, column, size in pieces:
+            grad = head_ref[device, :, at : at + size].astype(jnp.float32) * scale
+            step(which, slice(column, column + size), grad, rate, DECAY_MATRIX)
+    for pieces, which, scale in ((gateup, 2, two), (down, 3, clip)):
+        for half, device, at, column in pieces:
+            grad = halves[half][device, :, at : at + part].astype(jnp.float32) * scale
+            step(which, slice(column, column + part), grad, RATE_MATRIX, DECAY_MATRIX)
+    step(4, slice(0, 2), gain_grads_ref[...] * clip, RATE_GAIN, 0.0)
+
+
+def adam(clip, zero, one, head, gain_grads, weights, firsts, seconds):
+    state = (*weights, *firsts, *seconds)
+    arrays = (zero, one, head, gain_grads, *state)
+    return pl.pallas_call(
+        adam_kernel,
+        grid=(gain_grads.shape[0] // ROWS,),
+        out_shape=[jax.ShapeDtypeStruct(x.shape, x.dtype) for x in state],
+        in_specs=[pl.BlockSpec(memory_space=pltpu.SMEM)] + [rows_of(x) for x in arrays],
+        out_specs=[rows_of(x) for x in state],
+        compiler_params=pltpu.CompilerParams(vmem_limit_bytes=VMEM_LIMIT),
+    )(clip, *arrays)
 
 
 def product(left, right, left_dim, right_dim):
     return lax.dot_general(
         left, right, (((left_dim,), (right_dim,)), ((), ())), preferred_element_type=jnp.float32
     )
-
-
-CHUNKS = 2
 
 
 def shards(
@@ -593,7 +907,7 @@
     mine_q, mine_k = query_width // seq, key_width // seq
     mine_qkv = mine_q + 2 * mine_k
     units = FEED_UNITS // group
-    part = units // CHUNKS
+    part = units // 2
     factor = 1.0 / math.sqrt(HEAD_SIZE)
     low = jnp.bfloat16
 
@@ -603,6 +917,9 @@
     gains = norm_gains.astype(low).astype(jnp.float32)
     gain_one, gain_two = gains[:, :1], gains[:, 1:]
 
+    def after(x, *others):
+        return lax.optimization_barrier((x, *others))[0]
+
     def rounded(weight, gain=None):
         weight = weight.astype(low)
         return weight if gain is None else (weight.astype(jnp.float32) * gain).astype(low)
@@ -614,14 +931,18 @@
     def far_last(x):
         return x.reshape(-1, far, seq, 2 * rows).transpose(0, 2, 1, 3).reshape(-1, width)
 
-    gateup_low = rounded(gateup_weight, gain_two).reshape(rows, 2, group, CHUNKS, part)
-    down_low = rounded(down_weight).reshape(rows, 1, group, CHUNKS, part)
-    feed_pieces = jnp.concatenate([gateup_low, down_low], 1).transpose(3, 2, 0, 1, 4)
-    feed_pieces = feed_pieces.reshape(CHUNKS, group * rows, 3 * part)
-    feed = []
-    for c in range(CHUNKS):
-        piece = exchange_plane(feed_pieces[c], 1)
-        feed.append(lax.all_gather(piece, "far", axis=0, tiled=True))
+    def feed_piece(half):
+        start, size = half * FEED_UNITS // 2, FEED_UNITS // 2
+        columns = [
+            rounded(gateup_weight[:, start : start + size], gain_two),
+            rounded(gateup_weight[:, FEED_UNITS + start : FEED_UNITS + start + size], gain_two),
+            rounded(down_weight[:, start : start + size]),
+        ]
+        columns = [x.reshape(rows, group, part).transpose(1, 0, 2) for x in columns]
+        return jnp.concatenate(columns, 2)
+
+    (piece,) = exchange_plane([feed_piece(0).reshape(group * rows, 3 * part)], 1)
+    feed_zero = lax.all_gather(piece, "far", axis=0, tiled=True)
 
     qkv_low = rounded(query_key_value_weight, gain_one)
     head_pieces = jnp.concatenate(
@@ -635,7 +956,12 @@
     ).transpose(1, 0, 2)
     unit_one, scale_one = rms_normalize(inputs)
     spots = jnp.pad(positions.reshape(-1, 128), ((0, 8 - here // 128), (0, 0)))
-    head_w, normed_one, all_spots = gather_heads(head_pieces, unit_one.astype(low), spots, 2)
+    dout_here = far_first(cotangent.astype(low))
+    head_pieces = after(head_pieces, piece)
+    head_w, normed_one, all_spots, dout, piece = gather_heads(
+        head_pieces, unit_one.astype(low), spots, dout_here, feed_piece(1), 2
+    )
+    feed_one = lax.all_gather(piece.reshape(group * rows, -1), "far", axis=0, tiled=True)
     qkv, out = head_w[:, :mine_qkv], head_w[:, mine_qkv:]
     all_positions = all_spots[:, : here // 128].reshape(full)
 
@@ -662,34 +988,22 @@
     hidden = inputs + scatter_seq(product(heads, out, 1, 1).astype(low), 3)
     unit_two, scale_two = rms_normalize(hidden)
     normed_two = gather_plane(far_first(unit_two.astype(low)), 4)
-    dout = gather_plane(far_first(cotangent.astype(low)), 4)
-
-    dnormed_two, output_terms, feed_grads = 0.0, 0.0, []
-    for w in feed:
-        gateup_w, down_w = w[:, : 2 * part], w[:, 2 * part :]
-        gate = product(normed_two, gateup_w[:, :part], 1, 0)
-        upper = product(normed_two, gateup_w[:, part:], 1, 0)
-        sig = jax.nn.sigmoid(gate)
-        act = (gate * sig * upper).astype(low)
-        dact = product(dout, down_w, 1, 0)
-        dgate = dact * upper * sig * (1.0 + gate * (1.0 - sig))
-        dupper = dact * gate * sig
-        dgateup = jnp.concatenate([dgate.astype(low), dupper.astype(low)], 1)
-        terms = jnp.concatenate(
-            [
-                product(normed_two, dgateup, 0, 0).astype(low),
-                product(dout, act, 0, 0).astype(low),
-            ],
-            1,
-        )
-        feed_grads.append(lax.psum_scatter(terms, "far", scatter_dimension=0, tiled=True))
-        dnormed_two = dnormed_two + product(dgateup, gateup_w, 1, 1)
-        output_terms = output_terms + product(act, down_w, 1, 1)
-    dnormed_two = far_last(scatter_plane(dnormed_two.astype(low), 5))
+    act_zero, dgateup_zero, *sums = feed(normed_two, dout, feed_zero, ())
+    terms_zero = feed_grads(normed_two, dout, dgateup_zero, act_zero)
+    feed_one = after(feed_one, terms_zero)
+    act_one, dgateup_one, output_terms, dnormed_two = feed(normed_two, dout, feed_one, sums)
+    dnormed_two = scatter_plane(dnormed_two, 5)
+    dgateup_one = after(dgateup_one, dnormed_two)
+    terms_one = feed_grads(normed_two, dout, dgateup_one, act_one)
+    dnormed_two = far_last(dnormed_two)
+    grads_zero = lax.psum_scatter(terms_zero, "far", scatter_dimension=0, tiled=True)
+    grads_one = lax.psum_scatter(
+        after(terms_one, grads_zero), "far", scatter_dimension=0, tiled=True
+    )
     back_two = norm_backward(dnormed_two, unit_two, scale_two)
     dhidden = cotangent + back_two
 
-    dattended = gather_seq(dhidden.astype(low), 6)
+    dattended = gather_seq(after(dhidden.astype(low), terms_one), 6)
     dheads = product(dattended, out, 1, 0).astype(low).reshape(full, local_kv, per_kv, HEAD_SIZE)
     dheads = dheads * live.astype(low)
     dvalues = jnp.einsum("kgqj,qkgd->jkd", probs_low, dheads, preferred_element_type=jnp.float32)
@@ -715,57 +1029,33 @@
         ],
         1,
     )
-    head_terms = head_terms.reshape(seq, far * 2, rows, -1).transpose(1, 0, 2, 3)
+    head_terms = scatter_near(head_terms.reshape(seq, far, 2, rows, -1), 8)
+    head_terms = after(head_terms, grads_zero, grads_one)
     head_terms = lax.psum_scatter(
-        head_terms.reshape(width, -1), ("far", "near"), scatter_dimension=0, tiled=True
+        head_terms.reshape(far * seq * rows, -1), "far", scatter_dimension=0, tiled=True
     )
     dnormed_one = scatter_seq(product(dfused, qkv, 1, 1).astype(low), 3)
     back_one = norm_backward(dnormed_one, unit_one, scale_one)
     input_grad = dhidden + back_one
-    layer_output = hidden + far_last(scatter_plane(output_terms.astype(low), 5))
-
+    output_terms = scatter_plane(after(output_terms, dnormed_one), 5)
+    layer_output = hidden + far_last(output_terms)
+
+    halves = exchange_plane([grads_zero, grads_one], 7)
+    head_terms = after(head_terms, output_terms, halves[0])
+    halves = [x.reshape(group, rows, 3 * part) for x in halves]
     head_grads = lax.all_to_all(head_terms.reshape(seq, rows, -1), "seq", 0, 0, tiled=True)
-    head_grads = head_grads.astype(jnp.float32)
-
-    def head_rows(start, size):
-        return head_grads[:, :, start : start + size].transpose(1, 0, 2).reshape(rows, -1)
-
-    grad_qkv = jnp.concatenate(
-        [head_rows(0, mine_q), head_rows(mine_q, mine_k), head_rows(mine_q + mine_k, mine_k)], 1
+
+    weights = (query_key_value_weight, out_weight, gateup_weight, down_weight, norm_gains)
+    firsts = (query_key_value_moment, output_weight_moment, gate_up_moment, down_weight_moment, norm_gains_moment)
+    seconds = (query_key_value_variance, out_second, gateup_second, down_second, gains_second)
+    squares, gain_grads = gradient_norm(
+        *halves, head_grads, query_key_value_weight, gateup_weight, norm_gains
     )
-    grad_out = head_rows(mine_qkv, mine_q)
-    feed_grads = jnp.stack(
-        [exchange_plane(grads, 1).reshape(group, rows, 3, part) for grads in feed_grads], 3
-    ).astype(jnp.float32)
-    feed_grads = feed_grads.transpose(1, 2, 0, 3, 4)
-    grad_gateup = feed_grads[:, :2].reshape(rows, 2 * FEED_UNITS)
-    grad_down = feed_grads[:, 2].reshape(rows, FEED_UNITS)
-
-    gain_term_one = jnp.sum(rounded(query_key_value_weight) * grad_qkv, 1, keepdims=True)
-    gain_term_two = jnp.sum(rounded(gateup_weight) * grad_gateup, 1, keepdims=True)
-    grad_gains = jnp.concatenate([gain_term_one, gain_term_two], 1)
-    grad_qkv = grad_qkv * gain_one
-    grad_gateup = grad_gateup * gain_two
-
-    local_squares = (
-        jnp.sum(grad_qkv * grad_qkv)
-        + jnp.sum(grad_out * grad_out)
-        + jnp.sum(grad_gateup * grad_gateup)
-        + jnp.sum(grad_down * grad_down)
-        + jnp.sum(grad_gains * grad_gains)
-    )
-    grad_norm = jnp.sqrt(lax.psum(local_squares, EVERY))
+    squares = lax.psum(lax.psum(lax.psum(squares[0, 0], "seq"), "near"), "far")
+    grad_norm = jnp.sqrt(squares)
     clip = CLIP_NORM / jnp.maximum(grad_norm, CLIP_NORM)
-    steps = (
-        (query_key_value_weight, grad_qkv, query_key_value_moment, query_key_value_variance, RATE_MATRIX, DECAY_MATRIX),
-        (out_weight, grad_out, output_weight_moment, out_second, RATE_OUTPUT, DECAY_MATRIX),
-        (gateup_weight, grad_gateup, gate_up_moment, gateup_second, RATE_MATRIX, DECAY_MATRIX),
-        (down_weight, grad_down, down_weight_moment, down_second, RATE_MATRIX, DECAY_MATRIX),
-        (norm_gains, grad_gains, norm_gains_moment, gains_second, RATE_GAIN, 0.0),
-    )
-    stepped = [adam_step(w, g, m, v, clip, rate, decay) for w, g, m, v, rate, decay in steps]
-    nexts, firsts, seconds = zip(*stepped)
-    return (layer_output[None], input_grad[None], grad_norm, *nexts, *firsts, *seconds)
+    stepped = adam(clip.reshape(1, 1), *halves, head_grads, gain_grads, weights, firsts, seconds)
+    return (layer_output[None], input_grad[None], grad_norm, *stepped)
 
 
 def solution(mesh):

time: 1010 us -> 883 us (0.87)
  matrix products: 208 us -> 57.1 us
  Pallas kernels: 517 us -> 653 us
  local copies, waits for them, and re-layouts: 113 us -> 57.9 us
  other arithmetic: 94.9 us -> 45.7 us
  blocking collectives: 38.4 us -> 23.9 us
  waiting for transfers between devices: 6.97 us -> 18.5 us
    pallas_call x4 -> x9, Pallas kernels: 92.8 us -> 263 us  [the longest x1 71.3 us: scatter_near(): pl.pallas_call(scatter_near_kernel, out_shape=jax.ShapeDtypeStruct((far_s...]
    dot_general x20 -> x6, matrix products: 188 us -> 37 us  [product(): lax.dot_general(left, right, (((left_dim,), (right_dim,)), ((), ())), pre...]
    pallas_call x2 -> x1, Pallas kernels: 80.1 us -> 40 us  [gather_plane(): pl.pallas_call(functools.partial(gather_plane_kernel, rows), out_shape=ja...]
    sub x5 -> x0, other arithmetic: 19.9 us -> none  [adam_step(): return (weight - rate * (update + decay * weight), first_new, second_new)]
    another operation x4 -> x0, local copies, waits for them, and re-layouts: 19.3 us -> none  [shards(): jnp.stack([exchange_plane(grads, 1).reshape(group, rows, 3, part) for gra...]
    reshape x8, local copies, waits for them, and re-layouts: 17.6 us -> 2.68 us  [the longest x6 2.65 us: feed_piece(): columns = [x.reshape(rows, group, part).transpose(1, 0, 2) for x in columns]]
    psum x1 -> x3, blocking collectives: 38.4 us -> 23.9 us  [shards(): squares = lax.psum(lax.psum(lax.psum(squares[0, 0], 'seq'), 'near'), 'far')]
  transfers between devices with their start and end apart: 6 -> 6, of which waited for: 2 -> 2; matrix products, arithmetic and copies ran while one was open for 34% -> 15% of each run, Pallas kernels for 49% -> 69%
where the time goes in v3:
time: 883 us; the launch traced here: 877 us
  Pallas kernels  653 us (74%)
  local copies, waits for them, and re-layouts  57.9 us (7%)
  matrix products  57.1 us (6%)
  other arithmetic  45.7 us (5%)
  blocking collectives  23.9 us (3%)
  waiting for transfers between devices  18.5 us (2%)
  between operations  17.6 us (2%)
    pallas_call x1, Pallas kernels, gather_heads(): pl.pallas_call(functools.partial(gather_heads_kernel, far_size), out_shap...  172 us
    pallas_call x2, Pallas kernels, scatter_plane(): pl.pallas_call(functools.partial(scatter_plane_kernel, rows), out_shape=j...  84.7 us
    pallas_call x1, Pallas kernels, scatter_near(): pl.pallas_call(scatter_near_kernel, out_shape=jax.ShapeDtypeStruct((far_s...  71.3 us
    pallas_call x2, Pallas kernels, feed(): pl.pallas_call(feed_kernel, grid=(tokens // tile,), out_shape=[jax.ShapeD...  69.7 us
    pallas_call x2, Pallas kernels, exchange_plane(): pl.pallas_call(functools.partial(exchange_plane_kernel, count), out_shape...  60.3 us
    pallas_call x2, Pallas kernels, scatter_seq(): pl.pallas_call(functools.partial(scatter_seq_kernel, rows), out_shape=jax...  58.6 us
    pallas_call x1, Pallas kernels, gather_plane(): pl.pallas_call(functools.partial(gather_plane_kernel, rows), out_shape=ja...  40 us
    pallas_call x2, Pallas kernels, feed_grads(): pl.pallas_call(feed_grads_kernel, grid=(width // tile,), out_shape=jax.Sh...  38.3 us
  transfers between devices with their start and end apart: 6, of which 2 were waited for; matrix products, arithmetic and copies ran while one was open for 15% of the time, Pallas kernels for 69%

profile of v3, /device:TPU:0, one launch (start us, length us, event | category | flops | bytes accessed | tf_op | source)
XLA Modules:
  0.0 877.4 jit_solution(1254100857359673689)
XLA Ops:
  13.6 22.8 %shard_map.322 = bf16[512,1536]{1,0:T(8,128)(2,1)} custom-call(bf16[512,1536]{1,0:T(8,128)(2,1)} %bitcast.276), custom_call_target="tpu_custom_call" | custom-call | tf_op jit(solution)/shard_map/pallas_call | solution.py:350
  49.9 171.9 %shard_map.323 = (bf16[4,4,2,64,1536]{4,3,2,1,0:T(8,128)(2,1)}, bf16[4,256,2048]{2,1,0:T(8,128)(2,1)}, s32[4,8,128]{2,1,0:T(8,128)}, bf16[8,256,2048]{2,1,0:T(8,128)(2,1)}, bf16[8,64,1536]{2,1,0:T(8,128)(2,1)}) custom-call(bf16[4,64,1536]{2,1,0:T(8,128)(2,1)} %maximum_bitcast_fusion.w_ref, bf16[256,2048]{1,0:T(8,128)(2,1)} %fusion.23.x_ref, ...), custom_call_target="tpu_custom_call" | custom-call | tf_op jit(solution)/shard_map/pallas_call | solution.py:599
  222.1 7.6 fusion.14
  255.3 30.2 %shard_map.324 = f32[256,2048]{1,0:T(8,128)} custom-call(bf16[1024,2048]{1,0:T(8,128)(2,1)} %convolution_convert_fusion.p_ref), custom_call_target="tpu_custom_call" | custom-call | tf_op jit(solution)/shard_map/pallas_call | solution.py:299
  291.8 40.0 %shard_map.325.x_ref = bf16[2048,2048]{1,0:T(8,128)(2,1)} custom-call(bf16[256,2048]{1,0:T(8,128)(2,1)} %reshape.444.x_ref), custom_call_target="tpu_custom_call" | custom-call | tf_op jit(solution)/shard_map/pallas_call | solution.py:113
  331.9 32.8 %shard_map.326 = (bf16[2048,512]{1,0:T(8,128)(2,1)}, bf16[2048,1024]{1,0:T(8,128)(2,1)}, bf16[2048,2048]{1,0:T(8,128)(2,1)}, bf16[2048,2048]{1,0:T(8,128)(2,1)}) custom-call(bf16[2048,2048]{1,0:T(8,128)(2,1)} %shard_map.325.x_ref, bf16[2048,2048]{1,0:T(8,128)(2,1)} %bitcast.304, bf16[2048,1536]{1,0:T(8,128)(2,1)} %all-gather.5.cloned.1.call-done.w_ref), custom_call_target="tpu_custom_call" | custom-call | flops 25769803776 | bytes 60000000 | tf_op jit(solution)/shard_map/pallas_call | solution.py:654
  364.7 19.1 %shard_map.327 = bf16[2048,1536]{1,0:T(8,128)(2,1)} custom-call(bf16[2048,2048]{1,0:T(8,128)(2,1)} %shard_map.325.x_ref, bf16[2048,2048]{1,0:T(8,128)(2,1)} %bitcast.305, bf16[2048,1024]{1,0:T(8,128)(2,1)} %get-tuple-element.64.dgu_ref, bf16[2048,512]{1,0:T(8,128)(2,1)} %get-tuple-element.65.act_ref), custom_call_target="tpu_custom_call" | custom-call | flops 12884901888 | bytes 40000000 | tf_op jit(solution)/shard_map/pallas_call | solution.py:678
  383.9 36.9 %shard_map.328 = (bf16[2048,512]{1,0:T(8,128)(2,1)}, bf16[2048,1024]{1,0:T(8,128)(2,1)}, bf16[2048,2048]{1,0:T(8,128)(2,1)}, bf16[2048,2048]{1,0:T(8,128)(2,1)}) custom-call(bf16[2048,2048]{1,0:T(8,128)(2,1)} %shard_map.325.x_ref, bf16[2048,2048]{1,0:T(8,128)(2,1)} %bitcast.306, bf16[2048,1536]{1,0:T(8,128)(2,1)} %all-gather.3.cloned.1.call-done.w_ref, ...), custom_call_target="tpu_custom_call" | custom-call | flops 25769803776 | bytes 60000000 | tf_op jit(solution)/shard_map/pallas_call | solution.py:654
  420.8 41.6 %shard_map.329 = f32[256,2048]{1,0:T(8,128)} custom-call(bf16[2048,2048]{1,0:T(8,128)(2,1)} %get-tuple-element.70.p_ref), custom_call_target="tpu_custom_call" | custom-call | tf_op jit(solution)/shard_map/pallas_call | solution.py:240
  462.4 19.2 %shard_map.330 = bf16[2048,1536]{1,0:T(8,128)(2,1)} custom-call(bf16[2048,2048]{1,0:T(8,128)(2,1)} %shard_map.325.x_ref, bf16[2048,2048]{1,0:T(8,128)(2,1)} %bitcast.307, bf16[2048,1024]{1,0:T(8,128)(2,1)} %get-tuple-element.72.dgu_ref, bf16[2048,512]{1,0:T(8,128)(2,1)} %get-tuple-element.73.act_ref), custom_call_target="tpu_custom_call" | custom-call | flops 12884901888 | bytes 40000000 | tf_op jit(solution)/shard_map/pallas_call | solution.py:678
  481.6 10.7 %reduce-scatter.4.cloned.1.call-done.refs_0_ = bf16[512,1536]{1,0:T(8,128)(2,1)} async-done(((bf16[2048,1536]{1,0:T(8,128)(2,1)}), bf16[512,1536]{1,0:T(8,128)(2,1)}) %reduce-scatter.4.cloned.1.call-update) | async-done | bytes 1572880 | tf_op jit(solution)/shard_map/reduce_scatter | solution.py:999
  506.9 34.6 %shard_map.331 = bf16[1024,2048]{1,0:T(8,128)(2,1)} custom-call(bf16[256,2048]{1,0:T(8,128)(2,1)} %get-tuple-element.74.x_ref), custom_call_target="tpu_custom_call" | custom-call | tf_op jit(solution)/shard_map/pallas_call | solution.py:159
  541.5 6.3 broadcast_multiply_fusion
  576.8 6.4 convolution_convert_fusion.1
  586.6 8.7 copy.82
  595.3 71.3 %shard_map.335 = bf16[4,4,64,1536]{3,2,1,0:T(8,128)(2,1)} custom-call(bf16[4,4,2,64,1536]{4,3,2,1,0:T(8,128)(2,1)} %bitcast.266), custom_call_target="tpu_custom_call" | custom-call | tf_op jit(solution)/shard_map/pallas_call | solution.py:389
  669.4 8.3 convolution_convert_fusion.2.p_ref
  677.8 28.4 %shard_map.332 = f32[256,2048]{1,0:T(8,128)} custom-call(bf16[1024,2048]{1,0:T(8,128)(2,1)} %convolution_convert_fusion.2.p_ref), custom_call_target="tpu_custom_call" | custom-call | tf_op jit(solution)/shard_map/pallas_call | solution.py:299
  706.2 43.2 %shard_map.333 = f32[256,2048]{1,0:T(8,128)} custom-call(bf16[2048,2048]{1,0:T(8,128)(2,1)} %get-tuple-element.75.p_ref), custom_call_target="tpu_custom_call" | custom-call | tf_op jit(solution)/shard_map/pallas_call | solution.py:240
  757.3 37.5 %shard_map.334 = (bf16[512,1536]{1,0:T(8,128)(2,1)}, bf16[512,1536]{1,0:T(8,128)(2,1)}) custom-call(bf16[512,1536]{1,0:T(8,128)(2,1)} %reduce-scatter.4.cloned.1.call-done.refs_0_, bf16[512,1536]{1,0:T(8,128)(2,1)} %reduce-scatter.6.cloned.1.call-done.refs_1_), custom_call_target="tpu_custom_call" | custom-call | tf_op jit(solution)/shard_map/pallas_call | solution.py:350
  802.3 7.6 all-to-all-done.head_ref
  816.5 6.4 psum.21
  834.7 11.9 %psum.23 = f32[]{:T(128)} all-reduce(f32[]{:T(128)} %psum.22), channel_id=1, replica_groups=mesh['seq'=4,'far'=4,'near'=2] {'far'}, use_global_device_ids=true, to_apply=%region_12.13 | all-reduce | flops 1 | bytes 8 | tf_op jit(solution)/shard_map/psum | solution.py:1054
  847.3 17.8 %shard_map.337 = (f32[64,4096]{1,0:T(8,128)}, f32[64,2048]{1,0:T(8,128)}, f32[64,16384]{1,0:T(8,128)}, f32[64,8192]{1,0:T(8,128)}, f32[64,2]{1,0:T(8,128)}, /*in...) custom-call(f32[1,1]{1,0:T(1,128)} %bitcast.71.clip_ref, ...), custom_call_target="tpu_custom_call" | custom-call | tf_op jit(solution)/shard_map/pallas_call | solution.py:859
  (186 shorter events, 138.7 us)
Async XLA Ops:
  7.2 324.7 %all-gather.5.cloned.1.call-start = ((), (), s32[]{:S(2)}) async-start(), calls=%async_computation.5 | async-start | bytes 7864320 | tf_op jit(solution)/shard_map/all_gather | solution.py:945
  13.6 23.0 %copy-start.25 = (f32[64,2048]{1,0:T(8,128)S(1)}, f32[64,2048]{1,0:T(8,128)}, u32[]{:S(2)}) copy-start(f32[64,2048]{1,0:T(8,128)} %refs_1_.1) | copy-start | bytes 1572868
  36.4 347.5 %all-gather.3.cloned.1.call-start = ((), (), s32[]{:S(2)}) async-start(), calls=%async_computation.4 | async-start | bytes 7864320 | tf_op jit(solution)/shard_map/all_gather | solution.py:964
  36.6 3.5 copy-start.18
  40.2 4.9 copy-start.33
  40.2 5.5 copy-start
  221.8 270.4 %reduce-scatter.4.cloned.1.call-start = ((), (), s32[]{:S(2)}) async-start(), calls=%async_computation.6 | async-start | bytes 7864320 | tf_op jit(solution)/shard_map/reduce_scatter | solution.py:999
  229.7 14.2 %copy-start.16 = (f32[1024,1024]{0,1:T(8,128)}, f32[1024,1024]{0,1:T(8,128)S(1)}, u32[]{:S(2)}) copy-start(f32[1024,1024]{0,1:T(8,128)S(1)} %fusion.14) | copy-start | bytes 12582916
  232.1 4.8 copy-start.10
  383.8 282.9 %reduce-scatter.6.cloned.1.call-start = ((), (), s32[]{:S(2)}) async-start(), calls=%async_computation.7 | async-start | bytes 7864320 | tf_op jit(solution)/shard_map/reduce_scatter | solution.py:1000
  481.6 10.7 %copy-start.21 = (f32[256,2048]{1,0:T(8,128)S(1)}, f32[256,2048]{1,0:T(8,128)}, u32[]{:S(2)}) copy-start(f32[256,2048]{1,0:T(8,128)} %shard_map.329) | copy-start | bytes 6291460
  492.2 302.6 %reduce-scatter.8.cloned.1.call-start = ((), (), s32[]{:S(2)}) async-start(), calls=%async_computation.8 | async-start | bytes 3932160 | tf_op jit(solution)/shard_map/reduce_scatter | solution.py:1034
  547.8 6.0 slice-start
  547.8 6.4 slice-start.1
  554.1 3.5 copy-start.15
  554.1 3.5 copy-start.27
  567.5 3.9 copy-start.24
  567.5 3.9 copy-start.36
  576.8 6.4 copy-start.38
  753.3 3.6 copy-start.1
  753.3 3.6 copy-start.6
  753.3 3.6 copy-start.29
  794.8 15.1 %all-to-all-start = ((bf16[4,64,1536]{2,1,0:T(8,128)(2,1)}), bf16[4,64,1536]{2,1,0:T(8,128)(2,1)S(1)}, u32[]{:S(2)}, u32[]{:S(2)}) async-start(bf16[4,64,1536]{2,1,0:T(8,128)(2,1)} %bitcast.297), calls=%async_computation.3 | async-start | bytes 1572864 | tf_op jit(solution)/shard_map/all_to_all | solution.py:1046
  816.5 15.0 %copy-start.4 = (f32[256,2048]{1,0:T(8,128)S(1)}, f32[256,2048]{1,0:T(8,128)}, u32[]{:S(2)}) copy-start(f32[256,2048]{1,0:T(8,128)} %copy-done.2) | copy-start | bytes 6291460
  (24 other events, 49.3 us)
Sparse Core Ops, SparseCore 0:
  36.5 148.9 all-gather.4
  221.9 113.4 all-gather.2
  383.9 108.2 reduce-scatter.3
  494.4 111.2 reduce-scatter.5
  666.8 59.9 reduce-scatter.7

commit v4 on v3

--- a/solution.py
+++ b/solution.py
@@ -119,52 +119,6 @@
             pltpu.SemaphoreType.DMA,
             pltpu.SemaphoreType.DMA((14,)),
             pltpu.SemaphoreType.DMA((14,)),
-        ],
-        compiler_params=pltpu.CompilerParams(collective_id=collective_id, has_side_effects=True),
-    )(x)
-
-
-def gather_seq_kernel(rows, x_ref, o_ref, local_sem, send_sems, recv_sems):
-    s, _, core, across, _ = places()
-    half = rows // 2
-    to_core, to_y = {"seq": core}, {"seq": across}
-
-    def block(seq, part):
-        return o_ref.at[pl.ds(seq * rows + part * half, half)]
-
-    def own(part):
-        return x_ref.at[pl.ds(part * half, half)]
-
-    meet(to_core, to_y)
-    local = pltpu.make_async_copy(x_ref, o_ref.at[pl.ds(s * rows, rows)], local_sem)
-    local.start()
-    copies, send = sender(send_sems, recv_sems)
-    for part in range(2):
-        send(("y", part), own(part), block(s, part), to_y)
-    for part in range(2):
-        send(("c", part), own(part), block(s, part), to_core)
-    for part in range(2):
-        copies["y", part].wait_recv()
-        send(("yc", part), block(across, part), block(across, part), to_core)
-    for part in range(2):
-        copies["c", part].wait_recv()
-        copies["yc", part].wait_recv()
-    for copy in copies.values():
-        copy.wait_send()
-    local.wait()
-
-
-def gather_seq(x, collective_id):
-    rows, columns = x.shape
-    return pl.pallas_call(
-        functools.partial(gather_seq_kernel, rows),
-        out_shape=jax.ShapeDtypeStruct((4 * rows, columns), x.dtype),
-        in_specs=[ANYWHERE],
-        out_specs=ANYWHERE,
-        scratch_shapes=[
-            pltpu.SemaphoreType.DMA,
-            pltpu.SemaphoreType.DMA((6,)),
-            pltpu.SemaphoreType.DMA((6,)),
         ],
         compiler_params=pltpu.CompilerParams(collective_id=collective_id, has_side_effects=True),
     )(x)
@@ -361,50 +315,6 @@
     )(*arrays)
 
 
-def scatter_near_kernel(p_ref, o_ref, mine, theirs, local_sems, out_sems, send_sems, recv_sems):
-    _, n, _, _, beside = places()
-    to_x = {"near": beside}
-    far_size = p_ref.shape[1]
-    meet(to_x)
-    copies, send = sender(send_sems, recv_sems)
-    locals_, outs = [], []
-    for f in range(far_size):
-        send(f, p_ref.at[:, f, beside], theirs.at[f], to_x)
-        locals_.append(pltpu.make_async_copy(p_ref.at[:, f, n], mine.at[f], local_sems.at[f]))
-        locals_[f].start()
-    for f in range(far_size):
-        locals_[f].wait()
-        copies[f].wait_recv()
-        for q in range(4):
-            add_rows(mine.at[f, q], mine.at[f, q], theirs.at[f, q], step=16)
-        outs.append(pltpu.make_async_copy(mine.at[f], o_ref.at[f], out_sems.at[f]))
-        outs[f].start()
-    for f in range(far_size):
-        outs[f].wait()
-        copies[f].wait_send()
-
-
-def scatter_near(p, collective_id):
-    seq, far_size, _, rows, columns = p.shape
-    return pl.pallas_call(
-        scatter_near_kernel,
-        out_shape=jax.ShapeDtypeStruct((far_size, seq, rows, columns), p.dtype),
-        in_specs=[ANYWHERE],
-        out_specs=ANYWHERE,
-        scratch_shapes=[
-            pltpu.VMEM((far_size, seq, rows, columns), p.dtype),
-            pltpu.VMEM((far_size, seq, rows, columns), p.dtype),
-            pltpu.SemaphoreType.DMA((far_size,)),
-            pltpu.SemaphoreType.DMA((far_size,)),
-            pltpu.SemaphoreType.DMA((far_size,)),
-            pltpu.SemaphoreType.DMA((far_size,)),
-        ],
-        compiler_params=pltpu.CompilerParams(
-            collective_id=collective_id, has_side_effects=True, vmem_limit_bytes=VMEM_LIMIT
-        ),
-    )(p)
-
-
 def gather_heads_kernel(
     far_size,
     w_ref,
@@ -618,6 +528,345 @@
     return full.reshape(-1, columns), all_x, all_i, all_d, mine_e
 
 
+def tile_at(tile, rows):
+    return pl.ds(pl.multiple_of(tile * rows, rows), rows)
+
+
+def stacked(pair):
+    half = pair.shape[1] // 2
+    return jnp.concatenate([pair[:, :half], pair[:, half:]], 0)
+
+
+def turned(value, cos, sin):
+    half = value.shape[1] // 2
+    first, second = value[:, :half], value[:, half:]
+    return first * cos - second * sin, second * cos + first * sin
+
+
+def visible_keys(tile, rows, keys, length):
+    shape = (2 * rows, keys)
+    row = lax.broadcasted_iota(jnp.int32, shape, 0)
+    row = jnp.where(row >= rows, row - rows, row) + tile * rows
+    column = lax.broadcasted_iota(jnp.int32, shape, 1)
+    return (column <= row) & (column < length)
+
+
+def attention_kernel(length_ref, x_ref, w_ref, turn_ref, q_ref, k_ref, v_ref, heads_ref, lse_ref, p_ref):
+    rows = x_ref.shape[0] // 4
+    size = k_ref.shape[1]
+    low = jnp.bfloat16
+    length = length_ref[0]
+
+    def project(tile, carry):
+        at = tile_at(tile, rows)
+        merged = product(x_ref[at, :], w_ref[:, : 4 * size], 1, 0)
+        cos, sin = turn_ref[at, : size // 2], turn_ref[at, size // 2 :]
+        for ref, start, column, scale in (
+            (q_ref, 0, 0, size**-0.5),
+            (q_ref, size, size, size**-0.5),
+            (k_ref, 2 * size, 0, 1.0),
+        ):
+            first, second = turned(merged[:, start : start + size], cos, sin)
+            ref[at, column : column + size // 2] = (first * scale).astype(low)
+            ref[at, column + size // 2 : column + size] = (second * scale).astype(low)
+        v_ref[at, :] = merged[:, 3 * size :].astype(low)
+        return carry
+
+    lax.fori_loop(0, 4, project, 0)
+    for tile in range(4):
+        at = pl.ds(tile * rows, rows)
+        keys = (tile + 1) * rows
+        scores = product(stacked(q_ref[at, :]), k_ref[:keys, :], 1, 1)
+        scores = jnp.where(visible_keys(tile, rows, keys, length), scores, MASKED_SCORE)
+        peak = jnp.max(scores, 1, keepdims=True)
+        expo = jnp.exp(scores - peak)
+        total = jnp.sum(expo, 1, keepdims=True)
+        result = product((expo * (1.0 / total)).astype(low), v_ref[:keys, :], 1, 0)
+        live = lax.broadcasted_iota(jnp.int32, (rows, 1), 0) + tile * rows < length
+        lse = peak + jnp.log(total)
+        for head in range(2):
+            mine = slice(head * rows, (head + 1) * rows)
+            heads_ref[at, head * size : (head + 1) * size] = jnp.where(live, result[mine], 0.0).astype(low)
+            lse_ref[at, head : head + 1] = lse[mine]
+
+    def out(tile, carry):
+        at = tile_at(tile, rows)
+        p_ref[at, :] = product(heads_ref[at, :], w_ref[:, 4 * size :], 1, 1).astype(low)
+        return carry
+
+    lax.fori_loop(0, 4, out, 0)
+
+
+def attention(length, x, w, turns):
+    tokens, width = x.shape
+    size = w.shape[1] // 6
+    low = jnp.bfloat16
+    shapes = [(tokens, 2 * size), (tokens, size), (tokens, size), (tokens, 2 * size)]
+    return pl.pallas_call(
+        attention_kernel,
+        out_shape=[jax.ShapeDtypeStruct(shape, low) for shape in shapes]
+        + [jax.ShapeDtypeStruct((tokens, 128), jnp.float32), jax.ShapeDtypeStruct((tokens, width), low)],
+        in_specs=[pl.BlockSpec(memory_space=pltpu.SMEM)] + [IN_VMEM] * 3,
+        out_specs=[IN_VMEM] * 6,
+        compiler_params=pltpu.CompilerParams(vmem_limit_bytes=VMEM_LIMIT),
+        cost_estimate=pl.CostEstimate(flops=10_000_000_000, bytes_accessed=20_000_000, transcendentals=0),
+    )(length, x, w, turns)
+
+
+def attention_back_kernel(
+    length_ref,
+    q_ref,
+    k_ref,
+    v_ref,
+    heads_ref,
+    lse_ref,
+    turn_ref,
+    g_ref,
+    y_ref,
+    w_ref,
+    x_ref,
+    terms_ref,
+    dx_ref,
+    sum_ref,
+    weights,
+    tokens,
+    dheads,
+    dfused,
+    dk,
+    dv,
+    mine,
+    far,
+    hop_x,
+    hop_y,
+    last_x,
+    last_y,
+    far_d,
+    last_d,
+    out_grad,
+    qkv_grad,
+    out_there,
+    qkv_there,
+    local_sems,
+    send_sems,
+    recv_sems,
+):
+    s, n, core, across, beside = places()
+    other = (core + 2) % 4
+    to_core, to_y, to_x = {"seq": core}, {"seq": across}, {"near": beside}
+    rows = g_ref.shape[0]
+    half = rows // 2
+    size = k_ref.shape[1]
+    low = jnp.bfloat16
+    length = length_ref[0]
+    far_size = terms_ref.shape[0]
+
+    def local(source, target, at):
+        copy = pltpu.make_async_copy(source, target, local_sems.at[at])
+        copy.start()
+        return copy
+
+    def part(ref, p):
+        return ref.at[pl.ds(p * half, half)]
+
+    def token_rows(seq, p):
+        return tokens.at[pl.ds(seq * rows + p * half, half)]
+
+    def block(seq, near):
+        return y_ref.at[pl.ds((seq * 2 + near) * rows, rows)]
+
+    meet(to_core, to_y, to_x)
+    copies, send = sender(send_sems, recv_sems)
+    keep = local(g_ref, tokens.at[pl.ds(s * rows, rows)], 0)
+    for p in range(2):
+        send(("gy", p), part(g_ref, p), token_rows(s, p), to_y)
+    for p in range(2):
+        send(("gc", p), part(g_ref, p), token_rows(s, p), to_core)
+    given = [block(other, beside), block(other, n), block(core, beside), block(core, n)]
+    kept = [block(across, beside), block(across, n), block(s, beside), block(s, n)]
+    loads = []
+    for k in range(4):
+        send(k, given[k], far.at[k], to_core)
+        loads.append(local(kept[k], mine.at[k], 1 + k))
+    load_w = local(w_ref, weights, 5)
+    for k in range(3):
+        loads[k].wait()
+        copies[k].wait_recv()
+        add_rows(mine.at[k], mine.at[k], far.at[k])
+        if k == 0:
+            send("hx", part(mine.at[0], 0), hop_x, to_x)
+    send("x0", part(mine.at[2], 0), part(last_x, 0), to_x)
+    for p in range(2):
+        copies["gy", p].wait_recv()
+        send(("gyc", p), token_rows(across, p), token_rows(across, p), to_core)
+    send("hy", part(mine.at[0], 1), hop_y, to_y)
+    send("y1", part(mine.at[1], 1), part(last_y, 1), to_y)
+    loads[3].wait()
+    copies[3].wait_recv()
+    add_rows(sum_ref, mine.at[3], far.at[3])
+    keep.wait()
+    load_w.wait()
+    for p in range(2):
+        copies["gc", p].wait_recv()
+        copies["gyc", p].wait_recv()
+
+    def dheads_of(tile, carry):
+        at = tile_at(tile, rows)
+        live = lax.broadcasted_iota(jnp.int32, (rows, 1), 0) + tile * rows < length
+        value = product(tokens[at, :], weights[:, 4 * size :], 1, 0)
+        dheads[at, :] = jnp.where(live, value, 0.0).astype(low)
+        return carry
+
+    def by_rows(value):
+        return value.astype(low).reshape(far_size, 2, -1, value.shape[1])
+
+    width = tokens.shape[1]
+    quarter = width // 4
+    for q in range(4):
+        out_grad[q] = by_rows(product(tokens[:, q * quarter : (q + 1) * quarter], heads_ref[...], 0, 0))
+    send("out", out_grad.at[:, :, beside], out_there, to_x)
+    lax.fori_loop(0, 4, dheads_of, 0)
+    for copy in ("gyc", "gy", "gc"):
+        for p in range(2):
+            copies[copy, p].wait_send()
+    load_x = local(x_ref, tokens, 0)
+    copies["hx"].wait_recv()
+    add_rows(part(mine.at[1], 0), part(mine.at[1], 0), hop_x)
+    send("y0", part(mine.at[1], 0), part(last_y, 0), to_y)
+    copies["hy"].wait_recv()
+    add_rows(part(mine.at[2], 1), part(mine.at[2], 1), hop_y)
+    send("x1", part(mine.at[2], 1), part(last_x, 1), to_x)
+
+    dk[...] = jnp.zeros_like(dk)
+    dv[...] = jnp.zeros_like(dv)
+    for tile in range(4):
+        at = pl.ds(tile * rows, rows)
+        keys = (tile + 1) * rows
+        query = stacked(q_ref[at, :])
+        dhead = stacked(dheads[at, :])
+        scores = product(query, k_ref[:keys, :], 1, 1)
+        lse = jnp.concatenate([lse_ref[at, 0:1], lse_ref[at, 1:2]], 0)
+        probs = jnp.where(visible_keys(tile, rows, keys, length), jnp.exp(scores - lse), 0.0)
+        dprobs = product(dhead, v_ref[:keys, :], 1, 1)
+        inner = jnp.sum(probs * dprobs, 1, keepdims=True)
+        dscores = (probs * (dprobs - inner)).astype(low)
+        dv[:keys, :] += product(probs.astype(low), dhead, 0, 0)
+        dk[:keys, :] += product(dscores, query, 0, 0)
+        dquery = product(dscores, k_ref[:keys, :], 1, 0) * size**-0.5
+        cos, sin = turn_ref[at, : size // 2], turn_ref[at, size // 2 :]
+        for head in range(2):
+            rounded = dquery[head * rows : (head + 1) * rows].astype(low).astype(jnp.float32)
+            first, second = turned(rounded, cos, -sin)
+            dfused[at, head * size : head * size + size // 2] = first.astype(low)
+            dfused[at, head * size + size // 2 : (head + 1) * size] = second.astype(low)
+    first, second = turned(
+        dk[...].astype(low).astype(jnp.float32), turn_ref[:, : size // 2], -turn_ref[:, size // 2 :]
+    )
+    dfused[:, 2 * size : 2 * size + size // 2] = first.astype(low)
+    dfused[:, 2 * size + size // 2 : 3 * size] = second.astype(low)
+    dfused[:, 3 * size :] = dv[...].astype(low)
+
+    load_x.wait()
+    for q in range(4):
+        qkv_grad[q] = by_rows(product(tokens[:, q * quarter : (q + 1) * quarter], dfused[...], 0, 0))
+        send(("qkv", q), qkv_grad.at[q, :, beside], qkv_there.at[q], to_x)
+
+    for p, first, second in ((1, "y1", "x1"), (0, "x0", "y0")):
+        copies[first].wait_recv()
+        copies[second].wait_recv()
+        add_rows(part(sum_ref, p), part(sum_ref, p), part(last_x, p), part(last_y, p))
+    for key in ("hx", "hy", "y0", "y1", "x0", "x1"):
+        copies[key].wait_send()
+
+    def dx_of(k, tile):
+        mine[k] = product(dfused[tile_at(tile, rows), :], weights[:, : 4 * size], 1, 1).astype(low)
+
+    dx_of(0, other)
+    send("d0", mine.at[0], far_d.at[0], to_core)
+    dx_of(1, core)
+    send("d1", mine.at[1], far_d.at[1], to_core)
+    dx_of(2, across)
+    copies["d0"].wait_recv()
+    for p in range(2):
+        add_rows(part(mine.at[2], p), part(mine.at[2], p), part(far_d.at[0], p))
+        send(("dy", p), part(mine.at[2], p), part(last_d, p), to_y)
+    dx_of(3, s)
+    copies["d1"].wait_recv()
+    add_rows(dx_ref, mine.at[3], far_d.at[1])
+    outs = []
+    copies["out"].wait_recv()
+    for q in range(4):
+        for f in range(far_size):
+            out_there[q, f] = (
+                out_there[q, f].astype(jnp.float32) + out_grad[q, f, n].astype(jnp.float32)
+            ).astype(low)
+    for p in range(2):
+        copies["dy", p].wait_recv()
+        add_rows(part(dx_ref, p), part(dx_ref, p), part(last_d, p))
+    for q in range(4):
+        copies["qkv", q].wait_recv()
+        for f in range(far_size):
+            qkv_there[q, f] = (
+                qkv_there[q, f].astype(jnp.float32) + qkv_grad[q, f, n].astype(jnp.float32)
+            ).astype(low)
+        outs.append(local(out_there.at[q], terms_ref.at[:, q, :, 4 * size :], q))
+        outs.append(local(qkv_there.at[q], terms_ref.at[:, q, :, : 4 * size], 4 + q))
+    for copy in outs:
+        copy.wait()
+    waited = {"hx", "hy", "y0", "y1", "x0", "x1"}
+    for key, copy in copies.items():
+        if key not in waited and not (isinstance(key, tuple) and key[0] in ("gyc", "gy", "gc")):
+            copy.wait_send()
+
+
+def attention_back(length, saved, turns, g, y, w, x, collective_id):
+    q, k, v, heads, lse = saved
+    tokens, width = x.shape
+    size = k.shape[1]
+    rows = tokens // 4
+    far_size = lax.axis_size("far")
+    weight_rows = width // (8 * far_size)
+    low = jnp.bfloat16
+    block = pltpu.VMEM((rows, width), low)
+    half_block = pltpu.VMEM((rows // 2, width), low)
+    return pl.pallas_call(
+        attention_back_kernel,
+        out_shape=[
+            jax.ShapeDtypeStruct((far_size, 4, weight_rows, 6 * size), low),
+            jax.ShapeDtypeStruct((rows, width), jnp.float32),
+            jax.ShapeDtypeStruct((rows, width), jnp.float32),
+        ],
+        in_specs=[pl.BlockSpec(memory_space=pltpu.SMEM)] + [IN_VMEM] * 6 + [ANYWHERE] * 4,
+        out_specs=[ANYWHERE, IN_VMEM, IN_VMEM],
+        scratch_shapes=[
+            pltpu.VMEM(w.shape, low),
+            pltpu.VMEM((tokens, width), low),
+            pltpu.VMEM((tokens, 2 * size), low),
+            pltpu.VMEM((tokens, 4 * size), low),
+            pltpu.VMEM((tokens, size), jnp.float32),
+            pltpu.VMEM((tokens, size), jnp.float32),
+            pltpu.VMEM((4, rows, width), low),
+            pltpu.VMEM((4, rows, width), low),
+            half_block,
+            half_block,
+            block,
+            block,
+            pltpu.VMEM((2, rows, width), low),
+            block,
+            pltpu.VMEM((4, far_size, 2, weight_rows, 2 * size), low),
+            pltpu.VMEM((4, far_size, 2, weight_rows, 4 * size), low),
+            pltpu.VMEM((4, far_size, weight_rows, 2 * size), low),
+            pltpu.VMEM((4, far_size, weight_rows, 4 * size), low),
+            pltpu.SemaphoreType.DMA((8,)),
+            pltpu.SemaphoreType.DMA((25,)),
+            pltpu.SemaphoreType.DMA((25,)),
+        ],
+        compiler_params=pltpu.CompilerParams(
+            collective_id=collective_id, has_side_effects=True, vmem_limit_bytes=VMEM_LIMIT
+        ),
+        cost_estimate=pl.CostEstimate(flops=20_000_000_000, bytes_accessed=40_000_000, transcendentals=0),
+    )(length, q, k, v, heads, lse, turns, g, y, w, x)
+
+
 def feed_kernel(x_ref, d_ref, w_ref, *refs):
     before, (act_ref, dgu_ref, y_ref, dx_ref) = refs[:-4], refs[-4:]
     part = w_ref.shape[1] // 3
@@ -689,22 +938,8 @@
 def rotary_tables(positions, width):
     half = width // 2
     freqs = jnp.exp(-(jnp.arange(half, dtype=jnp.float32) * 2.0 / width) * math.log(ROPE_BASE))
-    angles = positions.astype(jnp.float32)[..., None] * freqs
-    angles = jnp.concatenate([angles, angles], -1)
-    return (jnp.cos(angles)[..., None, :], jnp.sin(angles)[..., None, :])
-
-
-def rotate_half(value_rows):
-    half = value_rows.shape[-1] // 2
-    return jnp.concatenate([-value_rows[..., half:], value_rows[..., :half]], -1)
-
-
-def apply_rotary(value_rows, cosine_table, sine_table):
-    return value_rows * cosine_table + rotate_half(value_rows) * sine_table
-
-
-def rope_back(grads, cosine_table, sine_table):
-    return grads * cosine_table - rotate_half(grads * sine_table)
+    angles = positions.astype(jnp.float32)[:, None] * freqs
+    return jnp.concatenate([jnp.cos(angles), jnp.sin(angles)], -1)
 
 
 def rms_normalize(value_rows):
@@ -893,27 +1128,20 @@
     down_second,
     gains_second,
 ):
-    _, here, width = inputs.shape
+    width = inputs.shape[2]
     seq = lax.axis_size("seq")
     far = lax.axis_size("far")
     group = seq * 2
     rows = out_weight.shape[0]
-    full = here * seq
-    heads_here = QUERY_HEAD_COUNT // seq
-    local_kv = KEY_VALUE_HEADS // seq
-    per_kv = QUERY_HEAD_COUNT // KEY_VALUE_HEADS
     query_width = QUERY_HEAD_COUNT * HEAD_SIZE
     key_width = KEY_VALUE_HEADS * HEAD_SIZE
     mine_q, mine_k = query_width // seq, key_width // seq
-    mine_qkv = mine_q + 2 * mine_k
     units = FEED_UNITS // group
     part = units // 2
-    factor = 1.0 / math.sqrt(HEAD_SIZE)
     low = jnp.bfloat16
 
     inputs = inputs[0]
     cotangent = cotangent[0]
-    length = lengths[0]
     gains = norm_gains.astype(low).astype(jnp.float32)
     gain_one, gain_two = gains[:, :1], gains[:, 1:]
 
@@ -955,37 +1183,16 @@
         2,
     ).transpose(1, 0, 2)
     unit_one, scale_one = rms_normalize(inputs)
-    spots = jnp.pad(positions.reshape(-1, 128), ((0, 8 - here // 128), (0, 0)))
+    turns = rotary_tables(positions.reshape(-1), HEAD_SIZE)
     dout_here = far_first(cotangent.astype(low))
     head_pieces = after(head_pieces, piece)
-    head_w, normed_one, all_spots, dout, piece = gather_heads(
-        head_pieces, unit_one.astype(low), spots, dout_here, feed_piece(1), 2
+    head_w, normed_one, all_turns, dout, piece = gather_heads(
+        head_pieces, unit_one.astype(low), turns, dout_here, feed_piece(1), 2
     )
     feed_one = lax.all_gather(piece.reshape(group * rows, -1), "far", axis=0, tiled=True)
-    qkv, out = head_w[:, :mine_qkv], head_w[:, mine_qkv:]
-    all_positions = all_spots[:, : here // 128].reshape(full)
-
-    cos, sin = rotary_tables(all_positions, HEAD_SIZE)
-    merged = product(normed_one, qkv, 1, 0)
-    queries = apply_rotary(merged[:, :mine_q].reshape(full, heads_here, HEAD_SIZE), cos, sin)
-    queries = queries.astype(low).reshape(full, local_kv, per_kv, HEAD_SIZE)
-    keys = apply_rotary(
-        merged[:, mine_q : mine_q + mine_k].reshape(full, local_kv, HEAD_SIZE), cos, sin
-    ).astype(low)
-    values = merged[:, mine_q + mine_k :].reshape(full, local_kv, HEAD_SIZE).astype(low)
-
-    spot = jnp.arange(full)
-    visible = (spot[None, :] <= spot[:, None]) & (spot < length)[None, :]
-    live = (spot < length)[:, None, None, None]
-    scores = jnp.einsum("qkgd,jkd->kgqj", queries, keys, preferred_element_type=jnp.float32)
-    scores = jnp.where(visible, scores * factor, MASKED_SCORE)
-    peak = jnp.max(scores, -1, keepdims=True)
-    expo = jnp.exp(scores - peak)
-    probs = expo / jnp.sum(expo, -1, keepdims=True)
-    probs_low = probs.astype(low)
-    heads = jnp.einsum("kgqj,jkd->qkgd", probs_low, values, preferred_element_type=jnp.float32)
-    heads = (heads * live).astype(low).reshape(full, mine_q)
-    hidden = inputs + scatter_seq(product(heads, out, 1, 1).astype(low), 3)
+    all_turns = all_turns.reshape(-1, HEAD_SIZE)
+    *saved, attended = attention(lengths, normed_one, head_w, all_turns)
+    hidden = inputs + scatter_seq(attended, 3)
     unit_two, scale_two = rms_normalize(hidden)
     normed_two = gather_plane(far_first(unit_two.astype(low)), 4)
     act_zero, dgateup_zero, *sums = feed(normed_two, dout, feed_zero, ())
@@ -1003,45 +1210,19 @@
     back_two = norm_backward(dnormed_two, unit_two, scale_two)
     dhidden = cotangent + back_two
 
-    dattended = gather_seq(after(dhidden.astype(low), terms_one), 6)
-    dheads = product(dattended, out, 1, 0).astype(low).reshape(full, local_kv, per_kv, HEAD_SIZE)
-    dheads = dheads * live.astype(low)
-    dvalues = jnp.einsum("kgqj,qkgd->jkd", probs_low, dheads, preferred_element_type=jnp.float32)
-    dprobs = jnp.einsum("qkgd,jkd->kgqj", dheads, values, preferred_element_type=jnp.float32)
-    inner = jnp.sum(probs * dprobs, -1, keepdims=True)
-    dscores = jnp.where(visible, (probs * (dprobs - inner)).astype(low), jnp.zeros((), low))
-    dqueries = jnp.einsum("kgqj,jkd->qkgd", dscores, keys, preferred_element_type=jnp.float32)
-    dkeys = jnp.einsum("kgqj,qkgd->jkd", dscores, queries, preferred_element_type=jnp.float32)
-    dqueries = (dqueries * factor).astype(low).reshape(full, heads_here, HEAD_SIZE)
-    dkeys = (dkeys * factor).astype(low)
-    dfused = jnp.concatenate(
-        [
-            rope_back(dqueries.astype(jnp.float32), cos, sin).astype(low).reshape(full, mine_q),
-            rope_back(dkeys.astype(jnp.float32), cos, sin).astype(low).reshape(full, mine_k),
-            dvalues.astype(low).reshape(full, mine_k),
-        ],
-        1,
+    dattended = after(dhidden.astype(low), terms_one)
+    head_terms, dnormed_one, output_terms = attention_back(
+        lengths, saved, all_turns, dattended, output_terms, head_w, normed_one, 6
     )
-    head_terms = jnp.concatenate(
-        [
-            product(normed_one, dfused, 0, 0).astype(low),
-            product(dattended, heads, 0, 0).astype(low),
-        ],
-        1,
-    )
-    head_terms = scatter_near(head_terms.reshape(seq, far, 2, rows, -1), 8)
     head_terms = after(head_terms, grads_zero, grads_one)
     head_terms = lax.psum_scatter(
         head_terms.reshape(far * seq * rows, -1), "far", scatter_dimension=0, tiled=True
     )
-    dnormed_one = scatter_seq(product(dfused, qkv, 1, 1).astype(low), 3)
-    back_one = norm_backward(dnormed_one, unit_one, scale_one)
-    input_grad = dhidden + back_one
-    output_terms = scatter_plane(after(output_terms, dnormed_one), 5)
+    input_grad = dhidden + norm_backward(dnormed_one, unit_one, scale_one)
     layer_output = hidden + far_last(output_terms)
 
     halves = exchange_plane([grads_zero, grads_one], 7)
-    head_terms = after(head_terms, output_terms, halves[0])
+    head_terms = after(head_terms, halves[0])
     halves = [x.reshape(group, rows, 3 * part) for x in halves]
     head_grads = lax.all_to_all(head_terms.reshape(seq, rows, -1), "seq", 0, 0, tiled=True)
 

time: 883 us -> 764 us (0.87)
  matrix products: 57.1 us -> 0 us
  Pallas kernels: 653 us -> 614 us
  other arithmetic: 45.7 us -> 27.8 us
  local copies, waits for them, and re-layouts: 57.9 us -> 42.6 us
  waiting for transfers between devices: 18.5 us -> 30.5 us
    dot_general x12 -> x0, matrix products: 57.1 us -> none  [the longest x6 37 us: product(): lax.dot_general(left, right, (((left_dim,), (right_dim,)), ((), ())), pre...]
    pallas_call x2 -> x1, Pallas kernels: 84.7 us -> 41.6 us  [scatter_plane(): pl.pallas_call(functools.partial(scatter_plane_kernel, rows), out_shape=j...]
    pallas_call x2 -> x1, Pallas kernels: 58.6 us -> 29.8 us  [scatter_seq(): pl.pallas_call(functools.partial(scatter_seq_kernel, rows), out_shape=jax...]
    pallas_call x2, Pallas kernels: 106 us -> 135 us  [the longest x1 116 us: attention_back(): pl.pallas_call(attention_back_kernel, out_shape=[jax.ShapeDtypeStruct((fa...]
    reduce_scatter x1, waiting for transfers between devices: 0.02 us -> 11.8 us  [shards(): lax.psum_scatter(head_terms.reshape(far * seq * rows, -1), 'far', scatter...]
    unnamed x90 -> x40, local copies, waits for them, and re-layouts: 17.9 us -> 10.8 us
    reshape x5 -> x6, local copies, waits for them, and re-layouts: 16.2 us -> 20.6 us  [far_last(): x.reshape(-1, far, seq, 2 * rows).transpose(0, 2, 1, 3).reshape(-1, width)]
  transfers between devices with their start and end apart: 6 -> 6, of which waited for: 2 -> 3; matrix products, arithmetic and copies ran while one was open for 15% -> 6% of each run, Pallas kernels for 69% -> 75%
where the time goes in v4:
time: 764 us; the launch traced here: 758 us
  Pallas kernels  614 us (80%)
  local copies, waits for them, and re-layouts  42.6 us (6%)
  waiting for transfers between devices  30.5 us (4%)
  other arithmetic  27.8 us (4%)
  blocking collectives  23 us (3%)
  between operations  17 us (2%)
    pallas_call x1, Pallas kernels, gather_heads(): pl.pallas_call(functools.partial(gather_heads_kernel, far_size), out_shap...  176 us
    pallas_call x1, Pallas kernels, attention_back(): pl.pallas_call(attention_back_kernel, out_shape=[jax.ShapeDtypeStruct((fa...  116 us
    pallas_call x2, Pallas kernels, feed(): pl.pallas_call(feed_kernel, grid=(tokens // tile,), out_shape=[jax.ShapeD...  69.2 us
    pallas_call x2, Pallas kernels, exchange_plane(): pl.pallas_call(functools.partial(exchange_plane_kernel, count), out_shape...  60.8 us
    pallas_call x1, Pallas kernels, scatter_plane(): pl.pallas_call(functools.partial(scatter_plane_kernel, rows), out_shape=j...  41.6 us
    pallas_call x1, Pallas kernels, gather_plane(): pl.pallas_call(functools.partial(gather_plane_kernel, rows), out_shape=ja...  39.7 us
    pallas_call x2, Pallas kernels, feed_grads(): pl.pallas_call(feed_grads_kernel, grid=(width // tile,), out_shape=jax.Sh...  38.7 us
    pallas_call x1, Pallas kernels, scatter_seq(): pl.pallas_call(functools.partial(scatter_seq_kernel, rows), out_shape=jax...  29.8 us
  transfers between devices with their start and end apart: 6, of which 3 were waited for; matrix products, arithmetic and copies ran while one was open for 6% of the time, Pallas kernels for 75%

profile of v4, /device:TPU:0, one launch (start us, length us, event | category | flops | bytes accessed | tf_op | source)
XLA Modules:
  0.0 758.3 jit_solution(16263136427654384674)
XLA Ops:
  14.5 22.8 %shard_map.322 = bf16[512,1536]{1,0:T(8,128)(2,1)} custom-call(bf16[512,1536]{1,0:T(8,128)(2,1)} %bitcast.113), custom_call_target="tpu_custom_call" | custom-call | tf_op jit(solution)/shard_map/pallas_call | solution.py:304
  47.7 175.9 %shard_map.323 = (bf16[4,4,2,64,1536]{4,3,2,1,0:T(8,128)(2,1)}, bf16[4,256,2048]{2,1,0:T(8,128)(2,1)}, f32[4,256,256]{2,1,0:T(8,128)}, bf16[8,256,2048]{2,1,0:T(8,128)(2,1)}, bf16[8,64,1536]{2,1,0:T(8,128)(2,1)}) custom-call(bf16[4,64,1536]{2,1,0:T(8,128)(2,1)} %maximum_bitcast_fusion.w_ref, bf16[256,2048]{1,0:T(8,128)(2,1)} %fusion.1.x_ref, ...), custom_call_target="tpu_custom_call" | custom-call | tf_op jit(solution)/shard_map/pallas_call | solution.py:509
  224.5 18.4 %shard_map.324 = (bf16[1024,512]{1,0:T(8,128)(2,1)}, bf16[1024,256]{1,0:T(8,128)(2,1)}, bf16[1024,256]{1,0:T(8,128)(2,1)}, bf16[1024,512]{1,0:T(8,128)(2,1)}, f3...) custom-call(s32[1]{0:T(128)S(6)} %copy.108.length_ref, bf16[1024,2048]{1,0:T(8,128)(2,1)} %bitcast.146, ...), custom_call_target="tpu_custom_call" | custom-call | flops 10000000000 | bytes 20000000 | tf_op jit(solution)/shard_map/pallas_call | solution.py:605
  242.9 29.8 %shard_map.325 = f32[256,2048]{1,0:T(8,128)} custom-call(bf16[1024,2048]{1,0:T(8,128)(2,1)} %get-tuple-element.70.p_ref), custom_call_target="tpu_custom_call" | custom-call | tf_op jit(solution)/shard_map/pallas_call | solution.py:253
  283.0 39.7 %shard_map.326.x_ref = bf16[2048,2048]{1,0:T(8,128)(2,1)} custom-call(bf16[256,2048]{1,0:T(8,128)(2,1)} %reshape.177.x_ref), custom_call_target="tpu_custom_call" | custom-call | tf_op jit(solution)/shard_map/pallas_call | solution.py:113
  322.8 32.8 %shard_map.327 = (bf16[2048,512]{1,0:T(8,128)(2,1)}, bf16[2048,1024]{1,0:T(8,128)(2,1)}, bf16[2048,2048]{1,0:T(8,128)(2,1)}, bf16[2048,2048]{1,0:T(8,128)(2,1)}) custom-call(bf16[2048,2048]{1,0:T(8,128)(2,1)} %shard_map.326.x_ref, bf16[2048,2048]{1,0:T(8,128)(2,1)} %bitcast.140, bf16[2048,1536]{1,0:T(8,128)(2,1)} %all-gather.5.cloned.1.call-done.w_ref), custom_call_target="tpu_custom_call" | custom-call | flops 25769803776 | bytes 60000000 | tf_op jit(solution)/shard_map/pallas_call | solution.py:903
  355.6 19.6 %shard_map.328 = bf16[2048,1536]{1,0:T(8,128)(2,1)} custom-call(bf16[2048,2048]{1,0:T(8,128)(2,1)} %shard_map.326.x_ref, bf16[2048,2048]{1,0:T(8,128)(2,1)} %bitcast.141, bf16[2048,1024]{1,0:T(8,128)(2,1)} %get-tuple-element.78.dgu_ref, bf16[2048,512]{1,0:T(8,128)(2,1)} %get-tuple-element.79.act_ref), custom_call_target="tpu_custom_call" | custom-call | flops 12884901888 | bytes 40000000 | tf_op jit(solution)/shard_map/pallas_call | solution.py:927
  375.2 36.4 %shard_map.329 = (bf16[2048,512]{1,0:T(8,128)(2,1)}, bf16[2048,1024]{1,0:T(8,128)(2,1)}, bf16[2048,2048]{1,0:T(8,128)(2,1)}, bf16[2048,2048]{1,0:T(8,128)(2,1)}) custom-call(bf16[2048,2048]{1,0:T(8,128)(2,1)} %shard_map.326.x_ref, bf16[2048,2048]{1,0:T(8,128)(2,1)} %bitcast.142, bf16[2048,1536]{1,0:T(8,128)(2,1)} %all-gather.3.cloned.1.call-done.w_ref, ...), custom_call_target="tpu_custom_call" | custom-call | flops 25769803776 | bytes 60000000 | tf_op jit(solution)/shard_map/pallas_call | solution.py:903
  411.6 41.6 %shard_map.330 = f32[256,2048]{1,0:T(8,128)} custom-call(bf16[2048,2048]{1,0:T(8,128)(2,1)} %get-tuple-element.83.p_ref), custom_call_target="tpu_custom_call" | custom-call | tf_op jit(solution)/shard_map/pallas_call | solution.py:194
  453.3 19.2 %shard_map.331 = bf16[2048,1536]{1,0:T(8,128)(2,1)} custom-call(bf16[2048,2048]{1,0:T(8,128)(2,1)} %shard_map.326.x_ref, bf16[2048,2048]{1,0:T(8,128)(2,1)} %bitcast.143, bf16[2048,1024]{1,0:T(8,128)(2,1)} %get-tuple-element.85.dgu_ref, bf16[2048,512]{1,0:T(8,128)(2,1)} %get-tuple-element.86.act_ref), custom_call_target="tpu_custom_call" | custom-call | flops 12884901888 | bytes 40000000 | tf_op jit(solution)/shard_map/pallas_call | solution.py:927
  472.4 10.9 %reduce-scatter.4.cloned.1.call-done.refs_0_ = bf16[512,1536]{1,0:T(8,128)(2,1)} async-done(((bf16[2048,1536]{1,0:T(8,128)(2,1)}), bf16[512,1536]{1,0:T(8,128)(2,1)}) %reduce-scatter.4.cloned.1.call-update) | async-done | bytes 1572880 | tf_op jit(solution)/shard_map/reduce_scatter | solution.py:1206
  483.4 3.6 reshape.180
  497.1 3.8 fusion.2
  500.9 116.2 %shard_map.332 = (bf16[4,4,64,1536]{3,2,1,0:T(8,128)(2,1)}, f32[256,2048]{1,0:T(8,128)}, f32[256,2048]{1,0:T(8,128)}) custom-call(s32[1]{0:T(128)S(6)} %copy.108.length_ref, bf16[1024,512]{1,0:T(8,128)(2,1)} %get-tuple-element.71.q_ref, bf16[1024,256]{1,0:T(8,128)(2,1)} %get-tuple-element.72.k_ref, bf16[1024,256]{1,0:T(8,128)(2,1)} %get-tuple-element.73.v_ref, ...), custom_call_target="tpu_custom_call" | custom-call | flops 20000000000 | bytes 40000000 | tf_op jit(solution)/shard_map/pallas_call | solution.py:831
  619.2 3.6 reshape.182
  626.9 38.0 %shard_map.333 = (bf16[512,1536]{1,0:T(8,128)(2,1)}, bf16[512,1536]{1,0:T(8,128)(2,1)}) custom-call(bf16[512,1536]{1,0:T(8,128)(2,1)} %reduce-scatter.4.cloned.1.call-done.refs_0_, bf16[512,1536]{1,0:T(8,128)(2,1)} %reduce-scatter.6.cloned.1.call-done.refs_1_), custom_call_target="tpu_custom_call" | custom-call | tf_op jit(solution)/shard_map/pallas_call | solution.py:304
  664.9 11.8 %reduce-scatter.8.cloned.1.call-done = bf16[256,1536]{1,0:T(8,128)(2,1)} async-done(((bf16[1024,1536]{1,0:T(8,128)(2,1)}), bf16[256,1536]{1,0:T(8,128)(2,1)}) %reduce-scatter.8.cloned.1.call-update) | async-done | bytes 786448 | tf_op jit(solution)/shard_map/reduce_scatter | solution.py:1218
  680.1 4.0 add_bitcast_fusion
  684.1 7.6 %all-to-all-done.head_ref = bf16[4,64,1536]{2,1,0:T(8,128)(2,1)S(1)} async-done(((bf16[4,64,1536]{2,1,0:T(8,128)(2,1)}), bf16[4,64,1536]{2,1,0:T(8,128)(2,1)S(1)}, u32[]{:S(2)}, u32[]{:S(2)}) %all-to-all-start) | async-done | bytes 786464 | tf_op jit(solution)/shard_map/all_to_all | solution.py:1227
  692.6 5.6 shard_map.334
  698.3 6.4 psum.21
  707.9 5.5 psum.22
  716.7 11.1 %psum.23 = f32[]{:T(128)} all-reduce(f32[]{:T(128)} %psum.22), channel_id=1, replica_groups=mesh['seq'=4,'far'=4,'near'=2] {'far'}, use_global_device_ids=true, to_apply=%region_9.0 | all-reduce | flops 1 | bytes 8 | tf_op jit(solution)/shard_map/psum | solution.py:1235
  728.5 17.8 %shard_map.335 = (f32[64,4096]{1,0:T(8,128)}, f32[64,2048]{1,0:T(8,128)}, f32[64,16384]{1,0:T(8,128)}, f32[64,8192]{1,0:T(8,128)}, f32[64,2]{1,0:T(8,128)}, /*in...) custom-call(f32[1,1]{1,0:T(1,128)} %bitcast.29.clip_ref, ...), custom_call_target="tpu_custom_call" | custom-call | tf_op jit(solution)/shard_map/pallas_call | solution.py:1094
  (102 shorter events, 59.3 us)
Async XLA Ops:
  7.2 2.6 copy-start.13
  7.2 2.9 copy-start.7
  7.2 315.6 %all-gather.5.cloned.1.call-start = ((), (), s32[]{:S(2)}) async-start(), calls=%async_computation.5 | async-start | bytes 7864320 | tf_op jit(solution)/shard_map/all_gather | solution.py:1173
  10.2 1.4 copy-start.5
  14.5 22.9 %copy-start.10 = (f32[64,2048]{1,0:T(8,128)S(1)}, f32[64,2048]{1,0:T(8,128)}, u32[]{:S(2)}) copy-start(f32[64,2048]{1,0:T(8,128)} %refs_1_.1) | copy-start | bytes 1572868
  37.3 337.9 %all-gather.3.cloned.1.call-start = ((), (), s32[]{:S(2)}) async-start(), calls=%async_computation.4 | async-start | bytes 7864320 | tf_op jit(solution)/shard_map/all_gather | solution.py:1192
  37.4 1.1 copy-start.16
  37.5 1.9 copy-start.6
  40.8 2.9 copy-start.12
  40.8 2.9 copy-start.11
  42.4 2.6 copy-start
  223.6 259.7 %reduce-scatter.4.cloned.1.call-start = ((), (), s32[]{:S(2)}) async-start(), calls=%async_computation.6 | async-start | bytes 7864320 | tf_op jit(solution)/shard_map/reduce_scatter | solution.py:1206
  274.6 1.3 copy-start.1
  375.2 241.9 %reduce-scatter.6.cloned.1.call-start = ((), (), s32[]{:S(2)}) async-start(), calls=%async_computation.7 | async-start | bytes 7864320 | tf_op jit(solution)/shard_map/reduce_scatter | solution.py:1207
  483.4 193.3 %reduce-scatter.8.cloned.1.call-start = ((), (), s32[]{:S(2)}) async-start(), calls=%async_computation.8 | async-start | bytes 3932160 | tf_op jit(solution)/shard_map/reduce_scatter | solution.py:1218
  493.6 2.9 copy-start.2
  493.6 3.5 copy-start.4
  617.0 0.8 copy-start.14
  617.1 1.5 copy-start.15
  622.8 3.6 copy-start.8
  676.6 15.1 %all-to-all-start = ((bf16[4,64,1536]{2,1,0:T(8,128)(2,1)}), bf16[4,64,1536]{2,1,0:T(8,128)(2,1)S(1)}, u32[]{:S(2)}, u32[]{:S(2)}) async-start(bf16[4,64,1536]{2,1,0:T(8,128)(2,1)} %bitcast.134), calls=%async_computation.3 | async-start | bytes 1572864 | tf_op jit(solution)/shard_map/all_to_all | solution.py:1227
  691.8 0.9 copy-start.9
  704.7 8.8 %copy-start.3 = (f32[256,2048]{1,0:T(8,128)S(1)}, f32[256,2048]{1,0:T(8,128)}, u32[]{:S(2)}) copy-start(f32[256,2048]{1,0:T(8,128)} %copy-done.1) | copy-start | bytes 6291460
Sparse Core Ops, SparseCore 0:
  37.5 148.9 all-gather.4
  223.7 112.5 all-gather.2
  375.3 108.0 reduce-scatter.3
  485.5 111.2 reduce-scatter.5
  617.2 59.3 reduce-scatter.7

commit v5 on v4

--- a/solution.py
+++ b/solution.py
@@ -27,7 +27,6 @@
 RATE_GAIN = 1.0
 
 EVERY = ("seq", "far", "near")
-TP = ("seq", "near")
 
 
 MESH_IDS = pl.DeviceIdType.MESH
@@ -66,64 +65,6 @@
     return copies, send
 
 
-def gather_plane_kernel(rows, x_ref, o_ref, local_sem, send_sems, recv_sems):
-    s, n, core, across, beside = places()
-    half = rows // 2
-    to_core, to_y, to_x = {"seq": core}, {"seq": across}, {"near": beside}
-
-    def block(seq, near, part):
-        return o_ref.at[pl.ds((seq * 2 + near) * rows + part * half, half)]
-
-    def own(part):
-        return x_ref.at[pl.ds(part * half, half)]
-
-    meet(to_core, to_y, to_x)
-    local = pltpu.make_async_copy(x_ref, o_ref.at[pl.ds((s * 2 + n) * rows, rows)], local_sem)
-    local.start()
-    copies, send = sender(send_sems, recv_sems)
-    send("y0", own(0), block(s, n, 0), to_y)
-    send("x1", own(1), block(s, n, 1), to_x)
-    send("y1", own(1), block(s, n, 1), to_y)
-    send("x0", own(0), block(s, n, 0), to_x)
-    send("c0", own(0), block(s, n, 0), to_core)
-    send("c1", own(1), block(s, n, 1), to_core)
-    copies["y0"].wait_recv()
-    send("yx", block(across, n, 0), block(across, n, 0), to_x)
-    send("yc0", block(across, n, 0), block(across, n, 0), to_core)
-    copies["x1"].wait_recv()
-    send("xy", block(s, beside, 1), block(s, beside, 1), to_y)
-    send("xc1", block(s, beside, 1), block(s, beside, 1), to_core)
-    copies["y1"].wait_recv()
-    send("yc1", block(across, n, 1), block(across, n, 1), to_core)
-    copies["x0"].wait_recv()
-    send("xc0", block(s, beside, 0), block(s, beside, 0), to_core)
-    copies["yx"].wait_recv()
-    send("dc0", block(across, beside, 0), block(across, beside, 0), to_core)
-    copies["xy"].wait_recv()
-    send("dc1", block(across, beside, 1), block(across, beside, 1), to_core)
-    for key in ("c0", "c1", "yc0", "yc1", "xc0", "xc1", "dc0", "dc1"):
-        copies[key].wait_recv()
-    for copy in copies.values():
-        copy.wait_send()
-    local.wait()
-
-
-def gather_plane(x, collective_id):
-    rows, columns = x.shape
-    return pl.pallas_call(
-        functools.partial(gather_plane_kernel, rows),
-        out_shape=jax.ShapeDtypeStruct((8 * rows, columns), x.dtype),
-        in_specs=[ANYWHERE],
-        out_specs=ANYWHERE,
-        scratch_shapes=[
-            pltpu.SemaphoreType.DMA,
-            pltpu.SemaphoreType.DMA((14,)),
-            pltpu.SemaphoreType.DMA((14,)),
-        ],
-        compiler_params=pltpu.CompilerParams(collective_id=collective_id, has_side_effects=True),
-    )(x)
-
-
 def add_rows(target, first, second, third=None, step=64):
     rows = target.shape[0]
 
@@ -136,81 +77,6 @@
         return carry
 
     lax.fori_loop(0, rows // step, body, 0)
-
-
-def scatter_plane_kernel(rows, p_ref, o_ref, mine, far, hop_x, hop_y, last_x, last_y, local_sems, send_sems, recv_sems):
-    s, n, core, across, beside = places()
-    half = rows // 2
-    to_core, to_y, to_x = {"seq": core}, {"seq": across}, {"near": beside}
-
-    def block(seq, near):
-        return p_ref.at[pl.ds((seq * 2 + near) * rows, rows)]
-
-    def part(ref, at, p):
-        return ref.at[at, pl.ds(p * half, half)]
-
-    meet(to_core, to_y, to_x)
-    copies, send = sender(send_sems, recv_sems)
-    other = (core + 2) % 4
-    given = [block(other, beside), block(other, n), block(core, beside), block(core, n)]
-    kept = [block(across, beside), block(across, n), block(s, beside), block(s, n)]
-    locals_ = []
-    for k in range(4):
-        send(k, given[k], far.at[k], to_core)
-        locals_.append(pltpu.make_async_copy(kept[k], mine.at[k], local_sems.at[k]))
-        locals_[k].start()
-    for k in range(3):
-        locals_[k].wait()
-        copies[k].wait_recv()
-        add_rows(mine.at[k], mine.at[k], far.at[k])
-        if k == 0:
-            send("hx", part(mine, 0, 0), hop_x, to_x)
-            send("hy", part(mine, 0, 1), hop_y, to_y)
-        elif k == 1:
-            send("y1", part(mine, 1, 1), part(last_y, 0, 1), to_y)
-        else:
-            send("x0", part(mine, 2, 0), part(last_x, 0, 0), to_x)
-    copies["hx"].wait_recv()
-    add_rows(part(mine, 1, 0), part(mine, 1, 0), hop_x)
-    send("y0", part(mine, 1, 0), part(last_y, 0, 0), to_y)
-    copies["hy"].wait_recv()
-    add_rows(part(mine, 2, 1), part(mine, 2, 1), hop_y)
-    send("x1", part(mine, 2, 1), part(last_x, 0, 1), to_x)
-    locals_[3].wait()
-    copies[3].wait_recv()
-    add_rows(o_ref, mine.at[3], far.at[3])
-    for p, first, second in ((1, "y1", "x1"), (0, "x0", "y0")):
-        copies[first].wait_recv()
-        copies[second].wait_recv()
-        here = o_ref.at[pl.ds(p * half, half)]
-        add_rows(here, here, part(last_x, 0, p), part(last_y, 0, p))
-    for copy in copies.values():
-        copy.wait_send()
-
-
-def scatter_plane(p, collective_id):
-    rows, columns = p.shape[0] // 8, p.shape[1]
-    low = jnp.bfloat16
-    return pl.pallas_call(
-        functools.partial(scatter_plane_kernel, rows),
-        out_shape=jax.ShapeDtypeStruct((rows, columns), jnp.float32),
-        in_specs=[ANYWHERE],
-        out_specs=IN_VMEM,
-        scratch_shapes=[
-            pltpu.VMEM((4, rows, columns), low),
-            pltpu.VMEM((4, rows, columns), low),
-            pltpu.VMEM((rows // 2, columns), low),
-            pltpu.VMEM((rows // 2, columns), low),
-            pltpu.VMEM((1, rows, columns), low),
-            pltpu.VMEM((1, rows, columns), low),
-            pltpu.SemaphoreType.DMA((4,)),
-            pltpu.SemaphoreType.DMA((10,)),
-            pltpu.SemaphoreType.DMA((10,)),
-        ],
-        compiler_params=pltpu.CompilerParams(
-            collective_id=collective_id, has_side_effects=True, vmem_limit_bytes=VMEM_LIMIT
-        ),
-    )(p)
 
 
 def scatter_seq_kernel(rows, p_ref, o_ref, mine, far, last, local_sems, send_sems, recv_sems):
@@ -378,75 +244,71 @@
     for k in range(3):
         copies["w", k].wait_recv()
 
-    def group(far, near):
-        return o_ref.at[:, far, near]
-
-    def along(key, far, device, sem):
+    def along(far, p, device, sem):
+        piece = o_ref.at[p, far, n]
         return pltpu.make_async_remote_copy(
-            src_ref=group(far, n),
-            dst_ref=group(far, n),
-            send_sem=send_sems.at[sem],
-            recv_sem=recv_sems.at[sem],
+            src_ref=piece,
+            dst_ref=piece,
+            send_sem=send_sems.at[base + 4 * sem + p],
+            recv_sem=recv_sems.at[base + 4 * sem + p],
             device_id=device,
             device_id_type=MESH_IDS,
         )
 
     base = 33
 
-    def beside_copy(far, sem):
-        return along("x", far, to_x, sem)
-
-    def to_right(k):
-        return along("r", (f + far_size - k) % far_size, right, base + k)
-
-    def to_left(k):
-        return along("l", (f + k) % far_size, left, base + far_size + k)
-
-    def x_from_left(k):
-        return beside_copy((f + far_size - k) % far_size, base + 2 * far_size + k)
-
-    def x_from_right(k):
-        return beside_copy((f + k) % far_size, base + 3 * far_size + k)
+    def to_right(k, p):
+        return along((f + far_size - k) % far_size, p, right, k)
+
+    def to_left(k, p):
+        return along((f + k) % far_size, p, left, far_size + k)
+
+    def x_from_left(k, p):
+        return along((f + far_size - k) % far_size, p, to_x, 2 * far_size + k)
+
+    def x_from_right(k, p):
+        return along((f + k) % far_size, p, to_x, 3 * far_size + k)
 
     for k in range(far_size):
-        if k > 0:
-
-            @pl.when(f >= k)
+        for p in range(4):
+            if k > 0:
+
+                @pl.when(f >= k)
+                def _():
+                    to_right(k - 1, p).wait_recv()
+
+            @pl.when((f >= k) & (f < far_size - 1))
             def _():
-                to_right(k - 1).wait_recv()
-
-        @pl.when((f >= k) & (f < far_size - 1))
-        def _():
-            to_right(k).start()
-
-        if k > 0:
-
-            @pl.when(f + k < far_size)
+                to_right(k, p).start()
+
+            if k > 0:
+
+                @pl.when(f + k < far_size)
+                def _():
+                    to_left(k - 1, p).wait_recv()
+
+            @pl.when((f + k < far_size) & (f > 0))
             def _():
-                to_left(k - 1).wait_recv()
-
-        @pl.when((f + k < far_size) & (f > 0))
-        def _():
-            to_left(k).start()
-
-        if k == 0:
-            x_from_left(0).start()
-        else:
-
-            @pl.when(f >= k)
-            def _():
-                x_from_left(k).start()
-
-            @pl.when(f + k < far_size)
-            def _():
-                x_from_right(k).start()
-
-        if k == 0:
+                to_left(k, p).start()
+
+            if k == 0:
+                x_from_left(0, p).start()
+            else:
+
+                @pl.when(f >= k)
+                def _():
+                    x_from_left(k, p).start()
+
+                @pl.when(f + k < far_size)
+                def _():
+                    x_from_right(k, p).start()
+
+        if k == min(1, far_size - 1):
             for p in range(2):
                 at = pl.ds(p * half, half)
                 copies["y", p].wait_recv()
                 send(("yc", p), ox_ref.at[across, at], ox_ref.at[across, at], to_core)
-        if k == 1:
+        if k == max(far_size - 2, 0):
             copies["y0"].wait_recv()
             send("yx", block(across, n, 0), block(across, n, 0), to_x)
             send("yc0", block(across, n, 0), block(across, n, 0), to_core)
@@ -457,11 +319,10 @@
             send("yc1", block(across, n, 1), block(across, n, 1), to_core)
             copies["x0"].wait_recv()
             send("xc0", block(s, beside, 0), block(s, beside, 0), to_core)
-        if k == min(2, far_size - 1):
-            copies["yx"].wait_recv()
-            send("dc0", block(across, beside, 0), block(across, beside, 0), to_core)
-            copies["xy"].wait_recv()
-            send("dc1", block(across, beside, 1), block(across, beside, 1), to_core)
+    copies["yx"].wait_recv()
+    send("dc0", block(across, beside, 0), block(across, beside, 0), to_core)
+    copies["xy"].wait_recv()
+    send("dc1", block(across, beside, 1), block(across, beside, 1), to_core)
     for key in ("c0", "c1", "yc0", "yc1", "xc0", "xc1", "dc0", "dc1"):
         copies[key].wait_recv()
     for p in range(2):
@@ -472,26 +333,27 @@
     for k in range(7):
         copies["e", k].wait_recv()
     for k in range(far_size):
-
-        @pl.when((f >= k) & (f < far_size - 1))
-        def _():
-            to_right(k).wait_send()
-
-        @pl.when((f + k < far_size) & (f > 0))
-        def _():
-            to_left(k).wait_send()
-
-        @pl.when(f >= k)
-        def _():
-            x_from_left(k).wait_recv()
-            x_from_left(k).wait_send()
-
-        if k > 0:
-
-            @pl.when(f + k < far_size)
+        for p in range(4):
+
+            @pl.when((f >= k) & (f < far_size - 1))
             def _():
-                x_from_right(k).wait_recv()
-                x_from_right(k).wait_send()
+                to_right(k, p).wait_send()
+
+            @pl.when((f + k < far_size) & (f > 0))
+            def _():
+                to_left(k, p).wait_send()
+
+            @pl.when(f >= k)
+            def _():
+                x_from_left(k, p).wait_recv()
+                x_from_left(k, p).wait_send()
+
+            if k > 0:
+
+                @pl.when(f + k < far_size)
+                def _():
+                    x_from_right(k, p).wait_recv()
+                    x_from_right(k, p).wait_send()
 
     for copy in copies.values():
         copy.wait_send()
@@ -505,7 +367,7 @@
     far_size = lax.axis_size("far")
     _, rows, columns = w.shape
     tokens, width = x.shape
-    sems = 33 + 4 * far_size
+    sems = 33 + 16 * far_size
     full, all_x, all_i, all_d, mine_e = pl.pallas_call(
         functools.partial(gather_heads_kernel, far_size),
         out_shape=[
@@ -867,72 +729,490 @@
     )(length, q, k, v, heads, lse, turns, g, y, w, x)
 
 
-def feed_kernel(x_ref, d_ref, w_ref, *refs):
-    before, (act_ref, dgu_ref, y_ref, dx_ref) = refs[:-4], refs[-4:]
-    part = w_ref.shape[1] // 3
+def hidden_units(x, d, w, part):
     low = jnp.bfloat16
-    x = x_ref[...]
-    gate = product(x, w_ref[:, :part], 1, 0)
-    upper = product(x, w_ref[:, part : 2 * part], 1, 0)
-    dact = product(d_ref[...], w_ref[:, 2 * part :], 1, 0)
+    gate = product(x, w[:, :part], 1, 0)
+    upper = product(x, w[:, part : 2 * part], 1, 0)
+    dact = product(d, w[:, 2 * part :], 1, 0)
     sig = 1.0 / (1.0 + jnp.exp(-gate))
     silu = gate * sig
     act = (silu * upper).astype(low)
+    dgate = (dact * upper * (sig + silu * (1.0 - sig))).astype(low)
+    dupper = (dact * silu).astype(low)
+    return act, dgate, dupper
+
+
+def load_weights(w_ref, weights, sems):
+    loads = [
+        pltpu.make_async_copy(w_ref.at[f], weights.at[:, f], sems.at[f]) for f in range(w_ref.shape[0])
+    ]
+    for load in loads:
+        load.start()
+    return loads
+
+
+def feed_first_kernel(
+    x_ref,
+    d_ref,
+    w_ref,
+    all_ref,
+    act_ref,
+    dgu_ref,
+    y_ref,
+    dx_ref,
+    weights,
+    tokens,
+    there,
+    acts,
+    dgus,
+    ys,
+    dxs,
+    local_sems,
+    d_sems,
+    out_sems,
+    send_sems,
+    recv_sems,
+):
+    s, n, core, across, beside = places()
+    other = (core + 2) % 4
+    rows = x_ref.shape[0]
+    half = rows // 2
+    to_core, to_y, to_x = {"seq": core}, {"seq": across}, {"near": beside}
+    part = weights.shape[3] // 3
+    width = x_ref.shape[1]
+    low = jnp.bfloat16
+
+    def block(seq, near, p):
+        return tokens.at[seq * 2 + near, pl.ds(p * half, half)]
+
+    def own(p):
+        return x_ref.at[pl.ds(p * half, half)]
+
+    order = [
+        s * 2 + n,
+        core * 2 + n,
+        across * 2 + n,
+        other * 2 + n,
+        s * 2 + beside,
+        core * 2 + beside,
+        across * 2 + beside,
+        other * 2 + beside,
+    ]
+
+    def tile_of(step):
+        tile = order[0]
+        for k in range(1, 8):
+            tile = jnp.where(step == k, order[k], tile)
+        return tile
+
+    def d_load(step):
+        slot = step % 2
+        at = tile_at(tile_of(step), rows)
+        return pltpu.make_async_copy(d_ref.at[at], there.at[slot], d_sems.at[slot])
+
+    def stores(step):
+        slot = step % 2
+        tile = tile_of(step)
+        at = tile_at(tile, rows)
+        pairs = (
+            (tokens.at[tile], all_ref),
+            (acts.at[slot], act_ref),
+            (dgus.at[slot], dgu_ref),
+            (ys.at[slot], y_ref),
+            (dxs.at[slot], dx_ref),
+        )
+        return [
+            pltpu.make_async_copy(source, target.at[at], out_sems.at[slot, k])
+            for k, (source, target) in enumerate(pairs)
+        ]
+
+    def piece(seq, near, p, device):
+        return block(seq, near, p), block(seq, near, p), device
+
+    plan = {
+        "y0": (own(0), block(s, n, 0), to_y),
+        "x1": (own(1), block(s, n, 1), to_x),
+        "y1": (own(1), block(s, n, 1), to_y),
+        "x0": (own(0), block(s, n, 0), to_x),
+        "c0": (own(0), block(s, n, 0), to_core),
+        "c1": (own(1), block(s, n, 1), to_core),
+        "yx": piece(across, n, 0, to_x),
+        "yc0": piece(across, n, 0, to_core),
+        "xy": piece(s, beside, 1, to_y),
+        "xc1": piece(s, beside, 1, to_core),
+        "yc1": piece(across, n, 1, to_core),
+        "xc0": piece(s, beside, 0, to_core),
+        "dc0": piece(across, beside, 0, to_core),
+        "dc1": piece(across, beside, 1, to_core),
+    }
+    places_of = {key: at for at, key in enumerate(plan)}
+
+    def copy_of(key):
+        source, target, device = plan[key]
+        at = places_of[key]
+        return pltpu.make_async_remote_copy(
+            src_ref=source,
+            dst_ref=target,
+            send_sem=send_sems.at[at],
+            recv_sem=recv_sems.at[at],
+            device_id=device,
+            device_id_type=MESH_IDS,
+        )
+
+    def send(*keys):
+        for key in keys:
+            copy_of(key).start()
+
+    def arrive(*keys):
+        for key in keys:
+            copy_of(key).wait_recv()
+
+    meet(to_core, to_y, to_x)
+    keep = pltpu.make_async_copy(x_ref, tokens.at[s * 2 + n], local_sems.at[0])
+    keep.start()
+    send("y0", "x1", "y1", "x0", "c0", "c1")
+    loads = load_weights(w_ref, weights, local_sems.at[pl.ds(1, w_ref.shape[0])])
+    d_load(0).start()
+    keep.wait()
+    for load in loads:
+        load.wait()
+
+    def before(step):
+        if step == 1:
+            arrive("c0", "c1")
+        elif step == 2:
+            arrive("y0")
+            send("yx", "yc0")
+            arrive("x1")
+            send("xy", "xc1")
+            arrive("y1")
+            send("yc1")
+            arrive("x0")
+            send("xc0")
+        elif step == 3:
+            arrive("yc0", "yc1")
+        elif step == 5:
+            arrive("xc0", "xc1")
+        elif step == 6:
+            arrive("yx")
+            send("dc0")
+            arrive("xy")
+            send("dc1")
+        elif step == 7:
+            arrive("dc0", "dc1")
+
+    def step_of(step, carry):
+        for k in (1, 2, 3, 5, 6, 7):
+
+            @pl.when(step == k)
+            def _():
+                before(k)
+
+        slot = step % 2
+
+        @pl.when(step < 7)
+        def _():
+            d_load(step + 1).start()
+
+        @pl.when(step >= 2)
+        def _():
+            for store in stores(step - 2):
+                store.wait()
+
+        d_load(step).wait()
+        w = weights[...].reshape(width, 3 * part)
+        act, dgate, dupper = hidden_units(tokens[tile_of(step)], there[slot], w, part)
+        acts[slot] = act
+        dgus[slot, :, :part] = dgate
+        dgus[slot, :, part:] = dupper
+        ys[slot] = product(act, w[:, 2 * part :], 1, 1).astype(low)
+        dxs[slot] = product(dgus[slot], w[:, : 2 * part], 1, 1).astype(low)
+        for store in stores(step):
+            store.start()
+        return carry
+
+    lax.fori_loop(0, 8, step_of, 0)
+    for step in (6, 7):
+        for store in stores(step):
+            store.wait()
+    for key in plan:
+        copy_of(key).wait_send()
+
+
+def feed_first(x, d, w, collective_id):
+    rows, width = x.shape
+    part = w.shape[3] // 3
+    tokens = 8 * rows
+    low = jnp.bfloat16
+    far, _, weight_rows, columns = w.shape
+    sizes = (width, part, 2 * part, width, width)
+    return pl.pallas_call(
+        feed_first_kernel,
+        out_shape=[jax.ShapeDtypeStruct((tokens, size), low) for size in sizes],
+        in_specs=[ANYWHERE] * 3,
+        out_specs=[ANYWHERE] * 5,
+        scratch_shapes=[
+            pltpu.VMEM((4, far, weight_rows, columns), low),
+            pltpu.VMEM((8, rows, width), low),
+            pltpu.VMEM((2, rows, width), low),
+            pltpu.VMEM((2, rows, part), low),
+            pltpu.VMEM((2, rows, 2 * part), low),
+            pltpu.VMEM((2, rows, width), low),
+            pltpu.VMEM((2, rows, width), low),
+            pltpu.SemaphoreType.DMA((1 + far,)),
+            pltpu.SemaphoreType.DMA((2,)),
+            pltpu.SemaphoreType.DMA((2, 5)),
+            pltpu.SemaphoreType.DMA((14,)),
+            pltpu.SemaphoreType.DMA((14,)),
+        ],
+        compiler_params=pltpu.CompilerParams(
+            collective_id=collective_id, has_side_effects=True, vmem_limit_bytes=VMEM_LIMIT
+        ),
+        cost_estimate=pl.CostEstimate(
+            flops=12 * tokens * width * part, bytes_accessed=60_000_000, transcendentals=0
+        ),
+    )(x, d, w)
+
+
+def feed_second_kernel(x_ref, d_ref, y0_ref, dx0_ref, w_ref, act_ref, dgu_ref, y_ref, dx_ref, weights, sems):
+    part = weights.shape[3] // 3
+    width = x_ref.shape[1]
+    low = jnp.bfloat16
+
+    @pl.when(pl.program_id(0) == 0)
+    def _():
+        for load in load_weights(w_ref, weights, sems):
+            load.wait()
+
+    w = weights[...].reshape(width, 3 * part)
+    act, dgate, dupper = hidden_units(x_ref[...], d_ref[...], w, part)
     act_ref[...] = act
-    dgu_ref[:, :part] = (dact * upper * (sig + silu * (1.0 - sig))).astype(low)
-    dgu_ref[:, part:] = (dact * silu).astype(low)
-    y = product(act, w_ref[:, 2 * part :], 1, 1)
-    dx = product(dgu_ref[...], w_ref[:, : 2 * part], 1, 1)
-    if before:
-        y = y + before[0][...].astype(jnp.float32)
-        dx = dx + before[1][...].astype(jnp.float32)
+    dgu_ref[:, :part] = dgate
+    dgu_ref[:, part:] = dupper
+    y = product(act, w[:, 2 * part :], 1, 1) + y0_ref[...].astype(jnp.float32)
     y_ref[...] = y.astype(low)
+    dx = product(dgu_ref[...], w[:, : 2 * part], 1, 1) + dx0_ref[...].astype(jnp.float32)
     dx_ref[...] = dx.astype(low)
 
 
-def feed(x, d, w, before, tile=512):
+def feed_second(x, d, y, dx, w, tile=512):
     tokens, width = x.shape
-    part = w.shape[1] // 3
+    part = w.shape[3] // 3
     low = jnp.bfloat16
+    far, _, weight_rows, columns = w.shape
 
     def tokens_of(columns):
         return pl.BlockSpec((tile, columns), lambda t: (t, 0))
 
-    whole = pl.BlockSpec(w.shape, lambda t: (0, 0), pipeline_mode=pl.Buffered(1))
     sizes = (part, 2 * part, width, width)
     return pl.pallas_call(
-        feed_kernel,
+        feed_second_kernel,
         grid=(tokens // tile,),
-        out_shape=[jax.ShapeDtypeStruct((tokens, columns), low) for columns in sizes],
-        in_specs=[tokens_of(width), tokens_of(width), whole] + [tokens_of(width)] * len(before),
-        out_specs=[tokens_of(columns) for columns in sizes],
+        out_shape=[jax.ShapeDtypeStruct((tokens, size), low) for size in sizes],
+        in_specs=[tokens_of(width)] * 4 + [ANYWHERE],
+        out_specs=[tokens_of(size) for size in sizes],
+        scratch_shapes=[pltpu.VMEM((4, far, weight_rows, columns), low), pltpu.SemaphoreType.DMA((far,))],
         compiler_params=pltpu.CompilerParams(vmem_limit_bytes=VMEM_LIMIT),
-        cost_estimate=pl.CostEstimate(flops=12 * tokens * width * part, bytes_accessed=60_000_000, transcendentals=0),
-    )(x, d, w, *before)
+        cost_estimate=pl.CostEstimate(
+            flops=12 * tokens * width * part, bytes_accessed=60_000_000, transcendentals=0
+        ),
+    )(x, d, y, dx, w)
 
 
 def feed_grads_kernel(x_ref, d_ref, dgu_ref, act_ref, o_ref):
     split = dgu_ref.shape[1]
-    o_ref[:, :split] = product(x_ref[...], dgu_ref[...], 0, 0).astype(o_ref.dtype)
-    o_ref[:, split:] = product(d_ref[...], act_ref[...], 0, 0).astype(o_ref.dtype)
-
-def feed_grads(x, d, dgu, act, tile=256):
+    far, _, rows, columns = o_ref.shape
+    gateup = product(x_ref[...], dgu_ref[...], 0, 0).astype(o_ref.dtype)
+    o_ref[:, 0, :, :split] = gateup.reshape(far, rows, split)
+    down = product(d_ref[...], act_ref[...], 0, 0).astype(o_ref.dtype)
+    o_ref[:, 0, :, split:] = down.reshape(far, rows, columns - split)
+
+
+def feed_grads(x, d, dgu, act, far):
     tokens, width = x.shape
     columns = dgu.shape[1] + act.shape[1]
-    some = pl.BlockSpec((tokens, tile), lambda t: (0, t))
+    rows = width // (4 * far)
+    some = pl.BlockSpec((tokens, width // 4), lambda t: (0, t))
 
     def whole(array):
         return pl.BlockSpec(array.shape, lambda t: (0, 0), pipeline_mode=pl.Buffered(1))
 
     return pl.pallas_call(
         feed_grads_kernel,
-        grid=(width // tile,),
-        out_shape=jax.ShapeDtypeStruct((width, columns), x.dtype),
+        grid=(4,),
+        out_shape=jax.ShapeDtypeStruct((far, 4, rows, columns), x.dtype),
         in_specs=[some, some, whole(dgu), whole(act)],
-        out_specs=pl.BlockSpec((tile, columns), lambda t: (t, 0)),
+        out_specs=pl.BlockSpec((far, 1, rows, columns), lambda t: (0, t, 0, 0)),
         compiler_params=pltpu.CompilerParams(vmem_limit_bytes=VMEM_LIMIT),
-        cost_estimate=pl.CostEstimate(flops=2 * tokens * width * columns, bytes_accessed=40_000_000, transcendentals=0),
+        cost_estimate=pl.CostEstimate(
+            flops=2 * tokens * width * columns, bytes_accessed=40_000_000, transcendentals=0
+        ),
     )(x, d, dgu, act)
+
+
+def feed_back_kernel(
+    hidden_ref,
+    cotangent_ref,
+    dgu_ref,
+    act_ref,
+    x_ref,
+    d_ref,
+    p_ref,
+    terms_ref,
+    dhidden_ref,
+    low_ref,
+    mine,
+    far,
+    hop_x,
+    hop_y,
+    last_x,
+    last_y,
+    xs,
+    ds,
+    outs,
+    local_sems,
+    x_sems,
+    out_sems,
+    send_sems,
+    recv_sems,
+):
+    s, n, core, across, beside = places()
+    other = (core + 2) % 4
+    to_core, to_y, to_x = {"seq": core}, {"seq": across}, {"near": beside}
+    rows, width = hidden_ref.shape
+    half = rows // 2
+    quarter = width // 4
+    split = dgu_ref.shape[1]
+    far_size, _, weight_rows, columns = terms_ref.shape
+
+    def block(seq, near):
+        return p_ref.at[pl.ds((seq * 2 + near) * rows, rows)]
+
+    def part(ref, p):
+        return ref.at[pl.ds(p * half, half)]
+
+    def columns_in(q):
+        slot = q % 2
+        at = pl.ds(q * quarter, quarter)
+        return (
+            pltpu.make_async_copy(x_ref.at[:, at], xs.at[slot], x_sems.at[slot, 0]),
+            pltpu.make_async_copy(d_ref.at[:, at], ds.at[slot], x_sems.at[slot, 1]),
+        )
+
+    def terms_out(q):
+        return pltpu.make_async_copy(outs.at[q % 2], terms_ref.at[:, q], out_sems.at[q % 2])
+
+    meet(to_core, to_y, to_x)
+    copies, send = sender(send_sems, recv_sems)
+    given = [block(other, beside), block(other, n), block(core, beside), block(core, n)]
+    kept = [block(across, beside), block(across, n), block(s, beside), block(s, n)]
+    loads = []
+    for k in range(4):
+        send(k, given[k], far.at[k], to_core)
+        loads.append(pltpu.make_async_copy(kept[k], mine.at[k], local_sems.at[k]))
+        loads[k].start()
+    for q in range(2):
+        for copy in columns_in(q):
+            copy.start()
+
+    def grads(q):
+        slot = q % 2
+        for copy in columns_in(q):
+            copy.wait()
+        if q >= 2:
+            terms_out(q - 2).wait()
+        gateup = product(xs[slot], dgu_ref[...], 0, 0).astype(jnp.bfloat16)
+        outs[slot, :, :, :split] = gateup.reshape(far_size, weight_rows, split)
+        down = product(ds[slot], act_ref[...], 0, 0).astype(jnp.bfloat16)
+        outs[slot, :, :, split:] = down.reshape(far_size, weight_rows, columns - split)
+        terms_out(q).start()
+        if q < 2:
+            for copy in columns_in(q + 2):
+                copy.start()
+
+    for k in range(3):
+        loads[k].wait()
+        copies[k].wait_recv()
+        add_rows(mine.at[k], mine.at[k], far.at[k])
+        if k == 0:
+            send("hx", part(mine.at[0], 0), hop_x, to_x)
+            send("hy", part(mine.at[0], 1), hop_y, to_y)
+        elif k == 1:
+            send("y1", part(mine.at[1], 1), part(last_y, 1), to_y)
+        else:
+            send("x0", part(mine.at[2], 0), part(last_x, 0), to_x)
+    grads(0)
+    grads(1)
+    copies["hx"].wait_recv()
+    add_rows(part(mine.at[1], 0), part(mine.at[1], 0), hop_x)
+    send("y0", part(mine.at[1], 0), part(last_y, 0), to_y)
+    copies["hy"].wait_recv()
+    add_rows(part(mine.at[2], 1), part(mine.at[2], 1), hop_y)
+    send("x1", part(mine.at[2], 1), part(last_x, 1), to_x)
+    loads[3].wait()
+    copies[3].wait_recv()
+    add_rows(dhidden_ref, mine.at[3], far.at[3])
+    grads(2)
+    grads(3)
+    for key in ("y1", "x0", "y0", "x1"):
+        copies[key].wait_recv()
+    step = 16
+
+    def backward(i, carry):
+        at = pl.ds(pl.multiple_of(i * step, step), step)
+        dx = dhidden_ref[at, :] + last_x[at, :].astype(jnp.float32) + last_y[at, :].astype(jnp.float32)
+        unit, scale = rms_normalize(hidden_ref[at, :])
+        dhidden = cotangent_ref[at, :] + norm_backward(dx, unit, scale)
+        dhidden_ref[at, :] = dhidden
+        low_ref[at, :] = dhidden.astype(low_ref.dtype)
+        return carry
+
+    lax.fori_loop(0, rows // step, backward, 0)
+    for q in (2, 3):
+        terms_out(q).wait()
+    for copy in copies.values():
+        copy.wait_send()
+
+
+def feed_back(hidden, cotangent, dgu, act, x, d, p, far, collective_id):
+    rows, width = hidden.shape
+    tokens, columns = x.shape[0], dgu.shape[1] + act.shape[1]
+    weight_rows = width // (4 * far)
+    low = jnp.bfloat16
+    block = pltpu.VMEM((rows, width), low)
+    half_block = pltpu.VMEM((rows // 2, width), low)
+    return pl.pallas_call(
+        feed_back_kernel,
+        out_shape=[
+            jax.ShapeDtypeStruct((far, 4, weight_rows, columns), low),
+            jax.ShapeDtypeStruct((rows, width), jnp.float32),
+            jax.ShapeDtypeStruct((rows, width), low),
+        ],
+        in_specs=[IN_VMEM] * 4 + [ANYWHERE] * 3,
+        out_specs=[ANYWHERE, IN_VMEM, IN_VMEM],
+        scratch_shapes=[
+            pltpu.VMEM((4, rows, width), low),
+            pltpu.VMEM((4, rows, width), low),
+            half_block,
+            half_block,
+            block,
+            block,
+            pltpu.VMEM((2, tokens, width // 4), low),
+            pltpu.VMEM((2, tokens, width // 4), low),
+            pltpu.VMEM((2, far, weight_rows, columns), low),
+            pltpu.SemaphoreType.DMA((4,)),
+            pltpu.SemaphoreType.DMA((2, 2)),
+            pltpu.SemaphoreType.DMA((2,)),
+            pltpu.SemaphoreType.DMA((10,)),
+            pltpu.SemaphoreType.DMA((10,)),
+        ],
+        compiler_params=pltpu.CompilerParams(
+            collective_id=collective_id, has_side_effects=True, vmem_limit_bytes=VMEM_LIMIT
+        ),
+        cost_estimate=pl.CostEstimate(
+            flops=2 * tokens * width * columns, bytes_accessed=60_000_000, transcendentals=0
+        ),
+    )(hidden, cotangent, dgu, act, x, d, p)
 
 
 def rotary_tables(positions, width):
@@ -985,15 +1265,11 @@
     return qkv, out
 
 
-def norm_kernel(zero_ref, one_ref, head_ref, qkv_ref, gateup_ref, gains_ref, square_ref, gain_grads_ref):
+def norm_kernel(zero_ref, one_ref, gateup_ref, gains_ref, square_ref, terms_ref):
     halves = (zero_ref, one_ref)
     part = zero_ref.shape[2] // 3
     gateup, down = feed_pieces(part)
-    qkv, out = head_pieces_of(head_ref.shape[2])
-    gains = gains_ref[...].astype(jnp.bfloat16).astype(jnp.float32)
-
-    def low(x):
-        return x.astype(jnp.bfloat16).astype(jnp.float32)
+    two = gains_ref[...].astype(jnp.bfloat16).astype(jnp.float32)[:, 1:2]
 
     def over(x):
         return jnp.sum(x, 1, keepdims=True)
@@ -1001,32 +1277,15 @@
     two_squares = two_terms = down_squares = 0.0
     for half, device, at, column in gateup:
         grad = halves[half][device, :, at : at + part].astype(jnp.float32)
+        weight = gateup_ref[:, column : column + part].astype(jnp.bfloat16).astype(jnp.float32)
         two_squares = two_squares + grad * grad
-        two_terms = two_terms + grad * low(gateup_ref[:, column : column + part])
+        two_terms = two_terms + grad * weight
     for half, device, at, column in down:
         grad = halves[half][device, :, at : at + part].astype(jnp.float32)
         down_squares = down_squares + grad * grad
-    one_squares = one_terms = out_squares = 0.0
-    for device, at, column, size in qkv:
-        grad = head_ref[device, :, at : at + size].astype(jnp.float32)
-        one_squares = one_squares + over(grad * grad)
-        one_terms = one_terms + over(grad * low(qkv_ref[:, column : column + size]))
-    for device, at, column, size in out:
-        grad = head_ref[device, :, at : at + size].astype(jnp.float32)
-        out_squares = out_squares + over(grad * grad)
     two_terms = over(two_terms)
-    gain_grads_ref[:, 0:1] = one_terms
-    gain_grads_ref[:, 1:2] = two_terms
-    one, two = gains[:, 0:1], gains[:, 1:2]
-    rows = (
-        one * one * one_squares
-        + two * two * over(two_squares)
-        + over(down_squares)
-        + out_squares
-        + one_terms * one_terms
-        + two_terms * two_terms
-    )
-    total = jnp.sum(rows)
+    terms_ref[...] = two_terms
+    total = jnp.sum(two * two * over(two_squares) + over(down_squares) + two_terms * two_terms)
 
     @pl.when(pl.program_id(0) == 0)
     def _():
@@ -1046,26 +1305,146 @@
     return pl.BlockSpec((ROWS, array.shape[1]), lambda r: (r, 0))
 
 
-def gradient_norm(zero, one, head, qkv, gateup, gains):
-    arrays = (zero, one, head, qkv, gateup, gains)
+def feed_norm(zero, one, gateup, gains):
+    arrays = (zero, one, gateup, gains)
+    rows = gains.shape[0]
+    terms = jax.ShapeDtypeStruct((rows, 1), jnp.float32)
     return pl.pallas_call(
         norm_kernel,
-        grid=(gains.shape[0] // ROWS,),
-        out_shape=[jax.ShapeDtypeStruct((1, 1), jnp.float32), jax.ShapeDtypeStruct(gains.shape, jnp.float32)],
+        grid=(rows // ROWS,),
+        out_shape=[jax.ShapeDtypeStruct((1, 1), jnp.float32), terms],
         in_specs=[rows_of(x) for x in arrays],
-        out_specs=[pl.BlockSpec(memory_space=pltpu.SMEM), rows_of(gains)],
+        out_specs=[pl.BlockSpec(memory_space=pltpu.SMEM), rows_of(terms)],
         compiler_params=pltpu.CompilerParams(vmem_limit_bytes=VMEM_LIMIT),
+        cost_estimate=pl.CostEstimate(flops=0, bytes_accessed=10_000_000, transcendentals=0),
     )(*arrays)
 
 
-def adam_kernel(clip_ref, zero_ref, one_ref, head_ref, gain_grads_ref, *refs):
+def settle_kernel(
+    square_ref,
+    terms_ref,
+    qkv_ref,
+    gains_ref,
+    p_ref,
+    head_ref,
+    norm_ref,
+    gain_grads_ref,
+    mine,
+    seq_parts,
+    near_parts,
+    far_parts,
+    local_sem,
+    send_sems,
+    recv_sems,
+    far_send_sems,
+    far_recv_sems,
+):
+    s, n, core, across, beside = places()
+    diagonal = (core + 2) % 4
+    f = lax.axis_index("far")
+    far_size = far_parts.shape[0]
+    seqs = ({"seq": diagonal}, {"seq": across}, {"seq": core})
+    fars = [{"far": (f + k) % far_size} for k in range(1, far_size)]
+    meet(*seqs, {"near": beside}, *fars)
+    copies, send = sender(send_sems, recv_sems)
+    for k, seq in enumerate((diagonal, across, core)):
+        send(("w", k), p_ref.at[seq], mine.at[s], seqs[k])
+    keep = pltpu.make_async_copy(p_ref.at[s], mine.at[s], local_sem)
+    keep.start()
+    gains = gains_ref[...].astype(jnp.bfloat16).astype(jnp.float32)
+    qkv, out = head_pieces_of(head_ref.shape[2])
+    keep.wait()
+    for k in range(3):
+        copies["w", k].wait_recv()
+
+    def over(x):
+        return jnp.sum(x, 1, keepdims=True)
+
+    one_squares = one_terms = out_squares = 0.0
+    for device, at, column, size in qkv:
+        grad = mine[device, :, at : at + size].astype(jnp.float32)
+        weight = qkv_ref[:, column : column + size].astype(jnp.bfloat16).astype(jnp.float32)
+        one_squares = one_squares + over(grad * grad)
+        one_terms = one_terms + over(grad * weight)
+    for device, at, column, size in out:
+        grad = mine[device, :, at : at + size].astype(jnp.float32)
+        out_squares = out_squares + over(grad * grad)
+    one = gains[:, 0:1]
+    rows = one * one * one_squares + out_squares + one_terms * one_terms
+    gain_grads_ref[:, 0:1] = one_terms
+    gain_grads_ref[:, 1:2] = terms_ref[...]
+    total = jnp.sum(rows) + square_ref[0, 0]
+
+    seq_parts[s] = jnp.full(seq_parts.shape[1:], total, jnp.float32)
+    for k in range(3):
+        send(("s", k), seq_parts.at[s], seq_parts.at[s], seqs[k])
+    head_ref[...] = mine[...]
+    for k in range(3):
+        copies["s", k].wait_recv()
+    near_parts[n] = (seq_parts[0] + seq_parts[1]) + (seq_parts[2] + seq_parts[3])
+    send("n", near_parts.at[n], near_parts.at[n], {"near": beside})
+    copies["n"].wait_recv()
+    far_parts[f] = near_parts[0] + near_parts[1]
+    far_copies = [
+        pltpu.make_async_remote_copy(
+            src_ref=far_parts.at[f],
+            dst_ref=far_parts.at[f],
+            send_sem=far_send_sems.at[k],
+            recv_sem=far_recv_sems.at[k],
+            device_id=far,
+            device_id_type=MESH_IDS,
+        )
+        for k, far in enumerate(fars)
+    ]
+    for copy in far_copies:
+        copy.start()
+    for copy in far_copies:
+        copy.wait_recv()
+    everywhere = far_parts[0]
+    for k in range(1, far_size):
+        everywhere = everywhere + far_parts[k]
+    norm_ref[...] = jnp.sqrt(everywhere)
+    for copy in (*copies.values(), *far_copies):
+        copy.wait_send()
+
+
+def settle(square, terms, qkv, gains, p, collective_id):
+    far = lax.axis_size("far")
+    tile = (8, 128)
+    return pl.pallas_call(
+        settle_kernel,
+        out_shape=[
+            jax.ShapeDtypeStruct(p.shape, p.dtype),
+            jax.ShapeDtypeStruct(tile, jnp.float32),
+            jax.ShapeDtypeStruct(gains.shape, jnp.float32),
+        ],
+        in_specs=[pl.BlockSpec(memory_space=pltpu.SMEM)] + [IN_VMEM] * 3 + [ANYWHERE],
+        out_specs=[IN_VMEM] * 3,
+        scratch_shapes=[
+            pltpu.VMEM(p.shape, p.dtype),
+            pltpu.VMEM((4, *tile), jnp.float32),
+            pltpu.VMEM((2, *tile), jnp.float32),
+            pltpu.VMEM((far, *tile), jnp.float32),
+            pltpu.SemaphoreType.DMA,
+            pltpu.SemaphoreType.DMA((7,)),
+            pltpu.SemaphoreType.DMA((7,)),
+            pltpu.SemaphoreType.DMA((far - 1,)),
+            pltpu.SemaphoreType.DMA((far - 1,)),
+        ],
+        compiler_params=pltpu.CompilerParams(
+            collective_id=collective_id, has_side_effects=True, vmem_limit_bytes=VMEM_LIMIT
+        ),
+    )(square, terms, qkv, gains, p)
+
+
+def adam_kernel(norm_ref, zero_ref, one_ref, head_ref, gain_grads_ref, *refs):
     weights, firsts, seconds = refs[0:5], refs[5:10], refs[10:15]
     weights_out, firsts_out, seconds_out = refs[15:20], refs[20:25], refs[25:30]
     halves = (zero_ref, one_ref)
     part = zero_ref.shape[2] // 3
     gateup, down = feed_pieces(part)
     qkv, out = head_pieces_of(head_ref.shape[2])
-    clip = clip_ref[0, 0]
+    clip = CLIP_NORM / jnp.maximum(norm_ref[0:1, 0:1], CLIP_NORM)
     gains = weights[4][...].astype(jnp.bfloat16).astype(jnp.float32) * clip
     one, two = gains[:, 0:1], gains[:, 1:2]
 
@@ -1088,17 +1467,17 @@
     step(4, slice(0, 2), gain_grads_ref[...] * clip, RATE_GAIN, 0.0)
 
 
-def adam(clip, zero, one, head, gain_grads, weights, firsts, seconds):
+def adam(norm, zero, one, head, gain_grads, weights, firsts, seconds):
     state = (*weights, *firsts, *seconds)
     arrays = (zero, one, head, gain_grads, *state)
     return pl.pallas_call(
         adam_kernel,
         grid=(gain_grads.shape[0] // ROWS,),
         out_shape=[jax.ShapeDtypeStruct(x.shape, x.dtype) for x in state],
-        in_specs=[pl.BlockSpec(memory_space=pltpu.SMEM)] + [rows_of(x) for x in arrays],
+        in_specs=[pl.BlockSpec(norm.shape, lambda r: (0, 0))] + [rows_of(x) for x in arrays],
         out_specs=[rows_of(x) for x in state],
         compiler_params=pltpu.CompilerParams(vmem_limit_bytes=VMEM_LIMIT),
-    )(clip, *arrays)
+    )(norm, *arrays)
 
 
 def product(left, right, left_dim, right_dim):
@@ -1152,12 +1531,7 @@
         weight = weight.astype(low)
         return weight if gain is None else (weight.astype(jnp.float32) * gain).astype(low)
 
-    def far_first(x):
-        x = x.reshape(-1, seq, far, 2 * rows).transpose(0, 2, 1, 3)
-        return x.reshape(-1, width)
-
-    def far_last(x):
-        return x.reshape(-1, far, seq, 2 * rows).transpose(0, 2, 1, 3).reshape(-1, width)
+    by_far = (far, seq, 2 * rows, 3 * part)
 
     def feed_piece(half):
         start, size = half * FEED_UNITS // 2, FEED_UNITS // 2
@@ -1170,7 +1544,7 @@
         return jnp.concatenate(columns, 2)
 
     (piece,) = exchange_plane([feed_piece(0).reshape(group * rows, 3 * part)], 1)
-    feed_zero = lax.all_gather(piece, "far", axis=0, tiled=True)
+    feed_zero = lax.all_gather(piece, "far", axis=0, tiled=True).reshape(by_far)
 
     qkv_low = rounded(query_key_value_weight, gain_one)
     head_pieces = jnp.concatenate(
@@ -1184,33 +1558,29 @@
     ).transpose(1, 0, 2)
     unit_one, scale_one = rms_normalize(inputs)
     turns = rotary_tables(positions.reshape(-1), HEAD_SIZE)
-    dout_here = far_first(cotangent.astype(low))
+    dout_here = cotangent.astype(low)
     head_pieces = after(head_pieces, piece)
     head_w, normed_one, all_turns, dout, piece = gather_heads(
         head_pieces, unit_one.astype(low), turns, dout_here, feed_piece(1), 2
     )
     feed_one = lax.all_gather(piece.reshape(group * rows, -1), "far", axis=0, tiled=True)
+    feed_one = feed_one.reshape(by_far)
     all_turns = all_turns.reshape(-1, HEAD_SIZE)
     *saved, attended = attention(lengths, normed_one, head_w, all_turns)
     hidden = inputs + scatter_seq(attended, 3)
-    unit_two, scale_two = rms_normalize(hidden)
-    normed_two = gather_plane(far_first(unit_two.astype(low)), 4)
-    act_zero, dgateup_zero, *sums = feed(normed_two, dout, feed_zero, ())
-    terms_zero = feed_grads(normed_two, dout, dgateup_zero, act_zero)
-    feed_one = after(feed_one, terms_zero)
-    act_one, dgateup_one, output_terms, dnormed_two = feed(normed_two, dout, feed_one, sums)
-    dnormed_two = scatter_plane(dnormed_two, 5)
-    dgateup_one = after(dgateup_one, dnormed_two)
-    terms_one = feed_grads(normed_two, dout, dgateup_one, act_one)
-    dnormed_two = far_last(dnormed_two)
-    grads_zero = lax.psum_scatter(terms_zero, "far", scatter_dimension=0, tiled=True)
-    grads_one = lax.psum_scatter(
-        after(terms_one, grads_zero), "far", scatter_dimension=0, tiled=True
+    unit_two, _ = rms_normalize(hidden)
+    normed_two, act, dgateup, *sums = feed_first(unit_two.astype(low), dout, feed_zero, 4)
+    terms = feed_grads(normed_two, dout, dgateup, act, far).reshape(width, 3 * part)
+    grads_zero = lax.psum_scatter(terms, "far", scatter_dimension=0, tiled=True)
+    act, dgateup, output_terms, dnormed_two = feed_second(
+        normed_two, dout, *sums, after(feed_one, terms)
     )
-    back_two = norm_backward(dnormed_two, unit_two, scale_two)
-    dhidden = cotangent + back_two
-
-    dattended = after(dhidden.astype(low), terms_one)
+    terms, dhidden, dattended = feed_back(
+        hidden, cotangent, dgateup, act, normed_two, dout, dnormed_two, far, 5
+    )
+    terms = terms.reshape(width, 3 * part)
+    grads_one = lax.psum_scatter(after(terms, grads_zero), "far", scatter_dimension=0, tiled=True)
+
     head_terms, dnormed_one, output_terms = attention_back(
         lengths, saved, all_turns, dattended, output_terms, head_w, normed_one, 6
     )
@@ -1219,24 +1589,19 @@
         head_terms.reshape(far * seq * rows, -1), "far", scatter_dimension=0, tiled=True
     )
     input_grad = dhidden + norm_backward(dnormed_one, unit_one, scale_one)
-    layer_output = hidden + far_last(output_terms)
-
-    halves = exchange_plane([grads_zero, grads_one], 7)
-    head_terms = after(head_terms, halves[0])
-    halves = [x.reshape(group, rows, 3 * part) for x in halves]
-    head_grads = lax.all_to_all(head_terms.reshape(seq, rows, -1), "seq", 0, 0, tiled=True)
-
+    layer_output = hidden + output_terms
+
+    halves = [x.reshape(group, rows, 3 * part) for x in exchange_plane([grads_zero, grads_one], 7)]
+    square, gain_terms = feed_norm(*halves, gateup_weight, norm_gains)
+    head_terms = after(head_terms, square, input_grad, layer_output)
+    head_grads, norm, gain_grads = settle(
+        square, gain_terms, query_key_value_weight, norm_gains, head_terms.reshape(seq, rows, -1), 8
+    )
     weights = (query_key_value_weight, out_weight, gateup_weight, down_weight, norm_gains)
     firsts = (query_key_value_moment, output_weight_moment, gate_up_moment, down_weight_moment, norm_gains_moment)
     seconds = (query_key_value_variance, out_second, gateup_second, down_second, gains_second)
-    squares, gain_grads = gradient_norm(
-        *halves, head_grads, query_key_value_weight, gateup_weight, norm_gains
-    )
-    squares = lax.psum(lax.psum(lax.psum(squares[0, 0], "seq"), "near"), "far")
-    grad_norm = jnp.sqrt(squares)
-    clip = CLIP_NORM / jnp.maximum(grad_norm, CLIP_NORM)
-    stepped = adam(clip.reshape(1, 1), *halves, head_grads, gain_grads, weights, firsts, seconds)
-    return (layer_output[None], input_grad[None], grad_norm, *stepped)
+    stepped = adam(norm, *halves, head_grads, gain_grads, weights, firsts, seconds)
+    return (layer_output[None], input_grad[None], norm[0, 0], *stepped)
 
 
 def solution(mesh):

time: 764 us -> 677 us (0.89)
  local copies, waits for them, and re-layouts: 42.6 us -> 13.1 us
  Pallas kernels: 614 us -> 591 us
  blocking collectives: 23 us -> 0 us
    reshape x9 -> x0, local copies, waits for them, and re-layouts: 26.6 us -> none  [the longest x6 20.6 us: far_last(): x.reshape(-1, far, seq, 2 * rows).transpose(0, 2, 1, 3).reshape(-1, width)]
    psum x3 -> x0, blocking collectives: 23 us -> none  [shards(): squares = lax.psum(lax.psum(lax.psum(squares[0, 0], 'seq'), 'near'), 'far')]
    reduce_scatter x2, waiting for transfers between devices: 11 us -> 23.7 us  [the longest x1 23.7 us: shards(): grads_zero = lax.psum_scatter(terms, 'far', scatter_dimension=0, tiled=True)]
    pallas_call x1, Pallas kernels: 176 us -> 165 us  [gather_heads(): pl.pallas_call(functools.partial(gather_heads_kernel, far_size), out_shap...]
    pallas_call x7 -> x6, Pallas kernels: 195 us -> 185 us  [the longest x1 49.5 us: feed_first(): pl.pallas_call(feed_first_kernel, out_shape=[jax.ShapeDtypeStruct((tokens...]
  transfers between devices with their start and end apart: 6 -> 5, of which waited for: 3 -> 2; matrix products, arithmetic and copies ran while one was open for 6% -> 3% of each run, Pallas kernels for 75% -> 78%
where the time goes in v5:
time: 677 us; the launch traced here: 673 us
  Pallas kernels  591 us (87%)
  waiting for transfers between devices  31.5 us (5%)
  other arithmetic  20.6 us (3%)
  between operations  15 us (2%)
  local copies, waits for them, and re-layouts  13.1 us (2%)
    pallas_call x1, Pallas kernels, gather_heads(): pl.pallas_call(functools.partial(gather_heads_kernel, far_size), out_shap...  165 us
    pallas_call x1, Pallas kernels, attention_back(): pl.pallas_call(attention_back_kernel, out_shape=[jax.ShapeDtypeStruct((fa...  116 us
    pallas_call x2, Pallas kernels, exchange_plane(): pl.pallas_call(functools.partial(exchange_plane_kernel, count), out_shape...  60.6 us
    pallas_call x1, Pallas kernels, feed_first(): pl.pallas_call(feed_first_kernel, out_shape=[jax.ShapeDtypeStruct((tokens...  49.5 us
    pallas_call x1, Pallas kernels, feed_back(): pl.pallas_call(feed_back_kernel, out_shape=[jax.ShapeDtypeStruct((far, 4,...  47.8 us
    pallas_call x1, Pallas kernels, feed_second(): pl.pallas_call(feed_second_kernel, grid=(tokens // tile,), out_shape=[jax...  37.7 us
    pallas_call x1, Pallas kernels, scatter_seq(): pl.pallas_call(functools.partial(scatter_seq_kernel, rows), out_shape=jax...  29.9 us
    pallas_call x1, Pallas kernels, settle(): pl.pallas_call(settle_kernel, out_shape=[jax.ShapeDtypeStruct(p.shape, p....  25.3 us
  transfers between devices with their start and end apart: 5, of which 2 were waited for; matrix products, arithmetic and copies ran while one was open for 3% of the time, Pallas kernels for 78%

profile of v5, /device:TPU:0, one launch (start us, length us, event | category | flops | bytes accessed | tf_op | source)
XLA Modules:
  0.0 672.6 jit_solution(8522950471786865811)
XLA Ops:
  7.3 2.5 convert.10
  11.6 1.4 multiply_convert_fusion.2
  13.1 1.3 pad_maximum_fusion
  14.4 22.8 %shard_map.322 = bf16[512,1536]{1,0:T(8,128)(2,1)} custom-call(bf16[512,1536]{1,0:T(8,128)(2,1)} %bitcast.103), custom_call_target="tpu_custom_call" | custom-call | tf_op jit(solution)/shard_map/pallas_call | solution.py:170
  44.8 164.9 %shard_map.323 = (bf16[4,4,2,64,1536]{4,3,2,1,0:T(8,128)(2,1)}, bf16[4,256,2048]{2,1,0:T(8,128)(2,1)}, f32[4,256,256]{2,1,0:T(8,128)}, bf16[8,256,2048]{2,1,0:T(8,128)(2,1)}, bf16[8,64,1536]{2,1,0:T(8,128)(2,1)}) custom-call(bf16[4,64,1536]{2,1,0:T(8,128)(2,1)} %maximum_bitcast_fusion.w_ref, bf16[256,2048]{1,0:T(8,128)(2,1)} %fusion.1.x_ref, ...), custom_call_target="tpu_custom_call" | custom-call | tf_op jit(solution)/shard_map/pallas_call | solution.py:371
  210.7 17.9 %shard_map.324 = (bf16[1024,512]{1,0:T(8,128)(2,1)}, bf16[1024,256]{1,0:T(8,128)(2,1)}, bf16[1024,256]{1,0:T(8,128)(2,1)}, bf16[1024,512]{1,0:T(8,128)(2,1)}, f3...) custom-call(s32[1]{0:T(128)S(6)} %copy.96.length_ref, bf16[1024,2048]{1,0:T(8,128)(2,1)} %bitcast.139, ...), custom_call_target="tpu_custom_call" | custom-call | flops 10000000000 | bytes 20000000 | tf_op jit(solution)/shard_map/pallas_call | solution.py:467
  228.5 29.9 %shard_map.325 = f32[256,2048]{1,0:T(8,128)} custom-call(bf16[1024,2048]{1,0:T(8,128)(2,1)} %get-tuple-element.75.p_ref), custom_call_target="tpu_custom_call" | custom-call | tf_op jit(solution)/shard_map/pallas_call | solution.py:119
  258.4 1.9 multiply_reduce_fusion.1
  262.8 49.5 %shard_map.326 = (bf16[2048,2048]{1,0:T(8,128)(2,1)}, bf16[2048,512]{1,0:T(8,128)(2,1)}, bf16[2048,1024]{1,0:T(8,128)(2,1)}, bf16[2048,2048]{1,0:T(8,128)(2,1)}, bf16[2048,2048]{1,0:T(8,128)(2,1)}) custom-call(bf16[256,2048]{1,0:T(8,128)(2,1)} %multiply_convert_fusion.x_ref, bf16[2048,2048]{1,0:T(8,128)(2,1)} %bitcast.131, bf16[4,4,128,1536]{3,2,1,0:T(8,128)(2,1)} %bitcast.135), custom_call_target="tpu_custom_call" | custom-call | flops 25769803776 | bytes 60000000 | tf_op jit(solution)/shard_map/pallas_call | solution.py:949
  312.3 19.2 %shard_map.327 = bf16[4,4,128,1536]{3,2,1,0:T(8,128)(2,1)} custom-call(bf16[2048,2048]{1,0:T(8,128)(2,1)} %get-tuple-element.82.x_ref, bf16[2048,2048]{1,0:T(8,128)(2,1)} %bitcast.132, bf16[2048,1024]{1,0:T(8,128)(2,1)} %get-tuple-element.86.dgu_ref, bf16[2048,512]{1,0:T(8,128)(2,1)} %get-tuple-element.87.act_ref), custom_call_target="tpu_custom_call" | custom-call | flops 12884901888 | bytes 40000000 | tf_op jit(solution)/shard_map/pallas_call | solution.py:1040
  332.0 37.7 %shard_map.328 = (bf16[2048,512]{1,0:T(8,128)(2,1)}, bf16[2048,1024]{1,0:T(8,128)(2,1)}, bf16[2048,2048]{1,0:T(8,128)(2,1)}, bf16[2048,2048]{1,0:T(8,128)(2,1)}) custom-call(bf16[2048,2048]{1,0:T(8,128)(2,1)} %get-tuple-element.82.x_ref, bf16[2048,2048]{1,0:T(8,128)(2,1)} %bitcast.133, bf16[2048,2048]{1,0:T(8,128)(2,1)} %get-tuple-element.83.y0_ref, ...), custom_call_target="tpu_custom_call" | custom-call | flops 25769803776 | bytes 60000000 | tf_op jit(solution)/shard_map/pallas_call | solution.py:1008
  369.8 47.8 %shard_map.329 = (bf16[4,4,128,1536]{3,2,1,0:T(8,128)(2,1)}, f32[256,2048]{1,0:T(8,128)}, bf16[256,2048]{1,0:T(8,128)(2,1)}) custom-call(f32[256,2048]{1,0:T(8,128)} %copy-done.1, f32[256,2048]{1,0:T(8,128)} %bitcast.111, bf16[2048,1024]{1,0:T(8,128)(2,1)} %get-tuple-element.89.dgu_ref, bf16[2048,512]{1,0:T(8,128)(2,1)} %get-tuple-element.90.act_ref, ...), custom_call_target="tpu_custom_call" | custom-call | flops 12884901888 | bytes 60000000 | tf_op jit(solution)/shard_map/pallas_call | solution.py:1184
  417.5 23.7 %reduce-scatter.4.cloned.1.call-done.refs_0_ = bf16[512,1536]{1,0:T(8,128)(2,1)} async-done(((bf16[2048,1536]{1,0:T(8,128)(2,1)}), bf16[512,1536]{1,0:T(8,128)(2,1)}) %reduce-scatter.4.cloned.1.call-update) | async-done | bytes 1572880 | tf_op jit(solution)/shard_map/reduce_scatter | solution.py:1574
  441.3 116.0 %shard_map.330 = (bf16[4,4,64,1536]{3,2,1,0:T(8,128)(2,1)}, f32[256,2048]{1,0:T(8,128)}, f32[256,2048]{1,0:T(8,128)}) custom-call(s32[1]{0:T(128)S(6)} %copy.96.length_ref, bf16[1024,512]{1,0:T(8,128)(2,1)} %get-tuple-element.76.q_ref, bf16[1024,256]{1,0:T(8,128)(2,1)} %get-tuple-element.77.k_ref, bf16[1024,256]{1,0:T(8,128)(2,1)} %get-tuple-element.78.v_ref, ...), custom_call_target="tpu_custom_call" | custom-call | flops 20000000000 | bytes 40000000 | tf_op jit(solution)/shard_map/pallas_call | solution.py:693
  559.5 4.0 add.34
  565.2 1.8 multiply_add_fusion
  566.9 37.8 %shard_map.331 = (bf16[512,1536]{1,0:T(8,128)(2,1)}, bf16[512,1536]{1,0:T(8,128)(2,1)}) custom-call(bf16[512,1536]{1,0:T(8,128)(2,1)} %reduce-scatter.4.cloned.1.call-done.refs_0_, bf16[512,1536]{1,0:T(8,128)(2,1)} %reduce-scatter.6.cloned.1.call-done.refs_1_), custom_call_target="tpu_custom_call" | custom-call | tf_op jit(solution)/shard_map/pallas_call | solution.py:170
  604.8 5.2 shard_map.332
  610.0 7.7 %reduce-scatter.8.cloned.1.call-done = bf16[256,1536]{1,0:T(8,128)(2,1)} async-done(((bf16[1024,1536]{1,0:T(8,128)(2,1)}), bf16[256,1536]{1,0:T(8,128)(2,1)}) %reduce-scatter.8.cloned.1.call-update) | async-done | bytes 786448 | tf_op jit(solution)/shard_map/reduce_scatter | solution.py:1588
  617.7 25.3 %shard_map.333 = (bf16[4,64,1536]{2,1,0:T(8,128)(2,1)}, f32[8,128]{1,0:T(8,128)}, f32[64,2]{1,0:T(8,128)}) custom-call(f32[1,1]{1,0:T(1,128)} %get-tuple-element.101.square_ref, f32[64,1]{1,0:T(8,128)} %get-tuple-element.102.terms_ref, f32[64,4096]{1,0:T(8,128)} %refs_0_.1, f32[64,2]{1,0:T(8,128)} %copy.58.gains_ref.refs_4_, bf16[4,64,1536]{2,1,0:T(8,128)(2,1)} %bitcast.125), custom_call_target="tpu_custom_call" | custom-call | tf_op jit(solution)/shard_map/pallas_call | solution.py:1414
  644.1 17.6 %shard_map.334 = (f32[64,4096]{1,0:T(8,128)}, f32[64,2048]{1,0:T(8,128)}, f32[64,16384]{1,0:T(8,128)}, f32[64,8192]{1,0:T(8,128)}, f32[64,2]{1,0:T(8,128)}, /*in...) custom-call(f32[8,128]{1,0:T(8,128)} %get-tuple-element.106.norm_ref, ...), custom_call_target="tpu_custom_call" | custom-call | tf_op jit(solution)/shard_map/pallas_call | solution.py:1473
  661.7 1.4 copy.63
  663.1 1.4 copy.64
  664.5 1.4 copy.65
  (76 shorter events, 17.6 us)
Async XLA Ops:
  7.2 2.6 copy-start.10
  7.2 2.9 copy-start.3
  7.2 255.6 %all-gather.3.cloned.1.call-start = ((), (), s32[]{:S(2)}) async-start(), calls=%async_computation.3 | async-start | bytes 7864320 | tf_op jit(solution)/shard_map/all_gather | solution.py:1547
  10.2 1.4 copy-start.2
  14.4 22.9 %copy-start.6 = (f32[64,2048]{1,0:T(8,128)S(1)}, f32[64,2048]{1,0:T(8,128)}, u32[]{:S(2)}) copy-start(f32[64,2048]{1,0:T(8,128)} %refs_1_.1) | copy-start | bytes 1572868
  37.2 294.8 %all-gather.5.cloned.1.call-start = ((), (), s32[]{:S(2)}) async-start(), calls=%async_computation.4 | async-start | bytes 7864320 | tf_op jit(solution)/shard_map/all_gather | solution.py:1566
  37.3 1.1 copy-start.13
  37.3 1.1 copy-start.9
  37.4 1.3 copy-start.7
  38.5 1.7 copy-start
  40.4 2.2 copy-start.8
  209.8 231.5 %reduce-scatter.4.cloned.1.call-start = ((), (), s32[]{:S(2)}) async-start(), calls=%async_computation.5 | async-start | bytes 7864320 | tf_op jit(solution)/shard_map/reduce_scatter | solution.py:1574
  260.3 1.3 copy-start.1
  331.5 225.9 %reduce-scatter.6.cloned.1.call-start = ((), (), s32[]{:S(2)}) async-start(), calls=%async_computation.6 | async-start | bytes 7864320 | tf_op jit(solution)/shard_map/reduce_scatter | solution.py:1582
  441.2 176.4 %reduce-scatter.8.cloned.1.call-start = ((), (), s32[]{:S(2)}) async-start(), calls=%async_computation.7 | async-start | bytes 3932160 | tf_op jit(solution)/shard_map/reduce_scatter | solution.py:1588
  557.3 0.8 copy-start.11
  557.3 1.5 copy-start.12
  559.5 4.0 copy-start.4
  563.5 1.7 copy-start.5
Sparse Core Ops, SparseCore 0:
  37.4 153.6 all-gather.2
  209.9 114.2 all-gather.4
  331.6 109.5 reduce-scatter.3
  443.4 111.2 reduce-scatter.5
  557.5 60.0 reduce-scatter.7

commit v6 on v5

--- a/solution.py
+++ b/solution.py
@@ -77,62 +77,6 @@
         return carry
 
     lax.fori_loop(0, rows // step, body, 0)
-
-
-def scatter_seq_kernel(rows, p_ref, o_ref, mine, far, last, local_sems, send_sems, recv_sems):
-    s, _, core, across, _ = places()
-    half = rows // 2
-    to_core, to_y = {"seq": core}, {"seq": across}
-
-    def block(seq):
-        return p_ref.at[pl.ds(seq * rows, rows)]
-
-    meet(to_core, to_y)
-    copies, send = sender(send_sems, recv_sems)
-    given = [block((core + 2) % 4), block(core)]
-    kept = [block(across), block(s)]
-    locals_ = []
-    for k in range(2):
-        send(k, given[k], far.at[k], to_core)
-        locals_.append(pltpu.make_async_copy(kept[k], mine.at[k], local_sems.at[k]))
-        locals_[k].start()
-    locals_[0].wait()
-    copies[0].wait_recv()
-    for p in range(2):
-        at = pl.ds(p * half, half)
-        add_rows(mine.at[0, at], mine.at[0, at], far.at[0, at])
-        send(("y", p), mine.at[0, at], last.at[at], to_y)
-    locals_[1].wait()
-    copies[1].wait_recv()
-    add_rows(o_ref, mine.at[1], far.at[1])
-    for p in range(2):
-        at = pl.ds(p * half, half)
-        copies["y", p].wait_recv()
-        add_rows(o_ref.at[at], o_ref.at[at], last.at[at])
-    for copy in copies.values():
-        copy.wait_send()
-
-
-def scatter_seq(p, collective_id):
-    rows, columns = p.shape[0] // 4, p.shape[1]
-    low = jnp.bfloat16
-    return pl.pallas_call(
-        functools.partial(scatter_seq_kernel, rows),
-        out_shape=jax.ShapeDtypeStruct((rows, columns), jnp.float32),
-        in_specs=[ANYWHERE],
-        out_specs=IN_VMEM,
-        scratch_shapes=[
-            pltpu.VMEM((2, rows, columns), low),
-            pltpu.VMEM((2, rows, columns), low),
-            pltpu.VMEM((rows, columns), low),
-            pltpu.SemaphoreType.DMA((2,)),
-            pltpu.SemaphoreType.DMA((4,)),
-            pltpu.SemaphoreType.DMA((4,)),
-        ],
-        compiler_params=pltpu.CompilerParams(
-            collective_id=collective_id, has_side_effects=True, vmem_limit_bytes=VMEM_LIMIT
-        ),
-    )(p)
 
 
 def exchange_plane_kernel(count, *refs):
@@ -413,29 +357,54 @@
     return (column <= row) & (column < length)
 
 
-def attention_kernel(length_ref, x_ref, w_ref, turn_ref, q_ref, k_ref, v_ref, heads_ref, lse_ref, p_ref):
+def attention_kernel(
+    length_ref,
+    x_ref,
+    w_ref,
+    turn_ref,
+    input_ref,
+    q_ref,
+    k_ref,
+    v_ref,
+    heads_ref,
+    lse_ref,
+    hidden_ref,
+    unit_ref,
+    terms,
+    far,
+    last,
+    send_sems,
+    recv_sems,
+):
+    s, _, core, across, _ = places()
+    to_core, to_y = {"seq": core}, {"seq": across}
     rows = x_ref.shape[0] // 4
+    half = rows // 2
     size = k_ref.shape[1]
     low = jnp.bfloat16
     length = length_ref[0]
-
-    def project(tile, carry):
+    order = [(core + 2) % 4, across, core, s]
+
+    def rotated(ref, at, column, value, scale):
+        cos, sin = turn_ref[at, : size // 2], turn_ref[at, size // 2 :]
+        first, second = turned(value, cos, sin)
+        ref[at, column : column + size // 2] = (first * scale).astype(low)
+        ref[at, column + size // 2 : column + size] = (second * scale).astype(low)
+
+    def keys_of(tile, carry):
         at = tile_at(tile, rows)
-        merged = product(x_ref[at, :], w_ref[:, : 4 * size], 1, 0)
-        cos, sin = turn_ref[at, : size // 2], turn_ref[at, size // 2 :]
-        for ref, start, column, scale in (
-            (q_ref, 0, 0, size**-0.5),
-            (q_ref, size, size, size**-0.5),
-            (k_ref, 2 * size, 0, 1.0),
-        ):
-            first, second = turned(merged[:, start : start + size], cos, sin)
-            ref[at, column : column + size // 2] = (first * scale).astype(low)
-            ref[at, column + size // 2 : column + size] = (second * scale).astype(low)
-        v_ref[at, :] = merged[:, 3 * size :].astype(low)
+        merged = product(x_ref[at, :], w_ref[:, 2 * size : 4 * size], 1, 0)
+        rotated(k_ref, at, 0, merged[:, :size], 1.0)
+        v_ref[at, :] = merged[:, size:].astype(low)
         return carry
 
-    lax.fori_loop(0, 4, project, 0)
-    for tile in range(4):
+    def part(ref, p):
+        return ref.at[pl.ds(p * half, half)]
+
+    meet(to_core, to_y)
+    lax.fori_loop(0, 4, keys_of, 0)
+
+    def attend(tile):
         at = pl.ds(tile * rows, rows)
         keys = (tile + 1) * rows
         scores = product(stacked(q_ref[at, :]), k_ref[:keys, :], 1, 1)
@@ -451,28 +420,99 @@
             heads_ref[at, head * size : (head + 1) * size] = jnp.where(live, result[mine], 0.0).astype(low)
             lse_ref[at, head : head + 1] = lse[mine]
 
-    def out(tile, carry):
+    plan = [
+        (terms.at[0], far.at[0], to_core),
+        (terms.at[2], far.at[1], to_core),
+        (part(terms.at[1], 0), part(last, 0), to_y),
+        (part(terms.at[1], 1), part(last, 1), to_y),
+    ]
+
+    def copy_of(k):
+        source, target, device = plan[k]
+        return pltpu.make_async_remote_copy(
+            src_ref=source,
+            dst_ref=target,
+            send_sem=send_sems.at[k],
+            recv_sem=recv_sems.at[k],
+            device_id=device,
+            device_id_type=MESH_IDS,
+        )
+
+    def tile_step(step, carry):
+        tile = order[0]
+        for k in range(1, 4):
+            tile = jnp.where(step == k, order[k], tile)
         at = tile_at(tile, rows)
-        p_ref[at, :] = product(heads_ref[at, :], w_ref[:, 4 * size :], 1, 1).astype(low)
+        merged = product(x_ref[at, :], w_ref[:, : 2 * size], 1, 0)
+        for head in range(2):
+            rotated(q_ref, at, head * size, merged[:, head * size : (head + 1) * size], size**-0.5)
+        for k in range(4):
+
+            @pl.when(tile == k)
+            def _():
+                attend(k)
+
+        terms[step] = product(heads_ref[at, :], w_ref[:, 4 * size :], 1, 1).astype(low)
+
+        @pl.when(step == 0)
+        def _():
+            copy_of(0).start()
+
+        @pl.when(step == 1)
+        def _():
+            copy_of(0).wait_recv()
+            for p in range(2):
+                add_rows(part(terms.at[1], p), part(terms.at[1], p), part(far.at[0], p))
+                copy_of(2 + p).start()
+
+        @pl.when(step == 2)
+        def _():
+            copy_of(1).start()
+
         return carry
 
-    lax.fori_loop(0, 4, out, 0)
-
-
-def attention(length, x, w, turns):
+    lax.fori_loop(0, 4, tile_step, 0)
+    copy_of(1).wait_recv()
+    add_rows(hidden_ref, terms.at[3], far.at[1])
+
+    def finish(i, carry):
+        at = pl.ds(pl.multiple_of(i * 16, 16), 16)
+        hidden = input_ref[at, :] + (hidden_ref[at, :] + last[at, :].astype(jnp.float32))
+        hidden_ref[at, :] = hidden
+        unit_ref[at, :] = rms_normalize(hidden)[0].astype(low)
+        return carry
+
+    for p in range(2):
+        copy_of(2 + p).wait_recv()
+        lax.fori_loop(p * half // 16, (p + 1) * half // 16, finish, 0)
+    for k in range(4):
+        copy_of(k).wait_send()
+
+
+def attention(length, x, w, turns, inputs, collective_id):
     tokens, width = x.shape
     size = w.shape[1] // 6
+    rows = tokens // 4
     low = jnp.bfloat16
-    shapes = [(tokens, 2 * size), (tokens, size), (tokens, size), (tokens, 2 * size)]
+    results = [((tokens, 2 * size), low), ((tokens, size), low), ((tokens, size), low), ((tokens, 2 * size), low)]
+    results += [((tokens, 128), jnp.float32), ((rows, width), jnp.float32), ((rows, width), low)]
     return pl.pallas_call(
         attention_kernel,
-        out_shape=[jax.ShapeDtypeStruct(shape, low) for shape in shapes]
-        + [jax.ShapeDtypeStruct((tokens, 128), jnp.float32), jax.ShapeDtypeStruct((tokens, width), low)],
-        in_specs=[pl.BlockSpec(memory_space=pltpu.SMEM)] + [IN_VMEM] * 3,
-        out_specs=[IN_VMEM] * 6,
-        compiler_params=pltpu.CompilerParams(vmem_limit_bytes=VMEM_LIMIT),
+        out_shape=[jax.ShapeDtypeStruct(*result) for result in results],
+        in_specs=[pl.BlockSpec(memory_space=pltpu.SMEM)] + [IN_VMEM] * 4,
+        out_specs=[IN_VMEM] * 7,
+        scratch_shapes=[
+            pltpu.VMEM((4, rows, width), low),
+            pltpu.VMEM((2, rows, width), low),
+            pltpu.VMEM((rows, width), low),
+            pltpu.SemaphoreType.DMA((4,)),
+            pltpu.SemaphoreType.DMA((4,)),
+        ],
+        compiler_params=pltpu.CompilerParams(
+            collective_id=collective_id, has_side_effects=True, vmem_limit_bytes=VMEM_LIMIT
+        ),
         cost_estimate=pl.CostEstimate(flops=10_000_000_000, bytes_accessed=20_000_000, transcendentals=0),
-    )(length, x, w, turns)
+    )(length, x, w, turns, inputs)
 
 
 def attention_back_kernel(
@@ -1330,8 +1370,7 @@
     norm_ref,
     gain_grads_ref,
     mine,
-    seq_parts,
-    near_parts,
+    plane_parts,
     far_parts,
     local_sem,
     send_sems,
@@ -1345,7 +1384,10 @@
     far_size = far_parts.shape[0]
     seqs = ({"seq": diagonal}, {"seq": across}, {"seq": core})
     fars = [{"far": (f + k) % far_size} for k in range(1, far_size)]
-    meet(*seqs, {"near": beside}, *fars)
+    plane = [
+        {"seq": seq, "near": near} for near in (beside, n) for seq in (diagonal, across, core, s)
+    ][:-1]
+    meet(*plane, *fars)
     copies, send = sender(send_sems, recv_sems)
     for k, seq in enumerate((diagonal, across, core)):
         send(("w", k), p_ref.at[seq], mine.at[s], seqs[k])
@@ -1375,16 +1417,16 @@
     gain_grads_ref[:, 1:2] = terms_ref[...]
     total = jnp.sum(rows) + square_ref[0, 0]
 
-    seq_parts[s] = jnp.full(seq_parts.shape[1:], total, jnp.float32)
-    for k in range(3):
-        send(("s", k), seq_parts.at[s], seq_parts.at[s], seqs[k])
+    plane_parts[s, n] = jnp.full(plane_parts.shape[2:], total, jnp.float32)
+    for k, device in enumerate(plane):
+        send(("s", k), plane_parts.at[s, n], plane_parts.at[s, n], device)
     head_ref[...] = mine[...]
-    for k in range(3):
+    for k in range(7):
         copies["s", k].wait_recv()
-    near_parts[n] = (seq_parts[0] + seq_parts[1]) + (seq_parts[2] + seq_parts[3])
-    send("n", near_parts.at[n], near_parts.at[n], {"near": beside})
-    copies["n"].wait_recv()
-    far_parts[f] = near_parts[0] + near_parts[1]
+    everywhere = 0.0
+    for seq in range(4):
+        everywhere = everywhere + (plane_parts[seq, 0] + plane_parts[seq, 1])
+    far_parts[f] = everywhere
     far_copies = [
         pltpu.make_async_remote_copy(
             src_ref=far_parts.at[f],
@@ -1422,12 +1464,11 @@
         out_specs=[IN_VMEM] * 3,
         scratch_shapes=[
             pltpu.VMEM(p.shape, p.dtype),
-            pltpu.VMEM((4, *tile), jnp.float32),
-            pltpu.VMEM((2, *tile), jnp.float32),
+            pltpu.VMEM((4, 2, *tile), jnp.float32),
             pltpu.VMEM((far, *tile), jnp.float32),
             pltpu.SemaphoreType.DMA,
-            pltpu.SemaphoreType.DMA((7,)),
-            pltpu.SemaphoreType.DMA((7,)),
+            pltpu.SemaphoreType.DMA((10,)),
+            pltpu.SemaphoreType.DMA((10,)),
             pltpu.SemaphoreType.DMA((far - 1,)),
             pltpu.SemaphoreType.DMA((far - 1,)),
         ],
@@ -1437,15 +1478,154 @@
     )(square, terms, qkv, gains, p)
 
 
-def adam_kernel(norm_ref, zero_ref, one_ref, head_ref, gain_grads_ref, *refs):
-    weights, firsts, seconds = refs[0:5], refs[5:10], refs[10:15]
-    weights_out, firsts_out, seconds_out = refs[15:20], refs[20:25], refs[25:30]
+def prepare_kernel(
+    gains_ref,
+    qkv_ref,
+    out_ref,
+    gateup_ref,
+    down_ref,
+    x_ref,
+    d_ref,
+    first_ref,
+    second_ref,
+    heads_ref,
+    unit_ref,
+    low_ref,
+    gateup,
+    down,
+    qkv,
+    out,
+    x,
+    d,
+    first,
+    second,
+    heads,
+    unit,
+    low,
+    load_sems,
+    store_sems,
+    send_sems,
+    recv_sems,
+):
+    s, n, core, across, beside = places()
+    mine = s * 2 + n
+    others = [(seq, near) for near in (beside, n) for seq in ((core + 2) % 4, across, core, s)][:-1]
+    rows = out.shape[0]
+    part = first.shape[2] // 3
+    units = 8 * part
+    half = jnp.bfloat16
+
+    def load(at, source, target):
+        copy = pltpu.make_async_copy(source, target, load_sems.at[at])
+        copy.start()
+        return copy
+
+    loads = []
+    for c in range(2):
+        for u in range(2):
+            columns = pl.ds((2 * u + c) * units, units)
+            loads.append(load(3 * c + u, gateup_ref.at[:, columns], gateup.at[:, columns]))
+        columns = pl.ds(c * units, units)
+        loads.append(load(3 * c + 2, down_ref.at[:, columns], down.at[:, columns]))
+    loads.append(load(6, qkv_ref, qkv))
+    loads.append(load(7, out_ref, out))
+    loads.append(load(8, x_ref, x))
+    loads.append(load(9, d_ref, d))
+    gains = gains_ref[...].astype(half).astype(jnp.float32)
+    one, two = gains[:, 0:1], gains[:, 1:2]
+
+    def rounded(weight, gain=None):
+        weight = weight.astype(half)
+        return weight if gain is None else (weight.astype(jnp.float32) * gain).astype(half)
+
+    def pieces(c, target):
+        for copy in loads[3 * c : 3 * c + 3]:
+            copy.wait()
+        for p in range(8):
+            start = c * units + p * part
+            for u in range(2):
+                at = slice(2 * u * units + start, 2 * u * units + start + part)
+                target[p, :, u * part : (u + 1) * part] = rounded(gateup[:, at], two)
+            target[p, :, 2 * part :] = rounded(down[:, start : start + part])
+
+    def store(at, source, target):
+        copy = pltpu.make_async_copy(source, target, store_sems.at[at])
+        copy.start()
+        return copy
+
+    meet(*[{"seq": seq, "near": near} for seq, near in others])
+    pieces(0, first)
+    copies, send = sender(send_sems, recv_sems)
+    for k, (seq, near) in enumerate(others):
+        send(k, first.at[seq * 2 + near], first_ref.at[mine], {"seq": seq, "near": near})
+    stores = [store(0, first.at[mine], first_ref.at[mine])]
+
+    pieces(1, second)
+    stores.append(store(1, second, second_ref))
+    loads[6].wait()
+    loads[7].wait()
+    qkv_pieces, out_pieces = head_pieces_of(heads.shape[2])
+    for p, at, column, size in qkv_pieces:
+        heads[p, :, at : at + size] = rounded(qkv[:, column : column + size], one)
+    for p, at, column, size in out_pieces:
+        heads[p, :, at : at + size] = rounded(out[:, column : column + size])
+    stores.append(store(2, heads, heads_ref))
+    loads[8].wait()
+    loads[9].wait()
+
+    def tokens(i, carry):
+        at = pl.ds(pl.multiple_of(i * 16, 16), 16)
+        unit[at, :] = rms_normalize(x[at, :])[0].astype(half)
+        low[at, :] = d[at, :].astype(half)
+        return carry
+
+    lax.fori_loop(0, x.shape[0] // 16, tokens, 0)
+    stores.append(store(3, unit, unit_ref))
+    stores.append(store(4, low, low_ref))
+    for copy in stores:
+        copy.wait()
+    for copy in copies.values():
+        copy.wait_recv()
+    for copy in copies.values():
+        copy.wait_send()
+
+
+def prepare(gains, qkv, out, gateup, down, x, d, collective_id):
+    rows = gains.shape[0]
+    tokens, width = x.shape
+    low = jnp.bfloat16
+    part = FEED_UNITS // 16
+    columns = (qkv.shape[1] + out.shape[1]) // 4
+    f32 = [(gateup.shape, jnp.float32), (down.shape, jnp.float32), (qkv.shape, jnp.float32), (out.shape, jnp.float32)]
+    f32 += [(x.shape, jnp.float32), (d.shape, jnp.float32)]
+    results = [((8, rows, 3 * part), low)] * 2 + [((4, rows, columns), low)] + [((tokens, width), low)] * 2
+    return pl.pallas_call(
+        prepare_kernel,
+        out_shape=[jax.ShapeDtypeStruct(*result) for result in results],
+        in_specs=[IN_VMEM] + [ANYWHERE] * 6,
+        out_specs=[ANYWHERE] * 5,
+        scratch_shapes=[pltpu.VMEM(*array) for array in f32 + results]
+        + [
+            pltpu.SemaphoreType.DMA((10,)),
+            pltpu.SemaphoreType.DMA((5,)),
+            pltpu.SemaphoreType.DMA((7,)),
+            pltpu.SemaphoreType.DMA((7,)),
+        ],
+        compiler_params=pltpu.CompilerParams(
+            collective_id=collective_id, has_side_effects=True, vmem_limit_bytes=VMEM_LIMIT
+        ),
+    )(gains, qkv, out, gateup, down, x, d)
+
+
+def adam_kernel(norm_ref, gains_ref, zero_ref, one_ref, head_ref, *refs):
+    weights, firsts, seconds = refs[0:4], refs[4:8], refs[8:12]
+    weights_out, firsts_out, seconds_out = refs[12:16], refs[16:20], refs[20:24]
     halves = (zero_ref, one_ref)
     part = zero_ref.shape[2] // 3
     gateup, down = feed_pieces(part)
     qkv, out = head_pieces_of(head_ref.shape[2])
     clip = CLIP_NORM / jnp.maximum(norm_ref[0:1, 0:1], CLIP_NORM)
-    gains = weights[4][...].astype(jnp.bfloat16).astype(jnp.float32) * clip
+    gains = gains_ref[...].astype(jnp.bfloat16).astype(jnp.float32) * clip
     one, two = gains[:, 0:1], gains[:, 1:2]
 
     def step(which, columns, grad, rate, decay):
@@ -1464,15 +1644,14 @@
         for half, device, at, column in pieces:
             grad = halves[half][device, :, at : at + part].astype(jnp.float32) * scale
             step(which, slice(column, column + part), grad, RATE_MATRIX, DECAY_MATRIX)
-    step(4, slice(0, 2), gain_grads_ref[...] * clip, RATE_GAIN, 0.0)
-
-
-def adam(norm, zero, one, head, gain_grads, weights, firsts, seconds):
+
+
+def adam(norm, gains, zero, one, head, weights, firsts, seconds):
     state = (*weights, *firsts, *seconds)
-    arrays = (zero, one, head, gain_grads, *state)
+    arrays = (gains, zero, one, head, *state)
     return pl.pallas_call(
         adam_kernel,
-        grid=(gain_grads.shape[0] // ROWS,),
+        grid=(gains.shape[0] // ROWS,),
         out_shape=[jax.ShapeDtypeStruct(x.shape, x.dtype) for x in state],
         in_specs=[pl.BlockSpec(norm.shape, lambda r: (0, 0))] + [rows_of(x) for x in arrays],
         out_specs=[rows_of(x) for x in state],
@@ -1512,64 +1691,33 @@
     far = lax.axis_size("far")
     group = seq * 2
     rows = out_weight.shape[0]
-    query_width = QUERY_HEAD_COUNT * HEAD_SIZE
-    key_width = KEY_VALUE_HEADS * HEAD_SIZE
-    mine_q, mine_k = query_width // seq, key_width // seq
     units = FEED_UNITS // group
     part = units // 2
-    low = jnp.bfloat16
 
     inputs = inputs[0]
     cotangent = cotangent[0]
-    gains = norm_gains.astype(low).astype(jnp.float32)
-    gain_one, gain_two = gains[:, :1], gains[:, 1:]
 
     def after(x, *others):
         return lax.optimization_barrier((x, *others))[0]
 
-    def rounded(weight, gain=None):
-        weight = weight.astype(low)
-        return weight if gain is None else (weight.astype(jnp.float32) * gain).astype(low)
-
     by_far = (far, seq, 2 * rows, 3 * part)
 
-    def feed_piece(half):
-        start, size = half * FEED_UNITS // 2, FEED_UNITS // 2
-        columns = [
-            rounded(gateup_weight[:, start : start + size], gain_two),
-            rounded(gateup_weight[:, FEED_UNITS + start : FEED_UNITS + start + size], gain_two),
-            rounded(down_weight[:, start : start + size]),
-        ]
-        columns = [x.reshape(rows, group, part).transpose(1, 0, 2) for x in columns]
-        return jnp.concatenate(columns, 2)
-
-    (piece,) = exchange_plane([feed_piece(0).reshape(group * rows, 3 * part)], 1)
-    feed_zero = lax.all_gather(piece, "far", axis=0, tiled=True).reshape(by_far)
-
-    qkv_low = rounded(query_key_value_weight, gain_one)
-    head_pieces = jnp.concatenate(
-        [
-            qkv_low[:, :query_width].reshape(rows, seq, mine_q),
-            qkv_low[:, query_width : query_width + key_width].reshape(rows, seq, mine_k),
-            qkv_low[:, query_width + key_width :].reshape(rows, seq, mine_k),
-            rounded(out_weight).reshape(rows, seq, mine_q),
-        ],
-        2,
-    ).transpose(1, 0, 2)
-    unit_one, scale_one = rms_normalize(inputs)
     turns = rotary_tables(positions.reshape(-1), HEAD_SIZE)
-    dout_here = cotangent.astype(low)
-    head_pieces = after(head_pieces, piece)
+    piece, second_pieces, head_pieces, unit_one, dout_here = prepare(
+        norm_gains, query_key_value_weight, out_weight, gateup_weight, down_weight, inputs, cotangent, 1
+    )
+    feed_zero = lax.all_gather(piece.reshape(group * rows, -1), "far", axis=0, tiled=True)
+    feed_zero = feed_zero.reshape(by_far)
+
     head_w, normed_one, all_turns, dout, piece = gather_heads(
-        head_pieces, unit_one.astype(low), turns, dout_here, feed_piece(1), 2
+        head_pieces, unit_one, turns, dout_here, second_pieces, 2
     )
     feed_one = lax.all_gather(piece.reshape(group * rows, -1), "far", axis=0, tiled=True)
     feed_one = feed_one.reshape(by_far)
+
     all_turns = all_turns.reshape(-1, HEAD_SIZE)
-    *saved, attended = attention(lengths, normed_one, head_w, all_turns)
-    hidden = inputs + scatter_seq(attended, 3)
-    unit_two, _ = rms_normalize(hidden)
-    normed_two, act, dgateup, *sums = feed_first(unit_two.astype(low), dout, feed_zero, 4)
+    *saved, hidden, unit_two = attention(lengths, normed_one, head_w, all_turns, inputs, 3)
+    normed_two, act, dgateup, *sums = feed_first(unit_two, dout, feed_zero, 4)
     terms = feed_grads(normed_two, dout, dgateup, act, far).reshape(width, 3 * part)
     grads_zero = lax.psum_scatter(terms, "far", scatter_dimension=0, tiled=True)
     act, dgateup, output_terms, dnormed_two = feed_second(
@@ -1588,7 +1736,7 @@
     head_terms = lax.psum_scatter(
         head_terms.reshape(far * seq * rows, -1), "far", scatter_dimension=0, tiled=True
     )
-    input_grad = dhidden + norm_backward(dnormed_one, unit_one, scale_one)
+    input_grad = dhidden + norm_backward(dnormed_one, *rms_normalize(inputs))
     layer_output = hidden + output_terms
 
     halves = [x.reshape(group, rows, 3 * part) for x in exchange_plane([grads_zero, grads_one], 7)]
@@ -1597,11 +1745,15 @@
     head_grads, norm, gain_grads = settle(
         square, gain_terms, query_key_value_weight, norm_gains, head_terms.reshape(seq, rows, -1), 8
     )
-    weights = (query_key_value_weight, out_weight, gateup_weight, down_weight, norm_gains)
-    firsts = (query_key_value_moment, output_weight_moment, gate_up_moment, down_weight_moment, norm_gains_moment)
-    seconds = (query_key_value_variance, out_second, gateup_second, down_second, gains_second)
-    stepped = adam(norm, *halves, head_grads, gain_grads, weights, firsts, seconds)
-    return (layer_output[None], input_grad[None], norm[0, 0], *stepped)
+    weights = (query_key_value_weight, out_weight, gateup_weight, down_weight)
+    firsts = (query_key_value_moment, output_weight_moment, gate_up_moment, down_weight_moment)
+    seconds = (query_key_value_variance, out_second, gateup_second, down_second)
+    stepped = adam(norm, norm_gains, *halves, head_grads, weights, firsts, seconds)
+    grad_norm = norm[0, 0]
+    gain_grads = gain_grads * (CLIP_NORM / jnp.maximum(grad_norm, CLIP_NORM))
+    gains = adam_step(norm_gains, gain_grads, norm_gains_moment, gains_second, RATE_GAIN, 0.0)
+    state = [x for k in range(3) for x in (*stepped[4 * k : 4 * k + 4], gains[k])]
+    return (layer_output[None], input_grad[None], grad_norm, *state)
 
 
 def solution(mesh):

time: 677 us -> 663 us (0.979)
  other arithmetic: 20.6 us -> 7.77 us
    pallas_call x2 -> x1, Pallas kernels: 60.6 us -> 37.7 us  [exchange_plane(): pl.pallas_call(functools.partial(exchange_plane_kernel, count), out_shape...]
    pallas_call x3, Pallas kernels: 65.3 us -> 83.9 us  [the longest x1 42.5 us: attention(): pl.pallas_call(attention_kernel, out_shape=[jax.ShapeDtypeStruct(*result)...]
  transfers between devices with their start and end apart: 5 -> 5, of which waited for: 2 -> 3; matrix products, arithmetic and copies ran while one was open for 3% -> 1% of each run, Pallas kernels for 78% -> 80%
where the time goes in v6:
time: 663 us; the launch traced here: 659 us
  Pallas kernels  594 us (90%)
  waiting for transfers between devices  32.5 us (5%)
  between operations  15.6 us (2%)
  local copies, waits for them, and re-layouts  8.84 us (1%)
  other arithmetic  7.77 us (1%)
    pallas_call x1, Pallas kernels, gather_heads(): pl.pallas_call(functools.partial(gather_heads_kernel, far_size), out_shap...  171 us
    pallas_call x1, Pallas kernels, attention_back(): pl.pallas_call(attention_back_kernel, out_shape=[jax.ShapeDtypeStruct((fa...  116 us
    pallas_call x1, Pallas kernels, feed_first(): pl.pallas_call(feed_first_kernel, out_shape=[jax.ShapeDtypeStruct((tokens...  50.1 us
    pallas_call x1, Pallas kernels, feed_back(): pl.pallas_call(feed_back_kernel, out_shape=[jax.ShapeDtypeStruct((far, 4,...  49.5 us
    pallas_call x1, Pallas kernels, attention(): pl.pallas_call(attention_kernel, out_shape=[jax.ShapeDtypeStruct(*result)...  42.5 us
    pallas_call x1, Pallas kernels, exchange_plane(): pl.pallas_call(functools.partial(exchange_plane_kernel, count), out_shape...  37.7 us
    pallas_call x1, Pallas kernels, feed_second(): pl.pallas_call(feed_second_kernel, grid=(tokens // tile,), out_shape=[jax...  37.7 us
    reduce_scatter x1, waiting for transfers between devices, shards(): grads_zero = lax.psum_scatter(terms, 'far', scatter_dimension=0, tiled=True)  24.1 us
  transfers between devices with their start and end apart: 5, of which 3 were waited for; matrix products, arithmetic and copies ran while one was open for 1% of the time, Pallas kernels for 80%

profile of v6, /device:TPU:0, one launch (start us, length us, event | category | flops | bytes accessed | tf_op | source)
XLA Modules:
  0.0 659.4 jit_solution(17382124700259486935)
XLA Ops:
  7.2 1.4 copy.53.gains_ref
  8.6 23.8 %shard_map.322 = (bf16[8,64,1536]{2,1,0:T(8,128)(2,1)}, bf16[8,64,1536]{2,1,0:T(8,128)(2,1)}, bf16[4,64,1536]{2,1,0:T(8,128)(2,1)}, bf16[256,2048]{1,0:T(8,128)(2,1)}, bf16[256,2048]{1,0:T(8,128)(2,1)}) custom-call(f32[64,2]{1,0:T(8,128)} %copy.53.gains_ref, f32[64,4096]{1,0:T(8,128)} %refs_0_.1, f32[64,2048]{1,0:T(8,128)} %refs_1_.1, f32[64,16384]{1,0:T(8,128)} %refs_2_.1, ...), custom_call_target="tpu_custom_call" | custom-call | tf_op jit(solution)/shard_map/pallas_call | solution.py:1602
  33.1 0.7 pad_maximum_fusion.i_ref
  33.8 171.1 %shard_map.323 = (bf16[4,4,2,64,1536]{4,3,2,1,0:T(8,128)(2,1)}, bf16[4,256,2048]{2,1,0:T(8,128)(2,1)}, f32[4,256,256]{2,1,0:T(8,128)}, bf16[8,256,2048]{2,1,0:T(8,128)(2,1)}, bf16[8,64,1536]{2,1,0:T(8,128)(2,1)}) custom-call(bf16[4,64,1536]{2,1,0:T(8,128)(2,1)} %get-tuple-element.73.w_ref, bf16[256,2048]{1,0:T(8,128)(2,1)} %get-tuple-element.74.x_ref, ...), custom_call_target="tpu_custom_call" | custom-call | tf_op jit(solution)/shard_map/pallas_call | solution.py:315
  205.9 42.5 %shard_map.324 = (bf16[1024,512]{1,0:T(8,128)(2,1)}, bf16[1024,256]{1,0:T(8,128)(2,1)}, bf16[1024,256]{1,0:T(8,128)(2,1)}, bf16[1024,512]{1,0:T(8,128)(2,1)}, f3...) custom-call(s32[1]{0:T(128)S(6)} %copy.67.length_ref, bf16[1024,2048]{1,0:T(8,128)(2,1)} %bitcast.48, ...), custom_call_target="tpu_custom_call" | custom-call | flops 10000000000 | bytes 20000000 | tf_op jit(solution)/shard_map/pallas_call | solution.py:499
  248.5 50.1 %shard_map.325 = (bf16[2048,2048]{1,0:T(8,128)(2,1)}, bf16[2048,512]{1,0:T(8,128)(2,1)}, bf16[2048,1024]{1,0:T(8,128)(2,1)}, bf16[2048,2048]{1,0:T(8,128)(2,1)}, bf16[2048,2048]{1,0:T(8,128)(2,1)}) custom-call(bf16[256,2048]{1,0:T(8,128)(2,1)} %get-tuple-element.86.x_ref, bf16[2048,2048]{1,0:T(8,128)(2,1)} %bitcast.40, bf16[4,4,128,1536]{3,2,1,0:T(8,128)(2,1)} %bitcast.46), custom_call_target="tpu_custom_call" | custom-call | flops 25769803776 | bytes 60000000 | tf_op jit(solution)/shard_map/pallas_call | solution.py:989
  298.6 19.1 %shard_map.326 = bf16[4,4,128,1536]{3,2,1,0:T(8,128)(2,1)} custom-call(bf16[2048,2048]{1,0:T(8,128)(2,1)} %get-tuple-element.89.x_ref, bf16[2048,2048]{1,0:T(8,128)(2,1)} %bitcast.41, bf16[2048,1024]{1,0:T(8,128)(2,1)} %get-tuple-element.93.dgu_ref, bf16[2048,512]{1,0:T(8,128)(2,1)} %get-tuple-element.94.act_ref), custom_call_target="tpu_custom_call" | custom-call | flops 12884901888 | bytes 40000000 | tf_op jit(solution)/shard_map/pallas_call | solution.py:1080
  318.3 0.9 all-gather.5.cloned.1.call-done
  319.2 37.7 %shard_map.327 = (bf16[2048,512]{1,0:T(8,128)(2,1)}, bf16[2048,1024]{1,0:T(8,128)(2,1)}, bf16[2048,2048]{1,0:T(8,128)(2,1)}, bf16[2048,2048]{1,0:T(8,128)(2,1)}) custom-call(bf16[2048,2048]{1,0:T(8,128)(2,1)} %get-tuple-element.89.x_ref, bf16[2048,2048]{1,0:T(8,128)(2,1)} %bitcast.42, bf16[2048,2048]{1,0:T(8,128)(2,1)} %get-tuple-element.90.y0_ref, ...), custom_call_target="tpu_custom_call" | custom-call | flops 25769803776 | bytes 60000000 | tf_op jit(solution)/shard_map/pallas_call | solution.py:1048
  356.9 49.5 %shard_map.328 = (bf16[4,4,128,1536]{3,2,1,0:T(8,128)(2,1)}, f32[256,2048]{1,0:T(8,128)}, bf16[256,2048]{1,0:T(8,128)(2,1)}) custom-call(f32[256,2048]{1,0:T(8,128)} %get-tuple-element.80.hidden_ref, f32[256,2048]{1,0:T(8,128)} %bitcast.35, bf16[2048,1024]{1,0:T(8,128)(2,1)} %get-tuple-element.96.dgu_ref, bf16[2048,512]{1,0:T(8,128)(2,1)} %get-tuple-element.97.act_ref, ...), custom_call_target="tpu_custom_call" | custom-call | flops 12884901888 | bytes 60000000 | tf_op jit(solution)/shard_map/pallas_call | solution.py:1224
  406.4 24.1 %reduce-scatter.4.cloned.1.call-done.refs_0_ = bf16[512,1536]{1,0:T(8,128)(2,1)} async-done(((bf16[2048,1536]{1,0:T(8,128)(2,1)}), bf16[512,1536]{1,0:T(8,128)(2,1)}) %reduce-scatter.4.cloned.1.call-update) | async-done | bytes 1572880 | tf_op jit(solution)/shard_map/reduce_scatter | solution.py:1722
  430.6 116.1 %shard_map.329 = (bf16[4,4,64,1536]{3,2,1,0:T(8,128)(2,1)}, f32[256,2048]{1,0:T(8,128)}, f32[256,2048]{1,0:T(8,128)}) custom-call(s32[1]{0:T(128)S(6)} %copy.67.length_ref, bf16[1024,512]{1,0:T(8,128)(2,1)} %get-tuple-element.81.q_ref, bf16[1024,256]{1,0:T(8,128)(2,1)} %get-tuple-element.82.k_ref, bf16[1024,256]{1,0:T(8,128)(2,1)} %get-tuple-element.83.v_ref, ...), custom_call_target="tpu_custom_call" | custom-call | flops 20000000000 | bytes 40000000 | tf_op jit(solution)/shard_map/pallas_call | solution.py:733
  547.6 0.7 copy-done
  548.6 1.4 copy-done.2
  549.9 3.4 add.38
  553.7 1.2 copy-done.3
  554.9 1.8 multiply_add_fusion
  556.6 37.7 %shard_map.330 = (bf16[512,1536]{1,0:T(8,128)(2,1)}, bf16[512,1536]{1,0:T(8,128)(2,1)}) custom-call(bf16[512,1536]{1,0:T(8,128)(2,1)} %reduce-scatter.4.cloned.1.call-done.refs_0_, bf16[512,1536]{1,0:T(8,128)(2,1)} %reduce-scatter.6.cloned.1.call-done.refs_1_), custom_call_target="tpu_custom_call" | custom-call | tf_op jit(solution)/shard_map/pallas_call | solution.py:114
  594.4 5.2 shard_map.331
  599.6 7.4 %reduce-scatter.8.cloned.1.call-done = bf16[256,1536]{1,0:T(8,128)(2,1)} async-done(((bf16[1024,1536]{1,0:T(8,128)(2,1)}), bf16[256,1536]{1,0:T(8,128)(2,1)}) %reduce-scatter.8.cloned.1.call-update) | async-done | bytes 786448 | tf_op jit(solution)/shard_map/reduce_scatter | solution.py:1736
  607.0 23.3 %shard_map.332 = (bf16[4,64,1536]{2,1,0:T(8,128)(2,1)}, f32[8,128]{1,0:T(8,128)}, f32[64,2]{1,0:T(8,128)}) custom-call(f32[1,1]{1,0:T(1,128)} %get-tuple-element.108.square_ref, f32[64,1]{1,0:T(8,128)} %get-tuple-element.109.terms_ref, f32[64,4096]{1,0:T(8,128)} %refs_0_.1, f32[64,2]{1,0:T(8,128)} %copy.53.gains_ref, bf16[4,64,1536]{2,1,0:T(8,128)(2,1)} %bitcast.38), custom_call_target="tpu_custom_call" | custom-call | tf_op jit(solution)/shard_map/pallas_call | solution.py:1456
  630.2 1.2 slice.3
  632.1 0.8 sqrt_add_fusion
  635.1 17.5 %shard_map.333 = (f32[64,4096]{1,0:T(8,128)}, f32[64,2048]{1,0:T(8,128)}, f32[64,16384]{1,0:T(8,128)}, f32[64,8192]{1,0:T(8,128)}, f32[64,4096]{1,0:T(8,128)}, /...) custom-call(f32[8,128]{1,0:T(8,128)} %get-tuple-element.113.norm_ref, ...), custom_call_target="tpu_custom_call" | custom-call | tf_op jit(solution)/shard_map/pallas_call | solution.py:1652
  (46 shorter events, 5.1 us)
Async XLA Ops:
  7.2 241.3 %all-gather.3.cloned.1.call-start = ((), (), s32[]{:S(2)}) async-start(), calls=%async_computation.3 | async-start | bytes 7864320 | tf_op jit(solution)/shard_map/all_gather | solution.py:1709
  8.6 23.9 %copy-start.6 = (s32[1,256]{1,0:T(1,128)S(1)}, s32[1,256]{1,0:T(1,128)}, u32[]{:S(2)}) copy-start(s32[1,256]{1,0:T(1,128)} %param.22) | copy-start | bytes 3076
  32.5 286.7 %all-gather.5.cloned.1.call-start = ((), (), s32[]{:S(2)}) async-start(), calls=%async_computation.4 | async-start | bytes 7864320 | tf_op jit(solution)/shard_map/all_gather | solution.py:1715
  205.0 225.5 %reduce-scatter.4.cloned.1.call-start = ((), (), s32[]{:S(2)}) async-start(), calls=%async_computation.5 | async-start | bytes 7864320 | tf_op jit(solution)/shard_map/reduce_scatter | solution.py:1722
  317.8 229.0 %reduce-scatter.6.cloned.1.call-start = ((), (), s32[]{:S(2)}) async-start(), calls=%async_computation.6 | async-start | bytes 7864320 | tf_op jit(solution)/shard_map/reduce_scatter | solution.py:1730
  430.5 176.4 %reduce-scatter.8.cloned.1.call-start = ((), (), s32[]{:S(2)}) async-start(), calls=%async_computation.7 | async-start | bytes 3932160 | tf_op jit(solution)/shard_map/reduce_scatter | solution.py:1736
  546.7 0.7 copy-start.7
  546.7 0.8 copy-start.8
  546.7 1.6 copy-start
  548.3 1.6 copy-start.2
  549.9 3.4 copy-start.1
  553.3 1.6 copy-start.3
  599.6 33.5 %copy-start.5 = (f32[64,2]{0,1:T(2,128)S(1)}, f32[64,2]{0,1:T(2,128)}, u32[]{:S(2)}) copy-start(f32[64,2]{0,1:T(2,128)} %param.27) | copy-start | bytes 1540
  599.6 33.6 %copy-start.4 = (f32[64,2]{1,0:T(8,128)S(1)}, f32[64,2]{1,0:T(8,128)}, u32[]{:S(2)}) copy-start(f32[64,2]{1,0:T(8,128)} %copy.53.gains_ref) | copy-start | bytes 1540
Sparse Core Ops, SparseCore 0:
  32.6 157.5 all-gather.2
  205.1 114.0 all-gather.4
  321.5 108.9 reduce-scatter.3
  432.7 111.2 reduce-scatter.5
  546.9 59.9 reduce-scatter.7

commit v7 on v6

--- a/solution.py
+++ b/solution.py
@@ -125,7 +125,42 @@
     )(*arrays)
 
 
-def gather_heads_kernel(
+def groups_of(w_ref, far_size, base, send_sems, recv_sems):
+    _, n, _, _, beside = places()
+    f = lax.axis_index("far")
+    right, left = {"far": (f + 1) % far_size}, {"far": (f + far_size - 1) % far_size}
+    to_x = {"near": beside}
+
+    def along(far, p, device, sem):
+        piece = w_ref.at[p, far, n]
+        return pltpu.make_async_remote_copy(
+            src_ref=piece,
+            dst_ref=piece,
+            send_sem=send_sems.at[base + 4 * sem + p],
+            recv_sem=recv_sems.at[base + 4 * sem + p],
+            device_id=device,
+            device_id_type=MESH_IDS,
+        )
+
+    def to_right(k, p):
+        return along((f + far_size - k) % far_size, p, right, k)
+
+    def to_left(k, p):
+        return along((f + k) % far_size, p, left, far_size + k)
+
+    def x_from_left(k, p):
+        return along((f + far_size - k) % far_size, p, to_x, 2 * far_size + k)
+
+    def x_from_right(k, p):
+        return along((f + k) % far_size, p, to_x, 3 * far_size + k)
+
+    return to_right, to_left, x_from_left, x_from_right
+
+
+NEAR_STEPS = 2
+
+
+def gather_tokens_kernel(
     far_size,
     w_ref,
     x_ref,
@@ -142,28 +177,43 @@
     recv_sems,
 ):
     s, n, core, across, beside = places()
-    diagonal = (core + 2) % 4
     f = lax.axis_index("far")
     half = x_ref.shape[0] // 2
     to_core, to_y, to_x = {"seq": core}, {"seq": across}, {"near": beside}
-    right, left = {"far": (f + 1) % far_size}, {"far": (f + far_size - 1) % far_size}
-
-    others = [(seq, near) for near in (beside, n) for seq in (diagonal, across, core, s)][:-1]
-    meet(*[{"seq": seq, "near": near} for seq, near in others], right, left)
+    others = [(seq, near) for near in (beside, n) for seq in ((core + 2) % 4, across, core, s)][:-1]
+
+    meet(*[{"seq": seq, "near": near} for seq, near in others])
     copies, send = sender(send_sems, recv_sems)
-    keep = pltpu.make_async_copy(w_ref.at[s], o_ref.at[s, f, n], local_sems.at[0])
-    keep.start()
-    keep_x = pltpu.make_async_copy(x_ref, ox_ref.at[s], local_sems.at[1])
-    keep_x.start()
-    keep_i = pltpu.make_async_copy(i_ref, oi_ref.at[s], local_sems.at[2])
-    keep_i.start()
-    for k, seq in enumerate((diagonal, across, core)):
-        send(("w", k), w_ref.at[seq], o_ref.at[s, f, n], {"seq": seq})
-        send(("i", k), i_ref, oi_ref.at[s], {"seq": seq})
+
+    def local(source, target, at):
+        copy = pltpu.make_async_copy(source, target, local_sems.at[at])
+        copy.start()
+        return copy
+
+    _, _, x_from_left, x_from_right = groups_of(o_ref, far_size, 30, send_sems, recv_sems)
+    for k in range(NEAR_STEPS, far_size):
+        for p in range(4):
+
+            @pl.when(f >= k)
+            def _():
+                x_from_left(k, p).start()
+
+            @pl.when(f + k < far_size)
+            def _():
+                x_from_right(k, p).start()
+
+    keeps = [
+        local(x_ref, ox_ref.at[s], 0),
+        local(i_ref, oi_ref.at[s], 1),
+        local(d_ref, od_ref.at[s * 2 + n], 2),
+        local(e_ref.at[s * 2 + n], oe_ref.at[s * 2 + n], 3),
+    ]
     for p in range(2):
         at = pl.ds(p * half, half)
         send(("y", p), x_ref.at[at], ox_ref.at[s, at], to_y)
         send(("c", p), x_ref.at[at], ox_ref.at[s, at], to_core)
+    for k, seq in enumerate(((core + 2) % 4, across, core)):
+        send(("i", k), i_ref, oi_ref.at[s], {"seq": seq})
 
     def block(seq, near, p):
         return od_ref.at[seq * 2 + near, pl.ds(p * half, half)]
@@ -171,98 +221,28 @@
     def own(p):
         return d_ref.at[pl.ds(p * half, half)]
 
-    keep_d = pltpu.make_async_copy(d_ref, od_ref.at[s * 2 + n], local_sems.at[3])
-    keep_d.start()
     send("y0", own(0), block(s, n, 0), to_y)
     send("x1", own(1), block(s, n, 1), to_x)
     send("y1", own(1), block(s, n, 1), to_y)
     send("x0", own(0), block(s, n, 0), to_x)
     send("c0", own(0), block(s, n, 0), to_core)
     send("c1", own(1), block(s, n, 1), to_core)
-    keep_e = pltpu.make_async_copy(e_ref.at[s * 2 + n], oe_ref.at[s * 2 + n], local_sems.at[4])
-    keep_e.start()
     for k, (seq, near) in enumerate(others):
-        target = {"seq": seq, "near": near}
-        send(("e", k), e_ref.at[seq * 2 + near], oe_ref.at[s * 2 + n], target)
-    keep.wait()
-    for k in range(3):
-        copies["w", k].wait_recv()
-
-    def along(far, p, device, sem):
-        piece = o_ref.at[p, far, n]
-        return pltpu.make_async_remote_copy(
-            src_ref=piece,
-            dst_ref=piece,
-            send_sem=send_sems.at[base + 4 * sem + p],
-            recv_sem=recv_sems.at[base + 4 * sem + p],
-            device_id=device,
-            device_id_type=MESH_IDS,
-        )
-
-    base = 33
-
-    def to_right(k, p):
-        return along((f + far_size - k) % far_size, p, right, k)
-
-    def to_left(k, p):
-        return along((f + k) % far_size, p, left, far_size + k)
-
-    def x_from_left(k, p):
-        return along((f + far_size - k) % far_size, p, to_x, 2 * far_size + k)
-
-    def x_from_right(k, p):
-        return along((f + k) % far_size, p, to_x, 3 * far_size + k)
-
-    for k in range(far_size):
-        for p in range(4):
-            if k > 0:
-
-                @pl.when(f >= k)
-                def _():
-                    to_right(k - 1, p).wait_recv()
-
-            @pl.when((f >= k) & (f < far_size - 1))
-            def _():
-                to_right(k, p).start()
-
-            if k > 0:
-
-                @pl.when(f + k < far_size)
-                def _():
-                    to_left(k - 1, p).wait_recv()
-
-            @pl.when((f + k < far_size) & (f > 0))
-            def _():
-                to_left(k, p).start()
-
-            if k == 0:
-                x_from_left(0, p).start()
-            else:
-
-                @pl.when(f >= k)
-                def _():
-                    x_from_left(k, p).start()
-
-                @pl.when(f + k < far_size)
-                def _():
-                    x_from_right(k, p).start()
-
-        if k == min(1, far_size - 1):
-            for p in range(2):
-                at = pl.ds(p * half, half)
-                copies["y", p].wait_recv()
-                send(("yc", p), ox_ref.at[across, at], ox_ref.at[across, at], to_core)
-        if k == max(far_size - 2, 0):
-            copies["y0"].wait_recv()
-            send("yx", block(across, n, 0), block(across, n, 0), to_x)
-            send("yc0", block(across, n, 0), block(across, n, 0), to_core)
-            copies["x1"].wait_recv()
-            send("xy", block(s, beside, 1), block(s, beside, 1), to_y)
-            send("xc1", block(s, beside, 1), block(s, beside, 1), to_core)
-            copies["y1"].wait_recv()
-            send("yc1", block(across, n, 1), block(across, n, 1), to_core)
-            copies["x0"].wait_recv()
-            send("xc0", block(s, beside, 0), block(s, beside, 0), to_core)
+        send(("e", k), e_ref.at[seq * 2 + near], oe_ref.at[s * 2 + n], {"seq": seq, "near": near})
+    for p in range(2):
+        at = pl.ds(p * half, half)
+        copies["y", p].wait_recv()
+        send(("yc", p), ox_ref.at[across, at], ox_ref.at[across, at], to_core)
+    copies["y0"].wait_recv()
+    send("yx", block(across, n, 0), block(across, n, 0), to_x)
+    send("yc0", block(across, n, 0), block(across, n, 0), to_core)
+    copies["x1"].wait_recv()
+    send("xy", block(s, beside, 1), block(s, beside, 1), to_y)
+    send("xc1", block(s, beside, 1), block(s, beside, 1), to_core)
+    copies["y1"].wait_recv()
+    send("yc1", block(across, n, 1), block(across, n, 1), to_core)
+    copies["x0"].wait_recv()
+    send("xc0", block(s, beside, 0), block(s, beside, 0), to_core)
     copies["yx"].wait_recv()
     send("dc0", block(across, beside, 0), block(across, beside, 0), to_core)
     copies["xy"].wait_recv()
@@ -276,62 +256,45 @@
         copies["i", k].wait_recv()
     for k in range(7):
         copies["e", k].wait_recv()
-    for k in range(far_size):
+    for k in range(NEAR_STEPS, far_size):
         for p in range(4):
-
-            @pl.when((f >= k) & (f < far_size - 1))
-            def _():
-                to_right(k, p).wait_send()
-
-            @pl.when((f + k < far_size) & (f > 0))
-            def _():
-                to_left(k, p).wait_send()
 
             @pl.when(f >= k)
             def _():
                 x_from_left(k, p).wait_recv()
                 x_from_left(k, p).wait_send()
 
-            if k > 0:
-
-                @pl.when(f + k < far_size)
-                def _():
-                    x_from_right(k, p).wait_recv()
-                    x_from_right(k, p).wait_send()
+            @pl.when(f + k < far_size)
+            def _():
+                x_from_right(k, p).wait_recv()
+                x_from_right(k, p).wait_send()
 
     for copy in copies.values():
         copy.wait_send()
-    keep_x.wait()
-    keep_i.wait()
-    keep_d.wait()
-    keep_e.wait()
-
-
-def gather_heads(w, x, i, d, e, collective_id):
-    far_size = lax.axis_size("far")
-    _, rows, columns = w.shape
-    tokens, width = x.shape
-    sems = 33 + 16 * far_size
-    full, all_x, all_i, all_d, mine_e = pl.pallas_call(
-        functools.partial(gather_heads_kernel, far_size),
-        out_shape=[
-            jax.ShapeDtypeStruct((4, far_size, 2, rows, columns), w.dtype),
-            jax.ShapeDtypeStruct((4, tokens, width), x.dtype),
-            jax.ShapeDtypeStruct((4, *i.shape), i.dtype),
-            jax.ShapeDtypeStruct((8, *d.shape), d.dtype),
-            jax.ShapeDtypeStruct(e.shape, e.dtype),
-        ],
+    for copy in keeps:
+        copy.wait()
+
+
+def gather_tokens(w, x, i, d, e, collective_id):
+    far_size = w.shape[1]
+    results = [w.shape, (4, *x.shape), (4, *i.shape), (8, *d.shape), e.shape]
+    arrays = (w, x, i, d, e)
+    sems = 30 + 16 * far_size
+    all_w, all_x, all_i, all_d, mine_e = pl.pallas_call(
+        functools.partial(gather_tokens_kernel, far_size),
+        out_shape=[jax.ShapeDtypeStruct(shape, a.dtype) for shape, a in zip(results, arrays)],
         in_specs=[ANYWHERE] * 5,
         out_specs=[ANYWHERE] * 5,
+        input_output_aliases={0: 0},
         scratch_shapes=[
-            pltpu.SemaphoreType.DMA((5,)),
+            pltpu.SemaphoreType.DMA((4,)),
             pltpu.SemaphoreType.DMA((sems,)),
             pltpu.SemaphoreType.DMA((sems,)),
         ],
         compiler_params=pltpu.CompilerParams(collective_id=collective_id, has_side_effects=True),
-    )(w, x, i, d, e)
-    all_x, all_d = all_x.reshape(-1, width), all_d.reshape(-1, d.shape[1])
-    return full.reshape(-1, columns), all_x, all_i, all_d, mine_e
+    )(*arrays)
+    all_x, all_d = all_x.reshape(-1, x.shape[1]), all_d.reshape(-1, d.shape[1])
+    return all_w.reshape(-1, w.shape[-1]), all_x, all_i, all_d, mine_e
 
 
 def tile_at(tile, rows):
@@ -1508,6 +1471,9 @@
     recv_sems,
 ):
     s, n, core, across, beside = places()
+    f = lax.axis_index("far")
+    far_size = heads_ref.shape[1]
+    ends = [{"far": (f + 1) % far_size}, {"far": (f + far_size - 1) % far_size}]
     mine = s * 2 + n
     others = [(seq, near) for near in (beside, n) for seq in ((core + 2) % 4, across, core, s)][:-1]
     rows = out.shape[0]
@@ -1521,16 +1487,14 @@
         return copy
 
     loads = []
+    load_heads = [load(6, qkv_ref, qkv), load(7, out_ref, out)]
     for c in range(2):
         for u in range(2):
             columns = pl.ds((2 * u + c) * units, units)
             loads.append(load(3 * c + u, gateup_ref.at[:, columns], gateup.at[:, columns]))
         columns = pl.ds(c * units, units)
         loads.append(load(3 * c + 2, down_ref.at[:, columns], down.at[:, columns]))
-    loads.append(load(6, qkv_ref, qkv))
-    loads.append(load(7, out_ref, out))
-    loads.append(load(8, x_ref, x))
-    loads.append(load(9, d_ref, d))
+    load_tokens = [load(8, x_ref, x), load(9, d_ref, d)]
     gains = gains_ref[...].astype(half).astype(jnp.float32)
     one, two = gains[:, 0:1], gains[:, 1:2]
 
@@ -1553,25 +1517,70 @@
         copy.start()
         return copy
 
-    meet(*[{"seq": seq, "near": near} for seq, near in others])
-    pieces(0, first)
-    copies, send = sender(send_sems, recv_sems)
-    for k, (seq, near) in enumerate(others):
-        send(k, first.at[seq * 2 + near], first_ref.at[mine], {"seq": seq, "near": near})
-    stores = [store(0, first.at[mine], first_ref.at[mine])]
-
-    pieces(1, second)
-    stores.append(store(1, second, second_ref))
-    loads[6].wait()
-    loads[7].wait()
+    meet(*[{"seq": seq, "near": near} for seq, near in others], *ends)
+    for copy in load_heads:
+        copy.wait()
     qkv_pieces, out_pieces = head_pieces_of(heads.shape[2])
     for p, at, column, size in qkv_pieces:
         heads[p, :, at : at + size] = rounded(qkv[:, column : column + size], one)
     for p, at, column, size in out_pieces:
         heads[p, :, at : at + size] = rounded(out[:, column : column + size])
-    stores.append(store(2, heads, heads_ref))
-    loads[8].wait()
-    loads[9].wait()
+    copies, send = sender(send_sems, recv_sems)
+    keep = store(2, heads.at[s], heads_ref.at[s, f, n])
+    for seq in (core, across, (core + 2) % 4):
+        send(("w", len(copies)), heads.at[seq], heads_ref.at[s, f, n], {"seq": seq})
+    to_right, to_left, x_from_left, x_from_right = groups_of(heads_ref, far_size, 10, send_sems, recv_sems)
+    order = (s, core, across, (core + 2) % 4)
+
+    def onward(k):
+        for at, p in enumerate(order):
+            if k == 0 and at == 0:
+                keep.wait()
+            elif k == 0:
+                copies["w", at - 1].wait_recv()
+            else:
+
+                @pl.when(f >= k)
+                def _():
+                    to_right(k - 1, p).wait_recv()
+
+            @pl.when((f >= k) & (f < far_size - 1))
+            def _():
+                to_right(k, p).start()
+
+            if k > 0:
+
+                @pl.when(f + k < far_size)
+                def _():
+                    to_left(k - 1, p).wait_recv()
+
+            @pl.when((f + k < far_size) & (f > 0))
+            def _():
+                to_left(k, p).start()
+
+            if k < NEAR_STEPS:
+
+                @pl.when(f >= k)
+                def _():
+                    x_from_left(k, p).start()
+
+                if k > 0:
+
+                    @pl.when(f + k < far_size)
+                    def _():
+                        x_from_right(k, p).start()
+
+    onward(0)
+    pieces(0, first)
+    for k, (seq, near) in enumerate(others):
+        send(k, first.at[seq * 2 + near], first_ref.at[mine], {"seq": seq, "near": near})
+    stores = [store(0, first.at[mine], first_ref.at[mine])]
+    for k in range(1, min(2, far_size)):
+        onward(k)
+    pieces(1, second)
+    stores.append(store(1, second, second_ref))
+    for copy in load_tokens:
+        copy.wait()
 
     def tokens(i, carry):
         at = pl.ds(pl.multiple_of(i * 16, 16), 16)
@@ -1582,12 +1591,38 @@
     lax.fori_loop(0, x.shape[0] // 16, tokens, 0)
     stores.append(store(3, unit, unit_ref))
     stores.append(store(4, low, low_ref))
+    for k in range(2, far_size):
+        onward(k)
     for copy in stores:
         copy.wait()
-    for copy in copies.values():
-        copy.wait_recv()
+    for k in range(7):
+        copies[k].wait_recv()
     for copy in copies.values():
         copy.wait_send()
+    for k in range(far_size):
+        for p in range(4):
+
+            @pl.when((f >= k) & (f < far_size - 1))
+            def _():
+                to_right(k, p).wait_send()
+
+            @pl.when((f + k < far_size) & (f > 0))
+            def _():
+                to_left(k, p).wait_send()
+
+            if k < NEAR_STEPS:
+
+                @pl.when(f >= k)
+                def _():
+                    x_from_left(k, p).wait_recv()
+                    x_from_left(k, p).wait_send()
+
+                if k > 0:
+
+                    @pl.when(f + k < far_size)
+                    def _():
+                        x_from_right(k, p).wait_recv()
+                        x_from_right(k, p).wait_send()
 
 
 def prepare(gains, qkv, out, gateup, down, x, d, collective_id):
@@ -1599,17 +1634,19 @@
     f32 = [(gateup.shape, jnp.float32), (down.shape, jnp.float32), (qkv.shape, jnp.float32), (out.shape, jnp.float32)]
     f32 += [(x.shape, jnp.float32), (d.shape, jnp.float32)]
     results = [((8, rows, 3 * part), low)] * 2 + [((4, rows, columns), low)] + [((tokens, width), low)] * 2
+    far = lax.axis_size("far")
+    outs = results[:2] + [((4, far, 2, rows, columns), low)] + results[3:]
     return pl.pallas_call(
         prepare_kernel,
-        out_shape=[jax.ShapeDtypeStruct(*result) for result in results],
+        out_shape=[jax.ShapeDtypeStruct(*result) for result in outs],
         in_specs=[IN_VMEM] + [ANYWHERE] * 6,
         out_specs=[ANYWHERE] * 5,
         scratch_shapes=[pltpu.VMEM(*array) for array in f32 + results]
         + [
             pltpu.SemaphoreType.DMA((10,)),
             pltpu.SemaphoreType.DMA((5,)),
-            pltpu.SemaphoreType.DMA((7,)),
-            pltpu.SemaphoreType.DMA((7,)),
+            pltpu.SemaphoreType.DMA((10 + 16 * far,)),
+            pltpu.SemaphoreType.DMA((10 + 16 * far,)),
         ],
         compiler_params=pltpu.CompilerParams(
             collective_id=collective_id, has_side_effects=True, vmem_limit_bytes=VMEM_LIMIT
@@ -1703,14 +1740,14 @@
     by_far = (far, seq, 2 * rows, 3 * part)
 
     turns = rotary_tables(positions.reshape(-1), HEAD_SIZE)
-    piece, second_pieces, head_pieces, unit_one, dout_here = prepare(
+    piece, second_pieces, head_w, unit_one, dout_here = prepare(
         norm_gains, query_key_value_weight, out_weight, gateup_weight, down_weight, inputs, cotangent, 1
     )
     feed_zero = lax.all_gather(piece.reshape(group * rows, -1), "far", axis=0, tiled=True)
     feed_zero = feed_zero.reshape(by_far)
 
-    head_w, normed_one, all_turns, dout, piece = gather_heads(
-        head_pieces, unit_one, turns, dout_here, second_pieces, 2
+    head_w, normed_one, all_turns, dout, piece = gather_tokens(
+        head_w, unit_one, turns, dout_here, second_pieces, 2
     )
     feed_one = lax.all_gather(piece.reshape(group * rows, -1), "far", axis=0, tiled=True)
     feed_one = feed_one.reshape(by_far)

time: 663 us -> 659 us (level)
  Pallas kernels: 594 us -> 552 us
  waiting for transfers between devices: 32.5 us -> 69.7 us
    pallas_call x1, Pallas kernels: 171 us -> 92.9 us  [gather_tokens(): pl.pallas_call(functools.partial(gather_tokens_kernel, far_size), out_sha...]
    pallas_call x1, Pallas kernels: 23.8 us -> 61 us  [prepare(): pl.pallas_call(prepare_kernel, out_shape=[jax.ShapeDtypeStruct(*result) f...]
    all_gather x2, waiting for transfers between devices: 0.91 us -> 38.1 us  [shards(): lax.all_gather(piece.reshape(group * rows, -1), 'far', axis=0, tiled=True)]
  transfers between devices with their start and end apart: 5 -> 5, of which waited for: 3 -> 3; matrix products, arithmetic and copies ran while one was open for 1% -> 1% of each run, Pallas kernels for 80% -> 69%
where the time goes in v7:
time: 659 us; the launch traced here: 655 us
  Pallas kernels  552 us (84%)
  waiting for transfers between devices  69.7 us (11%)
  between operations  15.6 us (2%)
  local copies, waits for them, and re-layouts  8.84 us (1%)
  other arithmetic  7.77 us (1%)
    pallas_call x1, Pallas kernels, attention_back(): pl.pallas_call(attention_back_kernel, out_shape=[jax.ShapeDtypeStruct((fa...  116 us
    pallas_call x1, Pallas kernels, gather_tokens(): pl.pallas_call(functools.partial(gather_tokens_kernel, far_size), out_sha...  92.9 us
    pallas_call x1, Pallas kernels, prepare(): pl.pallas_call(prepare_kernel, out_shape=[jax.ShapeDtypeStruct(*result) f...  61 us
    pallas_call x1, Pallas kernels, feed_first(): pl.pallas_call(feed_first_kernel, out_shape=[jax.ShapeDtypeStruct((tokens...  49.9 us
    pallas_call x1, Pallas kernels, feed_back(): pl.pallas_call(feed_back_kernel, out_shape=[jax.ShapeDtypeStruct((far, 4,...  49.5 us
    pallas_call x1, Pallas kernels, attention(): pl.pallas_call(attention_kernel, out_shape=[jax.ShapeDtypeStruct(*result)...  42.4 us
    all_gather x2, waiting for transfers between devices, shards(): lax.all_gather(piece.reshape(group * rows, -1), 'far', axis=0, tiled=True)  38.1 us
    pallas_call x1, Pallas kernels, exchange_plane(): pl.pallas_call(functools.partial(exchange_plane_kernel, count), out_shape...  37.7 us
  transfers between devices with their start and end apart: 5, of which 3 were waited for; matrix products, arithmetic and copies ran while one was open for 1% of the time, Pallas kernels for 69%

profile of v7, /device:TPU:0, one launch (start us, length us, event | category | flops | bytes accessed | tf_op | source)
XLA Modules:
  0.0 655.1 jit_solution(17189691848815105689)
XLA Ops:
  7.2 1.4 copy.54.gains_ref
  8.6 61.0 %shard_map.322 = (bf16[8,64,1536]{2,1,0:T(8,128)(2,1)}, bf16[8,64,1536]{2,1,0:T(8,128)(2,1)}, bf16[4,4,2,64,1536]{4,3,2,1,0:T(8,128)(2,1)}, bf16[256,2048]{1,0:T(8,128)(2,1)}, bf16[256,2048]{1,0:T(8,128)(2,1)}) custom-call(f32[64,2]{1,0:T(8,128)} %copy.54.gains_ref, f32[64,4096]{1,0:T(8,128)} %refs_0_.1, f32[64,2048]{1,0:T(8,128)} %refs_1_.1, ...), custom_call_target="tpu_custom_call" | custom-call | tf_op jit(solution)/shard_map/pallas_call | solution.py:1639
  70.3 0.7 pad_maximum_fusion.i_ref
  71.0 92.9 %shard_map.323 = (bf16[4,4,2,64,1536]{4,3,2,1,0:T(8,128)(2,1)}, bf16[4,256,2048]{2,1,0:T(8,128)(2,1)}, f32[4,256,256]{2,1,0:T(8,128)}, bf16[8,256,2048]{2,1,0:T(8,128)(2,1)}, bf16[8,64,1536]{2,1,0:T(8,128)(2,1)}) custom-call(bf16[4,4,2,64,1536]{4,3,2,1,0:T(8,128)(2,1)} %get-tuple-element.73.w_ref, ...), custom_call_target="tpu_custom_call", output_to_operand_aliasing={{0}: (0, {})} | custom-call | tf_op jit(solution)/shard_map/pallas_call | solution.py:283
  164.8 42.4 %shard_map.324 = (bf16[1024,512]{1,0:T(8,128)(2,1)}, bf16[1024,256]{1,0:T(8,128)(2,1)}, bf16[1024,256]{1,0:T(8,128)(2,1)}, bf16[1024,512]{1,0:T(8,128)(2,1)}, f3...) custom-call(s32[1]{0:T(128)S(6)} %copy.69.length_ref, bf16[1024,2048]{1,0:T(8,128)(2,1)} %bitcast.48, ...), custom_call_target="tpu_custom_call" | custom-call | flops 10000000000 | bytes 20000000 | tf_op jit(solution)/shard_map/pallas_call | solution.py:462
  207.2 49.9 %shard_map.325 = (bf16[2048,2048]{1,0:T(8,128)(2,1)}, bf16[2048,512]{1,0:T(8,128)(2,1)}, bf16[2048,1024]{1,0:T(8,128)(2,1)}, bf16[2048,2048]{1,0:T(8,128)(2,1)}, bf16[2048,2048]{1,0:T(8,128)(2,1)}) custom-call(bf16[256,2048]{1,0:T(8,128)(2,1)} %get-tuple-element.86.x_ref, bf16[2048,2048]{1,0:T(8,128)(2,1)} %bitcast.42, bf16[4,4,128,1536]{3,2,1,0:T(8,128)(2,1)} %bitcast.46), custom_call_target="tpu_custom_call" | custom-call | flops 25769803776 | bytes 60000000 | tf_op jit(solution)/shard_map/pallas_call | solution.py:952
  257.1 19.2 %shard_map.326 = bf16[4,4,128,1536]{3,2,1,0:T(8,128)(2,1)} custom-call(bf16[2048,2048]{1,0:T(8,128)(2,1)} %get-tuple-element.89.x_ref, bf16[2048,2048]{1,0:T(8,128)(2,1)} %bitcast.43, bf16[2048,1024]{1,0:T(8,128)(2,1)} %get-tuple-element.93.dgu_ref, bf16[2048,512]{1,0:T(8,128)(2,1)} %get-tuple-element.94.act_ref), custom_call_target="tpu_custom_call" | custom-call | flops 12884901888 | bytes 40000000 | tf_op jit(solution)/shard_map/pallas_call | solution.py:1043
  276.9 38.1 %all-gather.5.cloned.1.call-done = bf16[2048,1536]{1,0:T(8,128)(2,1)} async-done(((bf16[512,1536]{1,0:T(8,128)(2,1)}), bf16[2048,1536]{1,0:T(8,128)(2,1)}) %all-gather.5.cloned.1.call-update) | async-done | bytes 6291472 | tf_op jit(solution)/shard_map/all_gather | solution.py:1752
  315.0 37.7 %shard_map.327 = (bf16[2048,512]{1,0:T(8,128)(2,1)}, bf16[2048,1024]{1,0:T(8,128)(2,1)}, bf16[2048,2048]{1,0:T(8,128)(2,1)}, bf16[2048,2048]{1,0:T(8,128)(2,1)}) custom-call(bf16[2048,2048]{1,0:T(8,128)(2,1)} %get-tuple-element.89.x_ref, bf16[2048,2048]{1,0:T(8,128)(2,1)} %bitcast.44, bf16[2048,2048]{1,0:T(8,128)(2,1)} %get-tuple-element.90.y0_ref, ...), custom_call_target="tpu_custom_call" | custom-call | flops 25769803776 | bytes 60000000 | tf_op jit(solution)/shard_map/pallas_call | solution.py:1011
  352.7 49.5 %shard_map.328 = (bf16[4,4,128,1536]{3,2,1,0:T(8,128)(2,1)}, f32[256,2048]{1,0:T(8,128)}, bf16[256,2048]{1,0:T(8,128)(2,1)}) custom-call(f32[256,2048]{1,0:T(8,128)} %get-tuple-element.80.hidden_ref, f32[256,2048]{1,0:T(8,128)} %bitcast.37, bf16[2048,1024]{1,0:T(8,128)(2,1)} %get-tuple-element.96.dgu_ref, bf16[2048,512]{1,0:T(8,128)(2,1)} %get-tuple-element.97.act_ref, ...), custom_call_target="tpu_custom_call" | custom-call | flops 12884901888 | bytes 60000000 | tf_op jit(solution)/shard_map/pallas_call | solution.py:1187
  402.2 24.1 %reduce-scatter.4.cloned.1.call-done.refs_0_ = bf16[512,1536]{1,0:T(8,128)(2,1)} async-done(((bf16[2048,1536]{1,0:T(8,128)(2,1)}), bf16[512,1536]{1,0:T(8,128)(2,1)}) %reduce-scatter.4.cloned.1.call-update) | async-done | bytes 1572880 | tf_op jit(solution)/shard_map/reduce_scatter | solution.py:1759
  426.4 116.1 %shard_map.329 = (bf16[4,4,64,1536]{3,2,1,0:T(8,128)(2,1)}, f32[256,2048]{1,0:T(8,128)}, f32[256,2048]{1,0:T(8,128)}) custom-call(s32[1]{0:T(128)S(6)} %copy.69.length_ref, bf16[1024,512]{1,0:T(8,128)(2,1)} %get-tuple-element.81.q_ref, bf16[1024,256]{1,0:T(8,128)(2,1)} %get-tuple-element.82.k_ref, bf16[1024,256]{1,0:T(8,128)(2,1)} %get-tuple-element.83.v_ref, ...), custom_call_target="tpu_custom_call" | custom-call | flops 20000000000 | bytes 40000000 | tf_op jit(solution)/shard_map/pallas_call | solution.py:696
  543.4 0.7 copy-done
  544.3 1.4 copy-done.2
  545.7 3.4 add.38
  549.4 1.2 copy-done.3
  550.6 1.8 multiply_add_fusion
  552.4 37.7 %shard_map.330 = (bf16[512,1536]{1,0:T(8,128)(2,1)}, bf16[512,1536]{1,0:T(8,128)(2,1)}) custom-call(bf16[512,1536]{1,0:T(8,128)(2,1)} %reduce-scatter.4.cloned.1.call-done.refs_0_, bf16[512,1536]{1,0:T(8,128)(2,1)} %reduce-scatter.6.cloned.1.call-done.refs_1_), custom_call_target="tpu_custom_call" | custom-call | tf_op jit(solution)/shard_map/pallas_call | solution.py:114
  590.1 5.2 shard_map.331
  595.3 7.4 %reduce-scatter.8.cloned.1.call-done = bf16[256,1536]{1,0:T(8,128)(2,1)} async-done(((bf16[1024,1536]{1,0:T(8,128)(2,1)}), bf16[256,1536]{1,0:T(8,128)(2,1)}) %reduce-scatter.8.cloned.1.call-update) | async-done | bytes 786448 | tf_op jit(solution)/shard_map/reduce_scatter | solution.py:1773
  602.7 23.3 %shard_map.332 = (bf16[4,64,1536]{2,1,0:T(8,128)(2,1)}, f32[8,128]{1,0:T(8,128)}, f32[64,2]{1,0:T(8,128)}) custom-call(f32[1,1]{1,0:T(1,128)} %get-tuple-element.108.square_ref, f32[64,1]{1,0:T(8,128)} %get-tuple-element.109.terms_ref, f32[64,4096]{1,0:T(8,128)} %refs_0_.1, f32[64,2]{1,0:T(8,128)} %copy.54.gains_ref, bf16[4,64,1536]{2,1,0:T(8,128)(2,1)} %bitcast.40), custom_call_target="tpu_custom_call" | custom-call | tf_op jit(solution)/shard_map/pallas_call | solution.py:1419
  626.0 1.2 slice.3
  627.9 0.8 sqrt_add_fusion
  630.9 17.5 %shard_map.333 = (f32[64,4096]{1,0:T(8,128)}, f32[64,2048]{1,0:T(8,128)}, f32[64,16384]{1,0:T(8,128)}, f32[64,8192]{1,0:T(8,128)}, f32[64,4096]{1,0:T(8,128)}, /...) custom-call(f32[8,128]{1,0:T(8,128)} %get-tuple-element.113.norm_ref, ...), custom_call_target="tpu_custom_call" | custom-call | tf_op jit(solution)/shard_map/pallas_call | solution.py:1689
  (46 shorter events, 5.1 us)
Async XLA Ops:
  7.2 200.0 %all-gather.3.cloned.1.call-start = ((), (), s32[]{:S(2)}) async-start(), calls=%async_computation.3 | async-start | bytes 7864320 | tf_op jit(solution)/shard_map/all_gather | solution.py:1746
  8.6 61.1 %copy-start.6 = (s32[1,256]{1,0:T(1,128)S(1)}, s32[1,256]{1,0:T(1,128)}, u32[]{:S(2)}) copy-start(s32[1,256]{1,0:T(1,128)} %param.22) | copy-start | bytes 3076
  69.6 245.3 %all-gather.5.cloned.1.call-start = ((), (), s32[]{:S(2)}) async-start(), calls=%async_computation.4 | async-start | bytes 7864320 | tf_op jit(solution)/shard_map/all_gather | solution.py:1752
  163.9 262.4 %reduce-scatter.4.cloned.1.call-start = ((), (), s32[]{:S(2)}) async-start(), calls=%async_computation.5 | async-start | bytes 7864320 | tf_op jit(solution)/shard_map/reduce_scatter | solution.py:1759
  276.4 266.1 %reduce-scatter.6.cloned.1.call-start = ((), (), s32[]{:S(2)}) async-start(), calls=%async_computation.6 | async-start | bytes 7864320 | tf_op jit(solution)/shard_map/reduce_scatter | solution.py:1767
  426.3 176.4 %reduce-scatter.8.cloned.1.call-start = ((), (), s32[]{:S(2)}) async-start(), calls=%async_computation.7 | async-start | bytes 3932160 | tf_op jit(solution)/shard_map/reduce_scatter | solution.py:1773
  542.5 0.7 copy-start.7
  542.5 0.8 copy-start.8
  542.5 1.6 copy-start
  544.1 1.6 copy-start.2
  545.7 3.4 copy-start.1
  549.0 1.6 copy-start.3
  595.3 33.5 %copy-start.5 = (f32[64,2]{0,1:T(2,128)S(1)}, f32[64,2]{0,1:T(2,128)}, u32[]{:S(2)}) copy-start(f32[64,2]{0,1:T(2,128)} %param.27) | copy-start | bytes 1540
  595.3 33.6 %copy-start.4 = (f32[64,2]{1,0:T(8,128)S(1)}, f32[64,2]{1,0:T(8,128)}, u32[]{:S(2)}) copy-start(f32[64,2]{1,0:T(8,128)} %copy.54.gains_ref) | copy-start | bytes 1540
Sparse Core Ops, SparseCore 0:
  69.8 129.9 all-gather.2
  201.4 113.5 all-gather.4
  317.3 108.9 reduce-scatter.3
  428.4 111.2 reduce-scatter.5
  542.7 59.9 reduce-scatter.7

commit v8 on v7

--- a/solution.py
+++ b/solution.py
@@ -157,7 +157,7 @@
     return to_right, to_left, x_from_left, x_from_right
 
 
-NEAR_STEPS = 2
+FIRST_STEPS = 1
 
 
 def gather_tokens_kernel(
@@ -182,7 +182,8 @@
     to_core, to_y, to_x = {"seq": core}, {"seq": across}, {"near": beside}
     others = [(seq, near) for near in (beside, n) for seq in ((core + 2) % 4, across, core, s)][:-1]
 
-    meet(*[{"seq": seq, "near": near} for seq, near in others])
+    ends = [{"far": (f + 1) % far_size}, {"far": (f + far_size - 1) % far_size}]
+    meet(*[{"seq": seq, "near": near} for seq, near in others], *ends)
     copies, send = sender(send_sems, recv_sems)
 
     def local(source, target, at):
@@ -190,17 +191,45 @@
         copy.start()
         return copy
 
-    _, _, x_from_left, x_from_right = groups_of(o_ref, far_size, 30, send_sems, recv_sems)
-    for k in range(NEAR_STEPS, far_size):
+    to_right, to_left, x_from_left, x_from_right = groups_of(o_ref, far_size, 30, send_sems, recv_sems)
+
+    def onward(k):
+        for p in range(4):
+
+            @pl.when(f >= k)
+            def _():
+                if k > FIRST_STEPS:
+                    to_right(k - 1, p).wait_recv()
+                x_from_left(k, p).start()
+
+            @pl.when((f >= k) & (f < far_size - 1))
+            def _():
+                to_right(k, p).start()
+
+            @pl.when(f + k < far_size)
+            def _():
+                if k > FIRST_STEPS:
+                    to_left(k - 1, p).wait_recv()
+                x_from_right(k, p).start()
+
+            @pl.when((f + k < far_size) & (f > 0))
+            def _():
+                to_left(k, p).start()
+
+    if FIRST_STEPS < far_size:
+        onward(FIRST_STEPS)
+    for k in range(FIRST_STEPS):
         for p in range(4):
 
             @pl.when(f >= k)
             def _():
                 x_from_left(k, p).start()
 
-            @pl.when(f + k < far_size)
-            def _():
-                x_from_right(k, p).start()
+            if k > 0:
+
+                @pl.when(f + k < far_size)
+                def _():
+                    x_from_right(k, p).start()
 
     keeps = [
         local(x_ref, ox_ref.at[s], 0),
@@ -229,6 +258,8 @@
     send("c1", own(1), block(s, n, 1), to_core)
     for k, (seq, near) in enumerate(others):
         send(("e", k), e_ref.at[seq * 2 + near], oe_ref.at[s * 2 + n], {"seq": seq, "near": near})
+    for k in range(FIRST_STEPS + 1, far_size):
+        onward(k)
     for p in range(2):
         at = pl.ds(p * half, half)
         copies["y", p].wait_recv()
@@ -256,18 +287,29 @@
         copies["i", k].wait_recv()
     for k in range(7):
         copies["e", k].wait_recv()
-    for k in range(NEAR_STEPS, far_size):
+    for k in range(far_size):
         for p in range(4):
+            if k >= FIRST_STEPS:
+
+                @pl.when((f >= k) & (f < far_size - 1))
+                def _():
+                    to_right(k, p).wait_send()
+
+                @pl.when((f + k < far_size) & (f > 0))
+                def _():
+                    to_left(k, p).wait_send()
 
             @pl.when(f >= k)
             def _():
                 x_from_left(k, p).wait_recv()
                 x_from_left(k, p).wait_send()
 
-            @pl.when(f + k < far_size)
-            def _():
-                x_from_right(k, p).wait_recv()
-                x_from_right(k, p).wait_send()
+            if k > 0:
+
+                @pl.when(f + k < far_size)
+                def _():
+                    x_from_right(k, p).wait_recv()
+                    x_from_right(k, p).wait_send()
 
     for copy in copies.values():
         copy.wait_send()
@@ -1529,7 +1571,7 @@
     keep = store(2, heads.at[s], heads_ref.at[s, f, n])
     for seq in (core, across, (core + 2) % 4):
         send(("w", len(copies)), heads.at[seq], heads_ref.at[s, f, n], {"seq": seq})
-    to_right, to_left, x_from_left, x_from_right = groups_of(heads_ref, far_size, 10, send_sems, recv_sems)
+    to_right, to_left, _, _ = groups_of(heads_ref, far_size, 10, send_sems, recv_sems)
     order = (s, core, across, (core + 2) % 4)
 
     def onward(k):
@@ -1558,24 +1600,12 @@
             def _():
                 to_left(k, p).start()
 
-            if k < NEAR_STEPS:
-
-                @pl.when(f >= k)
-                def _():
-                    x_from_left(k, p).start()
-
-                if k > 0:
-
-                    @pl.when(f + k < far_size)
-                    def _():
-                        x_from_right(k, p).start()
-
     onward(0)
     pieces(0, first)
     for k, (seq, near) in enumerate(others):
         send(k, first.at[seq * 2 + near], first_ref.at[mine], {"seq": seq, "near": near})
     stores = [store(0, first.at[mine], first_ref.at[mine])]
-    for k in range(1, min(2, far_size)):
+    for k in range(1, FIRST_STEPS):
         onward(k)
     pieces(1, second)
     stores.append(store(1, second, second_ref))
@@ -1591,15 +1621,23 @@
     lax.fori_loop(0, x.shape[0] // 16, tokens, 0)
     stores.append(store(3, unit, unit_ref))
     stores.append(store(4, low, low_ref))
-    for k in range(2, far_size):
-        onward(k)
+    for p in order:
+
+        @pl.when(f >= FIRST_STEPS)
+        def _():
+            to_right(FIRST_STEPS - 1, p).wait_recv()
+
+        @pl.when(f + FIRST_STEPS < far_size)
+        def _():
+            to_left(FIRST_STEPS - 1, p).wait_recv()
+
     for copy in stores:
         copy.wait()
     for k in range(7):
         copies[k].wait_recv()
     for copy in copies.values():
         copy.wait_send()
-    for k in range(far_size):
+    for k in range(FIRST_STEPS):
         for p in range(4):
 
             @pl.when((f >= k) & (f < far_size - 1))
@@ -1609,20 +1647,6 @@
             @pl.when((f + k < far_size) & (f > 0))
             def _():
                 to_left(k, p).wait_send()
-
-            if k < NEAR_STEPS:
-
-                @pl.when(f >= k)
-                def _():
-                    x_from_left(k, p).wait_recv()
-                    x_from_left(k, p).wait_send()
-
-                if k > 0:
-
-                    @pl.when(f + k < far_size)
-                    def _():
-                        x_from_right(k, p).wait_recv()
-                        x_from_right(k, p).wait_send()
 
 
 def prepare(gains, qkv, out, gateup, down, x, d, collective_id):

time: 659 us -> 646 us (0.980)
  waiting for transfers between devices: 69.7 us -> 38.1 us
  Pallas kernels: 552 us -> 571 us
    pallas_call x1, Pallas kernels: 92.9 us -> 135 us  [gather_tokens(): pl.pallas_call(functools.partial(gather_tokens_kernel, far_size), out_sha...]
    all_gather x2, waiting for transfers between devices: 38.1 us -> 6.49 us  [shards(): lax.all_gather(piece.reshape(group * rows, -1), 'far', axis=0, tiled=True)]
    pallas_call x1, Pallas kernels: 61 us -> 36.6 us  [prepare(): pl.pallas_call(prepare_kernel, out_shape=[jax.ShapeDtypeStruct(*result) f...]
  transfers between devices with their start and end apart: 5 -> 5, of which waited for: 3 -> 3; matrix products, arithmetic and copies ran while one was open for 1% -> 1% of each run, Pallas kernels for 69% -> 77%
where the time goes in v8:
time: 646 us; the launch traced here: 643 us
  Pallas kernels  571 us (88%)
  waiting for transfers between devices  38.1 us (6%)
  between operations  15.6 us (2%)
  local copies, waits for them, and re-layouts  8.84 us (1%)
  other arithmetic  7.77 us (1%)
    pallas_call x1, Pallas kernels, gather_tokens(): pl.pallas_call(functools.partial(gather_tokens_kernel, far_size), out_sha...  135 us
    pallas_call x1, Pallas kernels, attention_back(): pl.pallas_call(attention_back_kernel, out_shape=[jax.ShapeDtypeStruct((fa...  116 us
    pallas_call x1, Pallas kernels, feed_first(): pl.pallas_call(feed_first_kernel, out_shape=[jax.ShapeDtypeStruct((tokens...  51.4 us
    pallas_call x1, Pallas kernels, feed_back(): pl.pallas_call(feed_back_kernel, out_shape=[jax.ShapeDtypeStruct((far, 4,...  49.5 us
    pallas_call x1, Pallas kernels, attention(): pl.pallas_call(attention_kernel, out_shape=[jax.ShapeDtypeStruct(*result)...  42.3 us
    pallas_call x1, Pallas kernels, exchange_plane(): pl.pallas_call(functools.partial(exchange_plane_kernel, count), out_shape...  37.7 us
    pallas_call x1, Pallas kernels, feed_second(): pl.pallas_call(feed_second_kernel, grid=(tokens // tile,), out_shape=[jax...  37.7 us
    pallas_call x1, Pallas kernels, prepare(): pl.pallas_call(prepare_kernel, out_shape=[jax.ShapeDtypeStruct(*result) f...  36.6 us
  transfers between devices with their start and end apart: 5, of which 3 were waited for; matrix products, arithmetic and copies ran while one was open for 1% of the time, Pallas kernels for 77%

profile of v8, /device:TPU:0, one launch (start us, length us, event | category | flops | bytes accessed | tf_op | source)
XLA Modules:
  0.0 642.6 jit_solution(1004891306418131569)
XLA Ops:
  7.2 1.4 copy.54.gains_ref
  8.6 36.6 %shard_map.322 = (bf16[8,64,1536]{2,1,0:T(8,128)(2,1)}, bf16[8,64,1536]{2,1,0:T(8,128)(2,1)}, bf16[4,4,2,64,1536]{4,3,2,1,0:T(8,128)(2,1)}, bf16[256,2048]{1,0:T(8,128)(2,1)}, bf16[256,2048]{1,0:T(8,128)(2,1)}) custom-call(f32[64,2]{1,0:T(8,128)} %copy.54.gains_ref, f32[64,4096]{1,0:T(8,128)} %refs_0_.1, f32[64,2048]{1,0:T(8,128)} %refs_1_.1, ...), custom_call_target="tpu_custom_call" | custom-call | tf_op jit(solution)/shard_map/pallas_call | solution.py:1663
  45.9 0.7 pad_maximum_fusion.i_ref
  46.6 135.0 %shard_map.323 = (bf16[4,4,2,64,1536]{4,3,2,1,0:T(8,128)(2,1)}, bf16[4,256,2048]{2,1,0:T(8,128)(2,1)}, f32[4,256,256]{2,1,0:T(8,128)}, bf16[8,256,2048]{2,1,0:T(8,128)(2,1)}, bf16[8,64,1536]{2,1,0:T(8,128)(2,1)}) custom-call(bf16[4,4,2,64,1536]{4,3,2,1,0:T(8,128)(2,1)} %get-tuple-element.73.w_ref, ...), custom_call_target="tpu_custom_call", output_to_operand_aliasing={{0}: (0, {})} | custom-call | tf_op jit(solution)/shard_map/pallas_call | solution.py:325
  182.5 42.3 %shard_map.324 = (bf16[1024,512]{1,0:T(8,128)(2,1)}, bf16[1024,256]{1,0:T(8,128)(2,1)}, bf16[1024,256]{1,0:T(8,128)(2,1)}, bf16[1024,512]{1,0:T(8,128)(2,1)}, f3...) custom-call(s32[1]{0:T(128)S(6)} %copy.69.length_ref, bf16[1024,2048]{1,0:T(8,128)(2,1)} %bitcast.48, ...), custom_call_target="tpu_custom_call" | custom-call | flops 10000000000 | bytes 20000000 | tf_op jit(solution)/shard_map/pallas_call | solution.py:504
  224.9 51.4 %shard_map.325 = (bf16[2048,2048]{1,0:T(8,128)(2,1)}, bf16[2048,512]{1,0:T(8,128)(2,1)}, bf16[2048,1024]{1,0:T(8,128)(2,1)}, bf16[2048,2048]{1,0:T(8,128)(2,1)}, bf16[2048,2048]{1,0:T(8,128)(2,1)}) custom-call(bf16[256,2048]{1,0:T(8,128)(2,1)} %get-tuple-element.86.x_ref, bf16[2048,2048]{1,0:T(8,128)(2,1)} %bitcast.42, bf16[4,4,128,1536]{3,2,1,0:T(8,128)(2,1)} %bitcast.46), custom_call_target="tpu_custom_call" | custom-call | flops 25769803776 | bytes 60000000 | tf_op jit(solution)/shard_map/pallas_call | solution.py:994
  276.3 19.2 %shard_map.326 = bf16[4,4,128,1536]{3,2,1,0:T(8,128)(2,1)} custom-call(bf16[2048,2048]{1,0:T(8,128)(2,1)} %get-tuple-element.89.x_ref, bf16[2048,2048]{1,0:T(8,128)(2,1)} %bitcast.43, bf16[2048,1024]{1,0:T(8,128)(2,1)} %get-tuple-element.93.dgu_ref, bf16[2048,512]{1,0:T(8,128)(2,1)} %get-tuple-element.94.act_ref), custom_call_target="tpu_custom_call" | custom-call | flops 12884901888 | bytes 40000000 | tf_op jit(solution)/shard_map/pallas_call | solution.py:1085
  296.0 6.5 %all-gather.5.cloned.1.call-done = bf16[2048,1536]{1,0:T(8,128)(2,1)} async-done(((bf16[512,1536]{1,0:T(8,128)(2,1)}), bf16[2048,1536]{1,0:T(8,128)(2,1)}) %all-gather.5.cloned.1.call-update) | async-done | bytes 6291472 | tf_op jit(solution)/shard_map/all_gather | solution.py:1776
  302.4 37.7 %shard_map.327 = (bf16[2048,512]{1,0:T(8,128)(2,1)}, bf16[2048,1024]{1,0:T(8,128)(2,1)}, bf16[2048,2048]{1,0:T(8,128)(2,1)}, bf16[2048,2048]{1,0:T(8,128)(2,1)}) custom-call(bf16[2048,2048]{1,0:T(8,128)(2,1)} %get-tuple-element.89.x_ref, bf16[2048,2048]{1,0:T(8,128)(2,1)} %bitcast.44, bf16[2048,2048]{1,0:T(8,128)(2,1)} %get-tuple-element.90.y0_ref, ...), custom_call_target="tpu_custom_call" | custom-call | flops 25769803776 | bytes 60000000 | tf_op jit(solution)/shard_map/pallas_call | solution.py:1053
  340.2 49.5 %shard_map.328 = (bf16[4,4,128,1536]{3,2,1,0:T(8,128)(2,1)}, f32[256,2048]{1,0:T(8,128)}, bf16[256,2048]{1,0:T(8,128)(2,1)}) custom-call(f32[256,2048]{1,0:T(8,128)} %get-tuple-element.80.hidden_ref, f32[256,2048]{1,0:T(8,128)} %bitcast.37, bf16[2048,1024]{1,0:T(8,128)(2,1)} %get-tuple-element.96.dgu_ref, bf16[2048,512]{1,0:T(8,128)(2,1)} %get-tuple-element.97.act_ref, ...), custom_call_target="tpu_custom_call" | custom-call | flops 12884901888 | bytes 60000000 | tf_op jit(solution)/shard_map/pallas_call | solution.py:1229
  389.6 24.1 %reduce-scatter.4.cloned.1.call-done.refs_0_ = bf16[512,1536]{1,0:T(8,128)(2,1)} async-done(((bf16[2048,1536]{1,0:T(8,128)(2,1)}), bf16[512,1536]{1,0:T(8,128)(2,1)}) %reduce-scatter.4.cloned.1.call-update) | async-done | bytes 1572880 | tf_op jit(solution)/shard_map/reduce_scatter | solution.py:1783
  413.8 116.1 %shard_map.329 = (bf16[4,4,64,1536]{3,2,1,0:T(8,128)(2,1)}, f32[256,2048]{1,0:T(8,128)}, f32[256,2048]{1,0:T(8,128)}) custom-call(s32[1]{0:T(128)S(6)} %copy.69.length_ref, bf16[1024,512]{1,0:T(8,128)(2,1)} %get-tuple-element.81.q_ref, bf16[1024,256]{1,0:T(8,128)(2,1)} %get-tuple-element.82.k_ref, bf16[1024,256]{1,0:T(8,128)(2,1)} %get-tuple-element.83.v_ref, ...), custom_call_target="tpu_custom_call" | custom-call | flops 20000000000 | bytes 40000000 | tf_op jit(solution)/shard_map/pallas_call | solution.py:738
  530.8 0.7 copy-done
  531.8 1.4 copy-done.2
  533.2 3.4 add.38
  536.9 1.2 copy-done.3
  538.1 1.8 multiply_add_fusion
  539.9 37.7 %shard_map.330 = (bf16[512,1536]{1,0:T(8,128)(2,1)}, bf16[512,1536]{1,0:T(8,128)(2,1)}) custom-call(bf16[512,1536]{1,0:T(8,128)(2,1)} %reduce-scatter.4.cloned.1.call-done.refs_0_, bf16[512,1536]{1,0:T(8,128)(2,1)} %reduce-scatter.6.cloned.1.call-done.refs_1_), custom_call_target="tpu_custom_call" | custom-call | tf_op jit(solution)/shard_map/pallas_call | solution.py:114
  577.6 5.2 shard_map.331
  582.8 7.4 %reduce-scatter.8.cloned.1.call-done = bf16[256,1536]{1,0:T(8,128)(2,1)} async-done(((bf16[1024,1536]{1,0:T(8,128)(2,1)}), bf16[256,1536]{1,0:T(8,128)(2,1)}) %reduce-scatter.8.cloned.1.call-update) | async-done | bytes 786448 | tf_op jit(solution)/shard_map/reduce_scatter | solution.py:1797
  590.2 23.3 %shard_map.332 = (bf16[4,64,1536]{2,1,0:T(8,128)(2,1)}, f32[8,128]{1,0:T(8,128)}, f32[64,2]{1,0:T(8,128)}) custom-call(f32[1,1]{1,0:T(1,128)} %get-tuple-element.108.square_ref, f32[64,1]{1,0:T(8,128)} %get-tuple-element.109.terms_ref, f32[64,4096]{1,0:T(8,128)} %refs_0_.1, f32[64,2]{1,0:T(8,128)} %copy.54.gains_ref, bf16[4,64,1536]{2,1,0:T(8,128)(2,1)} %bitcast.40), custom_call_target="tpu_custom_call" | custom-call | tf_op jit(solution)/shard_map/pallas_call | solution.py:1461
  613.5 1.2 slice.3
  615.3 0.8 sqrt_add_fusion
  618.3 17.5 %shard_map.333 = (f32[64,4096]{1,0:T(8,128)}, f32[64,2048]{1,0:T(8,128)}, f32[64,16384]{1,0:T(8,128)}, f32[64,8192]{1,0:T(8,128)}, f32[64,4096]{1,0:T(8,128)}, /...) custom-call(f32[8,128]{1,0:T(8,128)} %get-tuple-element.113.norm_ref, ...), custom_call_target="tpu_custom_call" | custom-call | tf_op jit(solution)/shard_map/pallas_call | solution.py:1713
  (46 shorter events, 5.1 us)
Async XLA Ops:
  7.2 217.7 %all-gather.3.cloned.1.call-start = ((), (), s32[]{:S(2)}) async-start(), calls=%async_computation.3 | async-start | bytes 7864320 | tf_op jit(solution)/shard_map/all_gather | solution.py:1770
  8.6 36.7 %copy-start.6 = (s32[1,256]{1,0:T(1,128)S(1)}, s32[1,256]{1,0:T(1,128)}, u32[]{:S(2)}) copy-start(s32[1,256]{1,0:T(1,128)} %param.22) | copy-start | bytes 3076
  45.2 257.2 %all-gather.5.cloned.1.call-start = ((), (), s32[]{:S(2)}) async-start(), calls=%async_computation.4 | async-start | bytes 7864320 | tf_op jit(solution)/shard_map/all_gather | solution.py:1776
  181.6 232.2 %reduce-scatter.4.cloned.1.call-start = ((), (), s32[]{:S(2)}) async-start(), calls=%async_computation.5 | async-start | bytes 7864320 | tf_op jit(solution)/shard_map/reduce_scatter | solution.py:1783
  295.5 234.6 %reduce-scatter.6.cloned.1.call-start = ((), (), s32[]{:S(2)}) async-start(), calls=%async_computation.6 | async-start | bytes 7864320 | tf_op jit(solution)/shard_map/reduce_scatter | solution.py:1791
  413.8 176.4 %reduce-scatter.8.cloned.1.call-start = ((), (), s32[]{:S(2)}) async-start(), calls=%async_computation.7 | async-start | bytes 3932160 | tf_op jit(solution)/shard_map/reduce_scatter | solution.py:1797
  530.0 0.7 copy-start.7
  530.0 0.8 copy-start.8
  530.0 1.6 copy-start
  531.6 1.6 copy-start.2
  533.2 3.4 copy-start.1
  536.5 1.6 copy-start.3
  582.8 33.5 %copy-start.5 = (f32[64,2]{0,1:T(2,128)S(1)}, f32[64,2]{0,1:T(2,128)}, u32[]{:S(2)}) copy-start(f32[64,2]{0,1:T(2,128)} %param.27) | copy-start | bytes 1540
  582.8 33.6 %copy-start.4 = (f32[64,2]{1,0:T(8,128)S(1)}, f32[64,2]{1,0:T(8,128)}, u32[]{:S(2)}) copy-start(f32[64,2]{1,0:T(8,128)} %copy.54.gains_ref) | copy-start | bytes 1540
Sparse Core Ops, SparseCore 0:
  45.4 140.1 all-gather.2
  187.1 115.2 all-gather.4
  304.7 108.9 reduce-scatter.3
  415.9 111.2 reduce-scatter.5
  530.2 59.9 reduce-scatter.7

commit v9 on v8

--- a/solution.py
+++ b/solution.py
@@ -1398,7 +1398,7 @@
         send(("w", k), p_ref.at[seq], mine.at[s], seqs[k])
     keep = pltpu.make_async_copy(p_ref.at[s], mine.at[s], local_sem)
     keep.start()
-    gains = gains_ref[...].astype(jnp.bfloat16).astype(jnp.float32)
+    one = as_column(gains_ref[0:1, :].astype(jnp.bfloat16).astype(jnp.float32))
     qkv, out = head_pieces_of(head_ref.shape[2])
     keep.wait()
     for k in range(3):
@@ -1416,10 +1416,9 @@
     for device, at, column, size in out:
         grad = mine[device, :, at : at + size].astype(jnp.float32)
         out_squares = out_squares + over(grad * grad)
-    one = gains[:, 0:1]
     rows = one * one * one_squares + out_squares + one_terms * one_terms
-    gain_grads_ref[:, 0:1] = one_terms
-    gain_grads_ref[:, 1:2] = terms_ref[...]
+    gain_grads_ref[0:1, :] = as_row(one_terms)
+    gain_grads_ref[1:2, :] = as_row(terms_ref[...])
     total = jnp.sum(rows) + square_ref[0, 0]
 
     plane_parts[s, n] = jnp.full(plane_parts.shape[2:], total, jnp.float32)
@@ -1450,7 +1449,7 @@
     everywhere = far_parts[0]
     for k in range(1, far_size):
         everywhere = everywhere + far_parts[k]
-    norm_ref[...] = jnp.sqrt(everywhere)
+    norm_ref[0, 0] = jnp.max(jnp.sqrt(everywhere))
     for copy in (*copies.values(), *far_copies):
         copy.wait_send()
 
@@ -1462,11 +1461,11 @@
         settle_kernel,
         out_shape=[
             jax.ShapeDtypeStruct(p.shape, p.dtype),
-            jax.ShapeDtypeStruct(tile, jnp.float32),
+            jax.ShapeDtypeStruct((1, 1), jnp.float32),
             jax.ShapeDtypeStruct(gains.shape, jnp.float32),
         ],
         in_specs=[pl.BlockSpec(memory_space=pltpu.SMEM)] + [IN_VMEM] * 3 + [ANYWHERE],
-        out_specs=[IN_VMEM] * 3,
+        out_specs=[IN_VMEM, pl.BlockSpec(memory_space=pltpu.SMEM), IN_VMEM],
         scratch_shapes=[
             pltpu.VMEM(p.shape, p.dtype),
             pltpu.VMEM((4, 2, *tile), jnp.float32),
@@ -1481,6 +1480,19 @@
             collective_id=collective_id, has_side_effects=True, vmem_limit_bytes=VMEM_LIMIT
         ),
     )(square, terms, qkv, gains, p)
+
+
+def diagonal_of(size):
+    shape = (size, size)
+    return lax.broadcasted_iota(jnp.int32, shape, 0) == lax.broadcasted_iota(jnp.int32, shape, 1)
+
+
+def as_column(row):
+    return jnp.sum(jnp.where(diagonal_of(row.shape[1]), row, 0.0), 1, keepdims=True)
+
+
+def as_row(column):
+    return jnp.sum(jnp.where(diagonal_of(column.shape[0]), column, 0.0), 0, keepdims=True)
 
 
 def prepare_kernel(
@@ -1538,7 +1550,7 @@
         loads.append(load(3 * c + 2, down_ref.at[:, columns], down.at[:, columns]))
     load_tokens = [load(8, x_ref, x), load(9, d_ref, d)]
     gains = gains_ref[...].astype(half).astype(jnp.float32)
-    one, two = gains[:, 0:1], gains[:, 1:2]
+    one, two = as_column(gains[0:1, :]), as_column(gains[1:2, :])
 
     def rounded(weight, gain=None):
         weight = weight.astype(half)
@@ -1650,7 +1662,7 @@
 
 
 def prepare(gains, qkv, out, gateup, down, x, d, collective_id):
-    rows = gains.shape[0]
+    rows = gains.shape[1]
     tokens, width = x.shape
     low = jnp.bfloat16
     part = FEED_UNITS // 16
@@ -1685,7 +1697,7 @@
     part = zero_ref.shape[2] // 3
     gateup, down = feed_pieces(part)
     qkv, out = head_pieces_of(head_ref.shape[2])
-    clip = CLIP_NORM / jnp.maximum(norm_ref[0:1, 0:1], CLIP_NORM)
+    clip = CLIP_NORM / jnp.maximum(jnp.full((1, 1), norm_ref[0, 0], jnp.float32), CLIP_NORM)
     gains = gains_ref[...].astype(jnp.bfloat16).astype(jnp.float32) * clip
     one, two = gains[:, 0:1], gains[:, 1:2]
 
@@ -1714,7 +1726,7 @@
         adam_kernel,
         grid=(gains.shape[0] // ROWS,),
         out_shape=[jax.ShapeDtypeStruct(x.shape, x.dtype) for x in state],
-        in_specs=[pl.BlockSpec(norm.shape, lambda r: (0, 0))] + [rows_of(x) for x in arrays],
+        in_specs=[pl.BlockSpec(memory_space=pltpu.SMEM)] + [rows_of(x) for x in arrays],
         out_specs=[rows_of(x) for x in state],
         compiler_params=pltpu.CompilerParams(vmem_limit_bytes=VMEM_LIMIT),
     )(norm, *arrays)
@@ -1765,7 +1777,7 @@
 
     turns = rotary_tables(positions.reshape(-1), HEAD_SIZE)
     piece, second_pieces, head_w, unit_one, dout_here = prepare(
-        norm_gains, query_key_value_weight, out_weight, gateup_weight, down_weight, inputs, cotangent, 1
+        norm_gains.T, query_key_value_weight, out_weight, gateup_weight, down_weight, inputs, cotangent, 1
     )
     feed_zero = lax.all_gather(piece.reshape(group * rows, -1), "far", axis=0, tiled=True)
     feed_zero = feed_zero.reshape(by_far)
@@ -1788,30 +1800,31 @@
         hidden, cotangent, dgateup, act, normed_two, dout, dnormed_two, far, 5
     )
     terms = terms.reshape(width, 3 * part)
-    grads_one = lax.psum_scatter(after(terms, grads_zero), "far", scatter_dimension=0, tiled=True)
+    grads_one = lax.psum_scatter(terms, "far", scatter_dimension=0, tiled=True)
 
     head_terms, dnormed_one, output_terms = attention_back(
         lengths, saved, all_turns, dattended, output_terms, head_w, normed_one, 6
     )
-    head_terms = after(head_terms, grads_zero, grads_one)
+    zero = exchange_plane([grads_zero], 7)
+    head_terms = after(head_terms, zero[0], grads_one)
     head_terms = lax.psum_scatter(
         head_terms.reshape(far * seq * rows, -1), "far", scatter_dimension=0, tiled=True
     )
     input_grad = dhidden + norm_backward(dnormed_one, *rms_normalize(inputs))
     layer_output = hidden + output_terms
 
-    halves = [x.reshape(group, rows, 3 * part) for x in exchange_plane([grads_zero, grads_one], 7)]
+    halves = [x.reshape(group, rows, 3 * part) for x in (*zero, *exchange_plane([grads_one], 7))]
     square, gain_terms = feed_norm(*halves, gateup_weight, norm_gains)
     head_terms = after(head_terms, square, input_grad, layer_output)
     head_grads, norm, gain_grads = settle(
-        square, gain_terms, query_key_value_weight, norm_gains, head_terms.reshape(seq, rows, -1), 8
+        square, gain_terms, query_key_value_weight, norm_gains.T, head_terms.reshape(seq, rows, -1), 8
     )
     weights = (query_key_value_weight, out_weight, gateup_weight, down_weight)
     firsts = (query_key_value_moment, output_weight_moment, gate_up_moment, down_weight_moment)
     seconds = (query_key_value_variance, out_second, gateup_second, down_second)
     stepped = adam(norm, norm_gains, *halves, head_grads, weights, firsts, seconds)
     grad_norm = norm[0, 0]
-    gain_grads = gain_grads * (CLIP_NORM / jnp.maximum(grad_norm, CLIP_NORM))
+    gain_grads = gain_grads.T * (CLIP_NORM / jnp.maximum(grad_norm, CLIP_NORM))
     gains = adam_step(norm_gains, gain_grads, norm_gains_moment, gains_second, RATE_GAIN, 0.0)
     state = [x for k in range(3) for x in (*stepped[4 * k : 4 * k + 4], gains[k])]
     return (layer_output[None], input_grad[None], grad_norm, *state)

time: 646 us -> 644 us (level)
    reduce_scatter x1, waiting for transfers between devices: 24.1 us -> 0.02 us  [shards(): grads_zero = lax.psum_scatter(terms, 'far', scatter_dimension=0, tiled=True)]
    reduce_scatter x1, waiting for transfers between devices: 7.38 us -> 27.4 us  [shards(): lax.psum_scatter(head_terms.reshape(far * seq * rows, -1), 'far', scatter...]
    pallas_call x1 -> x2, Pallas kernels: 37.7 us -> 42.9 us  [exchange_plane(): pl.pallas_call(functools.partial(exchange_plane_kernel, count), out_shape...]
  transfers between devices with their start and end apart: 5 -> 5, of which waited for: 3 -> 3; matrix products, arithmetic and copies ran while one was open for 1% -> 1% of each run, Pallas kernels for 77% -> 78%
where the time goes in v9:
time: 644 us; the launch traced here: 640 us
  Pallas kernels  576 us (89%)
  waiting for transfers between devices  34.6 us (5%)
  between operations  17.2 us (3%)
  other arithmetic  8.21 us (1%)
    pallas_call x1, Pallas kernels, gather_tokens(): pl.pallas_call(functools.partial(gather_tokens_kernel, far_size), out_sha...  135 us
    pallas_call x1, Pallas kernels, attention_back(): pl.pallas_call(attention_back_kernel, out_shape=[jax.ShapeDtypeStruct((fa...  115 us
    pallas_call x1, Pallas kernels, feed_first(): pl.pallas_call(feed_first_kernel, out_shape=[jax.ShapeDtypeStruct((tokens...  51.3 us
    pallas_call x1, Pallas kernels, feed_back(): pl.pallas_call(feed_back_kernel, out_shape=[jax.ShapeDtypeStruct((far, 4,...  49.5 us
    pallas_call x2, Pallas kernels, exchange_plane(): pl.pallas_call(functools.partial(exchange_plane_kernel, count), out_shape...  42.9 us
    pallas_call x1, Pallas kernels, attention(): pl.pallas_call(attention_kernel, out_shape=[jax.ShapeDtypeStruct(*result)...  42.3 us
    pallas_call x1, Pallas kernels, feed_second(): pl.pallas_call(feed_second_kernel, grid=(tokens // tile,), out_shape=[jax...  37.7 us
    pallas_call x1, Pallas kernels, prepare(): pl.pallas_call(prepare_kernel, out_shape=[jax.ShapeDtypeStruct(*result) f...  36.5 us
  transfers between devices with their start and end apart: 5, of which 3 were waited for; matrix products, arithmetic and copies ran while one was open for 1% of the time, Pallas kernels for 78%

profile of v9, /device:TPU:0, one launch (start us, length us, event | category | flops | bytes accessed | tf_op | source)
XLA Modules:
  0.0 640.3 jit_solution(5524605711719219940)
XLA Ops:
  7.2 36.5 %shard_map.322 = (bf16[8,64,1536]{2,1,0:T(8,128)(2,1)}, bf16[8,64,1536]{2,1,0:T(8,128)(2,1)}, bf16[4,4,2,64,1536]{4,3,2,1,0:T(8,128)(2,1)}, bf16[256,2048]{1,0:T(8,128)(2,1)}, bf16[256,2048]{1,0:T(8,128)(2,1)}) custom-call(f32[2,64]{1,0:T(2,128)} %bitcast.49, f32[64,4096]{1,0:T(8,128)} %refs_0_.1, f32[64,2048]{1,0:T(8,128)} %refs_1_.1, f32[64,16384]{1,0:T(8,128)} %refs_2_.1, ...), custom_call_target="tpu_custom_call" | custom-call | tf_op jit(solution)/shard_map/pallas_call | solution.py:1675
  43.9 0.5 multiply_cosine_fusion
  44.4 0.7 pad_maximum_fusion.i_ref
  45.1 134.9 %shard_map.323 = (bf16[4,4,2,64,1536]{4,3,2,1,0:T(8,128)(2,1)}, bf16[4,256,2048]{2,1,0:T(8,128)(2,1)}, f32[4,256,256]{2,1,0:T(8,128)}, bf16[8,256,2048]{2,1,0:T(8,128)(2,1)}, bf16[8,64,1536]{2,1,0:T(8,128)(2,1)}) custom-call(bf16[4,4,2,64,1536]{4,3,2,1,0:T(8,128)(2,1)} %get-tuple-element.70.w_ref, ...), custom_call_target="tpu_custom_call", output_to_operand_aliasing={{0}: (0, {})} | custom-call | tf_op jit(solution)/shard_map/pallas_call | solution.py:325
  181.0 42.3 %shard_map.324 = (bf16[1024,512]{1,0:T(8,128)(2,1)}, bf16[1024,256]{1,0:T(8,128)(2,1)}, bf16[1024,256]{1,0:T(8,128)(2,1)}, bf16[1024,512]{1,0:T(8,128)(2,1)}, f3...) custom-call(s32[1]{0:T(128)S(6)} %copy.42.length_ref, bf16[1024,2048]{1,0:T(8,128)(2,1)} %bitcast.58, ...), custom_call_target="tpu_custom_call" | custom-call | flops 10000000000 | bytes 20000000 | tf_op jit(solution)/shard_map/pallas_call | solution.py:504
  223.3 51.3 %shard_map.325 = (bf16[2048,2048]{1,0:T(8,128)(2,1)}, bf16[2048,512]{1,0:T(8,128)(2,1)}, bf16[2048,1024]{1,0:T(8,128)(2,1)}, bf16[2048,2048]{1,0:T(8,128)(2,1)}, bf16[2048,2048]{1,0:T(8,128)(2,1)}) custom-call(bf16[256,2048]{1,0:T(8,128)(2,1)} %get-tuple-element.83.x_ref, bf16[2048,2048]{1,0:T(8,128)(2,1)} %bitcast.52, bf16[4,4,128,1536]{3,2,1,0:T(8,128)(2,1)} %bitcast.56), custom_call_target="tpu_custom_call" | custom-call | flops 25769803776 | bytes 60000000 | tf_op jit(solution)/shard_map/pallas_call | solution.py:994
  274.7 19.1 %shard_map.326 = bf16[4,4,128,1536]{3,2,1,0:T(8,128)(2,1)} custom-call(bf16[2048,2048]{1,0:T(8,128)(2,1)} %get-tuple-element.86.x_ref, bf16[2048,2048]{1,0:T(8,128)(2,1)} %bitcast.53, bf16[2048,1024]{1,0:T(8,128)(2,1)} %get-tuple-element.90.dgu_ref, bf16[2048,512]{1,0:T(8,128)(2,1)} %get-tuple-element.91.act_ref), custom_call_target="tpu_custom_call" | custom-call | flops 12884901888 | bytes 40000000 | tf_op jit(solution)/shard_map/pallas_call | solution.py:1085
  293.8 0.6 reduce-scatter.6.cloned.1.call-start
  294.4 6.6 %all-gather.5.cloned.1.call-done = bf16[2048,1536]{1,0:T(8,128)(2,1)} async-done(((bf16[512,1536]{1,0:T(8,128)(2,1)}), bf16[2048,1536]{1,0:T(8,128)(2,1)}) %all-gather.5.cloned.1.call-update) | async-done | bytes 6291472 | tf_op jit(solution)/shard_map/all_gather | solution.py:1788
  301.0 37.7 %shard_map.327 = (bf16[2048,512]{1,0:T(8,128)(2,1)}, bf16[2048,1024]{1,0:T(8,128)(2,1)}, bf16[2048,2048]{1,0:T(8,128)(2,1)}, bf16[2048,2048]{1,0:T(8,128)(2,1)}) custom-call(bf16[2048,2048]{1,0:T(8,128)(2,1)} %get-tuple-element.86.x_ref, bf16[2048,2048]{1,0:T(8,128)(2,1)} %bitcast.54, bf16[2048,2048]{1,0:T(8,128)(2,1)} %get-tuple-element.87.y0_ref, ...), custom_call_target="tpu_custom_call" | custom-call | flops 25769803776 | bytes 60000000 | tf_op jit(solution)/shard_map/pallas_call | solution.py:1053
  338.7 49.5 %shard_map.328 = (bf16[4,4,128,1536]{3,2,1,0:T(8,128)(2,1)}, f32[256,2048]{1,0:T(8,128)}, bf16[256,2048]{1,0:T(8,128)(2,1)}) custom-call(f32[256,2048]{1,0:T(8,128)} %get-tuple-element.77.hidden_ref, f32[256,2048]{1,0:T(8,128)} %bitcast.45, bf16[2048,1024]{1,0:T(8,128)(2,1)} %get-tuple-element.93.dgu_ref, bf16[2048,512]{1,0:T(8,128)(2,1)} %get-tuple-element.94.act_ref, ...), custom_call_target="tpu_custom_call" | custom-call | flops 12884901888 | bytes 60000000 | tf_op jit(solution)/shard_map/pallas_call | solution.py:1229
  388.2 114.9 %shard_map.329 = (bf16[4,4,64,1536]{3,2,1,0:T(8,128)(2,1)}, f32[256,2048]{1,0:T(8,128)}, f32[256,2048]{1,0:T(8,128)}) custom-call(s32[1]{0:T(128)S(6)} %copy.42.length_ref, bf16[1024,512]{1,0:T(8,128)(2,1)} %get-tuple-element.78.q_ref, bf16[1024,256]{1,0:T(8,128)(2,1)} %get-tuple-element.79.k_ref, bf16[1024,256]{1,0:T(8,128)(2,1)} %get-tuple-element.80.v_ref, ...), custom_call_target="tpu_custom_call" | custom-call | flops 20000000000 | bytes 40000000 | tf_op jit(solution)/shard_map/pallas_call | solution.py:738
  503.2 22.0 %shard_map.330 = bf16[512,1536]{1,0:T(8,128)(2,1)} custom-call(bf16[512,1536]{1,0:T(8,128)(2,1)} %reduce-scatter.4.cloned.1.call-done.refs_0_), custom_call_target="tpu_custom_call" | custom-call | tf_op jit(solution)/shard_map/pallas_call | solution.py:114
  525.9 0.7 copy.38.gains_ref
  527.1 1.4 copy-done.2
  528.5 3.4 add.38
  532.2 1.2 copy-done.3
  533.4 1.8 multiply_add_fusion
  535.2 20.9 %shard_map.331 = bf16[512,1536]{1,0:T(8,128)(2,1)} custom-call(bf16[512,1536]{1,0:T(8,128)(2,1)} %reduce-scatter.6.cloned.1.call-done.refs_0_), custom_call_target="tpu_custom_call" | custom-call | tf_op jit(solution)/shard_map/pallas_call | solution.py:114
  556.1 5.2 shard_map.332
  561.3 27.4 %reduce-scatter.8.cloned.1.call-done = bf16[256,1536]{1,0:T(8,128)(2,1)} async-done(((bf16[1024,1536]{1,0:T(8,128)(2,1)}), bf16[256,1536]{1,0:T(8,128)(2,1)}) %reduce-scatter.8.cloned.1.call-update) | async-done | bytes 786448 | tf_op jit(solution)/shard_map/reduce_scatter | solution.py:1810
  588.7 23.4 %shard_map.333 = (bf16[4,64,1536]{2,1,0:T(8,128)(2,1)}, f32[1,1]{1,0:T(1,128)}, f32[2,64]{1,0:T(2,128)}) custom-call(f32[1,1]{1,0:T(1,128)} %get-tuple-element.102.square_ref, f32[64,1]{1,0:T(8,128)} %get-tuple-element.103.terms_ref, f32[64,4096]{1,0:T(8,128)} %refs_0_.1, f32[2,64]{1,0:T(2,128)} %bitcast.50, bf16[4,64,1536]{2,1,0:T(8,128)(2,1)} %bitcast.48), custom_call_target="tpu_custom_call" | custom-call | tf_op jit(solution)/shard_map/pallas_call | solution.py:1460
  612.7 1.3 add_subtract_fusion
  614.0 17.9 %shard_map.334 = (f32[64,4096]{1,0:T(8,128)}, f32[64,2048]{1,0:T(8,128)}, f32[64,16384]{1,0:T(8,128)}, f32[64,8192]{1,0:T(8,128)}, f32[64,4096]{1,0:T(8,128)}, /...) custom-call(f32[1,1]{1,0:T(1,128)} %get-tuple-element.107.norm_ref, ...), custom_call_target="tpu_custom_call" | custom-call | tf_op jit(solution)/shard_map/pallas_call | solution.py:1725
  (34 shorter events, 2.1 us)
Async XLA Ops:
  7.2 216.1 %all-gather.3.cloned.1.call-start = ((), (), s32[]{:S(2)}) async-start(), calls=%async_computation.3 | async-start | bytes 7864320 | tf_op jit(solution)/shard_map/all_gather | solution.py:1782
  7.2 36.6 %copy-start.8 = (s32[1,256]{1,0:T(1,128)S(1)}, s32[1,256]{1,0:T(1,128)}, u32[]{:S(2)}) copy-start(s32[1,256]{1,0:T(1,128)} %param.22) | copy-start | bytes 3076
  43.8 257.2 %all-gather.5.cloned.1.call-start = ((), (), s32[]{:S(2)}) async-start(), calls=%async_computation.4 | async-start | bytes 7864320 | tf_op jit(solution)/shard_map/all_gather | solution.py:1788
  180.1 323.1 %reduce-scatter.4.cloned.1.call-start = ((), (), s32[]{:S(2)}) async-start(), calls=%async_computation.5 | async-start | bytes 7864320 | tf_op jit(solution)/shard_map/reduce_scatter | solution.py:1795
  293.8 231.9 %reduce-scatter.6.cloned.1.call-start = ((), (), s32[]{:S(2)}) async-start(), calls=%async_computation.6 | async-start | bytes 7864320 | tf_op jit(solution)/shard_map/reduce_scatter | solution.py:1803
  388.2 200.5 %reduce-scatter.8.cloned.1.call-start = ((), (), s32[]{:S(2)}) async-start(), calls=%async_computation.7 | async-start | bytes 3932160 | tf_op jit(solution)/shard_map/reduce_scatter | solution.py:1810
  525.2 0.7 copy-start.4
  525.2 1.6 copy-start
  526.9 1.6 copy-start.2
  528.5 3.4 copy-start.1
  531.8 1.6 copy-start.3
  556.1 56.6 %copy-start.5 = (f32[64,2]{0,1:T(2,128)S(1)}, f32[64,2]{0,1:T(2,128)}, u32[]{:S(2)}) copy-start(f32[64,2]{0,1:T(2,128)} %param.27) | copy-start | bytes 1540
  556.1 56.6 %copy-start.6 = (f32[64,2]{0,1:T(2,128)S(1)}, f32[64,2]{0,1:T(2,128)}, u32[]{:S(2)}) copy-start(f32[64,2]{0,1:T(2,128)} %param.32) | copy-start | bytes 1540
  556.1 56.6 %copy-start.7 = (f32[64,2]{0,1:T(2,128)S(1)}, f32[64,2]{0,1:T(2,128)}, u32[]{:S(2)}) copy-start(f32[64,2]{0,1:T(2,128)} %param.37) | copy-start | bytes 1540
Sparse Core Ops, SparseCore 0:
  43.9 140.0 all-gather.2
  185.6 115.2 all-gather.4
  303.3 108.9 reduce-scatter.3
  414.4 111.2 reduce-scatter.5
  527.9 60.7 reduce-scatter.7
